TPU v7x, 128 devices: a whole 4x4x4 slice. The times are simulated.
128 devices in a mesh: section: 2 (over core), seq: 16 (over y, x), wshard: 4 (over z).
Axes of the slice: x: 4, y: 4, z: 4, core: 2. Of those that a mesh axis runs over, the one named last changes fastest.
Arguments:
- inputs: float32 [2, 4, 2048, 1024], P(None, 'wshard', 'seq'), may hold values from -6 to 6
- cotangent: float32 [2, 4, 2048, 1024], P(None, 'wshard', 'seq'), may hold values from -6 to 6
- segments: int32 [2, 4, 2048], P(None, 'wshard'), may hold values from 0 to 8, as said below
- norm_gains: float32 [2, 2, 1024], P('section'), may hold values from 0.5 to 1.5
- attend_in: bfloat16 [2, 1024, 3072], P('section', 'wshard'), may hold values from -0.1875 to 0.1875
- attend_out: bfloat16 [2, 1024, 1024], P('section', 'wshard'), may hold values from -2 to 2
- hidden_in: bfloat16 [2, 1024, 5248], P('section', 'wshard'), may hold values from -0.1875 to 0.1875
- hidden_out: bfloat16 [2, 2624, 1024], P('section', 'wshard'), may hold values from -0.125 to 0.125
Outputs:
- section_outputs: float32 [2, 2, 4, 2048, 1024], P('section', None, 'wshard', 'seq')
- section_input_grads: float32 [2, 2, 4, 2048, 1024], P('section', None, 'wshard', 'seq')
- attend_in_grad: float32 [2, 1024, 3072], P('section', ('seq', 'wshard'))
- attend_out_grad: float32 [2, 1024, 1024], P('section', ('seq', 'wshard'))
- hidden_in_grad: float32 [2, 1024, 5248], P('section', ('seq', 'wshard'))
- hidden_out_grad: float32 [2, 2624, 1024], P('section', ('seq', 'wshard'))
- gain_grads: float32 [2, 2, 1024], P('section', None, ('seq', 'wshard'))
Inputs may be any that keep to these rules, and one draw needn't show every extreme that they name: Segment numbers start at 0 at the start of each sequence, never fall along it and rise by at most one from token to token; a sequence holds at most 9 segments.
All inputs are finite; a program needn't handle non-finite values.
Results may differ from a plain program's by a relative error of at most 0.025.
Values may be sent and summed in bfloat16 or wider, within the bound.
No kernel may reach another device: no remote copies, remote signals or barrier semaphores. Data moves between devices by JAX's collectives and lax.ppermute only.
A program may use at most 192 MiB of HBM per device.

v0:
```python
import math

import jax
import jax.numpy as jnp
from jax import lax
from jax.sharding import PartitionSpec as P

HEADS = 16
HEAD_DIM = 64
FF = 2624
MB = 2
HALO = 64


norm_eps = 1e-05
root_half = 1.0 / math.sqrt(2.0)
root_two_pi = 1.0 / math.sqrt(2.0 * math.pi)


def with_halo(array, sides, width):
    for axis, dim in sides:
        devices, length = (lax.axis_size(axis), array.shape[dim])
        up = [(i, (i + 1) % devices) for i in range(devices - 1)]
        down = [(j, i) for i, j in up]
        last = lax.slice_in_dim(array, length - width, length, axis=dim)
        leading = lax.slice_in_dim(array, 0, width, axis=dim)
        before = lax.ppermute(last, axis, up)
        after = lax.ppermute(leading, axis, down)
        array = jnp.concatenate([before, array, after], axis=dim)
    return array


def in_one_piece(arrays, axis, dim, along):
    both = jnp.concatenate(arrays, axis=along)
    whole, at, outs = (lax.all_gather(both, axis, axis=dim, tiled=True), 0, [])
    for a in arrays:
        outs.append(lax.slice_in_dim(whole, at, at + a.shape[along], axis=along))
        at += a.shape[along]
    return tuple(outs)


def shifted(block, axis, distance):
    devices = range(lax.axis_size(axis))
    route = [(i - distance, i) for i in devices if i - distance in devices]
    return lax.ppermute(block, axis, route)


def in_one_piece_2(arrays, axis, dim, along):
    widths = [a.shape[along] for a in arrays]
    both = jnp.concatenate(arrays, axis=along)
    whole = lax.psum_scatter(both, axis, scatter_dimension=dim, tiled=True)
    return tuple(jnp.split(whole, [sum(widths[:k]) for k in range(1, len(widths))], axis=along))


def split_up(array, dim, devices):
    lengths = array.shape
    pieces = array.reshape(*lengths[:dim], devices, lengths[dim] // devices, *lengths[dim + 1 :])
    return jnp.moveaxis(pieces, dim, 0)


def summed_on_arrival(array, axis, dim):
    pieces = split_up(array, dim, lax.axis_size(axis))
    arrived = lax.all_to_all(pieces, axis, split_axis=0, concat_axis=0, tiled=True)
    return arrived.astype(jnp.float32).sum(axis=0)


def side_by_side(arrays, axis, dim, along):
    ends, at = ([], 0)
    for a in arrays[:-1]:
        at += a.shape[along]
        ends.append(at)
    both = jnp.concatenate(arrays, axis=along)
    return tuple(jnp.split(summed_on_arrival(both, axis, dim), ends, axis=along))


def norm_parts(rows_in):
    centred = rows_in - jnp.mean(rows_in, axis=1, keepdims=True)
    factor = lax.rsqrt(jnp.mean(centred * centred, axis=1, keepdims=True) + norm_eps)
    return (centred * factor, factor)


def norm_back(grad_norm, normed, factor):
    inner = jnp.mean(grad_norm, axis=1, keepdims=True)
    along = jnp.mean(grad_norm * normed, axis=1, keepdims=True)
    return factor * (grad_norm - inner - normed * along)


def matmul_t(left_rows, right_rows):
    return lax.dot_general(
        left_rows, right_rows, (((1,), (1,)), ((), ())), preferred_element_type=jnp.float32
    )


def inner_rows(left_rows, right_rows):
    return lax.dot_general(
        left_rows, right_rows, (((0,), (0,)), ((), ())), preferred_element_type=jnp.float32
    )


def split_heads(block):
    return block.reshape(block.shape[0], HEADS, HEAD_DIM)


def window_mask(segment_row, seq_place, row_count):
    padded = jnp.pad(segment_row, (HALO, HALO), constant_values=-1)
    first_row = seq_place * row_count
    query_seg = lax.dynamic_slice_in_dim(segment_row, first_row, row_count)
    key_seg = lax.dynamic_slice_in_dim(padded, first_row, row_count + 2 * HALO)
    query_pos = jnp.arange(row_count)[:, None]
    key_pos = jnp.arange(row_count + 2 * HALO)[None, :] - HALO
    nearby = jnp.abs(query_pos - key_pos) <= HALO
    return nearby & (query_seg[:, None] == key_seg[None, :])


def layer_forward(rows_in, gain_pair, weights, allowed):
    attend_w, attend_o, hidden_w, hidden_o = weights
    row_count, model_width = rows_in.shape
    score_scale = 1.0 / math.sqrt(HEAD_DIM)
    normed1, factor1 = norm_parts(rows_in)
    act_in = (normed1 * gain_pair[0]).astype(jnp.bfloat16)
    qkv = jnp.dot(act_in, attend_w, preferred_element_type=jnp.float32).astype(jnp.bfloat16)
    queries = qkv[:, :model_width]
    extended = with_halo(qkv[:, model_width:], (("seq", 0),), HALO)
    scores = (
        jnp.einsum(
            "qhd,khd->hqk",
            split_heads(queries),
            split_heads(extended[:, :model_width]),
            preferred_element_type=jnp.float32,
        )
        * score_scale
    )
    scores = jnp.where(allowed[None], scores, -1e30)
    row_max = jnp.max(scores, axis=2, keepdims=True)
    exponent = jnp.where(allowed[None], jnp.exp(scores - row_max), 0.0)
    row_total = jnp.sum(exponent, axis=2, keepdims=True)
    probs = (exponent / row_total).astype(jnp.bfloat16)
    log_total = row_max + jnp.log(row_total)
    mixed = jnp.einsum(
        "hqk,khd->qhd",
        probs,
        split_heads(extended[:, model_width:]),
        preferred_element_type=jnp.float32,
    )
    mixed = mixed.reshape(row_count, model_width).astype(jnp.bfloat16)
    middle = rows_in + jnp.dot(mixed, attend_o, preferred_element_type=jnp.float32)
    normed2, factor2 = norm_parts(middle)
    act_mid = (normed2 * gain_pair[1]).astype(jnp.bfloat16)
    hidden = jnp.dot(act_mid, hidden_w, preferred_element_type=jnp.float32)
    gate_part = hidden[:, :FF]
    normal_cum = 0.5 * (1.0 + lax.erf(gate_part * root_half))
    product = (gate_part * normal_cum * hidden[:, FF:]).astype(jnp.bfloat16)
    output = middle + jnp.dot(product, hidden_o, preferred_element_type=jnp.float32)
    kept_state = (
        normed1,
        factor1,
        act_in,
        queries,
        extended,
        log_total,
        mixed,
        normed2,
        factor2,
        act_mid,
        hidden,
        product,
        allowed,
    )
    return (output, kept_state)


def layer_backward(grad_out, kept_state, gain_pair, weights):
    attend_w, attend_o, hidden_w, hidden_o = weights
    (
        normed1,
        factor1,
        act_in,
        queries,
        extended,
        log_total,
        mixed,
        normed2,
        factor2,
        act_mid,
        hidden,
        product,
        allowed,
    ) = kept_state
    row_count, model_width = normed1.shape
    score_scale = 1.0 / math.sqrt(HEAD_DIM)
    grad_branch = grad_out.astype(jnp.bfloat16)
    grad_product = matmul_t(grad_branch, hidden_o)
    gate_part = hidden[:, :FF]
    up_part = hidden[:, FF:]
    normal_cum = 0.5 * (1.0 + lax.erf(gate_part * root_half))
    derivative = normal_cum + gate_part * jnp.exp(-0.5 * gate_part * gate_part) * root_two_pi
    grad_hidden = jnp.concatenate(
        [grad_product * up_part * derivative, grad_product * gate_part * normal_cum], axis=1
    ).astype(jnp.bfloat16)
    grad_norm2 = matmul_t(grad_hidden, hidden_w)
    gain_mid = jnp.sum(normed2 * grad_norm2, axis=0)
    grad_middle = grad_out + norm_back(grad_norm2 * gain_pair[1], normed2, factor2)
    grad_attn = grad_middle.astype(jnp.bfloat16)
    grad_mixed = split_heads(matmul_t(grad_attn, attend_o).astype(jnp.bfloat16))
    query_heads = split_heads(queries)
    key_heads = split_heads(extended[:, :model_width])
    value_heads = split_heads(extended[:, model_width:])
    scores = (
        jnp.einsum("qhd,khd->hqk", query_heads, key_heads, preferred_element_type=jnp.float32)
        * score_scale
    )
    probs = jnp.where(allowed[None], jnp.exp(scores - log_total), 0.0)
    grad_probs = jnp.einsum(
        "qhd,khd->hqk", grad_mixed, value_heads, preferred_element_type=jnp.float32
    )
    grad_scores = (
        probs * (grad_probs - jnp.sum(probs * grad_probs, axis=2, keepdims=True))
    ).astype(jnp.bfloat16)
    grad_query = (
        jnp.einsum("hqk,khd->qhd", grad_scores, key_heads, preferred_element_type=jnp.float32)
        * score_scale
    )
    grad_keys = (
        jnp.einsum("hqk,qhd->khd", grad_scores, query_heads, preferred_element_type=jnp.float32)
        * score_scale
    )
    grad_values = jnp.einsum(
        "hqk,qhd->khd", probs.astype(jnp.bfloat16), grad_mixed, preferred_element_type=jnp.float32
    )
    key_count = extended.shape[0]
    grad_pairs = jnp.concatenate(
        [grad_keys.reshape(key_count, model_width), grad_values.reshape(key_count, model_width)],
        axis=1,
    )
    border_rows = jnp.concatenate([grad_pairs[:HALO], grad_pairs[key_count - HALO :]], axis=0)
    returned = with_halo(border_rows.astype(jnp.bfloat16), (("seq", 0),), HALO).astype(
        border_rows.dtype
    )
    own_rows = grad_pairs[HALO : HALO + row_count]
    own_rows = own_rows.at[:HALO].add(returned[:HALO])
    own_rows = own_rows.at[row_count - HALO :].add(returned[3 * HALO :])
    grad_qkv = jnp.concatenate(
        [grad_query.reshape(row_count, model_width), own_rows], axis=1
    ).astype(jnp.bfloat16)
    grad_norm1 = matmul_t(grad_qkv, attend_w)
    gain_first = jnp.sum(normed1 * grad_norm1, axis=0)
    grad_inputs = grad_middle + norm_back(grad_norm1 * gain_pair[0], normed1, factor1)
    acts = (act_in, mixed, act_mid, product)
    grads = (grad_qkv, grad_attn, grad_hidden, grad_branch)
    return (grad_inputs, acts, grads, jnp.stack([gain_first, gain_mid]))


def per_device(
    inputs, cotangent, segments, norm_gains, attend_in, attend_out, hidden_in, hidden_out
):
    section_index = lax.axis_index("section")
    seq_place = lax.axis_index("seq")
    weights = (
        *in_one_piece((attend_in[0], attend_out[0], hidden_in[0]), "wshard", 0, 1),
        lax.all_gather(hidden_out[0], "wshard", axis=0, tiled=True),
    )
    gain_pair = norm_gains[0]
    row_count = inputs.shape[2]
    model_width = inputs.shape[3]
    first_section = section_index == 0
    masks_all = jnp.stack(
        [window_mask(segments[batch_index, 0], seq_place, row_count) for batch_index in range(MB)]
    )
    empty_rows = jnp.zeros((row_count, model_width), jnp.float32)
    received = empty_rows
    produced = []
    kept_all = []
    for step_index in range(MB + 1):
        fresh_rows = inputs[step_index, 0] if step_index < MB else empty_rows
        layer_in = jnp.where(first_section, fresh_rows, received)
        picked = jnp.clip(step_index - section_index, 0, MB - 1)
        allowed = lax.dynamic_index_in_dim(masks_all, picked, 0, keepdims=False)
        output, kept_state = layer_forward(layer_in, gain_pair, weights, allowed)
        produced.append(output)
        kept_all.append(kept_state)
        if step_index < MB:
            received = shifted(output, "section", 1)
    early_outputs = jnp.stack(produced[:MB])
    late_outputs = jnp.stack(produced[1:])
    section_outputs = jnp.where(first_section, early_outputs, late_outputs)[None, :, None]
    returned_grad = empty_rows
    input_grads = []
    act_lists = ([], [], [], [])
    grad_lists = ([], [], [], [])
    gain_total = jnp.zeros((2, model_width), jnp.float32)
    for step_index in range(MB + 1):
        upstream = cotangent[MB - 1 - step_index, 0] if step_index < MB else empty_rows
        grad_out = jnp.where(first_section, returned_grad, upstream)
        grad_inputs, acts, grads, gain_terms = layer_backward(
            grad_out, kept_all[MB - step_index], gain_pair, weights
        )
        input_grads.append(grad_inputs)
        for member in range(4):
            act_lists[member].append(acts[member])
            grad_lists[member].append(grads[member])
        gain_total = gain_total + gain_terms
        if step_index < MB:
            returned_grad = shifted(grad_inputs.astype(jnp.bfloat16), "section", -1).astype(
                grad_inputs.dtype
            )
    early_grads = jnp.stack([input_grads[MB - batch_index] for batch_index in range(MB)])
    late_grads = jnp.stack([input_grads[MB - 1 - batch_index] for batch_index in range(MB)])
    section_input_grads = jnp.where(first_section, early_grads, late_grads)[None, :, None]
    act_rows = [jnp.concatenate(member_list, axis=0) for member_list in act_lists]
    grad_rows = [jnp.concatenate(member_list, axis=0) for member_list in grad_lists]
    qkv_total = inner_rows(act_rows[0], grad_rows[0])
    attn_total = inner_rows(act_rows[1], grad_rows[1])
    down_total = inner_rows(act_rows[3], grad_rows[3])
    hidden_part = lax.psum_scatter(
        inner_rows(act_rows[2], grad_rows[2]).astype(jnp.bfloat16),
        "seq",
        scatter_dimension=0,
        tiled=True,
    )
    qkv_part, attn_part, down_part, gain_part = (
        *tuple(
            (
                part.astype(jnp.float32)
                for part in in_one_piece_2(
                    (qkv_total.astype(jnp.bfloat16), attn_total.astype(jnp.bfloat16)), "seq", 0, 1
                )
            )
        ),
        lax.psum_scatter(
            down_total.astype(jnp.bfloat16), "seq", scatter_dimension=0, tiled=True
        ).astype(jnp.float32),
        lax.psum_scatter(
            gain_total.astype(jnp.bfloat16), "seq", scatter_dimension=1, tiled=True
        ).astype(jnp.float32),
    )
    hidden_rows, qkv_rows, attn_rows, down_rows, gain_rows = (
        *side_by_side(
            (hidden_part, qkv_part.astype(jnp.bfloat16), attn_part.astype(jnp.bfloat16)),
            "wshard",
            0,
            1,
        ),
        summed_on_arrival(down_part.astype(jnp.bfloat16), "wshard", 0),
        summed_on_arrival(gain_part.astype(jnp.bfloat16), "wshard", 1),
    )
    return (
        section_outputs,
        section_input_grads,
        qkv_rows[None],
        attn_rows[None],
        hidden_rows[None],
        down_rows[None],
        gain_rows[None],
    )


def solution(mesh):
    placed = (
        P(None, "wshard", "seq", None),
        P(None, "wshard", "seq", None),
        P(None, "wshard", None),
        P("section", None, None),
        P("section", "wshard", None),
        P("section", "wshard", None),
        P("section", "wshard", None),
        P("section", "wshard", None),
    )
    return jax.shard_map(
        per_device,
        mesh=mesh,
        in_specs=placed,
        out_specs=(
            P("section", None, "wshard", "seq", None),
            P("section", None, "wshard", "seq", None),
            P("section", ("seq", "wshard"), None),
            P("section", ("seq", "wshard"), None),
            P("section", ("seq", "wshard"), None),
            P("section", ("seq", "wshard"), None),
            P("section", None, ("seq", "wshard")),
        ),
        check_vma=False,
    )
```

profile of v0, /device:TPU:1, one launch (start us, length us, event | category | flops | bytes accessed | tf_op | source)
XLA Modules:
  0.0 851.5 jit_solution(17419517563738422183)
XLA Ops:
  7.2 4.8 pad_maximum_fusion.1
  13.8 176.4 %all-gather.4.cloned.1.call-done = bf16[1024,9344]{1,0:T(8,128)(2,1)} async-done(((bf16[256,9344]{1,0:T(8,128)(2,1)}), bf16[1024,9344]{1,0:T(8,128)(2,1)}) %all-gather.4.cloned.1.call-update) | async-done | bytes 19136528 | tf_op jit(solution)/shard_map/all_gather | solution.py:35
  190.2 3.8 convolution_convert_fusion.5
  202.1 3.8 collective-permute-done.1
  212.5 5.8 fusion.23
  220.3 29.8 %all-gather.6.cloned.1.call-done = bf16[1,2624,1024]{2,1,0:T(8,128)(2,1)} async-done(((bf16[1,656,1024]{2,1,0:T(8,128)(2,1)}), bf16[1,2624,1024]{2,1,0:T(8,128)(2,1)}) %all-gather.6.cloned.1.call-update) | async-done | bytes 5373968 | tf_op jit(solution)/shard_map/all_gather | solution.py:260
  258.0 3.9 convolution_convert_fusion.4
  262.8 3.8 collective-permute-start.3
  271.7 4.5 collective-permute-done.4
  289.0 6.2 fusion.21
  301.9 3.9 convolution_convert_fusion.3
  315.6 3.8 collective-permute-done.7
  331.4 5.8 fusion.19
  340.7 7.6 multiply_reduce_fusion.7
  361.5 4.3 collective-permute-start.8
  368.7 7.3 collective-permute-done.8
  376.1 3.9 collective-permute-done.9
  383.2 5.4 scatter-add.20
  391.8 6.3 scatter-add.21
  400.1 6.3 multiply_reduce_fusion.8
  407.5 4.0 collective-permute-start.10
  416.0 7.0 multiply_reduce_fusion.5
  436.1 4.0 collective-permute-start.11
  442.1 8.9 %collective-permute-done.11 = bf16[64,2048]{0,1:T(8,128)(2,1)S(1)} collective-permute-done((bf16[64,2048]{0,1:T(8,128)(2,1)S(1)}, bf16[64,2048]{0,1:T(8,128)(2,1)S(1)}, u32[]{:S(2)}, u32[]{:S(2)}) %collective-permute-start.11) | collective-permute-done | bytes 262176 | tf_op jit(solution)/shard_map/ppermute | solution.py:27
  451.0 3.8 collective-permute-done.12
  458.2 5.4 scatter-add.24
  466.7 6.3 scatter-add.25
  475.1 6.1 multiply_reduce_fusion.6
  489.8 7.0 multiply_reduce_fusion.3
  508.8 4.0 collective-permute-start.14
  515.5 8.2 collective-permute-done.14
  523.7 3.8 collective-permute-done.15
  529.9 4.5 scatter-add.26
  536.3 6.1 scatter-add.29
  542.5 7.7 convolution_convert_fusion.2
  550.2 5.8 multiply_reduce_fusion.4
  557.1 7.6 pad_maximum_fusion
  566.0 10.4 %convolution_convert_fusion = bf16[1024,5248]{1,0:T(8,128)(2,1)} fusion(bf16[128,5248]{1,0:T(8,128)(2,1)} %copy-done.21, bf16[128,5248]{1,0:T(8,128)(2,1)} %copy-done.20, bf16[128,5248]{1,0:T(8,128)(2,1)S(1)} %copy-done.19, bf16[128,1024]{1,0:T(8,128)(2,1)S(1)} %copy-done.57, bf16[128,1024]{1,0:T(8,128)(2,1)} %copy-done.58, bf16[128,1024]{1,0:T(8,128)(2,1)} %copy-done.59), kind=kOutput, calls=%fused_computation | convolution fusion | flops 4147019776 | bytes 15564800 | tf_op jit(solution)/shard_map/dot_general | solution.py:95
  578.4 6.6 convolution_convert_fusion.1
  585.0 77.4 %fusion = bf16[176,1024]{1,0:T(8,128)(2,1)S(1)} fusion(bf16[2624,1024]{1,0:T(8,128)(2,1)} %convolution_convert_fusion.1), kind=kCustom, calls=%all-reduce-scatter | all-reduce-scatter fusion | flops 2883585 | bytes 5734912
  662.4 4.8 collective-permute-start.16
  667.2 3.7 fusion.88
  677.0 4.2 all-to-all-start.2
  685.4 3.8 all-to-all-start.1
  689.3 37.3 %reduce-scatter.10.cloned.1.call-done = bf16[64,4096]{1,0:T(8,128)(2,1)} async-done(((bf16[1024,4096]{1,0:T(8,128)(2,1)}), bf16[64,4096]{1,0:T(8,128)(2,1)}) %reduce-scatter.10.cloned.1.call-update) | async-done | bytes 524304 | tf_op jit(solution)/shard_map/reduce_scatter | solution.py:51
  726.5 93.7 %reduce-scatter.8.cloned.1.call-done = bf16[64,5248]{1,0:T(8,128)(2,1)} async-done(((bf16[1024,5248]{1,0:T(8,128)(2,1)}), bf16[64,5248]{1,0:T(8,128)(2,1)}) %reduce-scatter.8.cloned.1.call-update) | async-done | bytes 671760 | tf_op jit(solution)/shard_map/reduce_scatter | solution.py:314
  823.4 4.0 all-to-all-start
  831.5 10.9 %all-to-all-done = bf16[4,16,9344]{2,1,0:T(8,128)(2,1)S(1)} async-done(((bf16[4,16,9344]{2,1,0:T(8,128)(2,1)}), bf16[4,16,9344]{2,1,0:T(8,128)(2,1)S(1)}, u32[]{:S(2)}, u32[]{:S(2)}) %all-to-all-start) | async-done | bytes 1196064 | tf_op jit(solution)/shard_map/all_to_all | solution.py:63
  (438 shorter events, 180.0 us)
Async XLA Ops:
  7.2 183.1 %all-gather.4.cloned.1.call-start = ((), (), s32[]{:S(2)}) async-start(), calls=%async_computation.6 | async-start | bytes 23920640 | tf_op jit(solution)/shard_map/all_gather | solution.py:35
  12.1 238.0 %all-gather.6.cloned.1.call-start = ((), (), s32[]{:S(2)}) async-start(), calls=%async_computation.9 | async-start | bytes 6717440 | tf_op jit(solution)/shard_map/all_gather | solution.py:260
  12.8 662.8 %reduce-scatter.12.cloned.1.call-start = ((), (), s32[]{:S(2)}) async-start(), calls=%async_computation.10 | async-start | bytes 278528
  13.4 180.6 %copy-start.91 = (f32[128]{0:T(128)}, f32[128]{0:T(128)S(1)}, u32[]{:S(2)}) copy-start(f32[128]{0:T(128)S(1)} %broadcast_multiply_fusion.17) | copy-start | bytes 1540
  13.6 180.4 %copy-start.106 = (f32[128]{0:T(128)}, f32[128]{0:T(128)S(1)}, u32[]{:S(2)}) copy-start(f32[128]{0:T(128)S(1)} %add_rsqrt_fusion.5) | copy-start | bytes 1540
  13.8 180.2 %copy-start.79 = (bf16[128,1024]{1,0:T(8,128)(2,1)}, bf16[128,1024]{1,0:T(8,128)(2,1)S(1)}, u32[]{:S(2)}) copy-start(bf16[128,1024]{1,0:T(8,128)(2,1)S(1)} %multiply_convert_fusion.14) | copy-start | bytes 786436
  194.1 8.1 collective-permute-start
  197.2 8.8 %collective-permute-start.1 = (bf16[64,2048]{1,0:T(8,128)(2,1)S(1)}, bf16[64,2048]{1,0:T(8,128)(2,1)S(1)}, u32[]{:S(2)}, u32[]{:S(2)}) collective-permute-start(bf16[64,2048]{1,0:T(8,128)(2,1)S(1)} %get-tuple-element.133), channel_id=1, source_target_pairs={{4,0},{8,4},{12,8},{16,12},{20,16},{24,20},{28,24},{32,28},{36,32}... | collective-permute-start | bytes 786440 | tf_op jit(solution)/shard_map/ppermute | solution.py:28
  220.3 33.4 %copy-start.31 = (bf16[128,2624]{1,0:T(8,128)(2,1)}, bf16[128,2624]{1,0:T(8,128)(2,1)S(1)}, u32[]{:S(2)}) copy-start(bf16[128,2624]{1,0:T(8,128)(2,1)S(1)} %multiply_convert_fusion.8) | copy-start | bytes 2015236
  253.6 3.8 collective-permute-start.2
  257.6 28.7 %copy-start.9 = (f32[128,1024]{1,0:T(8,128)}, f32[128,1024]{1,0:T(8,128)S(1)}, u32[]{:S(2)}) copy-start(f32[128,1024]{1,0:T(8,128)S(1)} %get-tuple-element.108) | copy-start | bytes 1572868
  262.8 9.0 %collective-permute-start.3 = (bf16[64,2048]{1,0:T(8,128)(2,1)}, bf16[64,2048]{1,0:T(8,128)(2,1)}, u32[]{:S(2)}, u32[]{:S(2)}) collective-permute-start(bf16[64,2048]{1,0:T(8,128)(2,1)} %get-tuple-element.130), channel_id=1, source_target_pairs={{0,4},{4,8},{8,12},{12,16},{16,20},{20,24},{24,28},{28,32},{32,36}... | collective-permute-start | bytes 786440 | tf_op jit(solution)/shard_map/ppermute | solution.py:27
  266.6 9.6 %collective-permute-start.4 = (bf16[64,2048]{1,0:T(8,128)(2,1)}, bf16[64,2048]{1,0:T(8,128)(2,1)}, u32[]{:S(2)}, u32[]{:S(2)}) collective-permute-start(bf16[64,2048]{1,0:T(8,128)(2,1)} %get-tuple-element.131), channel_id=1, source_target_pairs={{4,0},{8,4},{12,8},{16,12},{20,16},{24,20},{28,24},{32,28},{36,32}... | collective-permute-start | bytes 786440 | tf_op jit(solution)/shard_map/ppermute | solution.py:28
  297.0 8.8 %copy-start.48 = (f32[128,1024]{1,0:T(8,128)}, f32[128,1024]{1,0:T(8,128)S(1)}, u32[]{:S(2)}) copy-start(f32[128,1024]{1,0:T(8,128)S(1)} %fusion.82) | copy-start | bytes 1572868
  297.0 3.9 collective-permute-start.5
  306.6 8.9 %collective-permute-start.6 = (bf16[64,2048]{1,0:T(8,128)(2,1)}, bf16[64,2048]{1,0:T(8,128)(2,1)}, u32[]{:S(2)}, u32[]{:S(2)}) collective-permute-start(bf16[64,2048]{1,0:T(8,128)(2,1)} %get-tuple-element.128), channel_id=1, source_target_pairs={{0,4},{4,8},{8,12},{12,16},{16,20},{20,24},{24,28},{28,32},{32,36}... | collective-permute-start | bytes 786440 | tf_op jit(solution)/shard_map/ppermute | solution.py:27
  309.8 9.6 %collective-permute-start.7 = (bf16[64,2048]{1,0:T(8,128)(2,1)}, bf16[64,2048]{1,0:T(8,128)(2,1)}, u32[]{:S(2)}, u32[]{:S(2)}) collective-permute-start(bf16[64,2048]{1,0:T(8,128)(2,1)} %get-tuple-element.129), channel_id=1, source_target_pairs={{4,0},{8,4},{12,8},{16,12},{20,16},{24,20},{28,24},{32,28},{36,32}... | collective-permute-start | bytes 786440 | tf_op jit(solution)/shard_map/ppermute | solution.py:28
  328.7 8.5 %slice-start.2 = ((s8[5373952]{0:T(1024)(128)(4,1)}), s8[4194304]{0:T(1024)(128)(4,1)S(1)}, s32[]{:S(2)}) async-start(s8[5373952]{0:T(1024)(128)(4,1)} %bitcast.204), calls=%async_computation.13 | async-start | bytes 8388608
  361.5 14.5 %collective-permute-start.8 = (bf16[64,2048]{0,1:T(8,128)(2,1)S(1)}, bf16[64,2048]{0,1:T(8,128)(2,1)S(1)}, u32[]{:S(2)}, u32[]{:S(2)}) collective-permute-start(bf16[64,2048]{0,1:T(8,128)(2,1)S(1)} %get-tuple-element.120), channel_id=1, source_target_pairs={{0,4},{4,8},{8,12},{12,16},{16,20},{20,24},{24,28},{28,32},{32,36}... | collective-permute-start | bytes 786440 | tf_op jit(solution)/shard_map/ppermute | solution.py:27
  365.8 14.1 %collective-permute-start.9 = (bf16[64,2048]{0,1:T(8,128)(2,1)S(1)}, bf16[64,2048]{0,1:T(8,128)(2,1)S(1)}, u32[]{:S(2)}, u32[]{:S(2)}) collective-permute-start(bf16[64,2048]{0,1:T(8,128)(2,1)S(1)} %get-tuple-element.121), channel_id=1, source_target_pairs={{4,0},{8,4},{12,8},{16,12},{20,16},{24,20},{28,24},{32,28},{36,32}... | collective-permute-start | bytes 786440 | tf_op jit(solution)/shard_map/ppermute | solution.py:28
  391.8 8.3 copy-start.90
  391.8 8.3 copy-start.101
  399.3 13.4 %slice-start.4 = ((s8[5373952]{0:T(1024)(128)(4,1)}), s8[4194304]{0:T(1024)(128)(4,1)S(1)}, s32[]{:S(2)}) async-start(s8[5373952]{0:T(1024)(128)(4,1)} %bitcast.206), calls=%async_computation.15 | async-start | bytes 8388608
  400.1 12.5 %copy-start.39 = (f32[2,1,128,1024]{3,2,1,0:T(8,128)S(1)}, f32[2,1,128,1024]{3,2,1,0:T(8,128)}, u32[]{:S(2)}) copy-start(f32[2,1,128,1024]{3,2,1,0:T(8,128)} %param.21) | copy-start | bytes 3145732
  400.1 12.6 %slice-start.5 = ((s8[5373952]{0:T(1024)(128)(4,1)}), s8[1179648]{0:T(1024)(128)(4,1)S(1)}, s32[]{:S(2)}) async-start(s8[5373952]{0:T(1024)(128)(4,1)} %bitcast.206), calls=%async_computation.16 | async-start | bytes 2359296
  407.5 5.1 collective-permute-start.10
  436.1 14.9 %collective-permute-start.11 = (bf16[64,2048]{0,1:T(8,128)(2,1)S(1)}, bf16[64,2048]{0,1:T(8,128)(2,1)S(1)}, u32[]{:S(2)}, u32[]{:S(2)}) collective-permute-start(bf16[64,2048]{0,1:T(8,128)(2,1)S(1)} %get-tuple-element.118), channel_id=1, source_target_pairs={{0,4},{4,8},{8,12},{12,16},{16,20},{20,24},{24,28},{28,32},{32,36}... | collective-permute-start | bytes 786440 | tf_op jit(solution)/shard_map/ppermute | solution.py:27
  440.1 14.7 %collective-permute-start.12 = (bf16[64,2048]{0,1:T(8,128)(2,1)S(1)}, bf16[64,2048]{0,1:T(8,128)(2,1)S(1)}, u32[]{:S(2)}, u32[]{:S(2)}) collective-permute-start(bf16[64,2048]{0,1:T(8,128)(2,1)S(1)} %get-tuple-element.119), channel_id=1, source_target_pairs={{4,0},{8,4},{12,8},{16,12},{20,16},{24,20},{28,24},{32,28},{36,32}... | collective-permute-start | bytes 786440 | tf_op jit(solution)/shard_map/ppermute | solution.py:28
  442.1 32.2 %copy-start.72 = (bf16[16,64,128]{2,1,0:T(8,128)(2,1)}, bf16[16,64,128]{2,1,0:T(8,128)(2,1)S(1)}, u32[]{:S(2)}) copy-start(bf16[16,64,128]{2,1,0:T(8,128)(2,1)S(1)} %fusion.92) | copy-start | bytes 786436
  466.7 8.3 copy-start.96
  466.7 8.3 copy-start.105
  474.3 12.6 %slice-start.6 = ((s8[5373952]{0:T(1024)(128)(4,1)}), s8[4194304]{0:T(1024)(128)(4,1)S(1)}, s32[]{:S(2)}) async-start(s8[5373952]{0:T(1024)(128)(4,1)} %bitcast.208), calls=%async_computation.17 | async-start | bytes 8388608
  475.1 11.8 %slice-start.7 = ((s8[5373952]{0:T(1024)(128)(4,1)}), s8[1179648]{0:T(1024)(128)(4,1)S(1)}, s32[]{:S(2)}) async-start(s8[5373952]{0:T(1024)(128)(4,1)} %bitcast.208), calls=%async_computation.18 | async-start | bytes 2359296
  482.2 4.6 collective-permute-start.13
  508.8 14.9 %collective-permute-start.14 = (bf16[64,2048]{0,1:T(8,128)(2,1)S(1)}, bf16[64,2048]{0,1:T(8,128)(2,1)S(1)}, u32[]{:S(2)}, u32[]{:S(2)}) collective-permute-start(bf16[64,2048]{0,1:T(8,128)(2,1)S(1)} %get-tuple-element.116), channel_id=1, source_target_pairs={{0,4},{4,8},{8,12},{12,16},{16,20},{20,24},{24,28},{28,32},{32,36}... | collective-permute-start | bytes 786440 | tf_op jit(solution)/shard_map/ppermute | solution.py:27
  512.8 14.7 %collective-permute-start.15 = (bf16[64,2048]{0,1:T(8,128)(2,1)S(1)}, bf16[64,2048]{0,1:T(8,128)(2,1)S(1)}, u32[]{:S(2)}, u32[]{:S(2)}) collective-permute-start(bf16[64,2048]{0,1:T(8,128)(2,1)S(1)} %get-tuple-element.117), channel_id=1, source_target_pairs={{4,0},{8,4},{12,8},{16,12},{20,16},{24,20},{28,24},{32,28},{36,32}... | collective-permute-start | bytes 786440 | tf_op jit(solution)/shard_map/ppermute | solution.py:28
  542.5 7.7 copy-start.14
  542.5 7.7 copy-start.75
  542.5 7.7 copy-start.92
  557.0 169.5 %reduce-scatter.10.cloned.1.call-start = ((), (), s32[]{:S(2)}) async-start(), calls=%async_computation.8 | async-start | bytes 8912896 | tf_op jit(solution)/shard_map/reduce_scatter | solution.py:51
  564.7 255.5 %reduce-scatter.8.cloned.1.call-start = ((), (), s32[]{:S(2)}) async-start(), calls=%async_computation.7 | async-start | bytes 11419648 | tf_op jit(solution)/shard_map/reduce_scatter | solution.py:314
  662.4 12.1 %copy-start.47 = (f32[128,1024]{1,0:T(8,128)S(1)}, f32[128,1024]{1,0:T(8,128)}, u32[]{:S(2)}) copy-start(f32[128,1024]{1,0:T(8,128)} %copy-done.46) | copy-start | bytes 1572868
  662.4 12.1 %copy-start.49 = (f32[128,1024]{1,0:T(8,128)S(1)}, f32[128,1024]{1,0:T(8,128)}, u32[]{:S(2)}) copy-start(f32[128,1024]{1,0:T(8,128)} %copy-done.48) | copy-start | bytes 1572868
  662.4 18.8 %collective-permute-start.16 = (bf16[176,1024]{1,0:T(8,128)(2,1)S(1)}, bf16[176,1024]{1,0:T(8,128)(2,1)}, u32[]{:S(2)}, u32[]{:S(2)}) collective-permute-start(bf16[176,1024]{1,0:T(8,128)(2,1)S(1)} %fusion), channel_id=1, source_target_pairs={{0,4},{4,8},{8,12},{12,16},{16,20},{20,24},{24,28},{28,32},{32,36}... | collective-permute-start | bytes 1081352
  671.0 10.3 %collective-permute-start.17 = (bf16[4,1024]{1,0:T(4,128)(2,1)S(1)}, bf16[4,1024]{1,0:T(4,128)(2,1)S(1)}, u32[]{:S(2)}, u32[]{:S(2)}) collective-permute-start(bf16[4,1024]{1,0:T(4,128)(2,1)S(1)} %slice.420), channel_id=1, source_target_pairs={{0,8},{4,12},{8,16},{12,20},{16,24},{20,28},{24,32},{28,36},{32,40... | collective-permute-start | bytes 24584
  677.0 8.4 all-to-all-start.2
  685.4 137.2 %all-to-all-start.1 = ((bf16[4,41,1024]{2,1,0:T(8,128)(2,1)}), bf16[4,41,1024]{2,1,0:T(8,128)(2,1)S(1)}, u32[]{:S(2)}, u32[]{:S(2)}) async-start(bf16[4,41,1024]{2,1,0:T(8,128)(2,1)} %reshape.731), calls=%async_computation.3 | async-start | bytes 786432 | tf_op jit(solution)/shard_map/all_to_all | solution.py:63
  823.4 18.9 %all-to-all-start = ((bf16[4,16,9344]{2,1,0:T(8,128)(2,1)}), bf16[4,16,9344]{2,1,0:T(8,128)(2,1)S(1)}, u32[]{:S(2)}, u32[]{:S(2)}) async-start(bf16[4,16,9344]{2,1,0:T(8,128)(2,1)} %bitcast.62), calls=%async_computation.2 | async-start | bytes 2392064 | tf_op jit(solution)/shard_map/all_to_all | solution.py:63
  (95 other events, 327.8 us)
Sparse Core Ops, SparseCore 0:
  12.2 178.0 all-gather.3
  191.9 58.1 all-gather.5
  557.1 73.7 reduce-scatter.11
  634.6 91.8 reduce-scatter.9
  730.2 89.9 reduce-scatter.7
where the time goes:
time: 863 us; the launch traced here: 852 us
  waiting for transfers between devices  409 us (47%)
  matrix products  147 us (17%)
  local copies, waits for them, and re-layouts  82 us (10%)
  blocking collectives  77.4 us (9%)
  starting transfers between devices  62.2 us (7%)
  other arithmetic  57.1 us (7%)
  between operations  17.1 us (2%)
    all_gather x1, waiting for transfers between devices, in_one_piece(): whole, at, outs = (lax.all_gather(both, axis, axis=dim, tiled=True), 0, [])  176 us
    reduce_scatter x1, waiting for transfers between devices, per_device(): lax.psum_scatter(inner_rows(act_rows[2], grad_rows[2]).astype(jnp.bfloat1...  93.7 us
    unnamed x1, blocking collectives  77.4 us
    dot_general x12, matrix products, matmul_t(): lax.dot_general(left_rows, right_rows, (((1,), (1,)), ((), ())), preferre...  56 us
    reduce_scatter x1, waiting for transfers between devices, in_one_piece_2(): whole = lax.psum_scatter(both, axis, scatter_dimension=dim, tiled=True)  37.3 us
    all_gather x1, waiting for transfers between devices, per_device(): lax.all_gather(hidden_out[0], 'wshard', axis=0, tiled=True)  29.8 us
    ppermute x6, waiting for transfers between devices, with_halo(): before = lax.ppermute(last, axis, up)  28.6 us
    dot_general x4, matrix products, inner_rows(): lax.dot_general(left_rows, right_rows, (((0,), (0,)), ((), ())), preferre...  27.3 us
  transfers between devices with their start and end apart: 26, of which 21 were waited for; matrix products, arithmetic and copies ran while one was open for 17% of the time, Pallas kernels for 0%

commit v1 on v0

v1 whole, which is shorter than its diff:
```python
import math

import jax
import jax.numpy as jnp
from jax import lax
from jax.experimental import pallas as pl
from jax.experimental.pallas import tpu as pltpu
from jax.sharding import PartitionSpec as P

HEADS = 16
HEAD_DIM = 64
FF = 2624
HALO = 64
SEQ_DEV = 16
W_DEV = 4
PAD_ROWS = 48

norm_eps = 1e-05
root_half = 1.0 / math.sqrt(2.0)
root_two_pi = 1.0 / math.sqrt(2.0 * math.pi)
score_scale = 1.0 / math.sqrt(HEAD_DIM)

SWAP = [(0, 1), (1, 0)]


def swapped(array):
    return lax.ppermute(array, "section", SWAP)


def norm_parts(rows_in):
    centred = rows_in - jnp.mean(rows_in, axis=1, keepdims=True)
    factor = lax.rsqrt(jnp.mean(centred * centred, axis=1, keepdims=True) + norm_eps)
    return (centred * factor, factor)


def norm_back(grad_norm, normed, factor):
    inner = jnp.mean(grad_norm, axis=1, keepdims=True)
    along = jnp.mean(grad_norm * normed, axis=1, keepdims=True)
    return factor * (grad_norm - inner - normed * along)


def matmul(left, right):
    return jnp.dot(left, right, preferred_element_type=jnp.float32)


def matmul_t(left, right):
    return lax.dot_general(
        left, right, (((1,), (1,)), ((), ())), preferred_element_type=jnp.float32
    )


def inner_rows(left, right):
    return lax.dot_general(
        left, right, (((0,), (0,)), ((), ())), preferred_element_type=jnp.float32
    )


def column_halves(array, on_first):
    even = jnp.concatenate([array[:, 256 * k : 256 * k + 128] for k in range(4)], axis=1)
    odd = jnp.concatenate([array[:, 256 * k + 128 : 256 * k + 256] for k in range(4)], axis=1)
    return (jnp.where(on_first, even, odd), jnp.where(on_first, odd, even))


def from_halves(own, other, on_first):
    even = jnp.where(on_first, own, other)
    odd = jnp.where(on_first, other, own)
    parts = []
    for k in range(4):
        parts += [even[:, 128 * k : 128 * k + 128], odd[:, 128 * k : 128 * k + 128]]
    return jnp.concatenate(parts, axis=1)


def window_allowed(query_seg, key_seg):
    rows, keys = (query_seg.shape[0], key_seg.shape[1])
    offset = lax.broadcasted_iota(jnp.int32, (rows, keys), 1) - lax.broadcasted_iota(
        jnp.int32, (rows, keys), 0
    )
    return (offset >= 0) & (offset <= 2 * HALO) & (query_seg == key_seg)


def attend_kernel(query_seg, key_seg, qkv, mixed, log_total):
    allowed = window_allowed(query_seg[...], key_seg[...])
    width = HEADS * HEAD_DIM
    rows = mixed.shape[0]
    for head in range(HEADS):
        at = head * HEAD_DIM
        q = qkv[HALO : HALO + rows, at : at + HEAD_DIM]
        k = qkv[:, width + at : width + at + HEAD_DIM]
        v = qkv[:, 2 * width + at : 2 * width + at + HEAD_DIM]
        scores = jnp.where(allowed, matmul_t(q, k) * score_scale, -1e30)
        row_max = jnp.max(scores, axis=1, keepdims=True)
        exponent = jnp.exp(scores - row_max)
        total = jnp.sum(exponent, axis=1, keepdims=True)
        probs = (exponent * (1.0 / total)).astype(jnp.bfloat16)
        mixed[:, at : at + HEAD_DIM] = matmul(probs, v).astype(jnp.bfloat16)
        log_total[:, at : at + HEAD_DIM] = jnp.broadcast_to(
            row_max + jnp.log(total), (rows, HEAD_DIM)
        )


def attend_back_kernel(
    query_seg, key_seg, qkv, log_total, grad_mixed, grad_query, own, before, after
):
    allowed = window_allowed(query_seg[...], key_seg[...])
    width = HEADS * HEAD_DIM
    rows = grad_mixed.shape[0]
    for head in range(HEADS):
        at = head * HEAD_DIM
        q = qkv[HALO : HALO + rows, at : at + HEAD_DIM]
        k = qkv[:, width + at : width + at + HEAD_DIM]
        v = qkv[:, 2 * width + at : 2 * width + at + HEAD_DIM]
        grad = grad_mixed[:, at : at + HEAD_DIM]
        scores = jnp.where(allowed, matmul_t(q, k) * score_scale, -1e30)
        probs = jnp.exp(scores - log_total[:, at : at + 1])
        grad_probs = matmul_t(grad, v)
        inner = jnp.sum(probs * grad_probs, axis=1, keepdims=True)
        grad_scores = (probs * (grad_probs - inner)).astype(jnp.bfloat16)
        grad_query[:, at : at + HEAD_DIM] = (matmul(grad_scores, k) * score_scale).astype(
            jnp.bfloat16
        )
        for place, piece in (
            (at, inner_rows(grad_scores, q) * score_scale),
            (width + at, inner_rows(probs.astype(jnp.bfloat16), grad)),
        ):
            columns = slice(place, place + HEAD_DIM)
            before[:, columns] = piece[:HALO].astype(jnp.bfloat16)
            own[:, columns] = piece[HALO : HALO + rows]
            after[:, columns] = piece[HALO + rows :].astype(jnp.bfloat16)


params = pltpu.CompilerParams(vmem_limit_bytes=40 * 1024 * 1024)


def attend(query_seg, key_seg, qkv):
    rows, width = (query_seg.shape[0], HEADS * HEAD_DIM)
    return pl.pallas_call(
        attend_kernel,
        out_shape=(
            jax.ShapeDtypeStruct((rows, width), jnp.bfloat16),
            jax.ShapeDtypeStruct((rows, width), jnp.float32),
        ),
        compiler_params=params,
        name="attend",
    )(query_seg, key_seg, qkv)


def attend_back(query_seg, key_seg, qkv, log_total, grad_mixed):
    rows, width = (query_seg.shape[0], HEADS * HEAD_DIM)
    return pl.pallas_call(
        attend_back_kernel,
        out_shape=(
            jax.ShapeDtypeStruct((rows, width), jnp.bfloat16),
            jax.ShapeDtypeStruct((rows, 2 * width), jnp.float32),
            jax.ShapeDtypeStruct((HALO, 2 * width), jnp.bfloat16),
            jax.ShapeDtypeStruct((HALO, 2 * width), jnp.bfloat16),
        ),
        compiler_params=params,
        name="attend_back",
    )(query_seg, key_seg, qkv, log_total, grad_mixed)


def to_next(array):
    return lax.ppermute(array, "seq", [(i, i + 1) for i in range(SEQ_DEV - 1)])


def to_previous(array):
    return lax.ppermute(array, "seq", [(i + 1, i) for i in range(SEQ_DEV - 1)])


def split_normal(gate):
    cumulative = 0.5 * (1.0 + lax.erf(gate * root_half))
    return cumulative


def layer_forward(rows_in, gain_pair, weights, segs, on_first):
    (attn_own, attn_other), (hidden_own, hidden_other), (down_own, down_other) = weights
    width = rows_in.shape[1]
    normed1, factor1 = norm_parts(rows_in)
    act_in = (normed1 * gain_pair[0]).astype(jnp.bfloat16)
    before = to_next(act_in[act_in.shape[0] - HALO :])
    after = to_previous(act_in[:HALO])
    extended = jnp.concatenate([before, act_in, after], axis=0)
    own, other = column_halves(extended, on_first)
    qkv = (
        matmul(own, attn_own[:, : 3 * width]) + matmul(other, attn_other[:, : 3 * width])
    ).astype(jnp.bfloat16)
    mixed, log_total = attend(*segs, qkv)
    own, other = column_halves(mixed, on_first)
    middle = (
        rows_in + matmul(own, attn_own[:, 3 * width :]) + matmul(other, attn_other[:, 3 * width :])
    )
    normed2, factor2 = norm_parts(middle)
    act_mid = (normed2 * gain_pair[1]).astype(jnp.bfloat16)
    own, other = column_halves(act_mid, on_first)
    hidden = matmul(own, hidden_own) + matmul(other, hidden_other)
    gate, up = (hidden[:, :FF], hidden[:, FF:])
    product = (gate * split_normal(gate) * up).astype(jnp.bfloat16)
    mine, theirs = (matmul(product, down_own), matmul(product, down_other))
    output = middle + jnp.concatenate(
        [jnp.where(on_first, mine, theirs), jnp.where(on_first, theirs, mine)], axis=1
    )
    kept = (normed1, factor1, act_in, qkv, log_total, mixed, normed2, factor2, act_mid, hidden, product)
    return (output, kept)


def padded_rows(product):
    pieces = product.reshape(product.shape[0], SEQ_DEV * W_DEV, FF // (SEQ_DEV * W_DEV))
    pieces = jnp.pad(pieces, ((0, 0), (0, 0), (0, PAD_ROWS - pieces.shape[2])))
    return pieces.reshape(product.shape[0], SEQ_DEV * W_DEV * PAD_ROWS)


def seq_sum(total):
    return lax.psum_scatter(total, "seq", scatter_dimension=0, tiled=True)


def half_exchange(arrays, on_first):
    keep, give = ([], [])
    for low, high in arrays:
        keep.append(jnp.where(on_first, low, high))
        give.append(jnp.where(on_first, high, low))
    widths = [g.shape[1] for g in give]
    got = swapped(jnp.concatenate(give, axis=1))
    outs, at = ([], 0)
    for mine, w in zip(keep, widths):
        outs.append(jnp.concatenate([mine, got[:, at : at + w]], axis=0))
        at += w
    return outs


def layer_backward(grad_out, kept, gain_pair, weights, segs, on_first):
    (attn_own, attn_other), (hidden_own, hidden_other), (down_own, down_other) = weights
    (normed1, factor1, act_in, qkv, log_total, mixed, normed2, factor2, act_mid, hidden, product) = kept
    rows, width = normed1.shape
    acts = jnp.concatenate([act_in, mixed, act_mid, padded_rows(product)], axis=1)
    acts = jnp.concatenate([acts, swapped(acts)], axis=0)
    both_in = acts[:, :width]
    both_mixed = acts[:, width : 2 * width]
    both_mid = acts[:, 2 * width : 3 * width]
    both_product = acts[:, 3 * width :]
    half = width // 2
    grad_branch = grad_out.astype(jnp.bfloat16)
    low, high = (grad_branch[:, :half], grad_branch[:, half:])
    grad_product = matmul_t(jnp.where(on_first, low, high), down_own) + matmul_t(
        jnp.where(on_first, high, low), down_other
    )
    gate, up = (hidden[:, :FF], hidden[:, FF:])
    cumulative = split_normal(gate)
    derivative = cumulative + gate * jnp.exp(-0.5 * gate * gate) * root_two_pi
    grad_gate = (grad_product * up * derivative).astype(jnp.bfloat16)
    grad_up = (grad_product * gate * cumulative).astype(jnp.bfloat16)
    branch_half, hidden_half = half_exchange(((low, high), (grad_gate, grad_up)), on_first)
    down_sum = seq_sum(inner_rows(both_product, branch_half).astype(jnp.bfloat16))
    hidden_sum = seq_sum(inner_rows(both_mid, hidden_half).astype(jnp.bfloat16))
    mine, theirs = [
        matmul_t(grad_gate, w[:, :FF]) + matmul_t(grad_up, w[:, FF:])
        for w in (hidden_own, hidden_other)
    ]
    grad_norm2 = from_halves(mine, theirs, on_first)
    gain_mid = jnp.sum(normed2 * grad_norm2, axis=0)
    grad_middle = grad_out + norm_back(grad_norm2 * gain_pair[1], normed2, factor2)
    grad_attn = grad_middle.astype(jnp.bfloat16)
    mine, theirs = [matmul_t(grad_attn, w[:, 3 * width :]) for w in (attn_own, attn_other)]
    grad_mixed = from_halves(mine, theirs, on_first).astype(jnp.bfloat16)
    grad_query, grad_own, grad_before, grad_after = attend_back(*segs, qkv, log_total, grad_mixed)
    from_previous = to_next(grad_after).astype(jnp.float32)
    from_next = to_previous(grad_before).astype(jnp.float32)
    grad_pairs = grad_own + jnp.concatenate([from_previous, from_next], axis=0)
    grad_qkv = jnp.concatenate([grad_query, grad_pairs.astype(jnp.bfloat16)], axis=1)
    qkv_half, attn_half = half_exchange(
        (
            (grad_qkv[:, : 3 * half], grad_qkv[:, 3 * half :]),
            (grad_attn[:, :half], grad_attn[:, half:]),
        ),
        on_first,
    )
    mine, theirs = [matmul_t(grad_qkv, w[:, : 3 * width]) for w in (attn_own, attn_other)]
    grad_norm1 = from_halves(mine, theirs, on_first)
    gain_first = jnp.sum(normed1 * grad_norm1, axis=0)
    grad_inputs = grad_middle + norm_back(grad_norm1 * gain_pair[0], normed1, factor1)
    gains = jnp.stack([gain_first, gain_mid]).astype(jnp.bfloat16)
    gain_columns = jnp.pad(gains, ((0, 126), (0, 0))).T
    late = jnp.concatenate(
        [
            inner_rows(both_in, qkv_half).astype(jnp.bfloat16),
            inner_rows(both_mixed, attn_half).astype(jnp.bfloat16),
            gain_columns,
        ],
        axis=1,
    )
    late_sum = seq_sum(late)
    return (grad_inputs, (late_sum, hidden_sum, down_sum))


def summed_over_w(block, place):
    rows = block.shape[0] // W_DEV
    total = lax.dynamic_slice_in_dim(block, place * rows, rows).astype(jnp.float32)
    for step in range(1, W_DEV):
        part = lax.dynamic_slice_in_dim(block, lax.rem(place + step, W_DEV) * rows, rows)
        got = lax.ppermute(part, "wshard", [(j, (j + step) % W_DEV) for j in range(W_DEV)])
        total = total + got.astype(jnp.float32)
    return total


def per_device(
    inputs, cotangent, segments, norm_gains, attend_in, attend_out, hidden_in, hidden_out
):
    on_first = lax.axis_index("section") == 0
    core = lax.axis_index("section")
    seq_place = lax.axis_index("seq")
    w_place = lax.axis_index("wshard")

    def by_core(first, second):
        return jnp.where(on_first, first, second)

    def sections(own, got):
        return (by_core(own, got), by_core(got, own))

    row_weights = jnp.concatenate([attend_in[0], attend_out[0], hidden_in[0]], axis=1)
    slice_rows = row_weights.shape[0] // (2 * SEQ_DEV)

    def row_slice(which):
        return lax.dynamic_slice_in_dim(
            row_weights, (which * SEQ_DEV + seq_place) * slice_rows, slice_rows
        )

    row_pieces = sections(row_slice(core), swapped(row_slice(1 - core)))
    half = hidden_out.shape[2] // 2
    low, high = (hidden_out[0, :, :half], hidden_out[0, :, half:])
    down_pieces = sections(by_core(low, high), swapped(by_core(high, low)))
    gains_other = swapped(norm_gains[0])
    gain_pairs = sections(norm_gains[0], gains_other)
    attn_width = attend_in.shape[2] + attend_out.shape[2]

    def gathered(piece, axes):
        own = lax.all_gather(piece, axes, axis=0, tiled=True)
        return (own, swapped(own))

    def weights_of(section):
        return (
            gathered(row_pieces[section][:, :attn_width], ("wshard", "seq")),
            gathered(row_pieces[section][:, attn_width:], ("wshard", "seq")),
            gathered(down_pieces[section], "wshard"),
        )

    weights = (weights_of(0), weights_of(1))
    rows_in = by_core(inputs[0, 0], inputs[1, 0])
    row_count = rows_in.shape[0]
    segment_row = by_core(segments[0, 0], segments[1, 0])
    padded = jnp.pad(segment_row, (HALO, HALO), constant_values=-1)
    first_row = seq_place * row_count
    segs = (
        lax.dynamic_slice_in_dim(segment_row, first_row, row_count)[:, None],
        lax.dynamic_slice_in_dim(padded, first_row, row_count + 2 * HALO)[None, :],
    )
    middle, kept0 = layer_forward(rows_in, gain_pairs[0], weights[0], segs, on_first)
    final, kept1 = layer_forward(middle, gain_pairs[1], weights[1], segs, on_first)
    upstream = by_core(cotangent[0, 0], cotangent[1, 0])
    grads1, sums1 = layer_backward(upstream, kept1, gain_pairs[1], weights[1], segs, on_first)
    grads0, sums0 = layer_backward(grads1, kept0, gain_pairs[0], weights[0], segs, on_first)

    def placed(first, second):
        mine, give = (by_core(first, second), by_core(second, first))
        got = swapped(give)
        return jnp.stack([by_core(mine, got), by_core(got, mine)])[None, :, None]

    section_outputs = placed(middle, final)
    section_input_grads = placed(grads0, grads1)

    def both_halves(first, second):
        mine, got = (by_core(first, second), swapped(by_core(second, first)))
        return (by_core(mine, got), by_core(got, mine))

    rows_first, rows_second = both_halves(
        *[jnp.concatenate([sums[0], sums[1]], axis=1) for sums in (sums0, sums1)]
    )
    width = rows_in.shape[1]
    attn_half, out_half = (3 * width // 2, width // 2)
    cuts = (0, attn_half, attn_half + out_half, attn_half + out_half + 128)
    pieces = [
        [rows[:, cuts[k] : (cuts + (rows.shape[1],))[k + 1]] for k in range(4)]
        for rows in (rows_first, rows_second)
    ]
    gain_part = pieces[0][2].astype(jnp.float32) + pieces[1][2].astype(jnp.float32)
    row_block = jnp.concatenate(
        [
            pieces[0][0],
            pieces[1][0],
            pieces[0][1],
            pieces[1][1],
            pieces[0][3],
            pieces[1][3],
            gain_part.astype(jnp.bfloat16),
        ],
        axis=1,
    )
    row_total = summed_over_w(row_block, w_place)
    down_block = jnp.concatenate(both_halves(sums0[2], sums1[2]), axis=1)
    down_total = summed_over_w(down_block, w_place)[: FF // (SEQ_DEV * W_DEV)]
    qkv_rows = row_total[:, : 3 * width]
    attn_rows = row_total[:, 3 * width : 4 * width]
    hidden_rows = row_total[:, 4 * width : 4 * width + 2 * FF]
    gain_rows = row_total[:, 4 * width + 2 * FF :][:, :2].T
    return (
        section_outputs,
        section_input_grads,
        qkv_rows[None],
        attn_rows[None],
        hidden_rows[None],
        down_total[None],
        gain_rows[None],
    )


def solution(mesh):
    placed = (
        P(None, "wshard", "seq", None),
        P(None, "wshard", "seq", None),
        P(None, "wshard", None),
        P("section", None, None),
        P("section", "wshard", None),
        P("section", "wshard", None),
        P("section", "wshard", None),
        P("section", "wshard", None),
    )
    return jax.shard_map(
        per_device,
        mesh=mesh,
        in_specs=placed,
        out_specs=(
            P("section", None, "wshard", "seq", None),
            P("section", None, "wshard", "seq", None),
            P("section", ("seq", "wshard"), None),
            P("section", ("seq", "wshard"), None),
            P("section", ("seq", "wshard"), None),
            P("section", ("seq", "wshard"), None),
            P("section", None, ("seq", "wshard")),
        ),
        check_vma=False,
    )
```

time: 863 us -> 1030 us (1.19)
  waiting for transfers between devices: 409 us -> 728 us
  blocking collectives: 77.4 us -> 0 us
  matrix products: 147 us -> 97.8 us
  starting transfers between devices: 62.2 us -> 44.6 us
  Pallas kernels: 0 us -> 17.5 us
    reduce_scatter x2 -> x6, waiting for transfers between devices: 131 us -> 364 us  [seq_sum(): return lax.psum_scatter(total, 'seq', scatter_dimension=0, tiled=True)]
    all_gather x2 -> x6, waiting for transfers between devices: 206 us -> 328 us  [gathered(): own = lax.all_gather(piece, axes, axis=0, tiled=True)]
    unnamed x1 -> x0, blocking collectives: 77.4 us -> none
    dot_general x46 -> x44, matrix products: 147 us -> 97.8 us  [the longest x20 45.6 us: matmul_t(): lax.dot_general(left, right, (((1,), (1,)), ((), ())), preferred_element_...]
    scatter-add x6 -> x0, local copies, waits for them, and re-layouts: 34 us -> none  [the longest x3 18.6 us: layer_backward(): own_rows = own_rows.at[row_count - HALO:].add(returned[3 * HALO:])]
    ppermute x16 -> x33, waiting for transfers between devices: 59.6 us -> 35 us  [the longest x4 12.9 us: to_previous(): return lax.ppermute(array, 'seq', [(i + 1, i) for i in range(SEQ_DEV - 1)])]
    pallas_call x0 -> x4, Pallas kernels: none -> 17.5 us  [the longest x2 11.6 us: attend_back(): pl.pallas_call(attend_back_kernel, out_shape=(jax.ShapeDtypeStruct((rows,...]
    select_n x2 -> x17, other arithmetic: 2.16 us -> 15.1 us  [the longest x10 7.93 us: by_core(): return jnp.where(on_first, first, second)]
  transfers between devices with their start and end apart: 26 -> 45, of which waited for: 21 -> 22; matrix products, arithmetic and copies ran while one was open for 17% -> 19% of each run, Pallas kernels for 0% -> 2%
where the time goes in v1:
time: 1030 us
  waiting for transfers between devices  728 us (71%)
  matrix products  97.8 us (9%)
  local copies, waits for them, and re-layouts  74.9 us (7%)
  other arithmetic  46.9 us (5%)
  starting transfers between devices  44.6 us (4%)
  Pallas kernels  17.5 us (2%)
  between operations  16.4 us (2%)
    reduce_scatter x6, waiting for transfers between devices, seq_sum(): return lax.psum_scatter(total, 'seq', scatter_dimension=0, tiled=True)  364 us
    all_gather x6, waiting for transfers between devices, gathered(): own = lax.all_gather(piece, axes, axis=0, tiled=True)  328 us
    dot_general x20, matrix products, matmul_t(): lax.dot_general(left, right, (((1,), (1,)), ((), ())), preferred_element_...  45.6 us
    dot_general x16, matrix products, matmul(): return jnp.dot(left, right, preferred_element_type=jnp.float32)  26.8 us
    dot_general x8, matrix products, inner_rows(): lax.dot_general(left, right, (((0,), (0,)), ((), ())), preferred_element_...  25.4 us
    unnamed x213, local copies, waits for them, and re-layouts  24.6 us
  transfers between devices with their start and end apart: 45, of which 22 were waited for; matrix products, arithmetic and copies ran while one was open for 19% of the time, Pallas kernels for 2%

profile of v1, /device:TPU:1, one launch (start us, length us, event | category | flops | bytes accessed | tf_op | source)
XLA Modules:
  0.0 1026.1 jit_solution(439863050467997441)
XLA Ops:
  7.2 2.6 pad_maximum_fusion
  22.6 64.0 %all-gather.7.cloned.1.call-done = bf16[512,4096]{1,0:T(8,128)(2,1)} async-done(((bf16[8,4096]{1,0:T(8,128)(2,1)}), bf16[512,4096]{1,0:T(8,128)(2,1)}) %all-gather.7.cloned.1.call-update) | async-done | bytes 4194320 | tf_op jit(solution)/shard_map/all_gather | solution.py:335
  88.5 34.7 %all-gather.17.cloned.1.call-done = bf16[2624,512]{1,0:T(8,128)(2,1)} async-done(((bf16[656,512]{1,0:T(8,128)(2,1)}), bf16[2624,512]{1,0:T(8,128)(2,1)}) %all-gather.17.cloned.1.call-update) | async-done | bytes 2686992 | tf_op jit(solution)/shard_map/all_gather | solution.py:335
  124.1 72.0 %all-gather.9.cloned.1.call-done = bf16[512,5248]{1,0:T(8,128)(2,1)} async-done(((bf16[8,5248]{1,0:T(8,128)(2,1)}), bf16[512,5248]{1,0:T(8,128)(2,1)}) %all-gather.9.cloned.1.call-update) | async-done | bytes 5373968 | tf_op jit(solution)/shard_map/all_gather | solution.py:335
  202.8 2.4 collective-permute-start.1
  208.1 3.9 collective-permute-done.2
  212.8 20.9 %all-gather.11.cloned.1.call-done = bf16[2624,512]{1,0:T(8,128)(2,1)} async-done(((bf16[656,512]{1,0:T(8,128)(2,1)}), bf16[2624,512]{1,0:T(8,128)(2,1)}) %all-gather.11.cloned.1.call-update) | async-done | bytes 2686992 | tf_op jit(solution)/shard_map/all_gather | solution.py:335
  234.3 3.1 fusion.225
  237.4 67.1 %all-gather.13.cloned.1.call-done = bf16[512,4096]{1,0:T(8,128)(2,1)} async-done(((bf16[8,4096]{1,0:T(8,128)(2,1)}), bf16[512,4096]{1,0:T(8,128)(2,1)}) %all-gather.13.cloned.1.call-update) | async-done | bytes 4194320 | tf_op jit(solution)/shard_map/all_gather | solution.py:335
  306.1 69.5 %all-gather.15.cloned.1.call-done = bf16[512,5248]{1,0:T(8,128)(2,1)} async-done(((bf16[8,5248]{1,0:T(8,128)(2,1)}), bf16[512,5248]{1,0:T(8,128)(2,1)}) %all-gather.15.cloned.1.call-update) | async-done | bytes 5373968 | tf_op jit(solution)/shard_map/all_gather | solution.py:335
  377.7 3.2 fusion.11
  381.9 2.9 attend.2
  390.2 3.6 fusion.162
  400.2 2.6 fusion.223
  405.1 3.0 collective-permute-start.8
  412.8 2.4 pad_maximum_fusion.19
  417.1 3.0 fusion.4
  421.3 2.9 attend.3
  426.8 3.6 fusion.157
  436.1 3.1 fusion.24
  441.6 2.9 broadcast_select_fusion.35
  447.9 5.8 attend_back.2
  453.7 4.3 collective-permute-start.14
  460.5 3.2 collective-permute-done.14
  463.7 3.8 collective-permute-done.15
  468.8 3.1 broadcast_select_fusion.33
  473.6 2.9 fusion.226
  498.7 3.8 convolution_convert_fusion.3
  503.4 2.5 pad_maximum_fusion.20
  509.6 3.3 fusion.16
  512.9 3.2 fusion.20
  516.1 2.8 fusion.58
  519.0 2.9 broadcast_select_fusion.29
  530.9 4.1 convolution_convert_fusion.2
  539.4 5.8 attend_back.3
  545.2 2.4 collective-permute-start.16
  549.7 5.1 collective-permute-done.16
  554.8 5.2 collective-permute-done.17
  563.7 3.1 broadcast_select_fusion.27
  594.3 5.5 convolution_convert_fusion.1
  603.3 5.3 convolution_convert_fusion
  613.6 44.5 %reduce-scatter.17.cloned.1.call-done = bf16[192,512]{1,0:T(8,128)(2,1)} async-done(((bf16[3072,512]{1,0:T(8,128)(2,1)}), bf16[192,512]{1,0:T(8,128)(2,1)}) %reduce-scatter.17.cloned.1.call-update) | async-done | bytes 196624 | tf_op jit(solution)/shard_map/reduce_scatter | solution.py:213
  662.1 76.9 %reduce-scatter.7.cloned.1.call-done = bf16[64,2176]{1,0:T(8,128)(2,1)} async-done(((bf16[1024,2176]{1,0:T(8,128)(2,1)}), bf16[64,2176]{1,0:T(8,128)(2,1)}) %reduce-scatter.7.cloned.1.call-update) | async-done | bytes 278544 | tf_op jit(solution)/shard_map/reduce_scatter | solution.py:213
  740.0 79.7 %reduce-scatter.11.cloned.1.call-done = bf16[64,2176]{1,0:T(8,128)(2,1)} async-done(((bf16[1024,2176]{1,0:T(8,128)(2,1)}), bf16[64,2176]{1,0:T(8,128)(2,1)}) %reduce-scatter.11.cloned.1.call-update) | async-done | bytes 278544 | tf_op jit(solution)/shard_map/reduce_scatter | solution.py:213
  820.7 81.9 %reduce-scatter.9.cloned.1.call-done = bf16[64,2624]{1,0:T(8,128)(2,1)} async-done(((bf16[1024,2624]{1,0:T(8,128)(2,1)}), bf16[64,2624]{1,0:T(8,128)(2,1)}) %reduce-scatter.9.cloned.1.call-update) | async-done | bytes 335888 | tf_op jit(solution)/shard_map/reduce_scatter | solution.py:213
  903.6 81.1 %reduce-scatter.13.cloned.1.call-done = bf16[64,2624]{1,0:T(8,128)(2,1)} async-done(((bf16[1024,2624]{1,0:T(8,128)(2,1)}), bf16[64,2624]{1,0:T(8,128)(2,1)}) %reduce-scatter.13.cloned.1.call-update) | async-done | bytes 335888 | tf_op jit(solution)/shard_map/reduce_scatter | solution.py:213
  991.9 2.5 collective-permute-start.31
  1005.8 9.7 collective-permute-done.26
  (461 shorter events, 181.5 us)
Async XLA Ops:
  7.2 79.5 %all-gather.7.cloned.1.call-start = ((), (), s32[]{:S(2)}) async-start(), calls=%async_computation.6 | async-start | bytes 4259840 | tf_op jit(solution)/shard_map/all_gather | solution.py:335
  12.1 2.5 collective-permute-start.3
  16.2 107.0 %all-gather.17.cloned.1.call-start = ((), (), s32[]{:S(2)}) async-start(), calls=%async_computation.11 | async-start | bytes 3358720 | tf_op jit(solution)/shard_map/all_gather | solution.py:335
  16.4 2.2 collective-permute-start.6
  19.8 176.2 %all-gather.9.cloned.1.call-start = ((), (), s32[]{:S(2)}) async-start(), calls=%async_computation.7 | async-start | bytes 5457920 | tf_op jit(solution)/shard_map/all_gather | solution.py:335
  20.6 213.1 %all-gather.11.cloned.1.call-start = ((), (), s32[]{:S(2)}) async-start(), calls=%async_computation.8 | async-start | bytes 3358720 | tf_op jit(solution)/shard_map/all_gather | solution.py:335
  21.2 283.4 %all-gather.13.cloned.1.call-start = ((), (), s32[]{:S(2)}) async-start(), calls=%async_computation.9 | async-start | bytes 4259840 | tf_op jit(solution)/shard_map/all_gather | solution.py:335
  21.9 353.7 %all-gather.15.cloned.1.call-start = ((), (), s32[]{:S(2)}) async-start(), calls=%async_computation.10 | async-start | bytes 5457920 | tf_op jit(solution)/shard_map/all_gather | solution.py:335
  22.6 591.0 %reduce-scatter.15.cloned.1.call-start = ((), (), s32[]{:S(2)}) async-start(), calls=%async_computation.16 | async-start | bytes 3342336 | tf_op jit(solution)/shard_map/reduce_scatter | solution.py:213
  86.6 291.0 %collective-permute-start.4 = (bf16[512,4096]{1,0:T(8,128)(2,1)}, bf16[512,4096]{1,0:T(8,128)(2,1)}, u32[]{:S(2)}, u32[]{:S(2)}) collective-permute-start(bf16[512,4096]{1,0:T(8,128)(2,1)} %all-gather.7.cloned.1.call-done), channel_id=1, source_target_pairs={{0,64},{64,0},{1,65},{65,1},{2,66},{66,2},{3,67},{67,3},{4,68},{68... | collective-permute-start | bytes 12582920 | tf_op jit(solution)/shard_map/ppermute | solution.py:27
  88.2 112.2 %collective-permute-start = (f32[2,1024]{1,0:T(2,128)S(1)}, f32[2,1024]{1,0:T(2,128)S(1)}, u32[]{:S(2)}, u32[]{:S(2)}) collective-permute-start(f32[2,1024]{1,0:T(2,128)S(1)} %bitcast.142), channel_id=1, source_target_pairs={{0,64},{64,0},{1,65},{65,1},{2,66},{66,2},{3,67},{67,3},{4,68},{68... | collective-permute-start | bytes 24584 | tf_op jit(solution)/shard_map/ppermute | solution.py:27
  88.5 297.3 %copy-start.8 = (f32[1,1,128,1024]{3,2,1,0:T(8,128)}, f32[1,1,128,1024]{3,2,1,0:T(8,128)S(1)}, u32[]{:S(2)}) copy-start(f32[1,1,128,1024]{3,2,1,0:T(8,128)S(1)} %get-tuple-element.81) | copy-start | bytes 1572868
  123.2 111.1 %collective-permute-start.12 = (bf16[2624,512]{1,0:T(8,128)(2,1)}, bf16[2624,512]{1,0:T(8,128)(2,1)S(1)}, u32[]{:S(2)}, u32[]{:S(2)}) collective-permute-start(bf16[2624,512]{1,0:T(8,128)(2,1)} %all-gather.17.cloned.1.call-done), channel_id=1, source_target_pairs={{0,64},{64,0},{1,65},{65,1},{2,66},{66,2},{3,67},{67,3},{4,68},{68... | collective-permute-start | bytes 8060936 | tf_op jit(solution)/shard_map/ppermute | solution.py:27
  196.0 194.2 %collective-permute-start.5 = (bf16[512,5248]{1,0:T(8,128)(2,1)}, bf16[512,5248]{1,0:T(8,128)(2,1)}, u32[]{:S(2)}, u32[]{:S(2)}) collective-permute-start(bf16[512,5248]{1,0:T(8,128)(2,1)} %all-gather.9.cloned.1.call-done), channel_id=1, source_target_pairs={{0,64},{64,0},{1,65},{65,1},{2,66},{66,2},{3,67},{67,3},{4,68},{68... | collective-permute-start | bytes 16121864 | tf_op jit(solution)/shard_map/ppermute | solution.py:27
  202.8 5.3 collective-permute-start.1
  205.2 6.8 collective-permute-start.2
  233.7 166.6 %collective-permute-start.7 = (bf16[2624,512]{1,0:T(8,128)(2,1)}, bf16[2624,512]{1,0:T(8,128)(2,1)}, u32[]{:S(2)}, u32[]{:S(2)}) collective-permute-start(bf16[2624,512]{1,0:T(8,128)(2,1)} %all-gather.11.cloned.1.call-done), channel_id=1, source_target_pairs={{0,64},{64,0},{1,65},{65,1},{2,66},{66,2},{3,67},{67,3},{4,68},{68... | collective-permute-start | bytes 8060936 | tf_op jit(solution)/shard_map/ppermute | solution.py:27
  234.3 143.3 %copy-start.14 = (bf16[2624,512]{1,0:T(8,128)(2,1)}, bf16[2624,512]{1,0:T(8,128)(2,1)S(1)}, u32[]{:S(2)}) copy-start(bf16[2624,512]{1,0:T(8,128)(2,1)S(1)} %collective-permute-done.12) | copy-start | bytes 8060932
  304.5 112.6 %collective-permute-start.10 = (bf16[512,4096]{1,0:T(8,128)(2,1)}, bf16[512,4096]{1,0:T(8,128)(2,1)}, u32[]{:S(2)}, u32[]{:S(2)}) collective-permute-start(bf16[512,4096]{1,0:T(8,128)(2,1)} %all-gather.13.cloned.1.call-done), channel_id=1, source_target_pairs={{0,64},{64,0},{1,65},{65,1},{2,66},{66,2},{3,67},{67,3},{4,68},{68... | collective-permute-start | bytes 12582920 | tf_op jit(solution)/shard_map/ppermute | solution.py:27
  375.6 51.2 %collective-permute-start.11 = (bf16[512,5248]{1,0:T(8,128)(2,1)}, bf16[512,5248]{1,0:T(8,128)(2,1)}, u32[]{:S(2)}, u32[]{:S(2)}) collective-permute-start(bf16[512,5248]{1,0:T(8,128)(2,1)} %all-gather.15.cloned.1.call-done), channel_id=1, source_target_pairs={{0,64},{64,0},{1,65},{65,1},{2,66},{66,2},{3,67},{67,3},{4,68},{68... | collective-permute-start | bytes 16121864 | tf_op jit(solution)/shard_map/ppermute | solution.py:27
  405.1 10.9 %collective-permute-start.8 = (bf16[64,1024]{1,0:T(8,128)(2,1)}, bf16[64,1024]{1,0:T(8,128)(2,1)}, u32[]{:S(2)}, u32[]{:S(2)}) collective-permute-start(bf16[64,1024]{1,0:T(8,128)(2,1)} %get-tuple-element.161), channel_id=1, source_target_pairs={{0,4},{4,8},{8,12},{12,16},{16,20},{20,24},{24,28},{28,32},{32,36}... | collective-permute-start | bytes 393224 | tf_op jit(solution)/shard_map/ppermute | solution.py:163
  408.2 7.8 collective-permute-start.9
  415.2 83.5 %collective-permute-start.19 = (bf16[128,6144]{0,1:T(8,128)(2,1)}, bf16[128,6144]{0,1:T(8,128)(2,1)}, u32[]{:S(2)}, u32[]{:S(2)}) collective-permute-start(bf16[128,6144]{0,1:T(8,128)(2,1)} %pad_maximum_fusion.19), channel_id=1, source_target_pairs={{0,64},{64,0},{1,65},{65,1},{2,66},{66,2},{3,67},{67,3},{4,68},{68... | collective-permute-start | bytes 4718600 | tf_op jit(solution)/shard_map/ppermute | solution.py:27
  453.7 10.0 collective-permute-start.14
  458.0 9.5 collective-permute-start.15
  483.3 12.2 %collective-permute-start.21 = (bf16[128,3136]{0,1:T(8,128)(2,1)}, bf16[128,3136]{0,1:T(8,128)(2,1)}, u32[]{:S(2)}, u32[]{:S(2)}) collective-permute-start(bf16[128,3136]{0,1:T(8,128)(2,1)} %copy.69), channel_id=1, source_target_pairs={{0,64},{64,0},{1,65},{65,1},{2,66},{66,2},{3,67},{67,3},{4,68},{68... | collective-permute-start | bytes 2408456 | tf_op jit(solution)/shard_map/ppermute | solution.py:27
  502.5 155.6 %reduce-scatter.17.cloned.1.call-start = ((), (), s32[]{:S(2)}) async-start(), calls=%async_computation.17 | async-start | bytes 3342336 | tf_op jit(solution)/shard_map/reduce_scatter | solution.py:213
  506.0 24.9 %collective-permute-start.22 = (bf16[128,6144]{0,1:T(8,128)(2,1)}, bf16[128,6144]{0,1:T(8,128)(2,1)}, u32[]{:S(2)}, u32[]{:S(2)}) collective-permute-start(bf16[128,6144]{0,1:T(8,128)(2,1)} %pad_maximum_fusion.20), channel_id=1, source_target_pairs={{0,64},{64,0},{1,65},{65,1},{2,66},{66,2},{3,67},{67,3},{4,68},{68... | collective-permute-start | bytes 4718600 | tf_op jit(solution)/shard_map/ppermute | solution.py:27
  509.1 18.0 %collective-permute-start.24 = (bf16[128,3136]{0,1:T(8,128)(2,1)}, bf16[128,3136]{0,1:T(8,128)(2,1)S(1)}, u32[]{:S(2)}, u32[]{:S(2)}) collective-permute-start(bf16[128,3136]{0,1:T(8,128)(2,1)} %copy.77), channel_id=1, source_target_pairs={{0,64},{64,0},{1,65},{65,1},{2,66},{66,2},{3,67},{67,3},{4,68},{68... | collective-permute-start | bytes 2408456 | tf_op jit(solution)/shard_map/ppermute | solution.py:27
  535.1 204.0 %reduce-scatter.7.cloned.1.call-start = ((), (), s32[]{:S(2)}) async-start(), calls=%async_computation.12 | async-start | bytes 4734976 | tf_op jit(solution)/shard_map/reduce_scatter | solution.py:213
  545.2 9.5 collective-permute-start.16
  547.7 12.3 %collective-permute-start.17 = (bf16[64,2048]{1,0:T(8,128)(2,1)S(1)}, bf16[64,2048]{1,0:T(8,128)(2,1)S(1)}, u32[]{:S(2)}, u32[]{:S(2)}) collective-permute-start(bf16[64,2048]{1,0:T(8,128)(2,1)S(1)} %get-tuple-element.30), channel_id=1, source_target_pairs={{4,0},{8,4},{12,8},{16,12},{20,16},{24,20},{28,24},{32,28},{36,32}... | collective-permute-start | bytes 786440 | tf_op jit(solution)/shard_map/ppermute | solution.py:167
  561.9 5.8 collective-permute-start.20
  575.4 244.3 %reduce-scatter.11.cloned.1.call-start = ((), (), s32[]{:S(2)}) async-start(), calls=%async_computation.14 | async-start | bytes 4734976 | tf_op jit(solution)/shard_map/reduce_scatter | solution.py:213
  580.0 2.3 collective-permute-start.23
  589.9 312.7 %reduce-scatter.9.cloned.1.call-start = ((), (), s32[]{:S(2)}) async-start(), calls=%async_computation.13 | async-start | bytes 5849088 | tf_op jit(solution)/shard_map/reduce_scatter | solution.py:213
  599.8 384.9 %reduce-scatter.13.cloned.1.call-start = ((), (), s32[]{:S(2)}) async-start(), calls=%async_computation.15 | async-start | bytes 5849088 | tf_op jit(solution)/shard_map/reduce_scatter | solution.py:213
  608.7 3.6 collective-permute-start.13
  612.1 375.6 %collective-permute-start.18 = (f32[128,1024]{1,0:T(8,128)}, f32[128,1024]{1,0:T(8,128)}, u32[]{:S(2)}, u32[]{:S(2)}) collective-permute-start(f32[128,1024]{1,0:T(8,128)} %get-tuple-element.70), channel_id=1, source_target_pairs={{0,64},{64,0},{1,65},{65,1},{2,66},{66,2},{3,67},{67,3},{4,68},{68... | collective-permute-start | bytes 1572872 | tf_op jit(solution)/shard_map/ppermute | solution.py:27
  613.6 374.1 %copy-start.49 = (f32[128,1024]{1,0:T(8,128)S(1)}, f32[128,1024]{1,0:T(8,128)}, u32[]{:S(2)}) copy-start(f32[128,1024]{1,0:T(8,128)} %get-tuple-element.71) | copy-start | bytes 1572868
  659.8 329.1 %collective-permute-start.29 = (bf16[192,512]{1,0:T(8,128)(2,1)}, bf16[192,512]{1,0:T(8,128)(2,1)}, u32[]{:S(2)}, u32[]{:S(2)}) collective-permute-start(bf16[192,512]{1,0:T(8,128)(2,1)} %broadcast_select_fusion.19), channel_id=1, source_target_pairs={{0,64},{64,0},{1,65},{65,1},{2,66},{66,2},{3,67},{67,3},{4,68},{68... | collective-permute-start | bytes 589832 | tf_op jit(solution)/shard_map/ppermute | solution.py:27
  985.9 9.7 collective-permute-start.25
  990.6 10.6 %collective-permute-start.30 = (bf16[48,1024]{1,0:T(8,128)(2,1)}, bf16[48,1024]{1,0:T(8,128)(2,1)}, u32[]{:S(2)}, u32[]{:S(2)}) collective-permute-start(bf16[48,1024]{1,0:T(8,128)(2,1)} %get-tuple-element.130), channel_id=1, source_target_pairs={{0,1},{1,2},{2,3},{3,0},{4,5},{5,6},{6,7},{7,4},{8,9},{9,10},{10,1... | collective-permute-start | bytes 294920 | tf_op jit(solution)/shard_map/ppermute | solution.py:299
  991.9 12.0 %collective-permute-start.31 = (bf16[48,1024]{1,0:T(8,128)(2,1)}, bf16[48,1024]{1,0:T(8,128)(2,1)}, u32[]{:S(2)}, u32[]{:S(2)}) collective-permute-start(bf16[48,1024]{1,0:T(8,128)(2,1)} %get-tuple-element.131), channel_id=1, source_target_pairs={{0,2},{1,3},{2,0},{3,1},{4,6},{5,7},{6,4},{7,5},{8,10},{9,11},{10,... | collective-permute-start | bytes 294920 | tf_op jit(solution)/shard_map/ppermute | solution.py:299
  994.5 9.5 collective-permute-start.32
  999.9 15.6 %collective-permute-start.26 = (bf16[16,9472]{1,0:T(8,128)(2,1)S(1)}, bf16[16,9472]{1,0:T(8,128)(2,1)S(1)}, u32[]{:S(2)}, u32[]{:S(2)}) collective-permute-start(bf16[16,9472]{1,0:T(8,128)(2,1)S(1)} %get-tuple-element.92), channel_id=1, source_target_pairs={{0,1},{1,2},{2,3},{3,0},{4,5},{5,6},{6,7},{7,4},{8,9},{9,10},{10,1... | collective-permute-start | bytes 909320 | tf_op jit(solution)/shard_map/ppermute | solution.py:299
  1000.4 15.2 %collective-permute-start.27 = (bf16[16,9472]{1,0:T(8,128)(2,1)S(1)}, bf16[16,9472]{1,0:T(8,128)(2,1)S(1)}, u32[]{:S(2)}, u32[]{:S(2)}) collective-permute-start(bf16[16,9472]{1,0:T(8,128)(2,1)S(1)} %get-tuple-element.94), channel_id=1, source_target_pairs={{0,2},{1,3},{2,0},{3,1},{4,6},{5,7},{6,4},{7,5},{8,10},{9,11},{10,... | collective-permute-start | bytes 909320 | tf_op jit(solution)/shard_map/ppermute | solution.py:299
  1001.2 15.0 %collective-permute-start.28 = (bf16[16,9472]{1,0:T(8,128)(2,1)S(1)}, bf16[16,9472]{1,0:T(8,128)(2,1)S(1)}, u32[]{:S(2)}, u32[]{:S(2)}) collective-permute-start(bf16[16,9472]{1,0:T(8,128)(2,1)S(1)} %get-tuple-element.93), channel_id=1, source_target_pairs={{0,3},{1,0},{2,1},{3,2},{4,7},{5,4},{6,5},{7,6},{8,11},{9,8},{10,9... | collective-permute-start | bytes 909320 | tf_op jit(solution)/shard_map/ppermute | solution.py:299
  (79 other events, 759.1 us)
Sparse Core Ops, SparseCore 0:
  16.3 70.2 all-gather.6
  88.9 34.2 all-gather.16
  126.5 69.4 all-gather.8
  198.1 35.4 all-gather.10
  236.4 68.0 all-gather.12
  307.7 67.8 all-gather.14
  502.6 77.1 reduce-scatter.14
  583.1 74.9 reduce-scatter.16
  661.5 77.5 reduce-scatter.6
  742.2 77.4 reduce-scatter.10
  823.1 79.4 reduce-scatter.8
  905.8 78.8 reduce-scatter.12

commit v2 on v1

--- a/solution.py
+++ b/solution.py
@@ -11,9 +11,12 @@
 HEAD_DIM = 64
 FF = 2624
 HALO = 64
+FF_PAD = 2688
 SEQ_DEV = 16
 W_DEV = 4
 PAD_ROWS = 48
+BLOCK = 256
+GRAD_PAD = 2816
 
 norm_eps = 1e-05
 root_half = 1.0 / math.sqrt(2.0)
@@ -193,68 +196,100 @@
     act_mid = (normed2 * gain_pair[1]).astype(jnp.bfloat16)
     own, other = column_halves(act_mid, on_first)
     hidden = matmul(own, hidden_own) + matmul(other, hidden_other)
-    gate, up = (hidden[:, :FF], hidden[:, FF:])
+    gate, up = (hidden[:, :FF_PAD], hidden[:, FF_PAD:])
     product = (gate * split_normal(gate) * up).astype(jnp.bfloat16)
     mine, theirs = (matmul(product, down_own), matmul(product, down_other))
     output = middle + jnp.concatenate(
         [jnp.where(on_first, mine, theirs), jnp.where(on_first, theirs, mine)], axis=1
     )
-    kept = (normed1, factor1, act_in, qkv, log_total, mixed, normed2, factor2, act_mid, hidden, product)
+    acts = jnp.concatenate([jnp.stack([act_in, mixed, act_mid]), row_groups(product)], axis=0)
+    kept = (normed1, factor1, qkv, log_total, normed2, factor2, hidden, acts, swapped(acts))
     return (output, kept)
 
 
-def padded_rows(product):
-    pieces = product.reshape(product.shape[0], SEQ_DEV * W_DEV, FF // (SEQ_DEV * W_DEV))
+def row_groups(product):
+    devices, groups = (SEQ_DEV * W_DEV, PAD_ROWS // 16)
+    pieces = product[:, :FF].reshape(product.shape[0], devices, FF // devices)
     pieces = jnp.pad(pieces, ((0, 0), (0, 0), (0, PAD_ROWS - pieces.shape[2])))
-    return pieces.reshape(product.shape[0], SEQ_DEV * W_DEV * PAD_ROWS)
+    pieces = pieces.reshape(product.shape[0], devices, groups, 16).transpose(2, 0, 1, 3)
+    return pieces.reshape(groups, product.shape[0], devices * 16)
 
 
 def seq_sum(total):
     return lax.psum_scatter(total, "seq", scatter_dimension=0, tiled=True)
 
 
-def half_exchange(arrays, on_first):
-    keep, give = ([], [])
-    for low, high in arrays:
-        keep.append(jnp.where(on_first, low, high))
-        give.append(jnp.where(on_first, high, low))
-    widths = [g.shape[1] for g in give]
-    got = swapped(jnp.concatenate(give, axis=1))
-    outs, at = ([], 0)
-    for mine, w in zip(keep, widths):
-        outs.append(jnp.concatenate([mine, got[:, at : at + w]], axis=0))
-        at += w
-    return outs
+def weight_grad_kernel(
+    act_index, grad_index, act_mine, act_got, grad_mine, grad_got, gains, out, turned, rows
+):
+    step = pl.program_id(0)
+    count = act_mine.shape[1]
+
+    @pl.when((step == 0) | (act_index[step] != act_index[jnp.maximum(step - 1, 0)]))
+    def _():
+        turned[:, :count] = act_mine[0].T
+        turned[:, count:] = act_got[0].T
+
+    rows[:count] = grad_mine[...]
+    rows[count:] = grad_got[...]
+    out[...] = matmul(turned[...], rows[...]).astype(jnp.bfloat16)
+
+    @pl.when(step == (2048 + GRAD_PAD) // BLOCK - 1)
+    def _():
+        out[:, BLOCK - gains.shape[1] :] = gains[...]
+
+
+def weight_grads(act_mine, act_got, grad_mine, grad_got, gains):
+    count, width = act_mine.shape[1:]
+    sizes = (1536 // BLOCK, 512 // BLOCK, GRAD_PAD // BLOCK) + (512 // BLOCK,) * 3
+    acts, grads, at = ([], [], 0)
+    for member, blocks in enumerate(sizes):
+        first = at if member < 3 else sum(sizes[:3])
+        acts += [member] * blocks
+        grads += list(range(first, first + blocks))
+        at += blocks
+    act_spec = pl.BlockSpec((1, count, width), lambda n, a, g: (a[n], 0, 0))
+    grad_spec = pl.BlockSpec((count, BLOCK), lambda n, a, g: (0, g[n]))
+    return pl.pallas_call(
+        weight_grad_kernel,
+        grid_spec=pltpu.PrefetchScalarGridSpec(
+            num_scalar_prefetch=2,
+            grid=(len(acts),),
+            in_specs=[
+                act_spec,
+                act_spec,
+                grad_spec,
+                grad_spec,
+                pl.BlockSpec((width, 128), lambda n, a, g: (0, 0)),
+            ],
+            out_specs=pl.BlockSpec((width, BLOCK), lambda n, a, g: (0, n)),
+            scratch_shapes=[
+                pltpu.VMEM((width, 2 * count), jnp.bfloat16),
+                pltpu.VMEM((2 * count, BLOCK), jnp.bfloat16),
+            ],
+        ),
+        out_shape=jax.ShapeDtypeStruct((width, len(acts) * BLOCK), jnp.bfloat16),
+        compiler_params=params,
+        name="weight_grads",
+    )(jnp.array(acts, jnp.int32), jnp.array(grads, jnp.int32), act_mine, act_got, grad_mine, grad_got, gains)
 
 
 def layer_backward(grad_out, kept, gain_pair, weights, segs, on_first):
     (attn_own, attn_other), (hidden_own, hidden_other), (down_own, down_other) = weights
-    (normed1, factor1, act_in, qkv, log_total, mixed, normed2, factor2, act_mid, hidden, product) = kept
+    (normed1, factor1, qkv, log_total, normed2, factor2, hidden, acts, acts_got) = kept
     rows, width = normed1.shape
-    acts = jnp.concatenate([act_in, mixed, act_mid, padded_rows(product)], axis=1)
-    acts = jnp.concatenate([acts, swapped(acts)], axis=0)
-    both_in = acts[:, :width]
-    both_mixed = acts[:, width : 2 * width]
-    both_mid = acts[:, 2 * width : 3 * width]
-    both_product = acts[:, 3 * width :]
     half = width // 2
     grad_branch = grad_out.astype(jnp.bfloat16)
     low, high = (grad_branch[:, :half], grad_branch[:, half:])
-    grad_product = matmul_t(jnp.where(on_first, low, high), down_own) + matmul_t(
-        jnp.where(on_first, high, low), down_other
-    )
-    gate, up = (hidden[:, :FF], hidden[:, FF:])
+    branch_own, branch_other = (jnp.where(on_first, low, high), jnp.where(on_first, high, low))
+    grad_product = matmul_t(branch_own, down_own) + matmul_t(branch_other, down_other)
+    gate, up = (hidden[:, :FF_PAD], hidden[:, FF_PAD:])
     cumulative = split_normal(gate)
     derivative = cumulative + gate * jnp.exp(-0.5 * gate * gate) * root_two_pi
     grad_gate = (grad_product * up * derivative).astype(jnp.bfloat16)
     grad_up = (grad_product * gate * cumulative).astype(jnp.bfloat16)
-    branch_half, hidden_half = half_exchange(((low, high), (grad_gate, grad_up)), on_first)
-    down_sum = seq_sum(inner_rows(both_product, branch_half).astype(jnp.bfloat16))
-    hidden_sum = seq_sum(inner_rows(both_mid, hidden_half).astype(jnp.bfloat16))
-    mine, theirs = [
-        matmul_t(grad_gate, w[:, :FF]) + matmul_t(grad_up, w[:, FF:])
-        for w in (hidden_own, hidden_other)
-    ]
+    grad_hidden = jnp.concatenate([grad_gate, grad_up], axis=1)
+    mine, theirs = [matmul_t(grad_hidden, w) for w in (hidden_own, hidden_other)]
     grad_norm2 = from_halves(mine, theirs, on_first)
     gain_mid = jnp.sum(normed2 * grad_norm2, axis=0)
     grad_middle = grad_out + norm_back(grad_norm2 * gain_pair[1], normed2, factor2)
@@ -266,29 +301,23 @@
     from_next = to_previous(grad_before).astype(jnp.float32)
     grad_pairs = grad_own + jnp.concatenate([from_previous, from_next], axis=0)
     grad_qkv = jnp.concatenate([grad_query, grad_pairs.astype(jnp.bfloat16)], axis=1)
-    qkv_half, attn_half = half_exchange(
-        (
-            (grad_qkv[:, : 3 * half], grad_qkv[:, 3 * half :]),
-            (grad_attn[:, :half], grad_attn[:, half:]),
-        ),
-        on_first,
-    )
+    halves = (
+        (grad_qkv[:, : 3 * half], grad_qkv[:, 3 * half :]),
+        (grad_attn[:, :half], grad_attn[:, half:]),
+        (grad_gate, grad_up),
+        (jnp.zeros((rows, GRAD_PAD - FF_PAD), jnp.bfloat16),) * 2,
+        (low, high),
+    )
+    first, second = [jnp.concatenate([h[k] for h in halves], axis=1) for k in range(2)]
+    grad_mine = jnp.where(on_first, first, second)
+    grad_got = swapped(jnp.where(on_first, second, first))
     mine, theirs = [matmul_t(grad_qkv, w[:, : 3 * width]) for w in (attn_own, attn_other)]
     grad_norm1 = from_halves(mine, theirs, on_first)
     gain_first = jnp.sum(normed1 * grad_norm1, axis=0)
     grad_inputs = grad_middle + norm_back(grad_norm1 * gain_pair[0], normed1, factor1)
-    gains = jnp.stack([gain_first, gain_mid]).astype(jnp.bfloat16)
-    gain_columns = jnp.pad(gains, ((0, 126), (0, 0))).T
-    late = jnp.concatenate(
-        [
-            inner_rows(both_in, qkv_half).astype(jnp.bfloat16),
-            inner_rows(both_mixed, attn_half).astype(jnp.bfloat16),
-            gain_columns,
-        ],
-        axis=1,
-    )
-    late_sum = seq_sum(late)
-    return (grad_inputs, (late_sum, hidden_sum, down_sum))
+    gains = jnp.stack([gain_first, gain_mid])
+    gain_columns = jnp.pad(gains, ((0, 126), (0, 0))).T.astype(jnp.bfloat16)
+    return (grad_inputs, seq_sum(weight_grads(acts, acts_got, grad_mine, grad_got, gain_columns)))
 
 
 def summed_over_w(block, place):
@@ -315,7 +344,10 @@
     def sections(own, got):
         return (by_core(own, got), by_core(got, own))
 
-    row_weights = jnp.concatenate([attend_in[0], attend_out[0], hidden_in[0]], axis=1)
+    pad = jnp.zeros((hidden_in.shape[1], FF_PAD - FF), jnp.bfloat16)
+    row_weights = jnp.concatenate(
+        [attend_in[0], attend_out[0], hidden_in[0, :, :FF], pad, hidden_in[0, :, FF:], pad], axis=1
+    )
     slice_rows = row_weights.shape[0] // (2 * SEQ_DEV)
 
     def row_slice(which):
@@ -324,22 +356,38 @@
         )
 
     row_pieces = sections(row_slice(core), swapped(row_slice(1 - core)))
+    all_own = lax.all_gather(
+        jnp.concatenate(row_pieces, axis=1), ("wshard", "seq"), axis=0, tiled=True
+    )
     half = hidden_out.shape[2] // 2
     low, high = (hidden_out[0, :, :half], hidden_out[0, :, half:])
-    down_pieces = sections(by_core(low, high), swapped(by_core(high, low)))
+    down_piece = jnp.concatenate(sections(by_core(low, high), swapped(by_core(high, low))), axis=1)
+    down_pieces = [down_piece]
+    for step in range(1, W_DEV):
+        down_pieces.append(
+            lax.ppermute(down_piece, "wshard", [(j, (j + step) % W_DEV) for j in range(W_DEV)])
+        )
     gains_other = swapped(norm_gains[0])
     gain_pairs = sections(norm_gains[0], gains_other)
     attn_width = attend_in.shape[2] + attend_out.shape[2]
 
-    def gathered(piece, axes):
-        own = lax.all_gather(piece, axes, axis=0, tiled=True)
+    def both(own):
         return (own, swapped(own))
 
     def weights_of(section):
+        at, rows = (section * row_weights.shape[1], down_piece.shape[0])
+        down_own = jnp.zeros((FF_PAD, half), jnp.bfloat16)
+        for step, piece in enumerate(down_pieces):
+            down_own = lax.dynamic_update_slice_in_dim(
+                down_own,
+                piece[:, section * half : (section + 1) * half],
+                lax.rem(w_place + W_DEV - step, W_DEV) * rows,
+                0,
+            )
         return (
-            gathered(row_pieces[section][:, :attn_width], ("wshard", "seq")),
-            gathered(row_pieces[section][:, attn_width:], ("wshard", "seq")),
-            gathered(down_pieces[section], "wshard"),
+            both(all_own[:, at : at + attn_width]),
+            both(all_own[:, at + attn_width : at + row_weights.shape[1]]),
+            both(down_own),
         )
 
     weights = (weights_of(0), weights_of(1))
@@ -366,40 +414,27 @@
     section_outputs = placed(middle, final)
     section_input_grads = placed(grads0, grads1)
 
-    def both_halves(first, second):
-        mine, got = (by_core(first, second), swapped(by_core(second, first)))
-        return (by_core(mine, got), by_core(got, mine))
-
-    rows_first, rows_second = both_halves(
-        *[jnp.concatenate([sums[0], sums[1]], axis=1) for sums in (sums0, sums1)]
-    )
+    totals = [summed_over_w(sums, w_place) for sums in (sums0, sums1)]
+    mine, got = (by_core(*totals), swapped(by_core(totals[1], totals[0])))
+    low, high = (by_core(mine, got), by_core(got, mine))
     width = rows_in.shape[1]
-    attn_half, out_half = (3 * width // 2, width // 2)
-    cuts = (0, attn_half, attn_half + out_half, attn_half + out_half + 128)
-    pieces = [
-        [rows[:, cuts[k] : (cuts + (rows.shape[1],))[k + 1]] for k in range(4)]
-        for rows in (rows_first, rows_second)
-    ]
-    gain_part = pieces[0][2].astype(jnp.float32) + pieces[1][2].astype(jnp.float32)
-    row_block = jnp.concatenate(
+    attn_end, hidden_at = (3 * width // 2, 2 * width)
+    down_at = hidden_at + GRAD_PAD
+    qkv_rows = jnp.concatenate([low[:, :attn_end], high[:, :attn_end]], axis=1)
+    attn_rows = jnp.concatenate([low[:, attn_end:hidden_at], high[:, attn_end:hidden_at]], axis=1)
+    hidden_rows = jnp.concatenate(
+        [low[:, hidden_at : hidden_at + FF], high[:, hidden_at : hidden_at + FF]], axis=1
+    )
+    gain_rows = (low + high)[:, down_at - 128 : down_at - 126].T
+    down_total = jnp.concatenate(
         [
-            pieces[0][0],
-            pieces[1][0],
-            pieces[0][1],
-            pieces[1][1],
-            pieces[0][3],
-            pieces[1][3],
-            gain_part.astype(jnp.bfloat16),
+            jnp.concatenate(
+                [h[:, at : at + width // 2] for h in (low, high)], axis=1
+            )
+            for at in range(down_at, low.shape[1], width // 2)
         ],
-        axis=1,
-    )
-    row_total = summed_over_w(row_block, w_place)
-    down_block = jnp.concatenate(both_halves(sums0[2], sums1[2]), axis=1)
-    down_total = summed_over_w(down_block, w_place)[: FF // (SEQ_DEV * W_DEV)]
-    qkv_rows = row_total[:, : 3 * width]
-    attn_rows = row_total[:, 3 * width : 4 * width]
-    hidden_rows = row_total[:, 4 * width : 4 * width + 2 * FF]
-    gain_rows = row_total[:, 4 * width + 2 * FF :][:, :2].T
+        axis=0,
+    )[: FF // (SEQ_DEV * W_DEV)]
     return (
         section_outputs,
         section_input_grads,

time: 1030 us -> 588 us (0.57)
  waiting for transfers between devices: 728 us -> 275 us
  Pallas kernels: 17.5 us -> 59.4 us
  matrix products: 97.8 us -> 80.6 us
  other arithmetic: 46.9 us -> 29.9 us
  local copies, waits for them, and re-layouts: 74.9 us -> 64 us
    reduce_scatter x6 -> x2, waiting for transfers between devices: 364 us -> 114 us  [seq_sum(): return lax.psum_scatter(total, 'seq', scatter_dimension=0, tiled=True)]
    all_gather x6 -> x1, waiting for transfers between devices: 328 us -> 83.5 us  [per_device(): lax.all_gather(jnp.concatenate(row_pieces, axis=1), ('wshard', 'seq'), ax...]
    ppermute x0 -> x3, waiting for transfers between devices: none -> 57 us  [per_device(): lax.ppermute(down_piece, 'wshard', [(j, (j + step) % W_DEV) for j in rang...]
    pallas_call x0 -> x2, Pallas kernels: none -> 40.3 us  [weight_grads(): pl.pallas_call(weight_grad_kernel, grid_spec=pltpu.PrefetchScalarGridSpec...]
    dot_general x8 -> x0, matrix products: 25.4 us -> none  [inner_rows(): lax.dot_general(left, right, (((0,), (0,)), ((), ())), preferred_element_...]
    concatenate x10 -> x4, other arithmetic: 16.3 us -> 3.93 us  [the longest x2 3.03 us: layer_forward(): jnp.concatenate([jnp.stack([act_in, mixed, act_mid]), row_groups(product)...]
    unnamed x213 -> x197, local copies, waits for them, and re-layouts: 24.6 us -> 17 us
    dot_general x20 -> x16, matrix products: 45.6 us -> 45.3 us  [matmul_t(): lax.dot_general(left, right, (((1,), (1,)), ((), ())), preferred_element_...]
  transfers between devices with their start and end apart: 45 -> 36, of which waited for: 22 -> 18; matrix products, arithmetic and copies ran while one was open for 19% -> 22% of each run, Pallas kernels for 2% -> 6%
where the time goes in v2:
time: 588 us; the launch traced here: 578 us
  waiting for transfers between devices  275 us (47%)
  matrix products  80.6 us (14%)
  local copies, waits for them, and re-layouts  64 us (11%)
  Pallas kernels  59.4 us (10%)
  starting transfers between devices  53.5 us (9%)
  other arithmetic  29.9 us (5%)
  between operations  16.2 us (3%)
    reduce_scatter x2, waiting for transfers between devices, seq_sum(): return lax.psum_scatter(total, 'seq', scatter_dimension=0, tiled=True)  114 us
    all_gather x1, waiting for transfers between devices, per_device(): lax.all_gather(jnp.concatenate(row_pieces, axis=1), ('wshard', 'seq'), ax...  83.5 us
    ppermute x3, waiting for transfers between devices, per_device(): lax.ppermute(down_piece, 'wshard', [(j, (j + step) % W_DEV) for j in rang...  57 us
    dot_general x16, matrix products, matmul_t(): lax.dot_general(left, right, (((1,), (1,)), ((), ())), preferred_element_...  45.3 us
    pallas_call x2, Pallas kernels, weight_grads(): pl.pallas_call(weight_grad_kernel, grid_spec=pltpu.PrefetchScalarGridSpec...  40.3 us
    dot_general x16, matrix products, matmul(): return jnp.dot(left, right, preferred_element_type=jnp.float32)  35.3 us
    ppermute x4, starting transfers between devices, to_next(): return lax.ppermute(array, 'seq', [(i, i + 1) for i in range(SEQ_DEV - 1)])  20 us
    unnamed x197, local copies, waits for them, and re-layouts  17 us
  transfers between devices with their start and end apart: 36, of which 18 were waited for; matrix products, arithmetic and copies ran while one was open for 22% of the time, Pallas kernels for 6%

profile of v2, /device:TPU:1, one launch (start us, length us, event | category | flops | bytes accessed | tf_op | source)
XLA Modules:
  0.0 578.1 jit_solution(3106814952711932366)
XLA Ops:
  7.2 2.4 slice_bitcast_fusion
  9.7 7.6 %concatenate.143 = bf16[256,9472]{1,0:T(8,128)(2,1)} concatenate(bf16[256,3072]{1,0:T(8,128)(2,1)} %bitcast.137, bf16[256,1024]{1,0:T(8,128)(2,1)S(1)} %bitcast.138, bf16[256,2624]{1,0:T(8,128)(2,1)S(1)} %get-tuple-element.99, bf16[256,64]{1,0:T(8,128)(2,1)S(1)} %broadcast_in_dim.22, bf16[256,2624]{1,0:T(8,128)(2,1)S(1)} %get-tuple-element.98, bf16[256,64]{1,0:T(8,128)(2,1)S(1)} %broadcast_in_dim.22), dimensions={1} | concatenate | bytes 9699328 | tf_op jit(solution)/shard_map/concatenate | solution.py:348
  30.2 3.3 collective-permute-start.8
  35.5 28.7 %collective-permute-done.7 = bf16[656,1024]{1,0:T(8,128)(2,1)} collective-permute-done((bf16[656,1024]{1,0:T(8,128)(2,1)S(1)}, bf16[656,1024]{1,0:T(8,128)(2,1)}, u32[]{:S(2)}, u32[]{:S(2)}) %collective-permute-start.7) | collective-permute-done | bytes 1343520 | tf_op jit(solution)/shard_map/ppermute | solution.py:368
  64.1 2.5 slice_dynamic-update-slice_fusion.2
  66.6 28.3 %collective-permute-done.8 = bf16[656,1024]{1,0:T(8,128)(2,1)} collective-permute-done((bf16[656,1024]{1,0:T(8,128)(2,1)S(1)}, bf16[656,1024]{1,0:T(8,128)(2,1)}, u32[]{:S(2)}, u32[]{:S(2)}) %collective-permute-start.8) | collective-permute-done | bytes 1343520 | tf_op jit(solution)/shard_map/ppermute | solution.py:368
  94.9 2.5 slice_dynamic-update-slice_fusion.1
  97.4 2.5 slice_dynamic-update-slice_fusion
  101.1 83.5 %all-gather.2.cloned.1.call-done = bf16[512,18944]{1,0:T(8,128)(2,1)} async-done(((bf16[8,18944]{1,0:T(8,128)(2,1)}), bf16[512,18944]{1,0:T(8,128)(2,1)}) %all-gather.2.cloned.1.call-update) | async-done | bytes 19398672 | tf_op jit(solution)/shard_map/all_gather | solution.py:359
  184.7 5.9 %fusion.127 = (bf16[512,4096]{1,0:T(8,128)(2,1)}, bf16[512,4096]{1,0:T(8,128)(2,1)}) fusion(bf16[512,18944]{1,0:T(8,128)(2,1)} %all-gather.2.cloned.1.call-done), kind=kLoop, calls=%fused_computation.362 | loop fusion | bytes 16777216 | tf_op jit(solution)/shard_map/slice | solution.py:388
  191.3 9.0 %fusion.126 = (bf16[512,5376]{1,0:T(8,128)(2,1)}, bf16[512,5376]{1,0:T(8,128)(2,1)}) fusion(bf16[512,18944]{1,0:T(8,128)(2,1)} %all-gather.2.cloned.1.call-done), kind=kLoop, calls=%fused_computation.361 | loop fusion | bytes 22020096 | tf_op jit(solution)/shard_map/slice | solution.py:389
  202.1 4.0 collective-permute-start.1
  210.0 3.9 fusion.62
  214.7 2.9 fusion.14
  217.5 2.9 fusion.qkv
  220.4 2.9 attend.2
  227.2 3.5 fusion.71
  230.7 3.5 convolution_add_fusion.1
  241.2 5.1 collective-permute-start.11
  248.8 2.9 fusion.7
  251.7 2.9 fusion.1.qkv
  254.6 2.9 attend.3
  261.2 3.5 fusion.66
  266.0 3.0 fusion.21
  269.1 5.2 fusion.43
  274.3 1.9 broadcast_select_fusion.21
  282.1 6.7 %attend_back.2 = (bf16[128,1024]{1,0:T(8,128)(2,1)S(1)}, f32[128,2048]{1,0:T(8,128)S(1)}, bf16[64,2048]{1,0:T(8,128)(2,1)}, bf16[64,2048]{1,0:T(8,128)(2,1)}) custom-call(s32[128,1]{1,0:T(8,128)S(1)} %copy.47.query_seg, s32[1,256]{1,0:T(1,128)S(1)} %bitcast.129, bf16[256,3072]{1,0:T(8,128)(2,1)S(1)} %fusion.1.qkv, ...), custom_call_target="tpu_custom_call" | custom-call | tf_op jit(solution)/shard_map/attend_back/pallas_call | solution.py:152
  291.8 5.4 collective-permute-start.17
  304.4 3.1 fusion.5
  307.4 3.1 broadcast_select_fusion.19
  318.5 20.2 %weight_grads.3 = bf16[1024,6400]{1,0:T(8,128)(2,1)} custom-call(s32[25]{0:T(128)S(1)} %copy-done.8, s32[25]{0:T(128)S(1)} %copy-done.9, bf16[6,128,1024]{2,1,0:T(8,128)(2,1)S(1)} %pad_maximum_fusion.1.act_mine, bf16[6,128,1024]{2,1,0:T(8,128)(2,1)} %collective-permute-done.27.act_got, bf16[128,5376]{1,0:T(8,128)(2,1)S(1)} %copy-done, ...), custom_call_target="tpu_custom_call" | custom-call | tf_op jit(solution)/shard_map/weight_grads/pallas_call | solution.py:253
  340.6 2.4 fusion.143
  343.0 2.5 broadcast_select_fusion.24
  351.0 4.9 fusion.41
  356.0 4.5 broadcast_select_fusion.17
  365.8 6.5 %attend_back.3 = (bf16[128,1024]{1,0:T(8,128)(2,1)S(1)}, f32[128,2048]{1,0:T(8,128)S(1)}, bf16[64,2048]{1,0:T(8,128)(2,1)}, bf16[64,2048]{1,0:T(8,128)(2,1)S(1)}) custom-call(s32[128,1]{1,0:T(8,128)S(1)} %copy.47.query_seg, s32[1,256]{1,0:T(1,128)S(1)} %bitcast.130, bf16[256,3072]{1,0:T(8,128)(2,1)S(1)} %fusion.qkv, f32[128,1024]{1,0:T(8,128)S(1)} %copy-done.5, ...), custom_call_target="tpu_custom_call" | custom-call | tf_op jit(solution)/shard_map/attend_back/pallas_call | solution.py:152
  373.6 5.5 collective-permute-start.19
  385.5 3.5 collective-permute-done.20
  392.3 3.1 fusion.12
  395.5 3.2 broadcast_select_fusion.15
  402.8 1.9 collective-permute-done.23.grad_got
  404.7 20.1 %weight_grads.2 = bf16[1024,6400]{1,0:T(8,128)(2,1)} custom-call(s32[25]{0:T(128)S(1)} %copy-done.8, s32[25]{0:T(128)S(1)} %copy-done.9, bf16[6,128,1024]{2,1,0:T(8,128)(2,1)S(1)} %pad_maximum_fusion.act_mine, bf16[6,128,1024]{2,1,0:T(8,128)(2,1)} %collective-permute-done.22.act_got, bf16[128,5376]{1,0:T(8,128)(2,1)S(1)} %get-tuple-element.96.grad_mine, ...), custom_call_target="tpu_custom_call" | custom-call | tf_op jit(solution)/shard_map/weight_grads/pallas_call | solution.py:253
  427.5 20.9 %reduce-scatter.5.cloned.1.call-done = bf16[64,6400]{1,0:T(8,128)(2,1)} async-done(((bf16[1024,6400]{1,0:T(8,128)(2,1)}), bf16[64,6400]{1,0:T(8,128)(2,1)}) %reduce-scatter.5.cloned.1.call-update) | async-done | bytes 819216 | tf_op jit(solution)/shard_map/reduce_scatter | solution.py:219
  448.5 1.8 constant_dynamic-slice_fusion.2
  450.3 2.7 collective-permute-start.31
  454.1 92.8 %reduce-scatter.3.cloned.1.call-done = bf16[64,6400]{1,0:T(8,128)(2,1)} async-done(((bf16[1024,6400]{1,0:T(8,128)(2,1)}), bf16[64,6400]{1,0:T(8,128)(2,1)}) %reduce-scatter.3.cloned.1.call-update) | async-done | bytes 819216 | tf_op jit(solution)/shard_map/reduce_scatter | solution.py:219
  548.1 2.8 collective-permute-start.26
  557.8 6.0 %collective-permute-done.24 = bf16[16,6400]{1,0:T(8,128)(2,1)S(1)} collective-permute-done((bf16[16,6400]{1,0:T(8,128)(2,1)S(1)}, bf16[16,6400]{1,0:T(8,128)(2,1)S(1)}, u32[]{:S(2)}, u32[]{:S(2)}) %collective-permute-start.24) | collective-permute-done | bytes 204832 | tf_op jit(solution)/shard_map/ppermute | solution.py:328
  (391 shorter events, 111.2 us)
Async XLA Ops:
  7.2 177.5 %all-gather.2.cloned.1.call-start = ((), (), s32[]{:S(2)}) async-start(), calls=%async_computation.2 | async-start | bytes 19701760 | tf_op jit(solution)/shard_map/all_gather | solution.py:359
  18.3 2.5 collective-permute-start.3
  22.6 425.9 %reduce-scatter.5.cloned.1.call-start = ((), (), s32[]{:S(2)}) async-start(), calls=%async_computation.4 | async-start | bytes 13926400 | tf_op jit(solution)/shard_map/reduce_scatter | solution.py:219
  22.7 2.2 collective-permute-start.6
  28.4 35.7 %collective-permute-start.7 = (bf16[656,1024]{1,0:T(8,128)(2,1)S(1)}, bf16[656,1024]{1,0:T(8,128)(2,1)}, u32[]{:S(2)}, u32[]{:S(2)}) collective-permute-start(bf16[656,1024]{1,0:T(8,128)(2,1)S(1)} %pad_maximum_fusion.4), channel_id=1, source_target_pairs={{0,1},{1,2},{2,3},{3,0},{4,5},{5,6},{6,7},{7,4},{8,9},{9,10},{10,1... | collective-permute-start | bytes 4030472 | tf_op jit(solution)/shard_map/ppermute | solution.py:368
  30.2 64.7 %collective-permute-start.8 = (bf16[656,1024]{1,0:T(8,128)(2,1)S(1)}, bf16[656,1024]{1,0:T(8,128)(2,1)}, u32[]{:S(2)}, u32[]{:S(2)}) collective-permute-start(bf16[656,1024]{1,0:T(8,128)(2,1)S(1)} %pad_maximum_fusion.4), channel_id=1, source_target_pairs={{0,2},{1,3},{2,0},{3,1},{4,6},{5,7},{6,4},{7,5},{8,10},{9,11},{10,... | collective-permute-start | bytes 4030472 | tf_op jit(solution)/shard_map/ppermute | solution.py:368
  33.5 167.1 %collective-permute-start = (f32[2,1024]{1,0:T(2,128)S(1)}, f32[2,1024]{1,0:T(2,128)S(1)}, u32[]{:S(2)}, u32[]{:S(2)}) collective-permute-start(f32[2,1024]{1,0:T(2,128)S(1)} %bitcast.156), channel_id=1, source_target_pairs={{0,64},{64,0},{1,65},{65,1},{2,66},{66,2},{3,67},{67,3},{4,68},{68... | collective-permute-start | bytes 24584 | tf_op jit(solution)/shard_map/ppermute | solution.py:30
  34.4 63.0 %collective-permute-start.9 = (bf16[656,1024]{1,0:T(8,128)(2,1)S(1)}, bf16[656,1024]{1,0:T(8,128)(2,1)}, u32[]{:S(2)}, u32[]{:S(2)}) collective-permute-start(bf16[656,1024]{1,0:T(8,128)(2,1)S(1)} %pad_maximum_fusion.4), channel_id=1, source_target_pairs={{0,3},{1,0},{2,1},{3,2},{4,7},{5,4},{6,5},{7,6},{8,11},{9,8},{10,9... | collective-permute-start | bytes 4030472 | tf_op jit(solution)/shard_map/ppermute | solution.py:368
  35.4 188.1 %copy-start.19 = (f32[1,1,128,1024]{3,2,1,0:T(8,128)}, f32[1,1,128,1024]{3,2,1,0:T(8,128)S(1)}, u32[]{:S(2)}) copy-start(f32[1,1,128,1024]{3,2,1,0:T(8,128)S(1)} %get-tuple-element.82) | copy-start | bytes 1572868
  99.9 110.2 %collective-permute-start.15 = (bf16[2688,512]{1,0:T(8,128)(2,1)}, bf16[2688,512]{1,0:T(8,128)(2,1)}, u32[]{:S(2)}, u32[]{:S(2)}) collective-permute-start(bf16[2688,512]{1,0:T(8,128)(2,1)} %get-tuple-element.104), channel_id=1, source_target_pairs={{0,64},{64,0},{1,65},{65,1},{2,66},{66,2},{3,67},{67,3},{4,68},{68... | collective-permute-start | bytes 8257544 | tf_op jit(solution)/shard_map/ppermute | solution.py:30
  190.6 9.9 %copy-start.41 = (f32[2,1,128,1024]{3,2,1,0:T(8,128)S(1)}, f32[2,1,128,1024]{3,2,1,0:T(8,128)}, u32[]{:S(2)}) copy-start(f32[2,1,128,1024]{3,2,1,0:T(8,128)} %param.13) | copy-start | bytes 3145732
  190.6 27.0 %collective-permute-start.4 = (bf16[512,4096]{1,0:T(8,128)(2,1)}, bf16[512,4096]{1,0:T(8,128)(2,1)}, u32[]{:S(2)}, u32[]{:S(2)}) collective-permute-start(bf16[512,4096]{1,0:T(8,128)(2,1)} %get-tuple-element.86), channel_id=1, source_target_pairs={{0,64},{64,0},{1,65},{65,1},{2,66},{66,2},{3,67},{67,3},{4,68},{68... | collective-permute-start | bytes 12582920 | tf_op jit(solution)/shard_map/ppermute | solution.py:30
  200.2 30.5 %collective-permute-start.5 = (bf16[512,5376]{1,0:T(8,128)(2,1)}, bf16[512,5376]{1,0:T(8,128)(2,1)}, u32[]{:S(2)}, u32[]{:S(2)}) collective-permute-start(bf16[512,5376]{1,0:T(8,128)(2,1)} %get-tuple-element.84), channel_id=1, source_target_pairs={{0,64},{64,0},{1,65},{65,1},{2,66},{66,2},{3,67},{67,3},{4,68},{68... | collective-permute-start | bytes 16515080 | tf_op jit(solution)/shard_map/ppermute | solution.py:30
  200.6 65.1 %copy-start.51 = (bf16[128,1024]{1,0:T(8,128)(2,1)}, bf16[128,1024]{1,0:T(8,128)(2,1)S(1)}, u32[]{:S(2)}) copy-start(bf16[128,1024]{1,0:T(8,128)(2,1)S(1)} %bitcast_convert_fusion) | copy-start | bytes 786436
  200.8 6.5 %collective-permute-start.2 = (bf16[64,1024]{1,0:T(8,128)(2,1)S(1)}, bf16[64,1024]{1,0:T(8,128)(2,1)S(1)}, u32[]{:S(2)}, u32[]{:S(2)}) collective-permute-start(bf16[64,1024]{1,0:T(8,128)(2,1)S(1)} %get-tuple-element.206), channel_id=1, source_target_pairs={{4,0},{8,4},{12,8},{16,12},{20,16},{24,20},{28,24},{32,28},{36,32}... | collective-permute-start | bytes 393224 | tf_op jit(solution)/shard_map/ppermute | solution.py:170
  202.1 5.9 %collective-permute-start.1 = (bf16[64,1024]{1,0:T(8,128)(2,1)S(1)}, bf16[64,1024]{1,0:T(8,128)(2,1)S(1)}, u32[]{:S(2)}, u32[]{:S(2)}) collective-permute-start(bf16[64,1024]{1,0:T(8,128)(2,1)S(1)} %get-tuple-element.205), channel_id=1, source_target_pairs={{0,4},{4,8},{8,12},{12,16},{16,20},{20,24},{24,28},{28,32},{32,36}... | collective-permute-start | bytes 393224 | tf_op jit(solution)/shard_map/ppermute | solution.py:166
  208.2 27.6 %collective-permute-start.10 = (bf16[2688,512]{1,0:T(8,128)(2,1)}, bf16[2688,512]{1,0:T(8,128)(2,1)S(1)}, u32[]{:S(2)}, u32[]{:S(2)}) collective-permute-start(bf16[2688,512]{1,0:T(8,128)(2,1)} %get-tuple-element.105), channel_id=1, source_target_pairs={{0,64},{64,0},{1,65},{65,1},{2,66},{66,2},{3,67},{67,3},{4,68},{68... | collective-permute-start | bytes 8257544 | tf_op jit(solution)/shard_map/ppermute | solution.py:30
  213.9 37.7 %collective-permute-start.13 = (bf16[512,4096]{1,0:T(8,128)(2,1)}, bf16[512,4096]{1,0:T(8,128)(2,1)}, u32[]{:S(2)}, u32[]{:S(2)}) collective-permute-start(bf16[512,4096]{1,0:T(8,128)(2,1)} %get-tuple-element.85), channel_id=1, source_target_pairs={{0,64},{64,0},{1,65},{65,1},{2,66},{66,2},{3,67},{67,3},{4,68},{68... | collective-permute-start | bytes 12582920 | tf_op jit(solution)/shard_map/ppermute | solution.py:30
  214.1 50.6 %collective-permute-start.14 = (bf16[512,5376]{1,0:T(8,128)(2,1)S(1)}, bf16[512,5376]{1,0:T(8,128)(2,1)S(1)}, u32[]{:S(2)}, u32[]{:S(2)}) collective-permute-start(bf16[512,5376]{1,0:T(8,128)(2,1)S(1)} %copy-done.36), channel_id=1, source_target_pairs={{0,64},{64,0},{1,65},{65,1},{2,66},{66,2},{3,67},{67,3},{4,68},{68... | collective-permute-start | bytes 16515080 | tf_op jit(solution)/shard_map/ppermute | solution.py:30
  226.8 12.5 %copy-start.17 = (f32[128,1024]{1,0:T(8,128)}, f32[128,1024]{1,0:T(8,128)S(1)}, u32[]{:S(2)}) copy-start(f32[128,1024]{1,0:T(8,128)S(1)} %get-tuple-element.214) | copy-start | bytes 1572868
  239.5 18.1 %copy-start.10 = (f32[128,1024]{1,0:T(8,128)}, f32[128,1024]{1,0:T(8,128)S(1)}, u32[]{:S(2)}) copy-start(f32[128,1024]{1,0:T(8,128)S(1)} %get-tuple-element.78) | copy-start | bytes 1572868
  239.9 7.9 %collective-permute-start.12 = (bf16[64,1024]{1,0:T(8,128)(2,1)S(1)}, bf16[64,1024]{1,0:T(8,128)(2,1)S(1)}, u32[]{:S(2)}, u32[]{:S(2)}) collective-permute-start(bf16[64,1024]{1,0:T(8,128)(2,1)S(1)} %get-tuple-element.188), channel_id=1, source_target_pairs={{4,0},{8,4},{12,8},{16,12},{20,16},{24,20},{28,24},{32,28},{36,32}... | collective-permute-start | bytes 393224 | tf_op jit(solution)/shard_map/ppermute | solution.py:170
  241.2 7.5 %collective-permute-start.11 = (bf16[64,1024]{1,0:T(8,128)(2,1)S(1)}, bf16[64,1024]{1,0:T(8,128)(2,1)S(1)}, u32[]{:S(2)}, u32[]{:S(2)}) collective-permute-start(bf16[64,1024]{1,0:T(8,128)(2,1)S(1)} %get-tuple-element.187), channel_id=1, source_target_pairs={{0,4},{4,8},{8,12},{12,16},{16,20},{20,24},{24,28},{28,32},{32,36}... | collective-permute-start | bytes 393224 | tf_op jit(solution)/shard_map/ppermute | solution.py:166
  260.8 36.5 %copy-start.14 = (f32[128,1024]{1,0:T(8,128)}, f32[128,1024]{1,0:T(8,128)S(1)}, u32[]{:S(2)}) copy-start(f32[128,1024]{1,0:T(8,128)S(1)} %get-tuple-element.216) | copy-start | bytes 1572868
  269.1 29.0 %copy-start.34 = (bf16[128,2688]{1,0:T(8,128)(2,1)}, bf16[128,2688]{1,0:T(8,128)(2,1)S(1)}, u32[]{:S(2)}) copy-start(bf16[128,2688]{1,0:T(8,128)(2,1)S(1)} %get-tuple-element.97) | copy-start | bytes 2064388
  290.5 12.5 %collective-permute-start.18 = (bf16[64,2048]{1,0:T(8,128)(2,1)}, bf16[64,2048]{1,0:T(8,128)(2,1)}, u32[]{:S(2)}, u32[]{:S(2)}) collective-permute-start(bf16[64,2048]{1,0:T(8,128)(2,1)} %get-tuple-element.25), channel_id=1, source_target_pairs={{4,0},{8,4},{12,8},{16,12},{20,16},{24,20},{28,24},{32,28},{36,32}... | collective-permute-start | bytes 786440 | tf_op jit(solution)/shard_map/ppermute | solution.py:170
  291.8 11.3 %collective-permute-start.17 = (bf16[64,2048]{1,0:T(8,128)(2,1)}, bf16[64,2048]{1,0:T(8,128)(2,1)}, u32[]{:S(2)}, u32[]{:S(2)}) collective-permute-start(bf16[64,2048]{1,0:T(8,128)(2,1)} %get-tuple-element.24), channel_id=1, source_target_pairs={{0,4},{4,8},{8,12},{12,16},{16,20},{20,24},{24,28},{28,32},{32,36}... | collective-permute-start | bytes 786440 | tf_op jit(solution)/shard_map/ppermute | solution.py:166
  301.7 15.0 %collective-permute-start.27 = (bf16[6,128,1024]{2,1,0:T(8,128)(2,1)S(1)}, bf16[6,128,1024]{2,1,0:T(8,128)(2,1)}, u32[]{:S(2)}, u32[]{:S(2)}) collective-permute-start(bf16[6,128,1024]{2,1,0:T(8,128)(2,1)S(1)} %pad_maximum_fusion.1.act_mine), channel_id=1, source_target_pairs={{0,64},{64,0},{1,65},{65,1},{2,66},{66,2},{3,67},{67,3},{4,68},{68... | collective-permute-start | bytes 4718600 | tf_op jit(solution)/shard_map/ppermute | solution.py:30
  313.6 3.6 collective-permute-start.28
  338.7 208.2 %reduce-scatter.3.cloned.1.call-start = ((), (), s32[]{:S(2)}) async-start(), calls=%async_computation.3 | async-start | bytes 13926400 | tf_op jit(solution)/shard_map/reduce_scatter | solution.py:219
  346.5 14.4 %copy-start.32 = (f32[128,1024]{1,0:T(8,128)}, f32[128,1024]{1,0:T(8,128)S(1)}, u32[]{:S(2)}) copy-start(f32[128,1024]{1,0:T(8,128)S(1)} %get-tuple-element.72) | copy-start | bytes 1572868
  372.3 16.8 %collective-permute-start.20 = (bf16[64,2048]{1,0:T(8,128)(2,1)}, bf16[64,2048]{1,0:T(8,128)(2,1)}, u32[]{:S(2)}, u32[]{:S(2)}) collective-permute-start(bf16[64,2048]{1,0:T(8,128)(2,1)} %get-tuple-element.30), channel_id=1, source_target_pairs={{4,0},{8,4},{12,8},{16,12},{20,16},{24,20},{28,24},{32,28},{36,32}... | collective-permute-start | bytes 786440 | tf_op jit(solution)/shard_map/ppermute | solution.py:170
  373.6 16.1 %collective-permute-start.19 = (bf16[64,2048]{1,0:T(8,128)(2,1)S(1)}, bf16[64,2048]{1,0:T(8,128)(2,1)}, u32[]{:S(2)}, u32[]{:S(2)}) collective-permute-start(bf16[64,2048]{1,0:T(8,128)(2,1)S(1)} %get-tuple-element.29), channel_id=1, source_target_pairs={{0,4},{4,8},{8,12},{12,16},{16,20},{20,24},{24,28},{28,32},{32,36}... | collective-permute-start | bytes 786440 | tf_op jit(solution)/shard_map/ppermute | solution.py:166
  384.5 18.3 %collective-permute-start.22 = (bf16[6,128,1024]{2,1,0:T(8,128)(2,1)S(1)}, bf16[6,128,1024]{2,1,0:T(8,128)(2,1)}, u32[]{:S(2)}, u32[]{:S(2)}) collective-permute-start(bf16[6,128,1024]{2,1,0:T(8,128)(2,1)S(1)} %pad_maximum_fusion.act_mine), channel_id=1, source_target_pairs={{0,64},{64,0},{1,65},{65,1},{2,66},{66,2},{3,67},{67,3},{4,68},{68... | collective-permute-start | bytes 4718600 | tf_op jit(solution)/shard_map/ppermute | solution.py:30
  400.0 4.7 collective-permute-start.23
  425.9 125.0 %collective-permute-start.16 = (f32[128,1024]{1,0:T(8,128)S(1)}, f32[128,1024]{1,0:T(8,128)}, u32[]{:S(2)}, u32[]{:S(2)}) collective-permute-start(f32[128,1024]{1,0:T(8,128)S(1)} %copy-done.68), channel_id=1, source_target_pairs={{0,64},{64,0},{1,65},{65,1},{2,66},{66,2},{3,67},{67,3},{4,68},{68... | collective-permute-start | bytes 1572872 | tf_op jit(solution)/shard_map/ppermute | solution.py:30
  427.5 124.5 %copy-start.13 = (f32[128,1024]{1,0:T(8,128)S(1)}, f32[128,1024]{1,0:T(8,128)}, u32[]{:S(2)}) copy-start(f32[128,1024]{1,0:T(8,128)} %copy-done.10) | copy-start | bytes 1572868
  427.5 124.5 %copy-start.16 = (f32[128,1024]{1,0:T(8,128)S(1)}, f32[128,1024]{1,0:T(8,128)}, u32[]{:S(2)}) copy-start(f32[128,1024]{1,0:T(8,128)} %copy-done.14) | copy-start | bytes 1572868
  427.5 124.5 %copy-start.44 = (f32[128,512]{1,0:T(8,128)S(1)}, f32[128,512]{1,0:T(8,128)}, u32[]{:S(2)}) copy-start(f32[128,512]{1,0:T(8,128)} %copy-done.43) | copy-start | bytes 786436
  427.5 124.5 %copy-start.46 = (f32[128,512]{1,0:T(8,128)S(1)}, f32[128,512]{1,0:T(8,128)}, u32[]{:S(2)}) copy-start(f32[128,512]{1,0:T(8,128)} %copy-done.45) | copy-start | bytes 786436
  450.3 101.1 %collective-permute-start.31 = (bf16[16,6400]{1,0:T(8,128)(2,1)}, bf16[16,6400]{1,0:T(8,128)(2,1)}, u32[]{:S(2)}, u32[]{:S(2)}) collective-permute-start(bf16[16,6400]{1,0:T(8,128)(2,1)} %get-tuple-element.113), channel_id=1, source_target_pairs={{0,3},{1,0},{2,1},{3,2},{4,7},{5,4},{6,5},{7,6},{8,11},{9,8},{10,9... | collective-permute-start | bytes 614408 | tf_op jit(solution)/shard_map/ppermute | solution.py:328
  453.0 101.3 %collective-permute-start.30 = (bf16[16,6400]{1,0:T(8,128)(2,1)S(1)}, bf16[16,6400]{1,0:T(8,128)(2,1)}, u32[]{:S(2)}, u32[]{:S(2)}) collective-permute-start(bf16[16,6400]{1,0:T(8,128)(2,1)S(1)} %get-tuple-element.114), channel_id=1, source_target_pairs={{0,2},{1,3},{2,0},{3,1},{4,6},{5,7},{6,4},{7,5},{8,10},{9,11},{10,... | collective-permute-start | bytes 614408 | tf_op jit(solution)/shard_map/ppermute | solution.py:328
  453.3 102.7 %collective-permute-start.29 = (bf16[16,6400]{1,0:T(8,128)(2,1)S(1)}, bf16[16,6400]{1,0:T(8,128)(2,1)}, u32[]{:S(2)}, u32[]{:S(2)}) collective-permute-start(bf16[16,6400]{1,0:T(8,128)(2,1)S(1)} %get-tuple-element.112), channel_id=1, source_target_pairs={{0,1},{1,2},{2,3},{3,0},{4,5},{5,6},{6,7},{7,4},{8,9},{9,10},{10,1... | collective-permute-start | bytes 614408 | tf_op jit(solution)/shard_map/ppermute | solution.py:328
  548.1 8.0 %collective-permute-start.26 = (bf16[16,6400]{1,0:T(8,128)(2,1)S(1)}, bf16[16,6400]{1,0:T(8,128)(2,1)S(1)}, u32[]{:S(2)}, u32[]{:S(2)}) collective-permute-start(bf16[16,6400]{1,0:T(8,128)(2,1)S(1)} %get-tuple-element.116), channel_id=1, source_target_pairs={{0,3},{1,0},{2,1},{3,2},{4,7},{5,4},{6,5},{7,6},{8,11},{9,8},{10,9... | collective-permute-start | bytes 614408 | tf_op jit(solution)/shard_map/ppermute | solution.py:328
  550.9 6.9 %collective-permute-start.25 = (bf16[16,6400]{1,0:T(8,128)(2,1)S(1)}, bf16[16,6400]{1,0:T(8,128)(2,1)S(1)}, u32[]{:S(2)}, u32[]{:S(2)}) collective-permute-start(bf16[16,6400]{1,0:T(8,128)(2,1)S(1)} %get-tuple-element.117), channel_id=1, source_target_pairs={{0,2},{1,3},{2,0},{3,1},{4,6},{5,7},{6,4},{7,5},{8,10},{9,11},{10,... | collective-permute-start | bytes 614408 | tf_op jit(solution)/shard_map/ppermute | solution.py:328
  551.4 12.4 %collective-permute-start.24 = (bf16[16,6400]{1,0:T(8,128)(2,1)S(1)}, bf16[16,6400]{1,0:T(8,128)(2,1)S(1)}, u32[]{:S(2)}, u32[]{:S(2)}) collective-permute-start(bf16[16,6400]{1,0:T(8,128)(2,1)S(1)} %get-tuple-element.115), channel_id=1, source_target_pairs={{0,1},{1,2},{2,3},{3,0},{4,5},{5,6},{6,7},{7,4},{8,9},{9,10},{10,1... | collective-permute-start | bytes 614408 | tf_op jit(solution)/shard_map/ppermute | solution.py:328
  554.4 11.5 %collective-permute-start.21 = (f32[128,1024]{1,0:T(8,128)S(1)}, f32[128,1024]{1,0:T(8,128)S(1)}, u32[]{:S(2)}, u32[]{:S(2)}) collective-permute-start(f32[128,1024]{1,0:T(8,128)S(1)} %copy-done.69), channel_id=1, source_target_pairs={{0,64},{64,0},{1,65},{65,1},{2,66},{66,2},{3,67},{67,3},{4,68},{68... | collective-permute-start | bytes 1572872 | tf_op jit(solution)/shard_map/ppermute | solution.py:30
  565.3 1.9 collective-permute-start.32
  (60 other events, 169.1 us)
Sparse Core Ops, SparseCore 0:
  22.7 161.9 all-gather.1
  338.8 109.6 reduce-scatter.4
  452.3 94.5 reduce-scatter.2

commit v3 on v2

--- a/solution.py
+++ b/solution.py
@@ -15,8 +15,9 @@
 SEQ_DEV = 16
 W_DEV = 4
 PAD_ROWS = 48
-BLOCK = 256
 GRAD_PAD = 2816
+HIDDEN_BLOCK = 384
+QKV_BLOCK = 768
 
 norm_eps = 1e-05
 root_half = 1.0 / math.sqrt(2.0)
@@ -175,35 +176,230 @@
     return cumulative
 
 
-def layer_forward(rows_in, gain_pair, weights, segs, on_first):
-    (attn_own, attn_other), (hidden_own, hidden_other), (down_own, down_other) = weights
-    width = rows_in.shape[1]
+def grid_call(kernel, name, scalars, grid, in_specs, out_specs, out_shape, scratch, args):
+    return pl.pallas_call(
+        kernel,
+        grid_spec=pltpu.PrefetchScalarGridSpec(
+            num_scalar_prefetch=len(scalars),
+            grid=grid,
+            in_specs=in_specs,
+            out_specs=out_specs,
+            scratch_shapes=scratch,
+        ),
+        out_shape=out_shape,
+        compiler_params=params,
+        name=name,
+    )(*scalars, *args)
+
+
+def whole(array):
+    return pl.BlockSpec(array.shape, lambda n, *_: (0,) * array.ndim)
+
+
+def columns_at(rows, block, first):
+    return pl.BlockSpec((rows, block), lambda n, *_: (0, first + n))
+
+
+def rows_at(block, columns):
+    return pl.BlockSpec((block, columns), lambda n, *_: (n, 0))
+
+
+def add_to(step, total, value):
+    @pl.when(step == 0)
+    def _():
+        total[...] = value
+
+    @pl.when(step > 0)
+    def _():
+        total[...] += value
+
+
+def store_halves(out, own, other, on_first):
+    for k in range(4):
+        block = slice(128 * k, 128 * k + 128)
+        out[:, 256 * k : 256 * k + 128] = jnp.where(on_first, own[:, block], other[:, block])
+        out[:, 256 * k + 128 : 256 * k + 256] = jnp.where(on_first, other[:, block], own[:, block])
+
+
+def qkv_kernel(own, other, weight_own, weight_other, out):
+    out[...] = (
+        matmul(own[...], weight_own[...]) + matmul(other[...], weight_other[...])
+    ).astype(jnp.bfloat16)
+
+
+def qkv_of(own, other, weights):
+    (w_own, at_own), (w_other, at_other) = weights["qkv"]
+    width = 3 * HEADS * HEAD_DIM
+    depth = own.shape[1]
+    return grid_call(
+        qkv_kernel,
+        "qkv",
+        (),
+        (width // QKV_BLOCK,),
+        [
+            whole(own),
+            whole(other),
+            columns_at(depth, QKV_BLOCK, at_own // QKV_BLOCK),
+            columns_at(depth, QKV_BLOCK, at_other // QKV_BLOCK),
+        ],
+        columns_at(own.shape[0], QKV_BLOCK, 0),
+        jax.ShapeDtypeStruct((own.shape[0], width), jnp.bfloat16),
+        [],
+        (own, other, w_own, w_other),
+    )
+
+
+def qkv_back_kernel(first, grad, weight_own, weight_other, out, total_own, total_other):
+    step = pl.program_id(0)
+    add_to(step, total_own, matmul_t(grad[...], weight_own[...]))
+    add_to(step, total_other, matmul_t(grad[...], weight_other[...]))
+
+    @pl.when(step == pl.num_programs(0) - 1)
+    def _():
+        store_halves(out, total_own[...], total_other[...], first[0] == 1)
+
+
+def qkv_back(first, grad, weights):
+    (w_own, at_own), (w_other, at_other) = weights["qkv"]
+    rows, width = grad.shape
+    depth = w_own.shape[0]
+    return grid_call(
+        qkv_back_kernel,
+        "qkv_back",
+        (first,),
+        (width // QKV_BLOCK,),
+        [
+            columns_at(rows, QKV_BLOCK, 0),
+            columns_at(depth, QKV_BLOCK, at_own // QKV_BLOCK),
+            columns_at(depth, QKV_BLOCK, at_other // QKV_BLOCK),
+        ],
+        pl.BlockSpec((rows, 2 * depth), lambda n, *_: (0, 0)),
+        jax.ShapeDtypeStruct((rows, 2 * depth), jnp.float32),
+        [pltpu.VMEM((rows, depth), jnp.float32)] * 2,
+        (grad, w_own, w_other),
+    )
+
+
+def hidden_kernel(
+    first, own, other, gate_own, gate_other, up_own, up_other, down_own, down_other, middle,
+    gate_out, up_out, product_out, out, total_own, total_other,
+):
+    step = pl.program_id(0)
+    gate = matmul(own[...], gate_own[...]) + matmul(other[...], gate_other[...])
+    up = matmul(own[...], up_own[...]) + matmul(other[...], up_other[...])
+    product = (gate * split_normal(gate) * up).astype(jnp.bfloat16)
+    gate_out[...] = gate
+    up_out[...] = up
+    product_out[...] = product
+    add_to(step, total_own, matmul(product, down_own[...]))
+    add_to(step, total_other, matmul(product, down_other[...]))
+
+    @pl.when(step == pl.num_programs(0) - 1)
+    def _():
+        half = total_own.shape[1]
+        mine, theirs, on_first = (total_own[...], total_other[...], first[0] == 1)
+        out[:, :half] = middle[:, :half] + jnp.where(on_first, mine, theirs)
+        out[:, half:] = middle[:, half:] + jnp.where(on_first, theirs, mine)
+
+
+def hidden_specs(weights, depth):
+    specs, arrays = ([], [])
+    for part in ("gate", "up"):
+        for array, at in weights[part]:
+            specs.append(columns_at(depth, HIDDEN_BLOCK, at // HIDDEN_BLOCK))
+            arrays.append(array)
+    for array in weights["down"]:
+        specs.append(rows_at(HIDDEN_BLOCK, array.shape[1]))
+        arrays.append(array)
+    return (specs, arrays)
+
+
+def hidden_forward(first, own, other, middle, weights):
+    rows, depth = own.shape
+    width = middle.shape[1]
+    specs, arrays = hidden_specs(weights, depth)
+    piece = columns_at(rows, HIDDEN_BLOCK, 0)
+    return grid_call(
+        hidden_kernel,
+        "hidden",
+        (first,),
+        (FF_PAD // HIDDEN_BLOCK,),
+        [whole(own), whole(other), *specs, whole(middle)],
+        (piece, piece, piece, whole(middle)),
+        (
+            jax.ShapeDtypeStruct((rows, FF_PAD), jnp.float32),
+            jax.ShapeDtypeStruct((rows, FF_PAD), jnp.float32),
+            jax.ShapeDtypeStruct((rows, FF_PAD), jnp.bfloat16),
+            jax.ShapeDtypeStruct((rows, width), jnp.float32),
+        ),
+        [pltpu.VMEM((rows, width // 2), jnp.float32)] * 2,
+        (own, other, *arrays, middle),
+    )
+
+
+def hidden_back_kernel(
+    first, grad_own, grad_other, gate_in, up_in, gate_own, gate_other, up_own, up_other, down_own,
+    down_other, grad_gate_out, grad_up_out, out, total_own, total_other,
+):
+    step = pl.program_id(0)
+    gate, up = (gate_in[...], up_in[...])
+    grad_product = matmul_t(grad_own[...], down_own[...]) + matmul_t(
+        grad_other[...], down_other[...]
+    )
+    cumulative = split_normal(gate)
+    derivative = cumulative + gate * jnp.exp(-0.5 * gate * gate) * root_two_pi
+    grad_gate = (grad_product * up * derivative).astype(jnp.bfloat16)
+    grad_up = (grad_product * gate * cumulative).astype(jnp.bfloat16)
+    grad_gate_out[...] = grad_gate
+    grad_up_out[...] = grad_up
+    add_to(step, total_own, matmul_t(grad_gate, gate_own[...]) + matmul_t(grad_up, up_own[...]))
+    add_to(
+        step, total_other, matmul_t(grad_gate, gate_other[...]) + matmul_t(grad_up, up_other[...])
+    )
+
+    @pl.when(step == pl.num_programs(0) - 1)
+    def _():
+        store_halves(out, total_own[...], total_other[...], first[0] == 1)
+
+
+def hidden_back(first, grad_own, grad_other, gate, up, weights):
+    rows, half = grad_own.shape
+    depth = half
+    specs, arrays = hidden_specs(weights, depth)
+    piece = columns_at(rows, HIDDEN_BLOCK, 0)
+    return grid_call(
+        hidden_back_kernel,
+        "hidden_back",
+        (first,),
+        (FF_PAD // HIDDEN_BLOCK,),
+        [whole(grad_own), whole(grad_other), piece, piece, *specs],
+        (piece, piece, pl.BlockSpec((rows, 2 * depth), lambda n, *_: (0, 0))),
+        (
+            jax.ShapeDtypeStruct((rows, FF_PAD), jnp.bfloat16),
+            jax.ShapeDtypeStruct((rows, FF_PAD), jnp.bfloat16),
+            jax.ShapeDtypeStruct((rows, 2 * depth), jnp.float32),
+        ),
+        [pltpu.VMEM((rows, depth), jnp.float32)] * 2,
+        (grad_own, grad_other, gate, up, *arrays),
+    )
+
+
+def layer_forward(rows_in, gain_pair, weights, segs, on_first, first):
     normed1, factor1 = norm_parts(rows_in)
     act_in = (normed1 * gain_pair[0]).astype(jnp.bfloat16)
     before = to_next(act_in[act_in.shape[0] - HALO :])
     after = to_previous(act_in[:HALO])
     extended = jnp.concatenate([before, act_in, after], axis=0)
-    own, other = column_halves(extended, on_first)
-    qkv = (
-        matmul(own, attn_own[:, : 3 * width]) + matmul(other, attn_other[:, : 3 * width])
-    ).astype(jnp.bfloat16)
+    qkv = qkv_of(*column_halves(extended, on_first), weights)
     mixed, log_total = attend(*segs, qkv)
     own, other = column_halves(mixed, on_first)
-    middle = (
-        rows_in + matmul(own, attn_own[:, 3 * width :]) + matmul(other, attn_other[:, 3 * width :])
-    )
+    middle = rows_in + matmul(own, weights["out"][0]) + matmul(other, weights["out"][1])
     normed2, factor2 = norm_parts(middle)
     act_mid = (normed2 * gain_pair[1]).astype(jnp.bfloat16)
     own, other = column_halves(act_mid, on_first)
-    hidden = matmul(own, hidden_own) + matmul(other, hidden_other)
-    gate, up = (hidden[:, :FF_PAD], hidden[:, FF_PAD:])
-    product = (gate * split_normal(gate) * up).astype(jnp.bfloat16)
-    mine, theirs = (matmul(product, down_own), matmul(product, down_other))
-    output = middle + jnp.concatenate(
-        [jnp.where(on_first, mine, theirs), jnp.where(on_first, theirs, mine)], axis=1
-    )
+    gate, up, product, output = hidden_forward(first, own, other, middle, weights)
     acts = jnp.concatenate([jnp.stack([act_in, mixed, act_mid]), row_groups(product)], axis=0)
-    kept = (normed1, factor1, qkv, log_total, normed2, factor2, hidden, acts, swapped(acts))
+    kept = (normed1, factor1, qkv, log_total, normed2, factor2, gate, up, acts, swapped(acts))
     return (output, kept)
 
 
@@ -219,82 +415,62 @@
     return lax.psum_scatter(total, "seq", scatter_dimension=0, tiled=True)
 
 
-def weight_grad_kernel(
-    act_index, grad_index, act_mine, act_got, grad_mine, grad_got, gains, out, turned, rows
-):
-    step = pl.program_id(0)
+GRAD_WIDTHS = (1536, 512, GRAD_PAD, 512, 512, 512)
+
+
+def weight_grad_kernel(act_mine, act_got, grad_mine, grad_got, gains, out, grads):
     count = act_mine.shape[1]
 
-    @pl.when((step == 0) | (act_index[step] != act_index[jnp.maximum(step - 1, 0)]))
+    @pl.when(pl.program_id(0) == 0)
     def _():
-        turned[:, :count] = act_mine[0].T
-        turned[:, count:] = act_got[0].T
-
-    rows[:count] = grad_mine[...]
-    rows[count:] = grad_got[...]
-    out[...] = matmul(turned[...], rows[...]).astype(jnp.bfloat16)
-
-    @pl.when(step == (2048 + GRAD_PAD) // BLOCK - 1)
-    def _():
-        out[:, BLOCK - gains.shape[1] :] = gains[...]
+        grads[:count] = grad_mine[...]
+        grads[count:] = grad_got[...]
+
+    at = 0
+    for member, width in enumerate(GRAD_WIDTHS):
+        acts = jnp.concatenate([act_mine[member], act_got[member]], axis=0)
+        place = at if member < 3 else sum(GRAD_WIDTHS[:3])
+        for part in range(0, width, 512):
+            size = min(512, width - part)
+            out[:, at + part : at + part + size] = inner_rows(
+                acts, grads[:, place + part : place + part + size]
+            ).astype(jnp.bfloat16)
+        at += width
+    end = sum(GRAD_WIDTHS[:3])
+    out[:, end - gains.shape[1] : end] = gains[...]
 
 
 def weight_grads(act_mine, act_got, grad_mine, grad_got, gains):
-    count, width = act_mine.shape[1:]
-    sizes = (1536 // BLOCK, 512 // BLOCK, GRAD_PAD // BLOCK) + (512 // BLOCK,) * 3
-    acts, grads, at = ([], [], 0)
-    for member, blocks in enumerate(sizes):
-        first = at if member < 3 else sum(sizes[:3])
-        acts += [member] * blocks
-        grads += list(range(first, first + blocks))
-        at += blocks
-    act_spec = pl.BlockSpec((1, count, width), lambda n, a, g: (a[n], 0, 0))
-    grad_spec = pl.BlockSpec((count, BLOCK), lambda n, a, g: (0, g[n]))
-    return pl.pallas_call(
+    members, count, width = act_mine.shape
+    block = 256
+    acts = pl.BlockSpec((members, count, block), lambda n: (0, 0, n))
+    return grid_call(
         weight_grad_kernel,
-        grid_spec=pltpu.PrefetchScalarGridSpec(
-            num_scalar_prefetch=2,
-            grid=(len(acts),),
-            in_specs=[
-                act_spec,
-                act_spec,
-                grad_spec,
-                grad_spec,
-                pl.BlockSpec((width, 128), lambda n, a, g: (0, 0)),
-            ],
-            out_specs=pl.BlockSpec((width, BLOCK), lambda n, a, g: (0, n)),
-            scratch_shapes=[
-                pltpu.VMEM((width, 2 * count), jnp.bfloat16),
-                pltpu.VMEM((2 * count, BLOCK), jnp.bfloat16),
-            ],
-        ),
-        out_shape=jax.ShapeDtypeStruct((width, len(acts) * BLOCK), jnp.bfloat16),
-        compiler_params=params,
-        name="weight_grads",
-    )(jnp.array(acts, jnp.int32), jnp.array(grads, jnp.int32), act_mine, act_got, grad_mine, grad_got, gains)
-
-
-def layer_backward(grad_out, kept, gain_pair, weights, segs, on_first):
-    (attn_own, attn_other), (hidden_own, hidden_other), (down_own, down_other) = weights
-    (normed1, factor1, qkv, log_total, normed2, factor2, hidden, acts, acts_got) = kept
+        "weight_grads",
+        (),
+        (width // block,),
+        [acts, acts, whole(grad_mine), whole(grad_got), rows_at(block, gains.shape[1])],
+        rows_at(block, sum(GRAD_WIDTHS)),
+        jax.ShapeDtypeStruct((width, sum(GRAD_WIDTHS)), jnp.bfloat16),
+        [pltpu.VMEM((2 * count, grad_mine.shape[1]), jnp.bfloat16)],
+        (act_mine, act_got, grad_mine, grad_got, gains),
+    )
+
+
+def layer_backward(grad_out, kept, gain_pair, weights, segs, on_first, first):
+    (normed1, factor1, qkv, log_total, normed2, factor2, gate, up, acts, acts_got) = kept
     rows, width = normed1.shape
     half = width // 2
     grad_branch = grad_out.astype(jnp.bfloat16)
     low, high = (grad_branch[:, :half], grad_branch[:, half:])
     branch_own, branch_other = (jnp.where(on_first, low, high), jnp.where(on_first, high, low))
-    grad_product = matmul_t(branch_own, down_own) + matmul_t(branch_other, down_other)
-    gate, up = (hidden[:, :FF_PAD], hidden[:, FF_PAD:])
-    cumulative = split_normal(gate)
-    derivative = cumulative + gate * jnp.exp(-0.5 * gate * gate) * root_two_pi
-    grad_gate = (grad_product * up * derivative).astype(jnp.bfloat16)
-    grad_up = (grad_product * gate * cumulative).astype(jnp.bfloat16)
-    grad_hidden = jnp.concatenate([grad_gate, grad_up], axis=1)
-    mine, theirs = [matmul_t(grad_hidden, w) for w in (hidden_own, hidden_other)]
-    grad_norm2 = from_halves(mine, theirs, on_first)
+    grad_gate, grad_up, grad_norm2 = hidden_back(
+        first, branch_own, branch_other, gate, up, weights
+    )
     gain_mid = jnp.sum(normed2 * grad_norm2, axis=0)
     grad_middle = grad_out + norm_back(grad_norm2 * gain_pair[1], normed2, factor2)
     grad_attn = grad_middle.astype(jnp.bfloat16)
-    mine, theirs = [matmul_t(grad_attn, w[:, 3 * width :]) for w in (attn_own, attn_other)]
+    mine, theirs = [matmul_t(grad_attn, w) for w in weights["out"]]
     grad_mixed = from_halves(mine, theirs, on_first).astype(jnp.bfloat16)
     grad_query, grad_own, grad_before, grad_after = attend_back(*segs, qkv, log_total, grad_mixed)
     from_previous = to_next(grad_after).astype(jnp.float32)
@@ -308,11 +484,10 @@
         (jnp.zeros((rows, GRAD_PAD - FF_PAD), jnp.bfloat16),) * 2,
         (low, high),
     )
-    first, second = [jnp.concatenate([h[k] for h in halves], axis=1) for k in range(2)]
-    grad_mine = jnp.where(on_first, first, second)
-    grad_got = swapped(jnp.where(on_first, second, first))
-    mine, theirs = [matmul_t(grad_qkv, w[:, : 3 * width]) for w in (attn_own, attn_other)]
-    grad_norm1 = from_halves(mine, theirs, on_first)
+    first_half, second_half = [jnp.concatenate([h[k] for h in halves], axis=1) for k in range(2)]
+    grad_mine = jnp.where(on_first, first_half, second_half)
+    grad_got = swapped(jnp.where(on_first, second_half, first_half))
+    grad_norm1 = qkv_back(first, grad_qkv, weights)
     gain_first = jnp.sum(normed1 * grad_norm1, axis=0)
     grad_inputs = grad_middle + norm_back(grad_norm1 * gain_pair[0], normed1, factor1)
     gains = jnp.stack([gain_first, gain_mid])
@@ -344,53 +519,79 @@
     def sections(own, got):
         return (by_core(own, got), by_core(got, own))
 
-    pad = jnp.zeros((hidden_in.shape[1], FF_PAD - FF), jnp.bfloat16)
-    row_weights = jnp.concatenate(
-        [attend_in[0], attend_out[0], hidden_in[0, :, :FF], pad, hidden_in[0, :, FF:], pad], axis=1
-    )
-    slice_rows = row_weights.shape[0] // (2 * SEQ_DEV)
+    slice_rows = attend_in.shape[1] // (2 * SEQ_DEV)
+    pad = jnp.zeros((slice_rows, FF_PAD - FF), jnp.bfloat16)
+    width = inputs.shape[3]
 
     def row_slice(which):
-        return lax.dynamic_slice_in_dim(
-            row_weights, (which * SEQ_DEV + seq_place) * slice_rows, slice_rows
-        )
+        at = (which * SEQ_DEV + seq_place) * slice_rows
+        hidden, qkv, out = [
+            lax.dynamic_slice_in_dim(w[0], at, slice_rows)
+            for w in (hidden_in, attend_in, attend_out)
+        ]
+        return jnp.concatenate([hidden[:, :FF], pad, hidden[:, FF:], pad, qkv, out], axis=1)
 
     row_pieces = sections(row_slice(core), swapped(row_slice(1 - core)))
+    up_at, qkv_at, out_at = (FF_PAD, 2 * FF_PAD, 2 * FF_PAD + 3 * width)
     all_own = lax.all_gather(
-        jnp.concatenate(row_pieces, axis=1), ("wshard", "seq"), axis=0, tiled=True
+        jnp.concatenate(
+            [piece[:, :out_at] for piece in row_pieces] + [piece[:, out_at:] for piece in row_pieces],
+            axis=1,
+        ),
+        ("wshard", "seq"),
+        axis=0,
+        tiled=True,
     )
     half = hidden_out.shape[2] // 2
     low, high = (hidden_out[0, :, :half], hidden_out[0, :, half:])
     down_piece = jnp.concatenate(sections(by_core(low, high), swapped(by_core(high, low))), axis=1)
-    down_pieces = [down_piece]
-    for step in range(1, W_DEV):
-        down_pieces.append(
-            lax.ppermute(down_piece, "wshard", [(j, (j + step) % W_DEV) for j in range(W_DEV)])
-        )
-    gains_other = swapped(norm_gains[0])
-    gain_pairs = sections(norm_gains[0], gains_other)
-    attn_width = attend_in.shape[2] + attend_out.shape[2]
-
-    def both(own):
+    w_up = [(j, (j + 1) % W_DEV) for j in range(W_DEV)]
+    w_down = [(j, i) for i, j in w_up]
+    below = lax.ppermute(down_piece, "wshard", w_up)
+    above = lax.ppermute(down_piece, "wshard", w_down)
+    far = (
+        lax.ppermute(below[:, :half], "wshard", w_up),
+        lax.ppermute(above[:, half:], "wshard", w_down),
+    )
+    gain_pairs = sections(norm_gains[0], swapped(norm_gains[0]))
+    piece_rows = down_piece.shape[0]
+
+    def down_of(section):
+        columns = slice(section * half, (section + 1) * half)
+        own = jnp.zeros((FF_PAD, half), jnp.bfloat16)
+        for step, piece in (
+            (0, down_piece[:, columns]),
+            (1, above[:, columns]),
+            (2, far[section]),
+            (3, below[:, columns]),
+        ):
+            own = lax.dynamic_update_slice_in_dim(
+                own, piece, lax.rem(w_place + step, W_DEV) * piece_rows, 0
+            )
         return (own, swapped(own))
 
-    def weights_of(section):
-        at, rows = (section * row_weights.shape[1], down_piece.shape[0])
-        down_own = jnp.zeros((FF_PAD, half), jnp.bfloat16)
-        for step, piece in enumerate(down_pieces):
-            down_own = lax.dynamic_update_slice_in_dim(
-                down_own,
-                piece[:, section * half : (section + 1) * half],
-                lax.rem(w_place + W_DEV - step, W_DEV) * rows,
-                0,
-            )
-        return (
-            both(all_own[:, at : at + attn_width]),
-            both(all_own[:, at + attn_width : at + row_weights.shape[1]]),
-            both(down_own),
-        )
-
-    weights = (weights_of(0), weights_of(1))
+    first_qkv = swapped(all_own[:, qkv_at:out_at])
+    first_out = swapped(all_own[:, 2 * out_at : 2 * out_at + width])
+    first_hidden = swapped(all_own[:, :qkv_at])
+    all_other = swapped(all_own)
+    out_own = [all_own[:, 2 * out_at + k * width : 2 * out_at + (k + 1) * width] for k in (0, 1)]
+    weights = (
+        {
+            "qkv": ((all_own, qkv_at), (first_qkv, 0)),
+            "gate": ((all_own, 0), (first_hidden, 0)),
+            "up": ((all_own, up_at), (first_hidden, up_at)),
+            "out": (out_own[0], first_out),
+            "down": down_of(0),
+        },
+        {
+            "qkv": ((all_own, out_at + qkv_at), (all_other, out_at + qkv_at)),
+            "gate": ((all_own, out_at), (all_other, out_at)),
+            "up": ((all_own, out_at + up_at), (all_other, out_at + up_at)),
+            "out": (out_own[1], all_other[:, 2 * out_at + width :]),
+            "down": down_of(1),
+        },
+    )
+    first = on_first.astype(jnp.int32)[None]
     rows_in = by_core(inputs[0, 0], inputs[1, 0])
     row_count = rows_in.shape[0]
     segment_row = by_core(segments[0, 0], segments[1, 0])
@@ -400,11 +601,11 @@
         lax.dynamic_slice_in_dim(segment_row, first_row, row_count)[:, None],
         lax.dynamic_slice_in_dim(padded, first_row, row_count + 2 * HALO)[None, :],
     )
-    middle, kept0 = layer_forward(rows_in, gain_pairs[0], weights[0], segs, on_first)
-    final, kept1 = layer_forward(middle, gain_pairs[1], weights[1], segs, on_first)
+    middle, kept0 = layer_forward(rows_in, gain_pairs[0], weights[0], segs, on_first, first)
+    final, kept1 = layer_forward(middle, gain_pairs[1], weights[1], segs, on_first, first)
     upstream = by_core(cotangent[0, 0], cotangent[1, 0])
-    grads1, sums1 = layer_backward(upstream, kept1, gain_pairs[1], weights[1], segs, on_first)
-    grads0, sums0 = layer_backward(grads1, kept0, gain_pairs[0], weights[0], segs, on_first)
+    grads1, sums1 = layer_backward(upstream, kept1, gain_pairs[1], weights[1], segs, on_first, first)
+    grads0, sums0 = layer_backward(grads1, kept0, gain_pairs[0], weights[0], segs, on_first, first)
 
     def placed(first, second):
         mine, give = (by_core(first, second), by_core(second, first))
@@ -417,7 +618,6 @@
     totals = [summed_over_w(sums, w_place) for sums in (sums0, sums1)]
     mine, got = (by_core(*totals), swapped(by_core(totals[1], totals[0])))
     low, high = (by_core(mine, got), by_core(got, mine))
-    width = rows_in.shape[1]
     attn_end, hidden_at = (3 * width // 2, 2 * width)
     down_at = hidden_at + GRAD_PAD
     qkv_rows = jnp.concatenate([low[:, :attn_end], high[:, :attn_end]], axis=1)

time: 588 us -> 604 us (1.027)
  matrix products: 80.6 us -> 13.6 us
  Pallas kernels: 59.4 us -> 103 us
  waiting for transfers between devices: 275 us -> 307 us
  other arithmetic: 29.9 us -> 36.1 us
    pallas_call x2 -> x10, Pallas kernels: 40.3 us -> 84 us  [grid_call(): pl.pallas_call(kernel, grid_spec=pltpu.PrefetchScalarGridSpec(num_scalar_...]
    dot_general x16 -> x4, matrix products: 45.3 us -> 7.12 us  [matmul_t(): lax.dot_general(left, right, (((1,), (1,)), ((), ())), preferred_element_...]
    all_gather x1, waiting for transfers between devices: 83.5 us -> 114 us  [per_device(): lax.all_gather(jnp.concatenate([piece[:, :out_at] for piece in row_pieces...]
    dot_general x16 -> x4, matrix products: 35.3 us -> 6.44 us  [matmul(): return jnp.dot(left, right, preferred_element_type=jnp.float32)]
    ppermute x3 -> x4, waiting for transfers between devices: 57 us -> 46.6 us  [the longest x1 18.2 us: per_device(): above = lax.ppermute(down_piece, 'wshard', w_down)]
    concatenate x1 -> x2, local copies, waits for them, and re-layouts: 7.62 us -> 0.18 us  [row_slice(): jnp.concatenate([hidden[:, :FF], pad, hidden[:, FF:], pad, qkv, out], axi...]
    unnamed x197 -> x145, local copies, waits for them, and re-layouts: 17 us -> 22.8 us
    slice x2 -> x9, local copies, waits for them, and re-layouts: 14.9 us -> 14 us  [the longest x1 5.31 us: per_device(): first_hidden = swapped(all_own[:, :qkv_at])]
  transfers between devices with their start and end apart: 36 -> 37, of which waited for: 18 -> 14; matrix products, arithmetic and copies ran while one was open for 22% -> 14% of each run, Pallas kernels for 6% -> 11%
where the time goes in v3:
time: 604 us; the launch traced here: 596 us
  waiting for transfers between devices  307 us (51%)
  Pallas kernels  103 us (17%)
  local copies, waits for them, and re-layouts  69.1 us (11%)
  starting transfers between devices  51.6 us (9%)
  other arithmetic  36.1 us (6%)
  between operations  15.3 us (3%)
  matrix products  13.6 us (2%)
    reduce_scatter x2, waiting for transfers between devices, seq_sum(): return lax.psum_scatter(total, 'seq', scatter_dimension=0, tiled=True)  120 us
    all_gather x1, waiting for transfers between devices, per_device(): lax.all_gather(jnp.concatenate([piece[:, :out_at] for piece in row_pieces...  114 us
    pallas_call x10, Pallas kernels, grid_call(): pl.pallas_call(kernel, grid_spec=pltpu.PrefetchScalarGridSpec(num_scalar_...  84 us
    unnamed x145, local copies, waits for them, and re-layouts  22.8 us
    ppermute x1, waiting for transfers between devices, per_device(): above = lax.ppermute(down_piece, 'wshard', w_down)  18.2 us
    ppermute x4, starting transfers between devices, to_next(): return lax.ppermute(array, 'seq', [(i, i + 1) for i in range(SEQ_DEV - 1)])  15.3 us
    ppermute x16, starting transfers between devices, swapped(): return lax.ppermute(array, 'section', SWAP)  14.7 us
    ppermute x1, waiting for transfers between devices, per_device(): lax.ppermute(above[:, half:], 'wshard', w_down)  14.5 us
  transfers between devices with their start and end apart: 37, of which 14 were waited for; matrix products, arithmetic and copies ran while one was open for 14% of the time, Pallas kernels for 11%

profile of v3, /device:TPU:1, one launch (start us, length us, event | category | flops | bytes accessed | tf_op | source)
XLA Modules:
  0.0 595.8 jit_solution(10485538697270992302)
XLA Ops:
  13.3 114.4 %all-gather.2.cloned.1.call-done.weight_own.gate_own.up_own = bf16[512,18944]{1,0:T(8,128)(2,1)} async-done(((bf16[8,18944]{1,0:T(8,128)(2,1)}), bf16[512,18944]{1,0:T(8,128)(2,1)}) %all-gather.2.cloned.1.call-update) | async-done | bytes 19398672 | tf_op jit(solution)/shard_map/all_gather | solution.py:536
  128.6 9.0 %collective-permute-done.7 = bf16[656,512]{1,0:T(8,128)(2,1)S(1)} collective-permute-done((bf16[656,512]{1,0:T(8,128)(2,1)S(1)}, bf16[656,512]{1,0:T(8,128)(2,1)S(1)}, u32[]{:S(2)}, u32[]{:S(2)}) %collective-permute-start.7) | collective-permute-done | bytes 671776 | tf_op jit(solution)/shard_map/ppermute | solution.py:31
  144.5 2.4 collective-permute-start.8
  148.5 5.3 slice.553
  153.9 3.8 slice.542
  157.8 18.2 %collective-permute-done.8 = bf16[656,1024]{1,0:T(8,128)(2,1)} collective-permute-done((bf16[656,1024]{1,0:T(8,128)(2,1)}, bf16[656,1024]{1,0:T(8,128)(2,1)}, u32[]{:S(2)}, u32[]{:S(2)}) %collective-permute-start.8) | collective-permute-done | bytes 1343520 | tf_op jit(solution)/shard_map/ppermute | solution.py:551
  177.0 2.5 fusion.40
  179.5 3.4 collective-permute-start.15
  182.9 14.5 %collective-permute-done.15 = bf16[656,512]{1,0:T(8,128)(2,1)S(1)} collective-permute-done((bf16[656,512]{1,0:T(8,128)(2,1)S(1)}, bf16[656,512]{1,0:T(8,128)(2,1)S(1)}, u32[]{:S(2)}, u32[]{:S(2)}) %collective-permute-start.15) | collective-permute-done | bytes 671776 | tf_op jit(solution)/shard_map/ppermute | solution.py:554
  198.3 2.3 slice_dynamic-update-slice_fusion
  202.2 2.6 collective-permute-start.1
  204.8 13.9 %collective-permute-done.10 = bf16[656,512]{1,0:T(8,128)(2,1)S(1)} collective-permute-done((bf16[656,512]{1,0:T(8,128)(2,1)S(1)}, bf16[656,512]{1,0:T(8,128)(2,1)S(1)}, u32[]{:S(2)}, u32[]{:S(2)}) %collective-permute-start.10) | collective-permute-done | bytes 671776 | tf_op jit(solution)/shard_map/ppermute | solution.py:553
  220.9 2.0 constant_dynamic-update-slice_fusion.27.down_own
  225.7 2.3 slice.543
  232.1 1.9 copy-done.1
  234.0 4.2 qkv.2
  238.2 2.9 attend.2
  245.0 10.4 %hidden.2 = (f32[128,2688]{1,0:T(8,128)S(1)}, f32[128,2688]{1,0:T(8,128)S(1)}, bf16[128,2688]{1,0:T(8,128)(2,1)S(1)}, f32[128,1024]{1,0:T(8,128)S(1)}) custom-call(s32[1]{0:T(128)} %bitcast.first, bf16[128,512]{1,0:T(8,128)(2,1)S(1)} %get-tuple-element.208.own, bf16[128,512]{1,0:T(8,128)(2,1)S(1)} %get-tuple-element.207.other, ...), custom_call_target="tpu_custom_call" | custom-call | tf_op jit(solution)/shard_map/hidden/pallas_call | solution.py:180
  259.0 4.3 collective-permute-start.12
  266.2 3.8 collective-permute-done.13
  270.3 4.7 qkv.3
  275.0 2.9 attend.3
  281.7 10.5 %hidden.3 = (f32[128,2688]{1,0:T(8,128)S(1)}, f32[128,2688]{1,0:T(8,128)S(1)}, bf16[128,2688]{1,0:T(8,128)(2,1)S(1)}, f32[128,1024]{1,0:T(8,128)S(1)}) custom-call(s32[1]{0:T(128)} %bitcast.first, bf16[128,512]{1,0:T(8,128)(2,1)S(1)} %get-tuple-element.188.own, bf16[128,512]{1,0:T(8,128)(2,1)S(1)} %get-tuple-element.187.other, ...), custom_call_target="tpu_custom_call" | custom-call | tf_op jit(solution)/shard_map/hidden/pallas_call | solution.py:180
  293.9 12.7 %hidden_back.2 = (bf16[128,2688]{1,0:T(8,128)(2,1)S(1)}, bf16[128,2688]{1,0:T(8,128)(2,1)S(1)}, f32[128,1024]{1,0:T(8,128)S(1)}) custom-call(s32[1]{0:T(128)} %bitcast.first, bf16[128,512]{1,0:T(8,128)(2,1)S(1)} %copy-done.29, bf16[128,512]{1,0:T(8,128)(2,1)S(1)} %copy-done.28, f32[128,2688]{1,0:T(8,128)S(1)} %get-tuple-element.37.gate_in, ...), custom_call_target="tpu_custom_call" | custom-call | tf_op jit(solution)/shard_map/hidden_back/pallas_call | solution.py:180
  313.1 6.6 %attend_back.2 = (bf16[128,1024]{1,0:T(8,128)(2,1)S(1)}, f32[128,2048]{1,0:T(8,128)S(1)}, bf16[64,2048]{1,0:T(8,128)(2,1)}, bf16[64,2048]{1,0:T(8,128)(2,1)}) custom-call(s32[128,1]{1,0:T(8,128)S(1)} %copy.41.query_seg, s32[1,256]{1,0:T(1,128)S(1)} %bitcast.124, bf16[256,3072]{1,0:T(8,128)(2,1)S(1)} %qkv.3, f32[128,1024]{1,0:T(8,128)S(1)} %get-tuple-element.40.log_total, ...), custom_call_target="tpu_custom_call" | custom-call | tf_op jit(solution)/shard_map/attend_back/pallas_call | solution.py:153
  320.7 3.3 collective-permute-start.18
  326.3 2.2 copy.49
  328.5 2.1 reshape.226
  332.8 2.3 copy.51
  335.1 2.7 pad_maximum_fusion.1.act_mine
  344.4 5.5 qkv_back.2
  353.5 9.2 %weight_grads.3 = bf16[1024,6400]{1,0:T(8,128)(2,1)} custom-call(bf16[6,128,1024]{2,1,0:T(8,128)(2,1)} %pad_maximum_fusion.1.act_mine, bf16[6,128,1024]{2,1,0:T(8,128)(2,1)} %collective-permute-done.28.act_got, bf16[128,5376]{1,0:T(8,128)(2,1)S(1)} %copy-done.3, bf16[128,5376]{1,0:T(8,128)(2,1)} %collective-permute-done.29.grad_got, ...), custom_call_target="tpu_custom_call" | custom-call | tf_op jit(solution)/shard_map/weight_grads/pallas_call | solution.py:180
  362.7 1.9 fusion.10
  364.6 2.2 fusion.37
  367.5 12.9 %hidden_back.3 = (bf16[128,2688]{1,0:T(8,128)(2,1)S(1)}, bf16[128,2688]{1,0:T(8,128)(2,1)S(1)}, f32[128,1024]{1,0:T(8,128)S(1)}) custom-call(s32[1]{0:T(128)} %bitcast.first, bf16[128,512]{1,0:T(8,128)(2,1)S(1)} %get-tuple-element.182.grad_own, bf16[128,512]{1,0:T(8,128)(2,1)S(1)} %get-tuple-element.181.grad_other, f32[128,2688]{1,0:T(8,128)S(1)} %copy-done.9, ...), custom_call_target="tpu_custom_call" | custom-call | tf_op jit(solution)/shard_map/hidden_back/pallas_call | solution.py:180
  381.8 1.8 fusion.33
  385.6 6.6 %attend_back.3 = (bf16[128,1024]{1,0:T(8,128)(2,1)S(1)}, f32[128,2048]{1,0:T(8,128)S(1)}, bf16[64,2048]{1,0:T(8,128)(2,1)}, bf16[64,2048]{1,0:T(8,128)(2,1)}) custom-call(s32[128,1]{1,0:T(8,128)S(1)} %copy.41.query_seg, s32[1,256]{1,0:T(1,128)S(1)} %bitcast.125, bf16[256,3072]{1,0:T(8,128)(2,1)S(1)} %qkv.2, f32[128,1024]{1,0:T(8,128)S(1)} %copy-done.31, ...), custom_call_target="tpu_custom_call" | custom-call | tf_op jit(solution)/shard_map/attend_back/pallas_call | solution.py:153
  393.1 5.1 collective-permute-start.20
  406.4 2.3 collective-permute-done.20
  408.8 6.6 %collective-permute-done.21 = bf16[64,2048]{1,0:T(8,128)(2,1)} collective-permute-done((bf16[64,2048]{1,0:T(8,128)(2,1)}, bf16[64,2048]{1,0:T(8,128)(2,1)}, u32[]{:S(2)}, u32[]{:S(2)}) %collective-permute-start.21) | collective-permute-done | bytes 262176 | tf_op jit(solution)/shard_map/ppermute | solution.py:171
  421.4 5.2 qkv_back.3
  429.6 8.7 %weight_grads.2 = bf16[1024,6400]{1,0:T(8,128)(2,1)} custom-call(bf16[6,128,1024]{2,1,0:T(8,128)(2,1)S(1)} %pad_maximum_fusion.act_mine, bf16[6,128,1024]{2,1,0:T(8,128)(2,1)} %collective-permute-done.23.act_got, bf16[128,5376]{1,0:T(8,128)(2,1)S(1)} %get-tuple-element.112.grad_mine, bf16[128,5376]{1,0:T(8,128)(2,1)} %collective-permute-done.24.grad_got, ...), custom_call_target="tpu_custom_call" | custom-call | tf_op jit(solution)/shard_map/weight_grads/pallas_call | solution.py:180
  440.9 27.1 %reduce-scatter.5.cloned.1.call-done = bf16[64,6400]{1,0:T(8,128)(2,1)} async-done(((bf16[1024,6400]{1,0:T(8,128)(2,1)}), bf16[64,6400]{1,0:T(8,128)(2,1)}) %reduce-scatter.5.cloned.1.call-update) | async-done | bytes 819216 | tf_op jit(solution)/shard_map/reduce_scatter | solution.py:415
  470.5 2.6 collective-permute-start.31
  474.2 92.5 %reduce-scatter.3.cloned.1.call-done = bf16[64,6400]{1,0:T(8,128)(2,1)} async-done(((bf16[1024,6400]{1,0:T(8,128)(2,1)}), bf16[64,6400]{1,0:T(8,128)(2,1)}) %reduce-scatter.3.cloned.1.call-update) | async-done | bytes 819216 | tf_op jit(solution)/shard_map/reduce_scatter | solution.py:415
  569.3 2.6 collective-permute-start.26
  577.8 2.7 collective-permute-done.26
  581.9 1.9 collective-permute-start.33
  (338 shorter events, 108.9 us)
Async XLA Ops:
  7.2 120.6 %all-gather.2.cloned.1.call-start = ((), (), s32[]{:S(2)}) async-start(), calls=%async_computation.2 | async-start | bytes 19701760 | tf_op jit(solution)/shard_map/all_gather | solution.py:536
  9.9 118.6 %copy-start.37 = (bf16[1,656,1024]{2,1,0:T(8,128)(2,1)S(1)}, bf16[1,656,1024]{2,1,0:T(8,128)(2,1)}, u32[]{:S(2)}) copy-start(bf16[1,656,1024]{2,1,0:T(8,128)(2,1)} %param.15) | copy-start | bytes 4030468
  10.0 2.5 collective-permute-start.3
  13.3 454.7 %reduce-scatter.5.cloned.1.call-start = ((), (), s32[]{:S(2)}) async-start(), calls=%async_computation.4 | async-start | bytes 13926400 | tf_op jit(solution)/shard_map/reduce_scatter | solution.py:415
  127.7 142.6 %collective-permute-start.14 = (bf16[512,18944]{1,0:T(8,128)(2,1)}, bf16[512,18944]{1,0:T(8,128)(2,1)}, u32[]{:S(2)}, u32[]{:S(2)}) collective-permute-start(bf16[512,18944]{1,0:T(8,128)(2,1)} %all-gather.2.cloned.1.call-done.weight_own.gate_own.up_own), channel_id=1, source_target_pairs={{0,64},{64,0},{1,65},{65,1},{2,66},{66,2},{3,67},{67,3},{4,68},{68... | collective-permute-start | bytes 58195976 | tf_op jit(solution)/shard_map/ppermute | solution.py:31
  128.5 9.1 %collective-permute-start.7 = (bf16[656,512]{1,0:T(8,128)(2,1)S(1)}, bf16[656,512]{1,0:T(8,128)(2,1)S(1)}, u32[]{:S(2)}, u32[]{:S(2)}) collective-permute-start(bf16[656,512]{1,0:T(8,128)(2,1)S(1)} %select_bitcast_fusion), channel_id=1, source_target_pairs={{0,64},{64,0},{1,65},{65,1},{2,66},{66,2},{3,67},{67,3},{4,68},{68... | collective-permute-start | bytes 2015240 | tf_op jit(solution)/shard_map/ppermute | solution.py:31
  144.5 31.5 %collective-permute-start.8 = (bf16[656,1024]{1,0:T(8,128)(2,1)}, bf16[656,1024]{1,0:T(8,128)(2,1)}, u32[]{:S(2)}, u32[]{:S(2)}) collective-permute-start(bf16[656,1024]{1,0:T(8,128)(2,1)} %pad_maximum_fusion.2), channel_id=1, source_target_pairs={{1,0},{2,1},{3,2},{0,3},{5,4},{6,5},{7,6},{4,7},{9,8},{10,9},{11,1... | collective-permute-start | bytes 4030472 | tf_op jit(solution)/shard_map/ppermute | solution.py:551
  146.9 32.5 %collective-permute-start = (f32[2,1024]{1,0:T(2,128)S(1)}, f32[2,1024]{1,0:T(2,128)S(1)}, u32[]{:S(2)}, u32[]{:S(2)}) collective-permute-start(f32[2,1024]{1,0:T(2,128)S(1)} %bitcast.147), channel_id=1, source_target_pairs={{0,64},{64,0},{1,65},{65,1},{2,66},{66,2},{3,67},{67,3},{4,68},{68... | collective-permute-start | bytes 24584 | tf_op jit(solution)/shard_map/ppermute | solution.py:31
  147.6 77.3 %copy-start.44 = (bf16[128,1024]{1,0:T(8,128)(2,1)}, bf16[128,1024]{1,0:T(8,128)(2,1)S(1)}, u32[]{:S(2)}) copy-start(bf16[128,1024]{1,0:T(8,128)(2,1)S(1)} %bitcast_convert_fusion) | copy-start | bytes 786436
  147.6 50.7 %collective-permute-start.9 = (bf16[656,1024]{1,0:T(8,128)(2,1)}, bf16[656,1024]{1,0:T(8,128)(2,1)}, u32[]{:S(2)}, u32[]{:S(2)}) collective-permute-start(bf16[656,1024]{1,0:T(8,128)(2,1)} %pad_maximum_fusion.2), channel_id=1, source_target_pairs={{0,1},{1,2},{2,3},{3,0},{4,5},{5,6},{6,7},{7,4},{8,9},{9,10},{10,1... | collective-permute-start | bytes 4030472 | tf_op jit(solution)/shard_map/ppermute | solution.py:550
  153.9 91.2 %collective-permute-start.6 = (bf16[512,5376]{1,0:T(8,128)(2,1)}, bf16[512,5376]{1,0:T(8,128)(2,1)}, u32[]{:S(2)}, u32[]{:S(2)}) collective-permute-start(bf16[512,5376]{1,0:T(8,128)(2,1)} %slice.553), channel_id=1, source_target_pairs={{0,64},{64,0},{1,65},{65,1},{2,66},{66,2},{3,67},{67,3},{4,68},{68... | collective-permute-start | bytes 16515080 | tf_op jit(solution)/shard_map/ppermute | solution.py:31
  176.0 53.4 %collective-permute-start.4 = (bf16[512,3072]{1,0:T(8,128)(2,1)}, bf16[512,3072]{1,0:T(8,128)(2,1)S(1)}, u32[]{:S(2)}, u32[]{:S(2)}) collective-permute-start(bf16[512,3072]{1,0:T(8,128)(2,1)} %slice.542), channel_id=1, source_target_pairs={{0,64},{64,0},{1,65},{65,1},{2,66},{66,2},{3,67},{67,3},{4,68},{68... | collective-permute-start | bytes 9437192 | tf_op jit(solution)/shard_map/ppermute | solution.py:31
  177.0 5.9 copy-start.58
  179.5 17.9 %collective-permute-start.15 = (bf16[656,512]{1,0:T(8,128)(2,1)S(1)}, bf16[656,512]{1,0:T(8,128)(2,1)S(1)}, u32[]{:S(2)}, u32[]{:S(2)}) collective-permute-start(bf16[656,512]{1,0:T(8,128)(2,1)S(1)} %get-tuple-element.123), channel_id=1, source_target_pairs={{1,0},{2,1},{3,2},{0,3},{5,4},{6,5},{7,6},{4,7},{9,8},{10,9},{11,1... | collective-permute-start | bytes 2015240 | tf_op jit(solution)/shard_map/ppermute | solution.py:554
  200.6 18.1 %collective-permute-start.10 = (bf16[656,512]{1,0:T(8,128)(2,1)S(1)}, bf16[656,512]{1,0:T(8,128)(2,1)S(1)}, u32[]{:S(2)}, u32[]{:S(2)}) collective-permute-start(bf16[656,512]{1,0:T(8,128)(2,1)S(1)} %get-tuple-element.122), channel_id=1, source_target_pairs={{0,1},{1,2},{2,3},{3,0},{4,5},{5,6},{6,7},{7,4},{8,9},{9,10},{10,1... | collective-permute-start | bytes 2015240 | tf_op jit(solution)/shard_map/ppermute | solution.py:553
  202.2 20.7 %collective-permute-start.1 = (bf16[64,1024]{1,0:T(8,128)(2,1)S(1)}, bf16[64,1024]{1,0:T(8,128)(2,1)S(1)}, u32[]{:S(2)}, u32[]{:S(2)}) collective-permute-start(bf16[64,1024]{1,0:T(8,128)(2,1)S(1)} %get-tuple-element.225), channel_id=1, source_target_pairs={{0,4},{4,8},{8,12},{12,16},{16,20},{20,24},{24,28},{28,32},{32,36}... | collective-permute-start | bytes 393224 | tf_op jit(solution)/shard_map/ppermute | solution.py:167
  218.7 9.3 %collective-permute-start.2 = (bf16[64,1024]{1,0:T(8,128)(2,1)}, bf16[64,1024]{1,0:T(8,128)(2,1)}, u32[]{:S(2)}, u32[]{:S(2)}) collective-permute-start(bf16[64,1024]{1,0:T(8,128)(2,1)} %get-tuple-element.226), channel_id=1, source_target_pairs={{4,0},{8,4},{12,8},{16,12},{20,16},{24,20},{28,24},{32,28},{36,32}... | collective-permute-start | bytes 393224 | tf_op jit(solution)/shard_map/ppermute | solution.py:171
  223.5 21.5 %collective-permute-start.11 = (bf16[2688,512]{1,0:T(8,128)(2,1)}, bf16[2688,512]{1,0:T(8,128)(2,1)}, u32[]{:S(2)}, u32[]{:S(2)}) collective-permute-start(bf16[2688,512]{1,0:T(8,128)(2,1)} %constant_dynamic-update-slice_fusion.27.down_own), channel_id=1, source_target_pairs={{0,64},{64,0},{1,65},{65,1},{2,66},{66,2},{3,67},{67,3},{4,68},{68... | collective-permute-start | bytes 8257544 | tf_op jit(solution)/shard_map/ppermute | solution.py:31
  228.0 14.9 %collective-permute-start.5 = (bf16[512,1024]{1,0:T(8,128)(2,1)}, bf16[512,1024]{1,0:T(8,128)(2,1)}, u32[]{:S(2)}, u32[]{:S(2)}) collective-permute-start(bf16[512,1024]{1,0:T(8,128)(2,1)} %slice.543), channel_id=1, source_target_pairs={{0,64},{64,0},{1,65},{65,1},{2,66},{66,2},{3,67},{67,3},{4,68},{68... | collective-permute-start | bytes 3145736 | tf_op jit(solution)/shard_map/ppermute | solution.py:31
  231.1 50.6 %collective-permute-start.16 = (bf16[2688,512]{1,0:T(8,128)(2,1)}, bf16[2688,512]{1,0:T(8,128)(2,1)}, u32[]{:S(2)}, u32[]{:S(2)}) collective-permute-start(bf16[2688,512]{1,0:T(8,128)(2,1)} %get-tuple-element.121.down_own), channel_id=1, source_target_pairs={{0,64},{64,0},{1,65},{65,1},{2,66},{66,2},{3,67},{67,3},{4,68},{68... | collective-permute-start | bytes 8257544 | tf_op jit(solution)/shard_map/ppermute | solution.py:31
  259.0 7.2 %collective-permute-start.12 = (bf16[64,1024]{1,0:T(8,128)(2,1)S(1)}, bf16[64,1024]{1,0:T(8,128)(2,1)S(1)}, u32[]{:S(2)}, u32[]{:S(2)}) collective-permute-start(bf16[64,1024]{1,0:T(8,128)(2,1)S(1)} %get-tuple-element.205), channel_id=1, source_target_pairs={{0,4},{4,8},{8,12},{12,16},{16,20},{20,24},{24,28},{28,32},{32,36}... | collective-permute-start | bytes 393224 | tf_op jit(solution)/shard_map/ppermute | solution.py:167
  263.3 6.7 %collective-permute-start.13 = (bf16[64,1024]{1,0:T(8,128)(2,1)S(1)}, bf16[64,1024]{1,0:T(8,128)(2,1)S(1)}, u32[]{:S(2)}, u32[]{:S(2)}) collective-permute-start(bf16[64,1024]{1,0:T(8,128)(2,1)S(1)} %get-tuple-element.206), channel_id=1, source_target_pairs={{4,0},{8,4},{12,8},{16,12},{20,16},{24,20},{28,24},{32,28},{36,32}... | collective-permute-start | bytes 393224 | tf_op jit(solution)/shard_map/ppermute | solution.py:171
  281.7 12.2 %copy-start.28 = (bf16[128,512]{1,0:T(8,128)(2,1)S(1)}, bf16[128,512]{1,0:T(8,128)(2,1)}, u32[]{:S(2)}) copy-start(bf16[128,512]{1,0:T(8,128)(2,1)} %get-tuple-element.185.grad_other) | copy-start | bytes 393220
  281.7 12.2 %copy-start.29 = (bf16[128,512]{1,0:T(8,128)(2,1)S(1)}, bf16[128,512]{1,0:T(8,128)(2,1)}, u32[]{:S(2)}) copy-start(bf16[128,512]{1,0:T(8,128)(2,1)} %get-tuple-element.186.grad_own) | copy-start | bytes 393220
  320.7 18.5 %collective-permute-start.18 = (bf16[64,2048]{1,0:T(8,128)(2,1)}, bf16[64,2048]{1,0:T(8,128)(2,1)}, u32[]{:S(2)}, u32[]{:S(2)}) collective-permute-start(bf16[64,2048]{1,0:T(8,128)(2,1)} %get-tuple-element.43), channel_id=1, source_target_pairs={{0,4},{4,8},{8,12},{12,16},{16,20},{20,24},{24,28},{28,32},{32,36}... | collective-permute-start | bytes 786440 | tf_op jit(solution)/shard_map/ppermute | solution.py:167
  324.0 15.2 %collective-permute-start.19 = (bf16[64,2048]{1,0:T(8,128)(2,1)}, bf16[64,2048]{1,0:T(8,128)(2,1)}, u32[]{:S(2)}, u32[]{:S(2)}) collective-permute-start(bf16[64,2048]{1,0:T(8,128)(2,1)} %get-tuple-element.44), channel_id=1, source_target_pairs={{4,0},{8,4},{12,8},{16,12},{20,16},{24,20},{28,24},{32,28},{36,32}... | collective-permute-start | bytes 786440 | tf_op jit(solution)/shard_map/ppermute | solution.py:171
  337.8 14.3 %collective-permute-start.28 = (bf16[6,128,1024]{2,1,0:T(8,128)(2,1)}, bf16[6,128,1024]{2,1,0:T(8,128)(2,1)}, u32[]{:S(2)}, u32[]{:S(2)}) collective-permute-start(bf16[6,128,1024]{2,1,0:T(8,128)(2,1)} %pad_maximum_fusion.1.act_mine), channel_id=1, source_target_pairs={{0,64},{64,0},{1,65},{65,1},{2,66},{66,2},{3,67},{67,3},{4,68},{68... | collective-permute-start | bytes 4718600 | tf_op jit(solution)/shard_map/ppermute | solution.py:31
  344.3 7.8 %collective-permute-start.29 = (bf16[128,5376]{1,0:T(8,128)(2,1)}, bf16[128,5376]{1,0:T(8,128)(2,1)}, u32[]{:S(2)}, u32[]{:S(2)}) collective-permute-start(bf16[128,5376]{1,0:T(8,128)(2,1)} %get-tuple-element.109), channel_id=1, source_target_pairs={{0,64},{64,0},{1,65},{65,1},{2,66},{66,2},{3,67},{67,3},{4,68},{68... | collective-permute-start | bytes 4128776 | tf_op jit(solution)/shard_map/ppermute | solution.py:31
  362.7 204.1 %reduce-scatter.3.cloned.1.call-start = ((), (), s32[]{:S(2)}) async-start(), calls=%async_computation.3 | async-start | bytes 13926400 | tf_op jit(solution)/shard_map/reduce_scatter | solution.py:415
  366.8 13.9 %copy-start.38 = (f32[128,1024]{1,0:T(8,128)}, f32[128,1024]{1,0:T(8,128)S(1)}, u32[]{:S(2)}) copy-start(f32[128,1024]{1,0:T(8,128)S(1)} %get-tuple-element.100) | copy-start | bytes 1572868
  393.1 7.4 %copy-start.16 = (bf16[128,1024]{1,0:T(8,128)(2,1)}, bf16[128,1024]{1,0:T(8,128)(2,1)S(1)}, u32[]{:S(2)}) copy-start(bf16[128,1024]{1,0:T(8,128)(2,1)S(1)} %get-tuple-element.49) | copy-start | bytes 786436
  393.1 15.6 %collective-permute-start.20 = (bf16[64,2048]{1,0:T(8,128)(2,1)}, bf16[64,2048]{1,0:T(8,128)(2,1)}, u32[]{:S(2)}, u32[]{:S(2)}) collective-permute-start(bf16[64,2048]{1,0:T(8,128)(2,1)} %get-tuple-element.51), channel_id=1, source_target_pairs={{0,4},{4,8},{8,12},{12,16},{16,20},{20,24},{24,28},{28,32},{32,36}... | collective-permute-start | bytes 786440 | tf_op jit(solution)/shard_map/ppermute | solution.py:167
  398.2 17.1 %collective-permute-start.21 = (bf16[64,2048]{1,0:T(8,128)(2,1)}, bf16[64,2048]{1,0:T(8,128)(2,1)}, u32[]{:S(2)}, u32[]{:S(2)}) collective-permute-start(bf16[64,2048]{1,0:T(8,128)(2,1)} %get-tuple-element.52), channel_id=1, source_target_pairs={{4,0},{8,4},{12,8},{16,12},{20,16},{24,20},{28,24},{32,28},{36,32}... | collective-permute-start | bytes 786440 | tf_op jit(solution)/shard_map/ppermute | solution.py:171
  403.6 11.7 %copy-start.13 = (f32[128,2048]{1,0:T(8,128)S(1)}, f32[128,2048]{1,0:T(8,128)}, u32[]{:S(2)}) copy-start(f32[128,2048]{1,0:T(8,128)} %copy-done.12) | copy-start | bytes 3145732
  405.2 11.4 %copy-start.17 = (bf16[128,1024]{1,0:T(8,128)(2,1)S(1)}, bf16[128,1024]{1,0:T(8,128)(2,1)}, u32[]{:S(2)}) copy-start(bf16[128,1024]{1,0:T(8,128)(2,1)} %copy-done.16) | copy-start | bytes 786436
  405.2 24.4 %collective-permute-start.23 = (bf16[6,128,1024]{2,1,0:T(8,128)(2,1)S(1)}, bf16[6,128,1024]{2,1,0:T(8,128)(2,1)}, u32[]{:S(2)}, u32[]{:S(2)}) collective-permute-start(bf16[6,128,1024]{2,1,0:T(8,128)(2,1)S(1)} %pad_maximum_fusion.act_mine), channel_id=1, source_target_pairs={{0,64},{64,0},{1,65},{65,1},{2,66},{66,2},{3,67},{67,3},{4,68},{68... | collective-permute-start | bytes 4718600 | tf_op jit(solution)/shard_map/ppermute | solution.py:31
  420.0 9.6 %collective-permute-start.24 = (bf16[128,5376]{1,0:T(8,128)(2,1)}, bf16[128,5376]{1,0:T(8,128)(2,1)}, u32[]{:S(2)}, u32[]{:S(2)}) collective-permute-start(bf16[128,5376]{1,0:T(8,128)(2,1)} %get-tuple-element.111), channel_id=1, source_target_pairs={{0,64},{64,0},{1,65},{65,1},{2,66},{66,2},{3,67},{67,3},{4,68},{68... | collective-permute-start | bytes 4128776 | tf_op jit(solution)/shard_map/ppermute | solution.py:31
  421.4 6.0 %copy-start.35 = (f32[1,1,128,1024]{3,2,1,0:T(8,128)S(1)}, f32[1,1,128,1024]{3,2,1,0:T(8,128)}, u32[]{:S(2)}) copy-start(f32[1,1,128,1024]{3,2,1,0:T(8,128)} %copy-done.32) | copy-start | bytes 1572868
  438.4 130.9 %collective-permute-start.17 = (f32[128,1024]{1,0:T(8,128)}, f32[128,1024]{1,0:T(8,128)}, u32[]{:S(2)}, u32[]{:S(2)}) collective-permute-start(f32[128,1024]{1,0:T(8,128)} %get-tuple-element.138), channel_id=1, source_target_pairs={{0,64},{64,0},{1,65},{65,1},{2,66},{66,2},{3,67},{67,3},{4,68},{68... | collective-permute-start | bytes 1572872 | tf_op jit(solution)/shard_map/ppermute | solution.py:31
  440.9 132.8 %copy-start.7 = (f32[128,1024]{1,0:T(8,128)S(1)}, f32[128,1024]{1,0:T(8,128)}, u32[]{:S(2)}) copy-start(f32[128,1024]{1,0:T(8,128)} %copy-done.6) | copy-start | bytes 1572868
  469.2 102.7 %collective-permute-start.30 = (bf16[16,6400]{1,0:T(8,128)(2,1)S(1)}, bf16[16,6400]{1,0:T(8,128)(2,1)S(1)}, u32[]{:S(2)}, u32[]{:S(2)}) collective-permute-start(bf16[16,6400]{1,0:T(8,128)(2,1)S(1)} %get-tuple-element.128), channel_id=1, source_target_pairs={{0,1},{1,2},{2,3},{3,0},{4,5},{5,6},{6,7},{7,4},{8,9},{9,10},{10,1... | collective-permute-start | bytes 614408 | tf_op jit(solution)/shard_map/ppermute | solution.py:503
  470.5 105.4 %collective-permute-start.31 = (bf16[16,6400]{1,0:T(8,128)(2,1)S(1)}, bf16[16,6400]{1,0:T(8,128)(2,1)}, u32[]{:S(2)}, u32[]{:S(2)}) collective-permute-start(bf16[16,6400]{1,0:T(8,128)(2,1)S(1)} %get-tuple-element.130), channel_id=1, source_target_pairs={{0,2},{1,3},{2,0},{3,1},{4,6},{5,7},{6,4},{7,5},{8,10},{9,11},{10,... | collective-permute-start | bytes 614408 | tf_op jit(solution)/shard_map/ppermute | solution.py:503
  473.1 104.6 %collective-permute-start.32 = (bf16[16,6400]{1,0:T(8,128)(2,1)S(1)}, bf16[16,6400]{1,0:T(8,128)(2,1)}, u32[]{:S(2)}, u32[]{:S(2)}) collective-permute-start(bf16[16,6400]{1,0:T(8,128)(2,1)S(1)} %get-tuple-element.129), channel_id=1, source_target_pairs={{0,3},{1,0},{2,1},{3,2},{4,7},{5,4},{6,5},{7,6},{8,11},{9,8},{10,9... | collective-permute-start | bytes 614408 | tf_op jit(solution)/shard_map/ppermute | solution.py:503
  567.9 9.8 %collective-permute-start.25 = (bf16[16,6400]{1,0:T(8,128)(2,1)S(1)}, bf16[16,6400]{1,0:T(8,128)(2,1)S(1)}, u32[]{:S(2)}, u32[]{:S(2)}) collective-permute-start(bf16[16,6400]{1,0:T(8,128)(2,1)S(1)} %get-tuple-element.131), channel_id=1, source_target_pairs={{0,1},{1,2},{2,3},{3,0},{4,5},{5,6},{6,7},{7,4},{8,9},{9,10},{10,1... | collective-permute-start | bytes 614408 | tf_op jit(solution)/shard_map/ppermute | solution.py:503
  569.3 11.2 %collective-permute-start.26 = (bf16[16,6400]{1,0:T(8,128)(2,1)S(1)}, bf16[16,6400]{1,0:T(8,128)(2,1)S(1)}, u32[]{:S(2)}, u32[]{:S(2)}) collective-permute-start(bf16[16,6400]{1,0:T(8,128)(2,1)S(1)} %get-tuple-element.133), channel_id=1, source_target_pairs={{0,2},{1,3},{2,0},{3,1},{4,6},{5,7},{6,4},{7,5},{8,10},{9,11},{10,... | collective-permute-start | bytes 614408 | tf_op jit(solution)/shard_map/ppermute | solution.py:503
  572.5 7.9 %collective-permute-start.27 = (bf16[16,6400]{1,0:T(8,128)(2,1)S(1)}, bf16[16,6400]{1,0:T(8,128)(2,1)S(1)}, u32[]{:S(2)}, u32[]{:S(2)}) collective-permute-start(bf16[16,6400]{1,0:T(8,128)(2,1)S(1)} %get-tuple-element.132), channel_id=1, source_target_pairs={{0,3},{1,0},{2,1},{3,2},{4,7},{5,4},{6,5},{7,6},{8,11},{9,8},{10,9... | collective-permute-start | bytes 614408 | tf_op jit(solution)/shard_map/ppermute | solution.py:503
  576.0 7.8 %collective-permute-start.22 = (f32[128,1024]{1,0:T(8,128)S(1)}, f32[128,1024]{1,0:T(8,128)S(1)}, u32[]{:S(2)}, u32[]{:S(2)}) collective-permute-start(f32[128,1024]{1,0:T(8,128)S(1)} %copy-done.53), channel_id=1, source_target_pairs={{0,64},{64,0},{1,65},{65,1},{2,66},{66,2},{3,67},{67,3},{4,68},{68... | collective-permute-start | bytes 1572872 | tf_op jit(solution)/shard_map/ppermute | solution.py:31
  581.9 3.3 collective-permute-start.33
  (49 other events, 88.9 us)
Sparse Core Ops, SparseCore 0:
  13.4 114.3 all-gather.1
  362.8 105.1 reduce-scatter.4
  471.8 94.8 reduce-scatter.2

commit v4 on v3

--- a/solution.py
+++ b/solution.py
@@ -16,8 +16,8 @@
 W_DEV = 4
 PAD_ROWS = 48
 GRAD_PAD = 2816
-HIDDEN_BLOCK = 384
-QKV_BLOCK = 768
+HIDDEN_BLOCK = 896
+QKV_BLOCK = 1536
 
 norm_eps = 1e-05
 root_half = 1.0 / math.sqrt(2.0)
@@ -82,7 +82,8 @@
     return (offset >= 0) & (offset <= 2 * HALO) & (query_seg == key_seg)
 
 
-def attend_kernel(query_seg, key_seg, qkv, mixed, log_total):
+def attend_kernel(query_seg, key_seg, qkv, *refs):
+    mixed, log_total = refs[-2:]
     allowed = window_allowed(query_seg[...], key_seg[...])
     width = HEADS * HEAD_DIM
     rows = mixed.shape[0]
@@ -135,7 +136,7 @@
 params = pltpu.CompilerParams(vmem_limit_bytes=40 * 1024 * 1024)
 
 
-def attend(query_seg, key_seg, qkv):
+def attend(query_seg, key_seg, qkv, ready):
     rows, width = (query_seg.shape[0], HEADS * HEAD_DIM)
     return pl.pallas_call(
         attend_kernel,
@@ -143,9 +144,11 @@
             jax.ShapeDtypeStruct((rows, width), jnp.bfloat16),
             jax.ShapeDtypeStruct((rows, width), jnp.float32),
         ),
+        in_specs=[pl.BlockSpec(memory_space=pltpu.VMEM)] * 3
+        + [pl.BlockSpec(memory_space=pl.ANY)] * len(ready),
         compiler_params=params,
         name="attend",
-    )(query_seg, key_seg, qkv)
+    )(query_seg, key_seg, qkv, *ready)
 
 
 def attend_back(query_seg, key_seg, qkv, log_total, grad_mixed):
@@ -384,81 +387,107 @@
     )
 
 
-def layer_forward(rows_in, gain_pair, weights, segs, on_first, first):
+def layer_forward(rows_in, gain_pair, weights, segs, on_first, first, later=(), ready=()):
     normed1, factor1 = norm_parts(rows_in)
     act_in = (normed1 * gain_pair[0]).astype(jnp.bfloat16)
     before = to_next(act_in[act_in.shape[0] - HALO :])
     after = to_previous(act_in[:HALO])
     extended = jnp.concatenate([before, act_in, after], axis=0)
     qkv = qkv_of(*column_halves(extended, on_first), weights)
-    mixed, log_total = attend(*segs, qkv)
+    mixed, log_total = attend(*segs, qkv, ready)
+    mixed, *later = lax.optimization_barrier((mixed, *later))
     own, other = column_halves(mixed, on_first)
     middle = rows_in + matmul(own, weights["out"][0]) + matmul(other, weights["out"][1])
     normed2, factor2 = norm_parts(middle)
     act_mid = (normed2 * gain_pair[1]).astype(jnp.bfloat16)
     own, other = column_halves(act_mid, on_first)
     gate, up, product, output = hidden_forward(first, own, other, middle, weights)
-    acts = jnp.concatenate([jnp.stack([act_in, mixed, act_mid]), row_groups(product)], axis=0)
-    kept = (normed1, factor1, qkv, log_total, normed2, factor2, gate, up, acts, swapped(acts))
-    return (output, kept)
-
-
-def row_groups(product):
-    devices, groups = (SEQ_DEV * W_DEV, PAD_ROWS // 16)
-    pieces = product[:, :FF].reshape(product.shape[0], devices, FF // devices)
-    pieces = jnp.pad(pieces, ((0, 0), (0, 0), (0, PAD_ROWS - pieces.shape[2])))
-    pieces = pieces.reshape(product.shape[0], devices, groups, 16).transpose(2, 0, 1, 3)
-    return pieces.reshape(groups, product.shape[0], devices * 16)
+    acts = (jnp.stack([act_in, mixed, act_mid]), product)
+    got = tuple(swapped(act) for act in acts)
+    kept = (normed1, factor1, qkv, log_total, normed2, factor2, gate, up, acts, got)
+    return (output, kept, later)
 
 
 def seq_sum(total):
     return lax.psum_scatter(total, "seq", scatter_dimension=0, tiled=True)
 
 
-GRAD_WIDTHS = (1536, 512, GRAD_PAD, 512, 512, 512)
-
-
-def weight_grad_kernel(act_mine, act_got, grad_mine, grad_got, gains, out, grads):
-    count = act_mine.shape[1]
-
-    @pl.when(pl.program_id(0) == 0)
+GRAD_WIDTHS = (1536, 512, GRAD_PAD)
+ROW_PIECE = FF // (SEQ_DEV * W_DEV)
+
+
+def weight_grad_kernel(
+    act_mine, act_got, product_mine, product_got, grad_mine, grad_got, gains, out,
+    grads, down, groups,
+):
+    count, block = (act_mine.shape[1], act_mine.shape[2])
+    step = pl.program_id(0)
+    end = sum(GRAD_WIDTHS)
+
+    @pl.when(step == 0)
     def _():
         grads[:count] = grad_mine[...]
         grads[count:] = grad_got[...]
+        for at in range(0, FF_PAD, 896):
+            product = jnp.concatenate(
+                [product_mine[:, at : at + 896], product_got[:, at : at + 896]], axis=0
+            )
+            down[at : at + 896] = inner_rows(product, grads[:, end:])
+        width = down.shape[1]
+        for piece in range(SEQ_DEV * W_DEV):
+            for group in range(PAD_ROWS // 16):
+                rows = piece * ROW_PIECE + group * 16
+                groups[16 * piece : 16 * piece + 16, group * width : (group + 1) * width] = down[
+                    rows : rows + 16
+                ].astype(jnp.bfloat16)
 
     at = 0
     for member, width in enumerate(GRAD_WIDTHS):
         acts = jnp.concatenate([act_mine[member], act_got[member]], axis=0)
-        place = at if member < 3 else sum(GRAD_WIDTHS[:3])
-        for part in range(0, width, 512):
-            size = min(512, width - part)
-            out[:, at + part : at + part + size] = inner_rows(
-                acts, grads[:, place + part : place + part + size]
-            ).astype(jnp.bfloat16)
+        for part in range(at, at + width, 512):
+            size = min(512, at + width - part)
+            out[:, part : part + size] = inner_rows(acts, grads[:, part : part + size]).astype(
+                jnp.bfloat16
+            )
         at += width
-    end = sum(GRAD_WIDTHS[:3])
     out[:, end - gains.shape[1] : end] = gains[...]
-
-
-def weight_grads(act_mine, act_got, grad_mine, grad_got, gains):
-    members, count, width = act_mine.shape
+    out[:, end:] = groups[pl.ds(pl.multiple_of(step * block, block), block)]
+
+
+def weight_grads(acts, acts_got, grad_mine, grad_got, gains):
+    members, count, width = acts[0].shape
     block = 256
-    acts = pl.BlockSpec((members, count, block), lambda n: (0, 0, n))
+    half = grad_mine.shape[1] - sum(GRAD_WIDTHS)
+    groups = half * PAD_ROWS // 16
+    act_spec = pl.BlockSpec((members, count, block), lambda n: (0, 0, n))
+    product_spec = whole(acts[1])
     return grid_call(
         weight_grad_kernel,
         "weight_grads",
         (),
         (width // block,),
-        [acts, acts, whole(grad_mine), whole(grad_got), rows_at(block, gains.shape[1])],
-        rows_at(block, sum(GRAD_WIDTHS)),
-        jax.ShapeDtypeStruct((width, sum(GRAD_WIDTHS)), jnp.bfloat16),
-        [pltpu.VMEM((2 * count, grad_mine.shape[1]), jnp.bfloat16)],
-        (act_mine, act_got, grad_mine, grad_got, gains),
+        [
+            act_spec,
+            act_spec,
+            product_spec,
+            product_spec,
+            whole(grad_mine),
+            whole(grad_got),
+            rows_at(block, gains.shape[1]),
+        ],
+        rows_at(block, sum(GRAD_WIDTHS) + groups),
+        jax.ShapeDtypeStruct((width, sum(GRAD_WIDTHS) + groups), jnp.bfloat16),
+        [
+            pltpu.VMEM((2 * count, grad_mine.shape[1]), jnp.bfloat16),
+            pltpu.VMEM((FF_PAD, half), jnp.float32),
+            pltpu.VMEM((width, groups), jnp.bfloat16),
+        ],
+        (acts[0], acts_got[0], acts[1], acts_got[1], grad_mine, grad_got, gains),
     )
 
 
 def layer_backward(grad_out, kept, gain_pair, weights, segs, on_first, first):
-    (normed1, factor1, qkv, log_total, normed2, factor2, gate, up, acts, acts_got) = kept
+    (normed1, factor1, qkv, log_total, normed2, factor2, gate, up, acts, got) = kept
     rows, width = normed1.shape
     half = width // 2
     grad_branch = grad_out.astype(jnp.bfloat16)
@@ -492,7 +521,8 @@
     grad_inputs = grad_middle + norm_back(grad_norm1 * gain_pair[0], normed1, factor1)
     gains = jnp.stack([gain_first, gain_mid])
     gain_columns = jnp.pad(gains, ((0, 126), (0, 0))).T.astype(jnp.bfloat16)
-    return (grad_inputs, seq_sum(weight_grads(acts, acts_got, grad_mine, grad_got, gain_columns)))
+    sums = seq_sum(weight_grads(acts, got, grad_mine, grad_got, gain_columns))
+    return (grad_inputs, sums)
 
 
 def summed_over_w(block, place):
@@ -531,17 +561,17 @@
         ]
         return jnp.concatenate([hidden[:, :FF], pad, hidden[:, FF:], pad, qkv, out], axis=1)
 
+    def in_order(first, second):
+        ends = (0, 2 * FF_PAD, 2 * FF_PAD + 3 * width, 2 * FF_PAD + 4 * width)
+        return jnp.concatenate(
+            [piece[:, a:b] for a, b in zip(ends, ends[1:]) for piece in (first, second)], axis=1
+        )
+
     row_pieces = sections(row_slice(core), swapped(row_slice(1 - core)))
-    up_at, qkv_at, out_at = (FF_PAD, 2 * FF_PAD, 2 * FF_PAD + 3 * width)
-    all_own = lax.all_gather(
-        jnp.concatenate(
-            [piece[:, :out_at] for piece in row_pieces] + [piece[:, out_at:] for piece in row_pieces],
-            axis=1,
-        ),
-        ("wshard", "seq"),
-        axis=0,
-        tiled=True,
-    )
+    hidden_width, qkv_width = (2 * FF_PAD, 3 * width)
+    qkv_at = 2 * hidden_width
+    out_at = qkv_at + 2 * qkv_width
+    all_own = lax.all_gather(in_order(*row_pieces), ("wshard", "seq"), axis=0, tiled=True)
     half = hidden_out.shape[2] // 2
     low, high = (hidden_out[0, :, :half], hidden_out[0, :, half:])
     down_piece = jnp.concatenate(sections(by_core(low, high), swapped(by_core(high, low))), axis=1)
@@ -568,29 +598,31 @@
             own = lax.dynamic_update_slice_in_dim(
                 own, piece, lax.rem(w_place + step, W_DEV) * piece_rows, 0
             )
-        return (own, swapped(own))
-
-    first_qkv = swapped(all_own[:, qkv_at:out_at])
-    first_out = swapped(all_own[:, 2 * out_at : 2 * out_at + width])
-    first_hidden = swapped(all_own[:, :qkv_at])
-    all_other = swapped(all_own)
-    out_own = [all_own[:, 2 * out_at + k * width : 2 * out_at + (k + 1) * width] for k in (0, 1)]
-    weights = (
-        {
-            "qkv": ((all_own, qkv_at), (first_qkv, 0)),
-            "gate": ((all_own, 0), (first_hidden, 0)),
-            "up": ((all_own, up_at), (first_hidden, up_at)),
-            "out": (out_own[0], first_out),
-            "down": down_of(0),
-        },
-        {
-            "qkv": ((all_own, out_at + qkv_at), (all_other, out_at + qkv_at)),
-            "gate": ((all_own, out_at), (all_other, out_at)),
-            "up": ((all_own, out_at + up_at), (all_other, out_at + up_at)),
-            "out": (out_own[1], all_other[:, 2 * out_at + width :]),
-            "down": down_of(1),
-        },
-    )
+        return own
+
+    all_own, *down_own = lax.optimization_barrier((all_own, down_of(0), down_of(1)))
+    first_qkv = swapped(all_own[:, qkv_at : qkv_at + qkv_width])
+    first_out = swapped(all_own[:, out_at : out_at + width])
+    first_hidden = swapped(all_own[:, :hidden_width])
+    out_own = [all_own[:, out_at + k * width : out_at + (k + 1) * width] for k in (0, 1)]
+    first_weights = {
+        "qkv": ((all_own, qkv_at), (first_qkv, 0)),
+        "gate": ((all_own, 0), (first_hidden, 0)),
+        "up": ((all_own, FF_PAD), (first_hidden, FF_PAD)),
+        "out": (all_own[:, out_at : out_at + width], first_out),
+        "down": (down_own[0], swapped(down_own[0])),
+    }
+
+    def second_weights(all_late):
+        all_other = swapped(all_late)
+        return {
+            "qkv": ((all_own, qkv_at + qkv_width), (all_other, qkv_at + qkv_width)),
+            "gate": ((all_own, hidden_width), (all_other, hidden_width)),
+            "up": ((all_own, hidden_width + FF_PAD), (all_other, hidden_width + FF_PAD)),
+            "out": (all_own[:, out_at + width :], all_other[:, out_at + width :]),
+            "down": (down_own[1], swapped(down_own[1])),
+        }
+
     first = on_first.astype(jnp.int32)[None]
     rows_in = by_core(inputs[0, 0], inputs[1, 0])
     row_count = rows_in.shape[0]
@@ -601,8 +633,11 @@
         lax.dynamic_slice_in_dim(segment_row, first_row, row_count)[:, None],
         lax.dynamic_slice_in_dim(padded, first_row, row_count + 2 * HALO)[None, :],
     )
-    middle, kept0 = layer_forward(rows_in, gain_pairs[0], weights[0], segs, on_first, first)
-    final, kept1 = layer_forward(middle, gain_pairs[1], weights[1], segs, on_first, first)
+    middle, kept0, (all_late,) = layer_forward(
+        rows_in, gain_pairs[0], first_weights, segs, on_first, first, (all_own,), (first_hidden, first_out)
+    )
+    weights = (first_weights, second_weights(all_late))
+    final, kept1, _ = layer_forward(middle, gain_pairs[1], weights[1], segs, on_first, first)
     upstream = by_core(cotangent[0, 0], cotangent[1, 0])
     grads1, sums1 = layer_backward(upstream, kept1, gain_pairs[1], weights[1], segs, on_first, first)
     grads0, sums0 = layer_backward(grads1, kept0, gain_pairs[0], weights[0], segs, on_first, first)

time: 604 us -> 568 us (0.940)
  local copies, waits for them, and re-layouts: 69.1 us -> 46.5 us
  Pallas kernels: 103 us -> 90.7 us
  other arithmetic: 36.1 us -> 26.2 us
    all_gather x1, waiting for transfers between devices: 114 us -> 33.3 us  [per_device(): lax.all_gather(in_order(*row_pieces), ('wshard', 'seq'), axis=0, tiled=True)]
    ppermute x16 -> x18, waiting for transfers between devices: 10.1 us -> 32.3 us  [swapped(): return lax.ppermute(array, 'section', SWAP)]
    ppermute x1, waiting for transfers between devices: 18.2 us -> 39.9 us  [per_device(): above = lax.ppermute(down_piece, 'wshard', w_down)]
    ppermute x1, waiting for transfers between devices: 13.9 us -> 30 us  [per_device(): lax.ppermute(below[:, :half], 'wshard', w_up)]
    ppermute x4, waiting for transfers between devices: 3.08 us -> 15.4 us  [to_next(): return lax.ppermute(array, 'seq', [(i, i + 1) for i in range(SEQ_DEV - 1)])]
    reduce_scatter x2, waiting for transfers between devices: 120 us -> 131 us  [seq_sum(): return lax.psum_scatter(total, 'seq', scatter_dimension=0, tiled=True)]
    pallas_call x10, Pallas kernels: 84 us -> 73.3 us  [grid_call(): pl.pallas_call(kernel, grid_spec=pltpu.PrefetchScalarGridSpec(num_scalar_...]
    unnamed x145 -> x92, local copies, waits for them, and re-layouts: 22.8 us -> 16 us
  transfers between devices with their start and end apart: 37 -> 39, of which waited for: 14 -> 20; matrix products, arithmetic and copies ran while one was open for 14% -> 9% of each run, Pallas kernels for 11% -> 10%
where the time goes in v4:
time: 568 us; the launch traced here: 558 us
  waiting for transfers between devices  313 us (55%)
  Pallas kernels  90.7 us (16%)
  starting transfers between devices  53.2 us (9%)
  local copies, waits for them, and re-layouts  46.5 us (8%)
  other arithmetic  26.2 us (5%)
  between operations  15.5 us (3%)
  matrix products  13.2 us (2%)
    reduce_scatter x2, waiting for transfers between devices, seq_sum(): return lax.psum_scatter(total, 'seq', scatter_dimension=0, tiled=True)  131 us
    pallas_call x10, Pallas kernels, grid_call(): pl.pallas_call(kernel, grid_spec=pltpu.PrefetchScalarGridSpec(num_scalar_...  73.3 us
    ppermute x1, waiting for transfers between devices, per_device(): above = lax.ppermute(down_piece, 'wshard', w_down)  39.9 us
    all_gather x1, waiting for transfers between devices, per_device(): lax.all_gather(in_order(*row_pieces), ('wshard', 'seq'), axis=0, tiled=True)  33.3 us
    ppermute x18, waiting for transfers between devices, swapped(): return lax.ppermute(array, 'section', SWAP)  32.3 us
    ppermute x1, waiting for transfers between devices, per_device(): lax.ppermute(below[:, :half], 'wshard', w_up)  30 us
    unnamed x92, local copies, waits for them, and re-layouts  16 us
    ppermute x4, starting transfers between devices, to_next(): return lax.ppermute(array, 'seq', [(i, i + 1) for i in range(SEQ_DEV - 1)])  15.8 us
  transfers between devices with their start and end apart: 39, of which 20 were waited for; matrix products, arithmetic and copies ran while one was open for 9% of the time, Pallas kernels for 10%

profile of v4, /device:TPU:1, one launch (start us, length us, event | category | flops | bytes accessed | tf_op | source)
XLA Modules:
  0.0 558.4 jit_solution(14329737305226037711)
XLA Ops:
  21.6 3.8 collective-permute-start.5
  25.5 39.9 %collective-permute-done.5 = bf16[656,1024]{1,0:T(8,128)(2,1)} collective-permute-done((bf16[656,1024]{1,0:T(8,128)(2,1)S(1)}, bf16[656,1024]{1,0:T(8,128)(2,1)}, u32[]{:S(2)}, u32[]{:S(2)}) %collective-permute-start.5) | collective-permute-done | bytes 1343520 | tf_op jit(solution)/shard_map/ppermute | solution.py:581
  65.4 2.7 fusion.40
  68.1 3.6 collective-permute-start.8
  71.6 13.6 %collective-permute-done.8 = bf16[656,512]{1,0:T(8,128)(2,1)S(1)} collective-permute-done((bf16[656,512]{1,0:T(8,128)(2,1)}, bf16[656,512]{1,0:T(8,128)(2,1)S(1)}, u32[]{:S(2)}, u32[]{:S(2)}) %collective-permute-start.8) | collective-permute-done | bytes 671776 | tf_op jit(solution)/shard_map/ppermute | solution.py:584
  87.0 30.0 %collective-permute-done.7 = bf16[656,512]{1,0:T(8,128)(2,1)S(1)} collective-permute-done((bf16[656,512]{1,0:T(8,128)(2,1)S(1)}, bf16[656,512]{1,0:T(8,128)(2,1)S(1)}, u32[]{:S(2)}, u32[]{:S(2)}) %collective-permute-start.7) | collective-permute-done | bytes 671776 | tf_op jit(solution)/shard_map/ppermute | solution.py:583
  118.9 33.3 %all-gather.2.cloned.1.call-done.weight_own.gate_own.up_own = bf16[512,18944]{1,0:T(8,128)(2,1)} async-done(((bf16[8,18944]{1,0:T(8,128)(2,1)}), bf16[512,18944]{1,0:T(8,128)(2,1)}) %all-gather.2.cloned.1.call-update) | async-done | bytes 19398672 | tf_op jit(solution)/shard_map/all_gather | solution.py:574
  152.1 5.3 slice.430
  158.1 3.7 slice.429
  163.5 3.3 collective-permute-done
  166.8 2.3 slice.431
  170.3 3.7 collective-permute-start.1
  176.5 4.4 collective-permute-done.2
  183.9 1.9 copy-done.1
  185.8 3.5 qkv.2
  189.3 2.9 attend.2
  193.7 1.9 bitcast_convert_fusion
  200.2 26.2 %collective-permute-done.12.down_other = bf16[2688,512]{1,0:T(8,128)(2,1)} collective-permute-done((bf16[2688,512]{1,0:T(8,128)(2,1)}, bf16[2688,512]{1,0:T(8,128)(2,1)}, u32[]{:S(2)}, u32[]{:S(2)}) %collective-permute-start.12) | collective-permute-done | bytes 2752544 | tf_op jit(solution)/shard_map/ppermute | solution.py:31
  226.4 8.8 %hidden.2 = (f32[128,2688]{1,0:T(8,128)S(1)}, f32[128,2688]{1,0:T(8,128)S(1)}, bf16[128,2688]{1,0:T(8,128)(2,1)}, f32[128,1024]{1,0:T(8,128)S(1)}) custom-call(s32[1]{0:T(128)} %bitcast.first, bf16[128,512]{1,0:T(8,128)(2,1)S(1)} %get-tuple-element.218.own, bf16[128,512]{1,0:T(8,128)(2,1)S(1)} %get-tuple-element.217.other, ...), custom_call_target="tpu_custom_call" | custom-call | tf_op jit(solution)/shard_map/hidden/pallas_call | solution.py:183
  237.9 2.5 collective-permute-start.13
  242.9 3.8 collective-permute-done.14
  247.0 4.0 qkv.3
  251.0 2.9 attend.3
  257.7 8.8 %hidden.3 = (f32[128,2688]{1,0:T(8,128)S(1)}, f32[128,2688]{1,0:T(8,128)S(1)}, bf16[128,2688]{1,0:T(8,128)(2,1)}, f32[128,1024]{1,0:T(8,128)S(1)}) custom-call(s32[1]{0:T(128)} %bitcast.first, bf16[128,512]{1,0:T(8,128)(2,1)S(1)} %get-tuple-element.198.own, bf16[128,512]{1,0:T(8,128)(2,1)S(1)} %get-tuple-element.197.other, ...), custom_call_target="tpu_custom_call" | custom-call | tf_op jit(solution)/shard_map/hidden/pallas_call | solution.py:183
  267.3 9.8 %hidden_back.2 = (bf16[128,2688]{1,0:T(8,128)(2,1)S(1)}, bf16[128,2688]{1,0:T(8,128)(2,1)S(1)}, f32[128,1024]{1,0:T(8,128)S(1)}) custom-call(s32[1]{0:T(128)} %bitcast.first, bf16[128,512]{1,0:T(8,128)(2,1)S(1)} %get-tuple-element.196.grad_own, bf16[128,512]{1,0:T(8,128)(2,1)S(1)} %get-tuple-element.195.grad_other, ...), custom_call_target="tpu_custom_call" | custom-call | tf_op jit(solution)/shard_map/hidden_back/pallas_call | solution.py:183
  282.9 5.8 %attend_back.2 = (bf16[128,1024]{1,0:T(8,128)(2,1)S(1)}, f32[128,2048]{1,0:T(8,128)S(1)}, bf16[64,2048]{1,0:T(8,128)(2,1)S(1)}, bf16[64,2048]{1,0:T(8,128)(2,1)S(1)}) custom-call(s32[128,1]{1,0:T(8,128)S(1)} %copy.35.query_seg, s32[1,256]{1,0:T(1,128)S(1)} %bitcast.108, bf16[256,3072]{1,0:T(8,128)(2,1)S(1)} %qkv.3, ...), custom_call_target="tpu_custom_call" | custom-call | tf_op jit(solution)/shard_map/attend_back/pallas_call | solution.py:156
  288.7 5.0 collective-permute-start.18
  295.0 3.1 collective-permute-done.18
  298.1 3.8 collective-permute-done.19
  303.1 1.8 broadcast_select_fusion
  304.9 2.4 collective-permute-start.31
  309.1 4.6 qkv_back.2
  317.3 9.8 %weight_grads.3 = bf16[1024,6400]{1,0:T(8,128)(2,1)} custom-call(bf16[3,128,1024]{2,1,0:T(8,128)(2,1)} %pad_maximum_fusion.4.act_mine, bf16[3,128,1024]{2,1,0:T(8,128)(2,1)} %collective-permute-done.29.act_got, bf16[128,2688]{1,0:T(8,128)(2,1)} %get-tuple-element.66.product_mine, bf16[128,2688]{1,0:T(8,128)(2,1)} %collective-permute-done.30.product_got, ...), custom_call_target="tpu_custom_call" | custom-call | tf_op jit(solution)/shard_map/weight_grads/pallas_call | solution.py:183
  327.2 2.1 fusion.37
  329.4 9.9 %hidden_back.3 = (bf16[128,2688]{1,0:T(8,128)(2,1)S(1)}, bf16[128,2688]{1,0:T(8,128)(2,1)S(1)}, f32[128,1024]{1,0:T(8,128)S(1)}) custom-call(s32[1]{0:T(128)} %bitcast.first, bf16[128,512]{1,0:T(8,128)(2,1)S(1)} %get-tuple-element.192.grad_own, bf16[128,512]{1,0:T(8,128)(2,1)S(1)} %get-tuple-element.191.grad_other, f32[128,2688]{1,0:T(8,128)S(1)} %copy-done.7, ...), custom_call_target="tpu_custom_call" | custom-call | tf_op jit(solution)/shard_map/hidden_back/pallas_call | solution.py:183
  342.3 1.8 select_convert_fusion
  344.3 5.8 %attend_back.3 = (bf16[128,1024]{1,0:T(8,128)(2,1)S(1)}, f32[128,2048]{1,0:T(8,128)S(1)}, bf16[64,2048]{1,0:T(8,128)(2,1)S(1)}, bf16[64,2048]{1,0:T(8,128)(2,1)S(1)}) custom-call(s32[128,1]{1,0:T(8,128)S(1)} %copy.35.query_seg, s32[1,256]{1,0:T(1,128)S(1)} %bitcast.109, bf16[256,3072]{1,0:T(8,128)(2,1)S(1)} %qkv.2, f32[128,1024]{1,0:T(8,128)S(1)} %copy-done.11, ...), custom_call_target="tpu_custom_call" | custom-call | tf_op jit(solution)/shard_map/attend_back/pallas_call | solution.py:156
  350.1 4.6 collective-permute-start.20
  356.0 10.2 %collective-permute-done.20 = bf16[64,2048]{1,0:T(8,128)(2,1)S(1)} collective-permute-done((bf16[64,2048]{1,0:T(8,128)(2,1)S(1)}, bf16[64,2048]{1,0:T(8,128)(2,1)S(1)}, u32[]{:S(2)}, u32[]{:S(2)}) %collective-permute-start.20) | collective-permute-done | bytes 262176 | tf_op jit(solution)/shard_map/ppermute | solution.py:170
  366.3 2.9 collective-permute-done.21
  375.0 4.4 qkv_back.3
  380.1 9.7 %weight_grads.2 = bf16[1024,6400]{1,0:T(8,128)(2,1)} custom-call(bf16[3,128,1024]{2,1,0:T(8,128)(2,1)S(1)} %pad_maximum_fusion.3.act_mine, bf16[3,128,1024]{2,1,0:T(8,128)(2,1)} %collective-permute-done.23.act_got, bf16[128,2688]{1,0:T(8,128)(2,1)} %get-tuple-element.63.product_mine, bf16[128,2688]{1,0:T(8,128)(2,1)} %collective-permute-done.24.product_got, ...), custom_call_target="tpu_custom_call" | custom-call | tf_op jit(solution)/shard_map/weight_grads/pallas_call | solution.py:183
  392.2 38.3 %reduce-scatter.5.cloned.1.call-done = bf16[64,6400]{1,0:T(8,128)(2,1)} async-done(((bf16[1024,6400]{1,0:T(8,128)(2,1)}), bf16[64,6400]{1,0:T(8,128)(2,1)}) %reduce-scatter.5.cloned.1.call-update) | async-done | bytes 819216 | tf_op jit(solution)/shard_map/reduce_scatter | solution.py:412
  433.0 2.6 collective-permute-start.33
  436.6 92.6 %reduce-scatter.3.cloned.1.call-done = bf16[64,6400]{1,0:T(8,128)(2,1)} async-done(((bf16[1024,6400]{1,0:T(8,128)(2,1)}), bf16[64,6400]{1,0:T(8,128)(2,1)}) %reduce-scatter.3.cloned.1.call-update) | async-done | bytes 819216 | tf_op jit(solution)/shard_map/reduce_scatter | solution.py:412
  531.7 2.5 collective-permute-start.27
  540.1 2.7 collective-permute-done.27
  544.3 1.9 collective-permute-start.35
  (275 shorter events, 88.1 us)
Async XLA Ops:
  7.2 145.0 %all-gather.2.cloned.1.call-start = ((), (), s32[]{:S(2)}) async-start(), calls=%async_computation.2 | async-start | bytes 19701760 | tf_op jit(solution)/shard_map/all_gather | solution.py:574
  8.2 5.2 copy-start.17
  10.1 2.5 collective-permute-start.3
  13.4 417.1 %reduce-scatter.5.cloned.1.call-start = ((), (), s32[]{:S(2)}) async-start(), calls=%async_computation.4 | async-start | bytes 13926400 | tf_op jit(solution)/shard_map/reduce_scatter | solution.py:412
  13.5 2.2 collective-permute-start.4
  21.6 43.8 %collective-permute-start.5 = (bf16[656,1024]{1,0:T(8,128)(2,1)S(1)}, bf16[656,1024]{1,0:T(8,128)(2,1)}, u32[]{:S(2)}, u32[]{:S(2)}) collective-permute-start(bf16[656,1024]{1,0:T(8,128)(2,1)S(1)} %pad_maximum_fusion), channel_id=1, source_target_pairs={{1,0},{2,1},{3,2},{0,3},{5,4},{6,5},{7,6},{4,7},{9,8},{10,9},{11,1... | collective-permute-start | bytes 4030472 | tf_op jit(solution)/shard_map/ppermute | solution.py:581
  25.4 60.6 %collective-permute-start.6 = (bf16[656,1024]{1,0:T(8,128)(2,1)S(1)}, bf16[656,1024]{1,0:T(8,128)(2,1)S(1)}, u32[]{:S(2)}, u32[]{:S(2)}) collective-permute-start(bf16[656,1024]{1,0:T(8,128)(2,1)S(1)} %pad_maximum_fusion), channel_id=1, source_target_pairs={{0,1},{1,2},{2,3},{3,0},{4,5},{5,6},{6,7},{7,4},{8,9},{9,10},{10,1... | collective-permute-start | bytes 4030472 | tf_op jit(solution)/shard_map/ppermute | solution.py:580
  68.1 17.1 %collective-permute-start.8 = (bf16[656,512]{1,0:T(8,128)(2,1)}, bf16[656,512]{1,0:T(8,128)(2,1)S(1)}, u32[]{:S(2)}, u32[]{:S(2)}) collective-permute-start(bf16[656,512]{1,0:T(8,128)(2,1)} %get-tuple-element.133), channel_id=1, source_target_pairs={{1,0},{2,1},{3,2},{0,3},{5,4},{6,5},{7,6},{4,7},{9,8},{10,9},{11,1... | collective-permute-start | bytes 2015240 | tf_op jit(solution)/shard_map/ppermute | solution.py:584
  87.0 30.1 %collective-permute-start.7 = (bf16[656,512]{1,0:T(8,128)(2,1)S(1)}, bf16[656,512]{1,0:T(8,128)(2,1)S(1)}, u32[]{:S(2)}, u32[]{:S(2)}) collective-permute-start(bf16[656,512]{1,0:T(8,128)(2,1)S(1)} %get-tuple-element.132), channel_id=1, source_target_pairs={{0,1},{1,2},{2,3},{3,0},{4,5},{5,6},{6,7},{7,4},{8,9},{9,10},{10,1... | collective-permute-start | bytes 2015240 | tf_op jit(solution)/shard_map/ppermute | solution.py:583
  157.4 4.5 copy-start.30
  157.4 4.9 copy-start.24
  157.5 31.8 %collective-permute-start.10 = (bf16[512,5376]{1,0:T(8,128)(2,1)}, bf16[512,5376]{1,0:T(8,128)(2,1)}, u32[]{:S(2)}, u32[]{:S(2)}) collective-permute-start(bf16[512,5376]{1,0:T(8,128)(2,1)} %slice.430), channel_id=1, source_target_pairs={{0,64},{64,0},{1,65},{65,1},{2,66},{66,2},{3,67},{67,3},{4,68},{68... | collective-permute-start | bytes 16515080 | tf_op jit(solution)/shard_map/ppermute | solution.py:31
  161.8 20.4 %collective-permute-start.9 = (bf16[512,3072]{1,0:T(8,128)(2,1)}, bf16[512,3072]{1,0:T(8,128)(2,1)S(1)}, u32[]{:S(2)}, u32[]{:S(2)}) collective-permute-start(bf16[512,3072]{1,0:T(8,128)(2,1)} %slice.429), channel_id=1, source_target_pairs={{0,64},{64,0},{1,65},{65,1},{2,66},{66,2},{3,67},{67,3},{4,68},{68... | collective-permute-start | bytes 9437192 | tf_op jit(solution)/shard_map/ppermute | solution.py:31
  161.9 4.9 collective-permute-start
  163.5 5.9 %copy-start.13 = (f32[1,1,128,1024]{3,2,1,0:T(8,128)S(1)}, f32[1,1,128,1024]{3,2,1,0:T(8,128)}, u32[]{:S(2)}) copy-start(f32[1,1,128,1024]{3,2,1,0:T(8,128)} %copy-done.12) | copy-start | bytes 1572868
  169.1 20.2 %collective-permute-start.11 = (bf16[512,1024]{1,0:T(8,128)(2,1)}, bf16[512,1024]{1,0:T(8,128)(2,1)}, u32[]{:S(2)}, u32[]{:S(2)}) collective-permute-start(bf16[512,1024]{1,0:T(8,128)(2,1)} %slice.431), channel_id=1, source_target_pairs={{0,64},{64,0},{1,65},{65,1},{2,66},{66,2},{3,67},{67,3},{4,68},{68... | collective-permute-start | bytes 3145736 | tf_op jit(solution)/shard_map/ppermute | solution.py:31
  170.3 6.2 %collective-permute-start.1 = (bf16[64,1024]{1,0:T(8,128)(2,1)}, bf16[64,1024]{1,0:T(8,128)(2,1)}, u32[]{:S(2)}, u32[]{:S(2)}) collective-permute-start(bf16[64,1024]{1,0:T(8,128)(2,1)} %get-tuple-element.235), channel_id=1, source_target_pairs={{0,4},{4,8},{8,12},{12,16},{16,20},{20,24},{24,28},{28,32},{32,36}... | collective-permute-start | bytes 393224 | tf_op jit(solution)/shard_map/ppermute | solution.py:170
  174.1 6.8 %collective-permute-start.2 = (bf16[64,1024]{1,0:T(8,128)(2,1)}, bf16[64,1024]{1,0:T(8,128)(2,1)}, u32[]{:S(2)}, u32[]{:S(2)}) collective-permute-start(bf16[64,1024]{1,0:T(8,128)(2,1)} %get-tuple-element.236), channel_id=1, source_target_pairs={{4,0},{8,4},{12,8},{16,12},{20,16},{24,20},{28,24},{32,28},{36,32}... | collective-permute-start | bytes 393224 | tf_op jit(solution)/shard_map/ppermute | solution.py:174
  189.3 7.2 %copy-start.14 = (f32[1,1,128,1024]{3,2,1,0:T(8,128)S(1)}, f32[1,1,128,1024]{3,2,1,0:T(8,128)}, u32[]{:S(2)}) copy-start(f32[1,1,128,1024]{3,2,1,0:T(8,128)} %copy-done.12) | copy-start | bytes 1572868
  192.2 5.9 %copy-start.10 = (f32[128,1024]{1,0:T(8,128)}, f32[128,1024]{1,0:T(8,128)S(1)}, u32[]{:S(2)}) copy-start(f32[128,1024]{1,0:T(8,128)S(1)} %get-tuple-element.58.log_total) | copy-start | bytes 1572868
  192.2 54.8 %collective-permute-start.15 = (bf16[512,18944]{1,0:T(8,128)(2,1)}, bf16[512,18944]{1,0:T(8,128)(2,1)}, u32[]{:S(2)}, u32[]{:S(2)}) collective-permute-start(bf16[512,18944]{1,0:T(8,128)(2,1)} %all-gather.2.cloned.1.call-done.weight_own.gate_own.up_own), channel_id=1, source_target_pairs={{0,64},{64,0},{1,65},{65,1},{2,66},{66,2},{3,67},{67,3},{4,68},{68... | collective-permute-start | bytes 58195976 | tf_op jit(solution)/shard_map/ppermute | solution.py:31
  193.6 32.8 %collective-permute-start.12 = (bf16[2688,512]{1,0:T(8,128)(2,1)}, bf16[2688,512]{1,0:T(8,128)(2,1)}, u32[]{:S(2)}, u32[]{:S(2)}) collective-permute-start(bf16[2688,512]{1,0:T(8,128)(2,1)} %constant_dynamic-update-slice_fusion.33.down_own), channel_id=1, source_target_pairs={{0,64},{64,0},{1,65},{65,1},{2,66},{66,2},{3,67},{67,3},{4,68},{68... | collective-permute-start | bytes 8257544 | tf_op jit(solution)/shard_map/ppermute | solution.py:31
  195.6 62.0 %collective-permute-start.16 = (bf16[2688,512]{1,0:T(8,128)(2,1)}, bf16[2688,512]{1,0:T(8,128)(2,1)}, u32[]{:S(2)}, u32[]{:S(2)}) collective-permute-start(bf16[2688,512]{1,0:T(8,128)(2,1)} %get-tuple-element.45.down_own), channel_id=1, source_target_pairs={{0,64},{64,0},{1,65},{65,1},{2,66},{66,2},{3,67},{67,3},{4,68},{68... | collective-permute-start | bytes 8257544 | tf_op jit(solution)/shard_map/ppermute | solution.py:31
  237.9 5.0 collective-permute-start.13
  240.4 6.3 %collective-permute-start.14 = (bf16[64,1024]{1,0:T(8,128)(2,1)S(1)}, bf16[64,1024]{1,0:T(8,128)(2,1)S(1)}, u32[]{:S(2)}, u32[]{:S(2)}) collective-permute-start(bf16[64,1024]{1,0:T(8,128)(2,1)S(1)} %get-tuple-element.216), channel_id=1, source_target_pairs={{4,0},{8,4},{12,8},{16,12},{20,16},{24,20},{28,24},{32,28},{36,32}... | collective-permute-start | bytes 393224 | tf_op jit(solution)/shard_map/ppermute | solution.py:174
  288.7 9.4 %collective-permute-start.18 = (bf16[64,2048]{1,0:T(8,128)(2,1)S(1)}, bf16[64,2048]{1,0:T(8,128)(2,1)S(1)}, u32[]{:S(2)}, u32[]{:S(2)}) collective-permute-start(bf16[64,2048]{1,0:T(8,128)(2,1)S(1)} %get-tuple-element.53), channel_id=1, source_target_pairs={{0,4},{4,8},{8,12},{12,16},{16,20},{20,24},{24,28},{28,32},{32,36}... | collective-permute-start | bytes 786440 | tf_op jit(solution)/shard_map/ppermute | solution.py:170
  293.7 8.2 %collective-permute-start.19 = (bf16[64,2048]{1,0:T(8,128)(2,1)S(1)}, bf16[64,2048]{1,0:T(8,128)(2,1)S(1)}, u32[]{:S(2)}, u32[]{:S(2)}) collective-permute-start(bf16[64,2048]{1,0:T(8,128)(2,1)S(1)} %get-tuple-element.54), channel_id=1, source_target_pairs={{4,0},{8,4},{12,8},{16,12},{20,16},{24,20},{28,24},{32,28},{36,32}... | collective-permute-start | bytes 786440 | tf_op jit(solution)/shard_map/ppermute | solution.py:174
  304.9 11.1 %collective-permute-start.31 = (bf16[128,5376]{1,0:T(8,128)(2,1)}, bf16[128,5376]{1,0:T(8,128)(2,1)}, u32[]{:S(2)}, u32[]{:S(2)}) collective-permute-start(bf16[128,5376]{1,0:T(8,128)(2,1)} %get-tuple-element.119), channel_id=1, source_target_pairs={{0,64},{64,0},{1,65},{65,1},{2,66},{66,2},{3,67},{67,3},{4,68},{68... | collective-permute-start | bytes 4128776 | tf_op jit(solution)/shard_map/ppermute | solution.py:31
  308.5 7.4 %collective-permute-start.29 = (bf16[3,128,1024]{2,1,0:T(8,128)(2,1)}, bf16[3,128,1024]{2,1,0:T(8,128)(2,1)}, u32[]{:S(2)}, u32[]{:S(2)}) collective-permute-start(bf16[3,128,1024]{2,1,0:T(8,128)(2,1)} %pad_maximum_fusion.4.act_mine), channel_id=1, source_target_pairs={{0,64},{64,0},{1,65},{65,1},{2,66},{66,2},{3,67},{67,3},{4,68},{68... | collective-permute-start | bytes 2359304 | tf_op jit(solution)/shard_map/ppermute | solution.py:31
  308.6 7.4 %collective-permute-start.30 = (bf16[128,2688]{1,0:T(8,128)(2,1)}, bf16[128,2688]{1,0:T(8,128)(2,1)}, u32[]{:S(2)}, u32[]{:S(2)}) collective-permute-start(bf16[128,2688]{1,0:T(8,128)(2,1)} %get-tuple-element.66.product_mine), channel_id=1, source_target_pairs={{0,64},{64,0},{1,65},{65,1},{2,66},{66,2},{3,67},{67,3},{4,68},{68... | collective-permute-start | bytes 2064392 | tf_op jit(solution)/shard_map/ppermute | solution.py:31
  327.1 202.0 %reduce-scatter.3.cloned.1.call-start = ((), (), s32[]{:S(2)}) async-start(), calls=%async_computation.3 | async-start | bytes 13926400 | tf_op jit(solution)/shard_map/reduce_scatter | solution.py:412
  329.4 10.2 %copy-start.18 = (f32[128,1024]{1,0:T(8,128)}, f32[128,1024]{1,0:T(8,128)S(1)}, u32[]{:S(2)}) copy-start(f32[128,1024]{1,0:T(8,128)S(1)} %get-tuple-element.110) | copy-start | bytes 1572868
  350.1 16.2 %collective-permute-start.20 = (bf16[64,2048]{1,0:T(8,128)(2,1)S(1)}, bf16[64,2048]{1,0:T(8,128)(2,1)S(1)}, u32[]{:S(2)}, u32[]{:S(2)}) collective-permute-start(bf16[64,2048]{1,0:T(8,128)(2,1)S(1)} %get-tuple-element.61), channel_id=1, source_target_pairs={{0,4},{4,8},{8,12},{12,16},{16,20},{20,24},{24,28},{28,32},{32,36}... | collective-permute-start | bytes 786440 | tf_op jit(solution)/shard_map/ppermute | solution.py:170
  354.7 14.5 %collective-permute-start.21 = (bf16[64,2048]{1,0:T(8,128)(2,1)S(1)}, bf16[64,2048]{1,0:T(8,128)(2,1)S(1)}, u32[]{:S(2)}, u32[]{:S(2)}) collective-permute-start(bf16[64,2048]{1,0:T(8,128)(2,1)S(1)} %get-tuple-element.62), channel_id=1, source_target_pairs={{4,0},{8,4},{12,8},{16,12},{20,16},{24,20},{28,24},{32,28},{36,32}... | collective-permute-start | bytes 786440 | tf_op jit(solution)/shard_map/ppermute | solution.py:174
  370.9 9.2 %collective-permute-start.25 = (bf16[128,5376]{1,0:T(8,128)(2,1)}, bf16[128,5376]{1,0:T(8,128)(2,1)}, u32[]{:S(2)}, u32[]{:S(2)}) collective-permute-start(bf16[128,5376]{1,0:T(8,128)(2,1)} %get-tuple-element.121), channel_id=1, source_target_pairs={{0,64},{64,0},{1,65},{65,1},{2,66},{66,2},{3,67},{67,3},{4,68},{68... | collective-permute-start | bytes 4128776 | tf_op jit(solution)/shard_map/ppermute | solution.py:31
  373.0 7.0 %collective-permute-start.23 = (bf16[3,128,1024]{2,1,0:T(8,128)(2,1)S(1)}, bf16[3,128,1024]{2,1,0:T(8,128)(2,1)}, u32[]{:S(2)}, u32[]{:S(2)}) collective-permute-start(bf16[3,128,1024]{2,1,0:T(8,128)(2,1)S(1)} %pad_maximum_fusion.3.act_mine), channel_id=1, source_target_pairs={{0,64},{64,0},{1,65},{65,1},{2,66},{66,2},{3,67},{67,3},{4,68},{68... | collective-permute-start | bytes 2359304 | tf_op jit(solution)/shard_map/ppermute | solution.py:31
  373.1 6.9 %collective-permute-start.24 = (bf16[128,2688]{1,0:T(8,128)(2,1)}, bf16[128,2688]{1,0:T(8,128)(2,1)}, u32[]{:S(2)}, u32[]{:S(2)}) collective-permute-start(bf16[128,2688]{1,0:T(8,128)(2,1)} %get-tuple-element.63.product_mine), channel_id=1, source_target_pairs={{0,64},{64,0},{1,65},{65,1},{2,66},{66,2},{3,67},{67,3},{4,68},{68... | collective-permute-start | bytes 2064392 | tf_op jit(solution)/shard_map/ppermute | solution.py:31
  389.8 141.9 %collective-permute-start.17 = (f32[128,1024]{1,0:T(8,128)}, f32[128,1024]{1,0:T(8,128)}, u32[]{:S(2)}, u32[]{:S(2)}) collective-permute-start(f32[128,1024]{1,0:T(8,128)} %get-tuple-element.148), channel_id=1, source_target_pairs={{0,64},{64,0},{1,65},{65,1},{2,66},{66,2},{3,67},{67,3},{4,68},{68... | collective-permute-start | bytes 1572872 | tf_op jit(solution)/shard_map/ppermute | solution.py:31
  392.2 143.9 %copy-start.5 = (f32[128,1024]{1,0:T(8,128)S(1)}, f32[128,1024]{1,0:T(8,128)}, u32[]{:S(2)}) copy-start(f32[128,1024]{1,0:T(8,128)} %copy-done.4) | copy-start | bytes 1572868
  431.7 102.6 %collective-permute-start.32 = (bf16[16,6400]{1,0:T(8,128)(2,1)S(1)}, bf16[16,6400]{1,0:T(8,128)(2,1)S(1)}, u32[]{:S(2)}, u32[]{:S(2)}) collective-permute-start(bf16[16,6400]{1,0:T(8,128)(2,1)S(1)} %get-tuple-element.138), channel_id=1, source_target_pairs={{0,1},{1,2},{2,3},{3,0},{4,5},{5,6},{6,7},{7,4},{8,9},{9,10},{10,1... | collective-permute-start | bytes 614408 | tf_op jit(solution)/shard_map/ppermute | solution.py:533
  433.0 105.4 %collective-permute-start.33 = (bf16[16,6400]{1,0:T(8,128)(2,1)S(1)}, bf16[16,6400]{1,0:T(8,128)(2,1)}, u32[]{:S(2)}, u32[]{:S(2)}) collective-permute-start(bf16[16,6400]{1,0:T(8,128)(2,1)S(1)} %get-tuple-element.140), channel_id=1, source_target_pairs={{0,2},{1,3},{2,0},{3,1},{4,6},{5,7},{6,4},{7,5},{8,10},{9,11},{10,... | collective-permute-start | bytes 614408 | tf_op jit(solution)/shard_map/ppermute | solution.py:533
  435.5 104.5 %collective-permute-start.34 = (bf16[16,6400]{1,0:T(8,128)(2,1)S(1)}, bf16[16,6400]{1,0:T(8,128)(2,1)}, u32[]{:S(2)}, u32[]{:S(2)}) collective-permute-start(bf16[16,6400]{1,0:T(8,128)(2,1)S(1)} %get-tuple-element.139), channel_id=1, source_target_pairs={{0,3},{1,0},{2,1},{3,2},{4,7},{5,4},{6,5},{7,6},{8,11},{9,8},{10,9... | collective-permute-start | bytes 614408 | tf_op jit(solution)/shard_map/ppermute | solution.py:533
  530.3 9.7 %collective-permute-start.26 = (bf16[16,6400]{1,0:T(8,128)(2,1)S(1)}, bf16[16,6400]{1,0:T(8,128)(2,1)S(1)}, u32[]{:S(2)}, u32[]{:S(2)}) collective-permute-start(bf16[16,6400]{1,0:T(8,128)(2,1)S(1)} %get-tuple-element.141), channel_id=1, source_target_pairs={{0,1},{1,2},{2,3},{3,0},{4,5},{5,6},{6,7},{7,4},{8,9},{9,10},{10,1... | collective-permute-start | bytes 614408 | tf_op jit(solution)/shard_map/ppermute | solution.py:533
  531.7 11.1 %collective-permute-start.27 = (bf16[16,6400]{1,0:T(8,128)(2,1)S(1)}, bf16[16,6400]{1,0:T(8,128)(2,1)S(1)}, u32[]{:S(2)}, u32[]{:S(2)}) collective-permute-start(bf16[16,6400]{1,0:T(8,128)(2,1)S(1)} %get-tuple-element.143), channel_id=1, source_target_pairs={{0,2},{1,3},{2,0},{3,1},{4,6},{5,7},{6,4},{7,5},{8,10},{9,11},{10,... | collective-permute-start | bytes 614408 | tf_op jit(solution)/shard_map/ppermute | solution.py:533
  534.9 7.9 %collective-permute-start.28 = (bf16[16,6400]{1,0:T(8,128)(2,1)S(1)}, bf16[16,6400]{1,0:T(8,128)(2,1)S(1)}, u32[]{:S(2)}, u32[]{:S(2)}) collective-permute-start(bf16[16,6400]{1,0:T(8,128)(2,1)S(1)} %get-tuple-element.142), channel_id=1, source_target_pairs={{0,3},{1,0},{2,1},{3,2},{4,7},{5,4},{6,5},{7,6},{8,11},{9,8},{10,9... | collective-permute-start | bytes 614408 | tf_op jit(solution)/shard_map/ppermute | solution.py:533
  537.3 5.6 copy-start.28
  538.4 7.8 %collective-permute-start.22 = (f32[128,1024]{1,0:T(8,128)S(1)}, f32[128,1024]{1,0:T(8,128)S(1)}, u32[]{:S(2)}, u32[]{:S(2)}) collective-permute-start(f32[128,1024]{1,0:T(8,128)S(1)} %copy-done.25), channel_id=1, source_target_pairs={{0,64},{64,0},{1,65},{65,1},{2,66},{66,2},{3,67},{67,3},{4,68},{68... | collective-permute-start | bytes 1572872 | tf_op jit(solution)/shard_map/ppermute | solution.py:31
  544.3 3.3 collective-permute-start.35
  (22 other events, 34.6 us)
Sparse Core Ops, SparseCore 0:
  13.5 138.5 all-gather.1
  327.2 103.1 reduce-scatter.4
  434.3 94.7 reduce-scatter.2

commit v5 on v4

--- a/solution.py
+++ b/solution.py
@@ -387,12 +387,16 @@
     )
 
 
-def layer_forward(rows_in, gain_pair, weights, segs, on_first, first, later=(), ready=()):
-    normed1, factor1 = norm_parts(rows_in)
-    act_in = (normed1 * gain_pair[0]).astype(jnp.bfloat16)
+def attention_input(rows_in, gain):
+    normed, factor = norm_parts(rows_in)
+    act_in = (normed * gain).astype(jnp.bfloat16)
     before = to_next(act_in[act_in.shape[0] - HALO :])
     after = to_previous(act_in[:HALO])
-    extended = jnp.concatenate([before, act_in, after], axis=0)
+    return (normed, factor, act_in, jnp.concatenate([before, act_in, after], axis=0))
+
+
+def layer_forward(rows_in, entry, gain_pair, weights, segs, on_first, first, later=(), ready=()):
+    normed1, factor1, act_in, extended = entry
     qkv = qkv_of(*column_halves(extended, on_first), weights)
     mixed, log_total = attend(*segs, qkv, ready)
     mixed, *later = lax.optimization_barrier((mixed, *later))
@@ -486,7 +490,7 @@
     )
 
 
-def layer_backward(grad_out, kept, gain_pair, weights, segs, on_first, first):
+def layer_backward(grad_out, kept, gain_pair, weights, segs, on_first, first, earlier_gains):
     (normed1, factor1, qkv, log_total, normed2, factor2, gate, up, acts, got) = kept
     rows, width = normed1.shape
     half = width // 2
@@ -520,9 +524,12 @@
     gain_first = jnp.sum(normed1 * grad_norm1, axis=0)
     grad_inputs = grad_middle + norm_back(grad_norm1 * gain_pair[0], normed1, factor1)
     gains = jnp.stack([gain_first, gain_mid])
-    gain_columns = jnp.pad(gains, ((0, 126), (0, 0))).T.astype(jnp.bfloat16)
-    sums = seq_sum(weight_grads(acts, got, grad_mine, grad_got, gain_columns))
-    return (grad_inputs, sums)
+    gains = jnp.concatenate([gains, earlier_gains], axis=0)
+    columns = jnp.pad(gains, ((0, 128 - gains.shape[0]), (0, 0))).T.astype(jnp.bfloat16)
+    if earlier_gains.shape[0] == 0:
+        columns = jnp.zeros(columns.shape, columns.dtype)
+    sums = seq_sum(weight_grads(acts, got, grad_mine, grad_got, columns))
+    return (grad_inputs, sums, gains)
 
 
 def summed_over_w(block, place):
@@ -600,30 +607,6 @@
             )
         return own
 
-    all_own, *down_own = lax.optimization_barrier((all_own, down_of(0), down_of(1)))
-    first_qkv = swapped(all_own[:, qkv_at : qkv_at + qkv_width])
-    first_out = swapped(all_own[:, out_at : out_at + width])
-    first_hidden = swapped(all_own[:, :hidden_width])
-    out_own = [all_own[:, out_at + k * width : out_at + (k + 1) * width] for k in (0, 1)]
-    first_weights = {
-        "qkv": ((all_own, qkv_at), (first_qkv, 0)),
-        "gate": ((all_own, 0), (first_hidden, 0)),
-        "up": ((all_own, FF_PAD), (first_hidden, FF_PAD)),
-        "out": (all_own[:, out_at : out_at + width], first_out),
-        "down": (down_own[0], swapped(down_own[0])),
-    }
-
-    def second_weights(all_late):
-        all_other = swapped(all_late)
-        return {
-            "qkv": ((all_own, qkv_at + qkv_width), (all_other, qkv_at + qkv_width)),
-            "gate": ((all_own, hidden_width), (all_other, hidden_width)),
-            "up": ((all_own, hidden_width + FF_PAD), (all_other, hidden_width + FF_PAD)),
-            "out": (all_own[:, out_at + width :], all_other[:, out_at + width :]),
-            "down": (down_own[1], swapped(down_own[1])),
-        }
-
-    first = on_first.astype(jnp.int32)[None]
     rows_in = by_core(inputs[0, 0], inputs[1, 0])
     row_count = rows_in.shape[0]
     segment_row = by_core(segments[0, 0], segments[1, 0])
@@ -633,14 +616,53 @@
         lax.dynamic_slice_in_dim(segment_row, first_row, row_count)[:, None],
         lax.dynamic_slice_in_dim(padded, first_row, row_count + 2 * HALO)[None, :],
     )
+    entry = attention_input(rows_in, gain_pairs[0][0])
+    down_own = (down_of(0), down_of(1))
+    all_own, down_own, down_other, entry, gain_pairs, segs = lax.optimization_barrier(
+        (all_own, down_own, tuple(swapped(d) for d in down_own), entry, gain_pairs, segs)
+    )
+    qkv_piece, all_own = lax.optimization_barrier(
+        (all_own[:, qkv_at : qkv_at + qkv_width], all_own)
+    )
+    first_qkv = swapped(qkv_piece)
+    first_out = swapped(all_own[:, out_at : out_at + width])
+    first_hidden = swapped(all_own[:, :hidden_width])
+    first_weights = {
+        "qkv": ((all_own, qkv_at), (first_qkv, 0)),
+        "gate": ((all_own, 0), (first_hidden, 0)),
+        "up": ((all_own, FF_PAD), (first_hidden, FF_PAD)),
+        "out": (all_own[:, out_at : out_at + width], first_out),
+        "down": (down_own[0], down_other[0]),
+    }
+
+    def second_weights(all_late):
+        all_other = swapped(all_late)
+        return {
+            "qkv": ((all_own, qkv_at + qkv_width), (all_other, qkv_at + qkv_width)),
+            "gate": ((all_own, hidden_width), (all_other, hidden_width)),
+            "up": ((all_own, hidden_width + FF_PAD), (all_other, hidden_width + FF_PAD)),
+            "out": (all_own[:, out_at + width :], all_other[:, out_at + width :]),
+            "down": (down_own[1], down_other[1]),
+        }
+
+    first = on_first.astype(jnp.int32)[None]
     middle, kept0, (all_late,) = layer_forward(
-        rows_in, gain_pairs[0], first_weights, segs, on_first, first, (all_own,), (first_hidden, first_out)
+        rows_in, entry, gain_pairs[0], first_weights, segs, on_first, first,
+        (all_own,), (first_hidden, first_out),
     )
     weights = (first_weights, second_weights(all_late))
-    final, kept1, _ = layer_forward(middle, gain_pairs[1], weights[1], segs, on_first, first)
+    entry = attention_input(middle, gain_pairs[1][0])
+    final, kept1, _ = layer_forward(
+        middle, entry, gain_pairs[1], weights[1], segs, on_first, first
+    )
     upstream = by_core(cotangent[0, 0], cotangent[1, 0])
-    grads1, sums1 = layer_backward(upstream, kept1, gain_pairs[1], weights[1], segs, on_first, first)
-    grads0, sums0 = layer_backward(grads1, kept0, gain_pairs[0], weights[0], segs, on_first, first)
+    no_gains = jnp.zeros((0, width), jnp.float32)
+    grads1, sums1, gains1 = layer_backward(
+        upstream, kept1, gain_pairs[1], weights[1], segs, on_first, first, no_gains
+    )
+    grads0, sums0, _ = layer_backward(
+        grads1, kept0, gain_pairs[0], weights[0], segs, on_first, first, gains1
+    )
 
     def placed(first, second):
         mine, give = (by_core(first, second), by_core(second, first))
@@ -660,7 +682,9 @@
     hidden_rows = jnp.concatenate(
         [low[:, hidden_at : hidden_at + FF], high[:, hidden_at : hidden_at + FF]], axis=1
     )
-    gain_rows = (low + high)[:, down_at - 128 : down_at - 126].T
+    gain_part = totals[0][:, down_at - 128 : down_at]
+    gain_part = gain_part + swapped(gain_part)
+    gain_rows = by_core(gain_part[:, :2], gain_part[:, 2:4]).T
     down_total = jnp.concatenate(
         [
             jnp.concatenate(

time: 568 us -> 525 us (0.924)
  waiting for transfers between devices: 313 us -> 268 us
  starting transfers between devices: 53.2 us -> 61.6 us
    all_gather x1, waiting for transfers between devices: 33.3 us -> 6.14 us  [per_device(): lax.all_gather(in_order(*row_pieces), ('wshard', 'seq'), axis=0, tiled=True)]
    ppermute x4, waiting for transfers between devices: 15.4 us -> 2.85 us  [to_next(): return lax.ppermute(array, 'seq', [(i, i + 1) for i in range(SEQ_DEV - 1)])]
    ppermute x18 -> x19, starting transfers between devices: 14.7 us -> 23.9 us  [swapped(): return lax.ppermute(array, 'section', SWAP)]
    ppermute x6, waiting for transfers between devices: 2.75 us -> 10.6 us  [summed_over_w(): lax.ppermute(part, 'wshard', [(j, (j + step) % W_DEV) for j in range(W_DE...]
    ppermute x1, waiting for transfers between devices: 30 us -> 23.1 us  [per_device(): lax.ppermute(below[:, :half], 'wshard', w_up)]
    ppermute x18 -> x19, waiting for transfers between devices: 32.3 us -> 26.4 us  [swapped(): return lax.ppermute(array, 'section', SWAP)]
    unnamed x92 -> x100, local copies, waits for them, and re-layouts: 16 us -> 13.8 us
  transfers between devices with their start and end apart: 39 -> 40, of which waited for: 20 -> 23; matrix products, arithmetic and copies ran while one was open for 9% -> 9% of each run, Pallas kernels for 10% -> 9%
where the time goes in v5:
time: 525 us; the launch traced here: 516 us
  waiting for transfers between devices  268 us (51%)
  Pallas kernels  87.5 us (17%)
  starting transfers between devices  61.6 us (12%)
  local copies, waits for them, and re-layouts  43.4 us (8%)
  other arithmetic  26.4 us (5%)
  between operations  15.5 us (3%)
  matrix products  13.4 us (3%)
    reduce_scatter x2, waiting for transfers between devices, seq_sum(): return lax.psum_scatter(total, 'seq', scatter_dimension=0, tiled=True)  126 us
    pallas_call x10, Pallas kernels, grid_call(): pl.pallas_call(kernel, grid_spec=pltpu.PrefetchScalarGridSpec(num_scalar_...  70.1 us
    ppermute x1, waiting for transfers between devices, per_device(): above = lax.ppermute(down_piece, 'wshard', w_down)  39.2 us
    ppermute x19, waiting for transfers between devices, swapped(): return lax.ppermute(array, 'section', SWAP)  26.4 us
    ppermute x19, starting transfers between devices, swapped(): return lax.ppermute(array, 'section', SWAP)  23.9 us
    ppermute x1, waiting for transfers between devices, per_device(): lax.ppermute(below[:, :half], 'wshard', w_up)  23.1 us
    ppermute x4, waiting for transfers between devices, to_previous(): return lax.ppermute(array, 'seq', [(i + 1, i) for i in range(SEQ_DEV - 1)])  19.3 us
    ppermute x4, starting transfers between devices, to_next(): return lax.ppermute(array, 'seq', [(i, i + 1) for i in range(SEQ_DEV - 1)])  17.5 us
  transfers between devices with their start and end apart: 40, of which 23 were waited for; matrix products, arithmetic and copies ran while one was open for 9% of the time, Pallas kernels for 9%

profile of v5, /device:TPU:1, one launch (start us, length us, event | category | flops | bytes accessed | tf_op | source)
XLA Modules:
  0.0 516.0 jit_solution(8201796297948216251)
XLA Ops:
  20.3 3.9 collective-permute-start.2
  24.2 39.2 %collective-permute-done.2 = bf16[656,1024]{1,0:T(8,128)(2,1)} collective-permute-done((bf16[656,1024]{1,0:T(8,128)(2,1)}, bf16[656,1024]{1,0:T(8,128)(2,1)}, u32[]{:S(2)}, u32[]{:S(2)}) %collective-permute-start.2) | collective-permute-done | bytes 1343520 | tf_op jit(solution)/shard_map/ppermute | solution.py:588
  63.3 2.5 fusion.39
  65.9 3.4 collective-permute-start.5
  69.3 14.8 %collective-permute-done.5 = bf16[656,512]{1,0:T(8,128)(2,1)S(1)} collective-permute-done((bf16[656,512]{1,0:T(8,128)(2,1)}, bf16[656,512]{1,0:T(8,128)(2,1)S(1)}, u32[]{:S(2)}, u32[]{:S(2)}) %collective-permute-start.5) | collective-permute-done | bytes 671776 | tf_op jit(solution)/shard_map/ppermute | solution.py:591
  85.6 7.8 %collective-permute-start.7 = (bf16[2688,512]{1,0:T(8,128)(2,1)S(1)}, bf16[2688,512]{1,0:T(8,128)(2,1)}, u32[]{:S(2)}, u32[]{:S(2)}) collective-permute-start(bf16[2688,512]{1,0:T(8,128)(2,1)S(1)} %get-tuple-element.65.down_own), channel_id=1, source_target_pairs={{0,64},{64,0},{1,65},{65,1},{2,66},{66,2},{3,67},{67,3},{4,68},{68... | collective-permute-start | bytes 8257544 | tf_op jit(solution)/shard_map/ppermute | solution.py:31
  93.4 23.1 %collective-permute-done.4 = bf16[656,512]{1,0:T(8,128)(2,1)S(1)} collective-permute-done((bf16[656,512]{1,0:T(8,128)(2,1)S(1)}, bf16[656,512]{1,0:T(8,128)(2,1)S(1)}, u32[]{:S(2)}, u32[]{:S(2)}) %collective-permute-start.4) | collective-permute-done | bytes 671776 | tf_op jit(solution)/shard_map/ppermute | solution.py:590
  117.4 2.0 constant_dynamic-update-slice_fusion.33.down_own
  119.4 8.1 %collective-permute-start.6 = (bf16[2688,512]{1,0:T(8,128)(2,1)}, bf16[2688,512]{1,0:T(8,128)(2,1)}, u32[]{:S(2)}, u32[]{:S(2)}) collective-permute-start(bf16[2688,512]{1,0:T(8,128)(2,1)} %constant_dynamic-update-slice_fusion.33.down_own), channel_id=1, source_target_pairs={{0,64},{64,0},{1,65},{65,1},{2,66},{66,2},{3,67},{67,3},{4,68},{68... | collective-permute-start | bytes 8257544 | tf_op jit(solution)/shard_map/ppermute | solution.py:31
  128.5 3.6 collective-permute-done.8
  136.1 4.6 collective-permute-start.9
  140.8 3.4 collective-permute-done.10
  144.2 1.9 pad_maximum_fusion.5
  146.0 6.1 %all-gather.2.cloned.1.call-done.weight_own.gate_own.up_own = bf16[512,18944]{1,0:T(8,128)(2,1)} async-done(((bf16[8,18944]{1,0:T(8,128)(2,1)}), bf16[512,18944]{1,0:T(8,128)(2,1)}) %all-gather.2.cloned.1.call-update) | async-done | bytes 19398672 | tf_op jit(solution)/shard_map/all_gather | solution.py:581
  152.2 3.7 slice.437
  155.9 5.3 %slice.438 = bf16[512,5376]{1,0:T(8,128)(2,1)} slice(bf16[512,18944]{1,0:T(8,128)(2,1)} %all-gather.2.cloned.1.call-done.weight_own.gate_own.up_own), slice={[0:512], [0:5376]} | slice | bytes 11010048 | tf_op jit(solution)/shard_map/slice | solution.py:629
  161.9 2.3 slice.439
  166.1 10.6 %collective-permute-done.11.weight_other = bf16[512,3072]{1,0:T(8,128)(2,1)S(1)} collective-permute-done((bf16[512,3072]{1,0:T(8,128)(2,1)}, bf16[512,3072]{1,0:T(8,128)(2,1)S(1)}, u32[]{:S(2)}, u32[]{:S(2)}) %collective-permute-start.11) | collective-permute-done | bytes 3145760 | tf_op jit(solution)/shard_map/ppermute | solution.py:31
  178.3 1.9 copy-done.3
  180.2 3.5 qkv.2
  183.7 2.9 attend.2
  193.1 8.9 %hidden.2 = (f32[128,2688]{1,0:T(8,128)S(1)}, f32[128,2688]{1,0:T(8,128)S(1)}, bf16[128,2688]{1,0:T(8,128)(2,1)}, f32[128,1024]{1,0:T(8,128)S(1)}) custom-call(s32[1]{0:T(128)} %bitcast.first, bf16[128,512]{1,0:T(8,128)(2,1)S(1)} %get-tuple-element.244.own, bf16[128,512]{1,0:T(8,128)(2,1)S(1)} %get-tuple-element.243.other, ...), custom_call_target="tpu_custom_call" | custom-call | tf_op jit(solution)/shard_map/hidden/pallas_call | solution.py:183
  206.0 4.0 collective-permute-start.14
  212.5 4.7 collective-permute-done.16.weight_other.gate_other.up_other
  217.1 4.0 qkv.3
  221.1 2.9 attend.3
  227.9 7.5 %hidden.3 = (f32[128,2688]{1,0:T(8,128)S(1)}, f32[128,2688]{1,0:T(8,128)S(1)}, bf16[128,2688]{1,0:T(8,128)(2,1)S(1)}, f32[128,1024]{1,0:T(8,128)S(1)}) custom-call(s32[1]{0:T(128)} %bitcast.first, bf16[128,512]{1,0:T(8,128)(2,1)S(1)} %get-tuple-element.224.own, bf16[128,512]{1,0:T(8,128)(2,1)S(1)} %get-tuple-element.223.other, ...), custom_call_target="tpu_custom_call" | custom-call | tf_op jit(solution)/shard_map/hidden/pallas_call | solution.py:183
  235.5 9.4 %hidden_back.2 = (bf16[128,2688]{1,0:T(8,128)(2,1)S(1)}, bf16[128,2688]{1,0:T(8,128)(2,1)S(1)}, f32[128,1024]{1,0:T(8,128)S(1)}) custom-call(s32[1]{0:T(128)} %bitcast.first, bf16[128,512]{1,0:T(8,128)(2,1)S(1)} %get-tuple-element.222.grad_own, bf16[128,512]{1,0:T(8,128)(2,1)S(1)} %get-tuple-element.221.grad_other, ...), custom_call_target="tpu_custom_call" | custom-call | tf_op jit(solution)/shard_map/hidden_back/pallas_call | solution.py:183
  250.8 5.8 %attend_back.2 = (bf16[128,1024]{1,0:T(8,128)(2,1)S(1)}, f32[128,2048]{1,0:T(8,128)S(1)}, bf16[64,2048]{1,0:T(8,128)(2,1)S(1)}, bf16[64,2048]{1,0:T(8,128)(2,1)S(1)}) custom-call(s32[128,1]{1,0:T(8,128)S(1)} %copy.35.query_seg, s32[1,256]{1,0:T(1,128)S(1)} %bitcast.95, bf16[256,3072]{1,0:T(8,128)(2,1)S(1)} %qkv.3, ...), custom_call_target="tpu_custom_call" | custom-call | tf_op jit(solution)/shard_map/attend_back/pallas_call | solution.py:156
  257.9 4.0 collective-permute-start.18
  261.9 4.3 collective-permute-done.19
  270.9 3.9 collective-permute-done.30.product_got
  274.9 7.6 %weight_grads.3 = bf16[1024,6400]{1,0:T(8,128)(2,1)} custom-call(bf16[3,128,1024]{2,1,0:T(8,128)(2,1)S(1)} %pad_maximum_fusion.4.act_mine, bf16[3,128,1024]{2,1,0:T(8,128)(2,1)S(1)} %collective-permute-done.29.act_got, bf16[128,2688]{1,0:T(8,128)(2,1)S(1)} %get-tuple-element.90.product_mine, bf16[128,2688]{1,0:T(8,128)(2,1)S(1)} %collective-permute-done.30.product_got, ...), custom_call_target="tpu_custom_call" | custom-call | tf_op jit(solution)/shard_map/weight_grads/pallas_call | solution.py:183
  283.6 4.9 qkv_back.2
  291.6 10.2 %hidden_back.3 = (bf16[128,2688]{1,0:T(8,128)(2,1)S(1)}, bf16[128,2688]{1,0:T(8,128)(2,1)S(1)}, f32[128,1024]{1,0:T(8,128)S(1)}) custom-call(s32[1]{0:T(128)} %bitcast.first, bf16[128,512]{1,0:T(8,128)(2,1)S(1)} %get-tuple-element.218.grad_own, bf16[128,512]{1,0:T(8,128)(2,1)S(1)} %get-tuple-element.217.grad_other, f32[128,2688]{1,0:T(8,128)S(1)} %copy-done.8, ...), custom_call_target="tpu_custom_call" | custom-call | tf_op jit(solution)/shard_map/hidden_back/pallas_call | solution.py:183
  304.9 1.8 select_convert_fusion
  306.8 5.8 %attend_back.3 = (bf16[128,1024]{1,0:T(8,128)(2,1)S(1)}, f32[128,2048]{1,0:T(8,128)S(1)}, bf16[64,2048]{1,0:T(8,128)(2,1)S(1)}, bf16[64,2048]{1,0:T(8,128)(2,1)S(1)}) custom-call(s32[128,1]{1,0:T(8,128)S(1)} %copy.35.query_seg, s32[1,256]{1,0:T(1,128)S(1)} %bitcast.96, bf16[256,3072]{1,0:T(8,128)(2,1)S(1)} %qkv.2, f32[128,1024]{1,0:T(8,128)S(1)} %copy-done.14, ...), custom_call_target="tpu_custom_call" | custom-call | tf_op jit(solution)/shard_map/attend_back/pallas_call | solution.py:156
  313.9 4.9 collective-permute-start.20
  318.8 10.3 %collective-permute-done.21 = bf16[64,2048]{1,0:T(8,128)(2,1)S(1)} collective-permute-done((bf16[64,2048]{1,0:T(8,128)(2,1)S(1)}, bf16[64,2048]{1,0:T(8,128)(2,1)S(1)}, u32[]{:S(2)}, u32[]{:S(2)}) %collective-permute-start.21) | collective-permute-done | bytes 262176 | tf_op jit(solution)/shard_map/ppermute | solution.py:174
  335.2 4.4 qkv_back.3
  340.2 9.8 %weight_grads.2 = bf16[1024,6400]{1,0:T(8,128)(2,1)} custom-call(bf16[3,128,1024]{2,1,0:T(8,128)(2,1)S(1)} %pad_maximum_fusion.3.act_mine, bf16[3,128,1024]{2,1,0:T(8,128)(2,1)} %collective-permute-done.23.act_got, bf16[128,2688]{1,0:T(8,128)(2,1)} %get-tuple-element.87.product_mine, bf16[128,2688]{1,0:T(8,128)(2,1)} %collective-permute-done.24.product_got, ...), custom_call_target="tpu_custom_call" | custom-call | tf_op jit(solution)/shard_map/weight_grads/pallas_call | solution.py:183
  353.6 31.7 %reduce-scatter.5.cloned.1.call-done = bf16[64,6400]{1,0:T(8,128)(2,1)} async-done(((bf16[1024,6400]{1,0:T(8,128)(2,1)}), bf16[64,6400]{1,0:T(8,128)(2,1)}) %reduce-scatter.5.cloned.1.call-update) | async-done | bytes 819216 | tf_op jit(solution)/shard_map/reduce_scatter | solution.py:416
  386.5 2.8 collective-permute-start.34
  390.3 94.0 %reduce-scatter.3.cloned.1.call-done = bf16[64,6400]{1,0:T(8,128)(2,1)} async-done(((bf16[1024,6400]{1,0:T(8,128)(2,1)}), bf16[64,6400]{1,0:T(8,128)(2,1)}) %reduce-scatter.3.cloned.1.call-update) | async-done | bytes 819216 | tf_op jit(solution)/shard_map/reduce_scatter | solution.py:416
  485.4 2.7 collective-permute-start.28
  490.4 2.1 collective-permute-done.28
  492.6 2.5 collective-permute-done.27
  495.1 6.0 %collective-permute-done.26 = bf16[16,6400]{1,0:T(8,128)(2,1)S(1)} collective-permute-done((bf16[16,6400]{1,0:T(8,128)(2,1)S(1)}, bf16[16,6400]{1,0:T(8,128)(2,1)S(1)}, u32[]{:S(2)}, u32[]{:S(2)}) %collective-permute-start.26) | collective-permute-done | bytes 204832 | tf_op jit(solution)/shard_map/ppermute | solution.py:540
  (286 shorter events, 85.2 us)
Async XLA Ops:
  7.2 145.0 %all-gather.2.cloned.1.call-start = ((), (), s32[]{:S(2)}) async-start(), calls=%async_computation.2 | async-start | bytes 19701760 | tf_op jit(solution)/shard_map/all_gather | solution.py:581
  10.1 2.5 collective-permute-start
  13.4 371.9 %reduce-scatter.5.cloned.1.call-start = ((), (), s32[]{:S(2)}) async-start(), calls=%async_computation.4 | async-start | bytes 13926400 | tf_op jit(solution)/shard_map/reduce_scatter | solution.py:416
  13.5 2.2 collective-permute-start.1
  20.3 43.0 %collective-permute-start.2 = (bf16[656,1024]{1,0:T(8,128)(2,1)}, bf16[656,1024]{1,0:T(8,128)(2,1)}, u32[]{:S(2)}, u32[]{:S(2)}) collective-permute-start(bf16[656,1024]{1,0:T(8,128)(2,1)} %pad_maximum_fusion), channel_id=1, source_target_pairs={{1,0},{2,1},{3,2},{0,3},{5,4},{6,5},{7,6},{4,7},{9,8},{10,9},{11,1... | collective-permute-start | bytes 4030472 | tf_op jit(solution)/shard_map/ppermute | solution.py:588
  24.2 59.9 %collective-permute-start.3 = (bf16[656,1024]{1,0:T(8,128)(2,1)}, bf16[656,1024]{1,0:T(8,128)(2,1)}, u32[]{:S(2)}, u32[]{:S(2)}) collective-permute-start(bf16[656,1024]{1,0:T(8,128)(2,1)} %pad_maximum_fusion), channel_id=1, source_target_pairs={{0,1},{1,2},{2,3},{3,0},{4,5},{5,6},{6,7},{7,4},{8,9},{9,10},{10,1... | collective-permute-start | bytes 4030472 | tf_op jit(solution)/shard_map/ppermute | solution.py:587
  65.9 18.1 %collective-permute-start.5 = (bf16[656,512]{1,0:T(8,128)(2,1)}, bf16[656,512]{1,0:T(8,128)(2,1)S(1)}, u32[]{:S(2)}, u32[]{:S(2)}) collective-permute-start(bf16[656,512]{1,0:T(8,128)(2,1)} %get-tuple-element.159), channel_id=1, source_target_pairs={{1,0},{2,1},{3,2},{0,3},{5,4},{6,5},{7,6},{4,7},{9,8},{10,9},{11,1... | collective-permute-start | bytes 2015240 | tf_op jit(solution)/shard_map/ppermute | solution.py:591
  85.5 42.2 %copy-start = (bf16[2688,512]{1,0:T(8,128)(2,1)}, bf16[2688,512]{1,0:T(8,128)(2,1)S(1)}, u32[]{:S(2)}) copy-start(bf16[2688,512]{1,0:T(8,128)(2,1)S(1)} %get-tuple-element.65.down_own) | copy-start | bytes 8257540
  85.5 42.0 %copy-start.33 = (f32[1,2,1024]{2,1,0:T(2,128)S(1)}, f32[1,2,1024]{2,1,0:T(2,128)}, u32[]{:S(2)}) copy-start(f32[1,2,1024]{2,1,0:T(2,128)} %param.11) | copy-start | bytes 24580
  85.5 42.1 %copy-start.29 = (f32[2,1,128,1024]{3,2,1,0:T(8,128)S(1)}, f32[2,1,128,1024]{3,2,1,0:T(8,128)}, u32[]{:S(2)}) copy-start(f32[2,1,128,1024]{3,2,1,0:T(8,128)} %param.8) | copy-start | bytes 3145732
  85.5 31.0 %collective-permute-start.4 = (bf16[656,512]{1,0:T(8,128)(2,1)S(1)}, bf16[656,512]{1,0:T(8,128)(2,1)S(1)}, u32[]{:S(2)}, u32[]{:S(2)}) collective-permute-start(bf16[656,512]{1,0:T(8,128)(2,1)S(1)} %get-tuple-element.158), channel_id=1, source_target_pairs={{0,1},{1,2},{2,3},{3,0},{4,5},{5,6},{6,7},{7,4},{8,9},{9,10},{10,1... | collective-permute-start | bytes 2015240 | tf_op jit(solution)/shard_map/ppermute | solution.py:590
  85.6 60.4 %collective-permute-start.7 = (bf16[2688,512]{1,0:T(8,128)(2,1)S(1)}, bf16[2688,512]{1,0:T(8,128)(2,1)}, u32[]{:S(2)}, u32[]{:S(2)}) collective-permute-start(bf16[2688,512]{1,0:T(8,128)(2,1)S(1)} %get-tuple-element.65.down_own), channel_id=1, source_target_pairs={{0,64},{64,0},{1,65},{65,1},{2,66},{66,2},{3,67},{67,3},{4,68},{68... | collective-permute-start | bytes 8257544 | tf_op jit(solution)/shard_map/ppermute | solution.py:31
  119.4 8.5 %copy-start.32 = (s32[2,1,2048]{2,1,0:T(1,128)S(1)}, s32[2,1,2048]{2,1,0:T(1,128)}, u32[]{:S(2)}) copy-start(s32[2,1,2048]{2,1,0:T(1,128)} %param.10) | copy-start | bytes 49156
  119.4 26.6 %collective-permute-start.6 = (bf16[2688,512]{1,0:T(8,128)(2,1)}, bf16[2688,512]{1,0:T(8,128)(2,1)}, u32[]{:S(2)}, u32[]{:S(2)}) collective-permute-start(bf16[2688,512]{1,0:T(8,128)(2,1)} %constant_dynamic-update-slice_fusion.33.down_own), channel_id=1, source_target_pairs={{0,64},{64,0},{1,65},{65,1},{2,66},{66,2},{3,67},{67,3},{4,68},{68... | collective-permute-start | bytes 8257544 | tf_op jit(solution)/shard_map/ppermute | solution.py:31
  127.5 4.6 collective-permute-start.8
  127.7 18.3 %copy-start.22 = (f32[1,1,128,1024]{3,2,1,0:T(8,128)}, f32[1,1,128,1024]{3,2,1,0:T(8,128)S(1)}, u32[]{:S(2)}) copy-start(f32[1,1,128,1024]{3,2,1,0:T(8,128)S(1)} %get-tuple-element.140) | copy-start | bytes 1572868
  134.8 9.4 %collective-permute-start.10 = (bf16[64,1024]{1,0:T(8,128)(2,1)}, bf16[64,1024]{1,0:T(8,128)(2,1)}, u32[]{:S(2)}, u32[]{:S(2)}) collective-permute-start(bf16[64,1024]{1,0:T(8,128)(2,1)} %get-tuple-element.262), channel_id=1, source_target_pairs={{4,0},{8,4},{12,8},{16,12},{20,16},{24,20},{28,24},{32,28},{36,32}... | collective-permute-start | bytes 393224 | tf_op jit(solution)/shard_map/ppermute | solution.py:174
  136.1 8.1 %collective-permute-start.9 = (bf16[64,1024]{1,0:T(8,128)(2,1)S(1)}, bf16[64,1024]{1,0:T(8,128)(2,1)}, u32[]{:S(2)}, u32[]{:S(2)}) collective-permute-start(bf16[64,1024]{1,0:T(8,128)(2,1)S(1)} %get-tuple-element.261), channel_id=1, source_target_pairs={{0,4},{4,8},{8,12},{12,16},{16,20},{20,24},{24,28},{28,32},{32,36}... | collective-permute-start | bytes 393224 | tf_op jit(solution)/shard_map/ppermute | solution.py:170
  161.2 22.5 %collective-permute-start.12 = (bf16[512,5376]{1,0:T(8,128)(2,1)}, bf16[512,5376]{1,0:T(8,128)(2,1)}, u32[]{:S(2)}, u32[]{:S(2)}) collective-permute-start(bf16[512,5376]{1,0:T(8,128)(2,1)} %slice.438), channel_id=1, source_target_pairs={{0,64},{64,0},{1,65},{65,1},{2,66},{66,2},{3,67},{67,3},{4,68},{68... | collective-permute-start | bytes 16515080 | tf_op jit(solution)/shard_map/ppermute | solution.py:31
  161.9 14.7 %collective-permute-start.11 = (bf16[512,3072]{1,0:T(8,128)(2,1)}, bf16[512,3072]{1,0:T(8,128)(2,1)S(1)}, u32[]{:S(2)}, u32[]{:S(2)}) collective-permute-start(bf16[512,3072]{1,0:T(8,128)(2,1)} %slice.437), channel_id=1, source_target_pairs={{0,64},{64,0},{1,65},{65,1},{2,66},{66,2},{3,67},{67,3},{4,68},{68... | collective-permute-start | bytes 9437192 | tf_op jit(solution)/shard_map/ppermute | solution.py:31
  164.2 19.5 %collective-permute-start.13 = (bf16[512,1024]{1,0:T(8,128)(2,1)}, bf16[512,1024]{1,0:T(8,128)(2,1)}, u32[]{:S(2)}, u32[]{:S(2)}) collective-permute-start(bf16[512,1024]{1,0:T(8,128)(2,1)} %slice.439), channel_id=1, source_target_pairs={{0,64},{64,0},{1,65},{65,1},{2,66},{66,2},{3,67},{67,3},{4,68},{68... | collective-permute-start | bytes 3145736 | tf_op jit(solution)/shard_map/ppermute | solution.py:31
  187.4 29.7 %collective-permute-start.16 = (bf16[512,18944]{1,0:T(8,128)(2,1)}, bf16[512,18944]{1,0:T(8,128)(2,1)}, u32[]{:S(2)}, u32[]{:S(2)}) collective-permute-start(bf16[512,18944]{1,0:T(8,128)(2,1)} %all-gather.2.cloned.1.call-done.weight_own.gate_own.up_own), channel_id=1, source_target_pairs={{0,64},{64,0},{1,65},{65,1},{2,66},{66,2},{3,67},{67,3},{4,68},{68... | collective-permute-start | bytes 58195976 | tf_op jit(solution)/shard_map/ppermute | solution.py:31
  189.3 20.7 %copy-start.25 = (bf16[128,1024]{1,0:T(8,128)(2,1)}, bf16[128,1024]{1,0:T(8,128)(2,1)S(1)}, u32[]{:S(2)}) copy-start(bf16[128,1024]{1,0:T(8,128)(2,1)S(1)} %bitcast_convert_fusion) | copy-start | bytes 786436
  204.7 6.6 %collective-permute-start.15 = (bf16[64,1024]{1,0:T(8,128)(2,1)S(1)}, bf16[64,1024]{1,0:T(8,128)(2,1)S(1)}, u32[]{:S(2)}, u32[]{:S(2)}) collective-permute-start(bf16[64,1024]{1,0:T(8,128)(2,1)S(1)} %get-tuple-element.242), channel_id=1, source_target_pairs={{4,0},{8,4},{12,8},{16,12},{20,16},{24,20},{28,24},{32,28},{36,32}... | collective-permute-start | bytes 393224 | tf_op jit(solution)/shard_map/ppermute | solution.py:174
  206.0 6.2 %collective-permute-start.14 = (bf16[64,1024]{1,0:T(8,128)(2,1)S(1)}, bf16[64,1024]{1,0:T(8,128)(2,1)S(1)}, u32[]{:S(2)}, u32[]{:S(2)}) collective-permute-start(bf16[64,1024]{1,0:T(8,128)(2,1)S(1)} %get-tuple-element.241), channel_id=1, source_target_pairs={{0,4},{4,8},{8,12},{12,16},{16,20},{20,24},{24,28},{28,32},{32,36}... | collective-permute-start | bytes 393224 | tf_op jit(solution)/shard_map/ppermute | solution.py:170
  235.5 53.3 %copy-start.5 = (f32[128,1024]{1,0:T(8,128)}, f32[128,1024]{1,0:T(8,128)S(1)}, u32[]{:S(2)}) copy-start(f32[128,1024]{1,0:T(8,128)S(1)} %get-tuple-element.67) | copy-start | bytes 1572868
  256.6 9.6 %collective-permute-start.19 = (bf16[64,2048]{1,0:T(8,128)(2,1)S(1)}, bf16[64,2048]{1,0:T(8,128)(2,1)S(1)}, u32[]{:S(2)}, u32[]{:S(2)}) collective-permute-start(bf16[64,2048]{1,0:T(8,128)(2,1)S(1)} %get-tuple-element.75), channel_id=1, source_target_pairs={{4,0},{8,4},{12,8},{16,12},{20,16},{24,20},{28,24},{32,28},{36,32}... | collective-permute-start | bytes 786440 | tf_op jit(solution)/shard_map/ppermute | solution.py:174
  257.9 9.2 %collective-permute-start.18 = (bf16[64,2048]{1,0:T(8,128)(2,1)S(1)}, bf16[64,2048]{1,0:T(8,128)(2,1)S(1)}, u32[]{:S(2)}, u32[]{:S(2)}) collective-permute-start(bf16[64,2048]{1,0:T(8,128)(2,1)S(1)} %get-tuple-element.74), channel_id=1, source_target_pairs={{0,4},{4,8},{8,12},{12,16},{16,20},{20,24},{24,28},{28,32},{32,36}... | collective-permute-start | bytes 786440 | tf_op jit(solution)/shard_map/ppermute | solution.py:170
  268.6 6.2 %collective-permute-start.31 = (bf16[128,5376]{1,0:T(8,128)(2,1)S(1)}, bf16[128,5376]{1,0:T(8,128)(2,1)S(1)}, u32[]{:S(2)}, u32[]{:S(2)}) collective-permute-start(bf16[128,5376]{1,0:T(8,128)(2,1)S(1)} %get-tuple-element.145), channel_id=1, source_target_pairs={{0,64},{64,0},{1,65},{65,1},{2,66},{66,2},{3,67},{67,3},{4,68},{68... | collective-permute-start | bytes 4128776 | tf_op jit(solution)/shard_map/ppermute | solution.py:31
  270.3 4.5 collective-permute-start.29
  270.4 4.4 collective-permute-start.30
  282.4 201.8 %reduce-scatter.3.cloned.1.call-start = ((), (), s32[]{:S(2)}) async-start(), calls=%async_computation.3 | async-start | bytes 13926400 | tf_op jit(solution)/shard_map/reduce_scatter | solution.py:416
  290.5 11.6 %copy-start.17 = (f32[128,1024]{1,0:T(8,128)}, f32[128,1024]{1,0:T(8,128)S(1)}, u32[]{:S(2)}) copy-start(f32[128,1024]{1,0:T(8,128)S(1)} %get-tuple-element.134) | copy-start | bytes 1572868
  312.6 16.5 %collective-permute-start.21 = (bf16[64,2048]{1,0:T(8,128)(2,1)S(1)}, bf16[64,2048]{1,0:T(8,128)(2,1)S(1)}, u32[]{:S(2)}, u32[]{:S(2)}) collective-permute-start(bf16[64,2048]{1,0:T(8,128)(2,1)S(1)} %get-tuple-element.84), channel_id=1, source_target_pairs={{4,0},{8,4},{12,8},{16,12},{20,16},{24,20},{28,24},{32,28},{36,32}... | collective-permute-start | bytes 786440 | tf_op jit(solution)/shard_map/ppermute | solution.py:174
  313.9 16.3 %collective-permute-start.20 = (bf16[64,2048]{1,0:T(8,128)(2,1)S(1)}, bf16[64,2048]{1,0:T(8,128)(2,1)S(1)}, u32[]{:S(2)}, u32[]{:S(2)}) collective-permute-start(bf16[64,2048]{1,0:T(8,128)(2,1)S(1)} %get-tuple-element.83), channel_id=1, source_target_pairs={{0,4},{4,8},{8,12},{12,16},{16,20},{20,24},{24,28},{28,32},{32,36}... | collective-permute-start | bytes 786440 | tf_op jit(solution)/shard_map/ppermute | solution.py:170
  332.0 8.2 %collective-permute-start.25 = (bf16[128,5376]{1,0:T(8,128)(2,1)}, bf16[128,5376]{1,0:T(8,128)(2,1)}, u32[]{:S(2)}, u32[]{:S(2)}) collective-permute-start(bf16[128,5376]{1,0:T(8,128)(2,1)} %get-tuple-element.147), channel_id=1, source_target_pairs={{0,64},{64,0},{1,65},{65,1},{2,66},{66,2},{3,67},{67,3},{4,68},{68... | collective-permute-start | bytes 4128776 | tf_op jit(solution)/shard_map/ppermute | solution.py:31
  334.4 5.8 %collective-permute-start.23 = (bf16[3,128,1024]{2,1,0:T(8,128)(2,1)S(1)}, bf16[3,128,1024]{2,1,0:T(8,128)(2,1)}, u32[]{:S(2)}, u32[]{:S(2)}) collective-permute-start(bf16[3,128,1024]{2,1,0:T(8,128)(2,1)S(1)} %pad_maximum_fusion.3.act_mine), channel_id=1, source_target_pairs={{0,64},{64,0},{1,65},{65,1},{2,66},{66,2},{3,67},{67,3},{4,68},{68... | collective-permute-start | bytes 2359304 | tf_op jit(solution)/shard_map/ppermute | solution.py:31
  334.5 5.7 %collective-permute-start.24 = (bf16[128,2688]{1,0:T(8,128)(2,1)}, bf16[128,2688]{1,0:T(8,128)(2,1)}, u32[]{:S(2)}, u32[]{:S(2)}) collective-permute-start(bf16[128,2688]{1,0:T(8,128)(2,1)} %get-tuple-element.87.product_mine), channel_id=1, source_target_pairs={{0,64},{64,0},{1,65},{65,1},{2,66},{66,2},{3,67},{67,3},{4,68},{68... | collective-permute-start | bytes 2064392 | tf_op jit(solution)/shard_map/ppermute | solution.py:31
  350.1 2.3 collective-permute-start.17
  352.4 135.7 %collective-permute-start.22 = (f32[128,1024]{1,0:T(8,128)}, f32[128,1024]{1,0:T(8,128)S(1)}, u32[]{:S(2)}, u32[]{:S(2)}) collective-permute-start(f32[128,1024]{1,0:T(8,128)} %get-tuple-element.129), channel_id=1, source_target_pairs={{0,64},{64,0},{1,65},{65,1},{2,66},{66,2},{3,67},{67,3},{4,68},{68... | collective-permute-start | bytes 1572872 | tf_op jit(solution)/shard_map/ppermute | solution.py:31
  386.5 102.1 %collective-permute-start.34 = (bf16[16,6400]{1,0:T(8,128)(2,1)S(1)}, bf16[16,6400]{1,0:T(8,128)(2,1)S(1)}, u32[]{:S(2)}, u32[]{:S(2)}) collective-permute-start(bf16[16,6400]{1,0:T(8,128)(2,1)S(1)} %get-tuple-element.165), channel_id=1, source_target_pairs={{0,3},{1,0},{2,1},{3,2},{4,7},{5,4},{6,5},{7,6},{8,11},{9,8},{10,9... | collective-permute-start | bytes 614408 | tf_op jit(solution)/shard_map/ppermute | solution.py:540
  389.3 101.1 %collective-permute-start.33 = (bf16[16,6400]{1,0:T(8,128)(2,1)S(1)}, bf16[16,6400]{1,0:T(8,128)(2,1)S(1)}, u32[]{:S(2)}, u32[]{:S(2)}) collective-permute-start(bf16[16,6400]{1,0:T(8,128)(2,1)S(1)} %get-tuple-element.166), channel_id=1, source_target_pairs={{0,2},{1,3},{2,0},{3,1},{4,6},{5,7},{6,4},{7,5},{8,10},{9,11},{10,... | collective-permute-start | bytes 614408 | tf_op jit(solution)/shard_map/ppermute | solution.py:540
  389.7 100.7 %collective-permute-start.32 = (bf16[16,6400]{1,0:T(8,128)(2,1)S(1)}, bf16[16,6400]{1,0:T(8,128)(2,1)}, u32[]{:S(2)}, u32[]{:S(2)}) collective-permute-start(bf16[16,6400]{1,0:T(8,128)(2,1)S(1)} %get-tuple-element.164), channel_id=1, source_target_pairs={{0,1},{1,2},{2,3},{3,0},{4,5},{5,6},{6,7},{7,4},{8,9},{9,10},{10,1... | collective-permute-start | bytes 614408 | tf_op jit(solution)/shard_map/ppermute | solution.py:540
  485.4 7.2 %collective-permute-start.28 = (bf16[16,6400]{1,0:T(8,128)(2,1)S(1)}, bf16[16,6400]{1,0:T(8,128)(2,1)S(1)}, u32[]{:S(2)}, u32[]{:S(2)}) collective-permute-start(bf16[16,6400]{1,0:T(8,128)(2,1)S(1)} %get-tuple-element.168), channel_id=1, source_target_pairs={{0,3},{1,0},{2,1},{3,2},{4,7},{5,4},{6,5},{7,6},{8,11},{9,8},{10,9... | collective-permute-start | bytes 614408 | tf_op jit(solution)/shard_map/ppermute | solution.py:540
  488.2 6.9 %collective-permute-start.27 = (bf16[16,6400]{1,0:T(8,128)(2,1)S(1)}, bf16[16,6400]{1,0:T(8,128)(2,1)S(1)}, u32[]{:S(2)}, u32[]{:S(2)}) collective-permute-start(bf16[16,6400]{1,0:T(8,128)(2,1)S(1)} %get-tuple-element.169), channel_id=1, source_target_pairs={{0,2},{1,3},{2,0},{3,1},{4,6},{5,7},{6,4},{7,5},{8,10},{9,11},{10,... | collective-permute-start | bytes 614408 | tf_op jit(solution)/shard_map/ppermute | solution.py:540
  488.6 12.4 %collective-permute-start.26 = (bf16[16,6400]{1,0:T(8,128)(2,1)S(1)}, bf16[16,6400]{1,0:T(8,128)(2,1)S(1)}, u32[]{:S(2)}, u32[]{:S(2)}) collective-permute-start(bf16[16,6400]{1,0:T(8,128)(2,1)S(1)} %get-tuple-element.167), channel_id=1, source_target_pairs={{0,1},{1,2},{2,3},{3,0},{4,5},{5,6},{6,7},{7,4},{8,9},{9,10},{10,1... | collective-permute-start | bytes 614408 | tf_op jit(solution)/shard_map/ppermute | solution.py:540
  502.4 1.6 collective-permute-start.36
  504.0 1.7 collective-permute-start.35
  (27 other events, 52.3 us)
Sparse Core Ops, SparseCore 0:
  13.5 138.6 all-gather.1
  282.6 102.6 reduce-scatter.4
  389.1 95.0 reduce-scatter.2

commit v6 on v5

--- a/solution.py
+++ b/solution.py
@@ -15,7 +15,6 @@
 SEQ_DEV = 16
 W_DEV = 4
 PAD_ROWS = 48
-GRAD_PAD = 2816
 HIDDEN_BLOCK = 896
 QKV_BLOCK = 1536
 
@@ -179,7 +178,7 @@
     return cumulative
 
 
-def grid_call(kernel, name, scalars, grid, in_specs, out_specs, out_shape, scratch, args):
+def grid_call(kernel, name, scalars, grid, in_specs, out_specs, out_shape, scratch, args, aliases=None):
     return pl.pallas_call(
         kernel,
         grid_spec=pltpu.PrefetchScalarGridSpec(
@@ -190,6 +189,7 @@
             scratch_shapes=scratch,
         ),
         out_shape=out_shape,
+        input_output_aliases=aliases or {},
         compiler_params=params,
         name=name,
     )(*scalars, *args)
@@ -416,81 +416,101 @@
     return lax.psum_scatter(total, "seq", scatter_dimension=0, tiled=True)
 
 
-GRAD_WIDTHS = (1536, 512, GRAD_PAD)
 ROW_PIECE = FF // (SEQ_DEV * W_DEV)
-
-
-def weight_grad_kernel(
-    act_mine, act_got, product_mine, product_got, grad_mine, grad_got, gains, out,
-    grads, down, groups,
-):
-    count, block = (act_mine.shape[1], act_mine.shape[2])
-    step = pl.program_id(0)
-    end = sum(GRAD_WIDTHS)
-
-    @pl.when(step == 0)
-    def _():
-        grads[:count] = grad_mine[...]
-        grads[count:] = grad_got[...]
-        for at in range(0, FF_PAD, 896):
-            product = jnp.concatenate(
-                [product_mine[:, at : at + 896], product_got[:, at : at + 896]], axis=0
-            )
-            down[at : at + 896] = inner_rows(product, grads[:, end:])
-        width = down.shape[1]
-        for piece in range(SEQ_DEV * W_DEV):
-            for group in range(PAD_ROWS // 16):
-                rows = piece * ROW_PIECE + group * 16
-                groups[16 * piece : 16 * piece + 16, group * width : (group + 1) * width] = down[
-                    rows : rows + 16
-                ].astype(jnp.bfloat16)
-
-    at = 0
-    for member, width in enumerate(GRAD_WIDTHS):
-        acts = jnp.concatenate([act_mine[member], act_got[member]], axis=0)
-        for part in range(at, at + width, 512):
-            size = min(512, at + width - part)
-            out[:, part : part + size] = inner_rows(acts, grads[:, part : part + size]).astype(
-                jnp.bfloat16
-            )
-        at += width
-    out[:, end - gains.shape[1] : end] = gains[...]
-    out[:, end:] = groups[pl.ds(pl.multiple_of(step * block, block), block)]
-
-
-def weight_grads(acts, acts_got, grad_mine, grad_got, gains):
-    members, count, width = acts[0].shape
+ROW_GROUPS = PAD_ROWS // 16
+
+
+def weight_grads(name, items, grads, total, product=None, gains=None, base=None):
+    count, width = items[0][0].shape[1:]
     block = 256
-    half = grad_mine.shape[1] - sum(GRAD_WIDTHS)
-    groups = half * PAD_ROWS // 16
-    act_spec = pl.BlockSpec((members, count, block), lambda n: (0, 0, n))
-    product_spec = whole(acts[1])
+    in_specs, args = ([], [])
+    for acts, got, member, *_ in items:
+        for array in (acts, got):
+            in_specs.append(pl.BlockSpec((1, count, block), lambda n, m=member: (m, 0, n)))
+            args.append(array)
+    for pair in grads:
+        in_specs += [whole(array) for array in pair]
+        args += list(pair)
+    scratch = [pltpu.VMEM((2 * count, pair[0].shape[1]), jnp.bfloat16) for pair in grads]
+    if product is not None:
+        in_specs += [whole(array) for array in product[:2]]
+        args += list(product[:2])
+        half = grads[product[2]][0].shape[1] - product[3]
+        scratch += [
+            pltpu.VMEM((FF_PAD, half), jnp.float32),
+            pltpu.VMEM((width, ROW_GROUPS * half), jnp.bfloat16),
+        ]
+    if gains is not None:
+        in_specs.append(rows_at(block, gains[0].shape[1]))
+        args.append(gains[0])
+    aliases = {}
+    columns = total
+    if base is not None:
+        aliases = {len(args): 0}
+        in_specs.append(pl.BlockSpec(memory_space=pl.ANY))
+        args.append(base)
+        columns = gains[1] + gains[0].shape[1]
+
+    def kernel(*refs):
+        act_refs = refs[: 2 * len(items)]
+        grad_refs = refs[2 * len(items) : 2 * (len(items) + len(grads))]
+        rest = refs[2 * (len(items) + len(grads)) : len(args)]
+        out = refs[len(args)]
+        rows = refs[len(args) + 1 :]
+        step = pl.program_id(0)
+
+        @pl.when(step == 0)
+        def _():
+            for k in range(len(grads)):
+                rows[k][:count] = grad_refs[2 * k][...]
+                rows[k][count:] = grad_refs[2 * k + 1][...]
+            if product is not None:
+                down, groups = rows[-2:]
+                for at in range(0, FF_PAD, 896):
+                    part = jnp.concatenate([r[:, at : at + 896] for r in rest[:2]], axis=0)
+                    down[at : at + 896] = inner_rows(part, rows[product[2]][:, product[3] :])
+                for piece in range(SEQ_DEV * W_DEV):
+                    for group in range(ROW_GROUPS):
+                        first_row = piece * ROW_PIECE + group * 16
+                        groups[
+                            16 * piece : 16 * piece + 16, group * half : (group + 1) * half
+                        ] = down[first_row : first_row + 16].astype(jnp.bfloat16)
+
+        for k, (_, _, _, which, at, size, place) in enumerate(items):
+            acts = jnp.concatenate([act_refs[2 * k][0], act_refs[2 * k + 1][0]], axis=0)
+            for part in range(0, size, 512):
+                wide = min(512, size - part)
+                out[:, place + part : place + part + wide] = inner_rows(
+                    acts, rows[which][:, at + part : at + part + wide]
+                ).astype(jnp.bfloat16)
+        if product is not None:
+            place = product[4]
+            out[:, place : place + ROW_GROUPS * half] = rows[-1][
+                pl.ds(pl.multiple_of(step * block, block), block)
+            ]
+        if gains is not None:
+            out[:, gains[1] : gains[1] + gains[0].shape[1]] = rest[0][...]
+
     return grid_call(
-        weight_grad_kernel,
-        "weight_grads",
+        kernel,
+        name,
         (),
         (width // block,),
-        [
-            act_spec,
-            act_spec,
-            product_spec,
-            product_spec,
-            whole(grad_mine),
-            whole(grad_got),
-            rows_at(block, gains.shape[1]),
-        ],
-        rows_at(block, sum(GRAD_WIDTHS) + groups),
-        jax.ShapeDtypeStruct((width, sum(GRAD_WIDTHS) + groups), jnp.bfloat16),
-        [
-            pltpu.VMEM((2 * count, grad_mine.shape[1]), jnp.bfloat16),
-            pltpu.VMEM((FF_PAD, half), jnp.float32),
-            pltpu.VMEM((width, groups), jnp.bfloat16),
-        ],
-        (acts[0], acts_got[0], acts[1], acts_got[1], grad_mine, grad_got, gains),
-    )
-
-
-def layer_backward(grad_out, kept, gain_pair, weights, segs, on_first, first, earlier_gains):
+        in_specs,
+        rows_at(block, columns),
+        jax.ShapeDtypeStruct((width, total), jnp.bfloat16),
+        scratch,
+        args,
+        aliases,
+    )
+
+
+def core_halves(pairs, on_first):
+    low, high = [jnp.concatenate([p[k] for p in pairs], axis=1) for k in range(2)]
+    return (jnp.where(on_first, low, high), swapped(jnp.where(on_first, high, low)))
+
+
+def layer_backward(grad_out, kept, gain_pair, weights, segs, on_first, first):
     (normed1, factor1, qkv, log_total, normed2, factor2, gate, up, acts, got) = kept
     rows, width = normed1.shape
     half = width // 2
@@ -500,6 +520,7 @@
     grad_gate, grad_up, grad_norm2 = hidden_back(
         first, branch_own, branch_other, gate, up, weights
     )
+    hidden_pair = core_halves(((grad_gate, grad_up), (low, high)), on_first)
     gain_mid = jnp.sum(normed2 * grad_norm2, axis=0)
     grad_middle = grad_out + norm_back(grad_norm2 * gain_pair[1], normed2, factor2)
     grad_attn = grad_middle.astype(jnp.bfloat16)
@@ -510,26 +531,18 @@
     from_next = to_previous(grad_before).astype(jnp.float32)
     grad_pairs = grad_own + jnp.concatenate([from_previous, from_next], axis=0)
     grad_qkv = jnp.concatenate([grad_query, grad_pairs.astype(jnp.bfloat16)], axis=1)
-    halves = (
-        (grad_qkv[:, : 3 * half], grad_qkv[:, 3 * half :]),
-        (grad_attn[:, :half], grad_attn[:, half:]),
-        (grad_gate, grad_up),
-        (jnp.zeros((rows, GRAD_PAD - FF_PAD), jnp.bfloat16),) * 2,
-        (low, high),
-    )
-    first_half, second_half = [jnp.concatenate([h[k] for h in halves], axis=1) for k in range(2)]
-    grad_mine = jnp.where(on_first, first_half, second_half)
-    grad_got = swapped(jnp.where(on_first, second_half, first_half))
+    attn_pair = core_halves(
+        (
+            (grad_qkv[:, : 3 * half], grad_qkv[:, 3 * half :]),
+            (grad_attn[:, :half], grad_attn[:, half:]),
+        ),
+        on_first,
+    )
     grad_norm1 = qkv_back(first, grad_qkv, weights)
     gain_first = jnp.sum(normed1 * grad_norm1, axis=0)
     grad_inputs = grad_middle + norm_back(grad_norm1 * gain_pair[0], normed1, factor1)
     gains = jnp.stack([gain_first, gain_mid])
-    gains = jnp.concatenate([gains, earlier_gains], axis=0)
-    columns = jnp.pad(gains, ((0, 128 - gains.shape[0]), (0, 0))).T.astype(jnp.bfloat16)
-    if earlier_gains.shape[0] == 0:
-        columns = jnp.zeros(columns.shape, columns.dtype)
-    sums = seq_sum(weight_grads(acts, got, grad_mine, grad_got, columns))
-    return (grad_inputs, sums, gains)
+    return (grad_inputs, hidden_pair, attn_pair, gains)
 
 
 def summed_over_w(block, place):
@@ -621,10 +634,9 @@
     all_own, down_own, down_other, entry, gain_pairs, segs = lax.optimization_barrier(
         (all_own, down_own, tuple(swapped(d) for d in down_own), entry, gain_pairs, segs)
     )
-    qkv_piece, all_own = lax.optimization_barrier(
-        (all_own[:, qkv_at : qkv_at + qkv_width], all_own)
-    )
-    first_qkv = swapped(qkv_piece)
+    first_qkv, all_own = lax.optimization_barrier(
+        (swapped(all_own[:, qkv_at : qkv_at + qkv_width]), all_own)
+    )
     first_out = swapped(all_own[:, out_at : out_at + width])
     first_hidden = swapped(all_own[:, :hidden_width])
     first_weights = {
@@ -656,12 +668,54 @@
         middle, entry, gain_pairs[1], weights[1], segs, on_first, first
     )
     upstream = by_core(cotangent[0, 0], cotangent[1, 0])
-    no_gains = jnp.zeros((0, width), jnp.float32)
-    grads1, sums1, gains1 = layer_backward(
-        upstream, kept1, gain_pairs[1], weights[1], segs, on_first, first, no_gains
-    )
-    grads0, sums0, _ = layer_backward(
-        grads1, kept0, gain_pairs[0], weights[0], segs, on_first, first, gains1
+    attn_cols, out_cols, down_cols = (qkv_width // 2, half, ROW_GROUPS * half)
+    hidden_end = FF_PAD + down_cols
+    second_at = attn_cols + out_cols + 128
+    hidden_at = second_at + attn_cols + out_cols
+    total = hidden_at + hidden_end
+
+    def attn_items(kept, which, at):
+        acts, got = (kept[-2][0], kept[-1][0])
+        return [
+            (acts, got, 0, which, 0, attn_cols, at),
+            (acts, got, 1, which, attn_cols, out_cols, at + attn_cols),
+        ]
+
+    def hidden_items(kept, which, at):
+        acts, got = (kept[-2], kept[-1])
+        return (
+            [(acts[0], got[0], 2, which, 0, FF_PAD, at)],
+            (acts[1], got[1], which, FF_PAD, at + FF_PAD),
+        )
+
+    grads1, hidden_pair1, attn_pair1, gains1 = layer_backward(
+        upstream, kept1, gain_pairs[1], weights[1], segs, on_first, first
+    )
+    items, product = hidden_items(kept1, 0, 0)
+    early = seq_sum(weight_grads("hidden_grads", items, [hidden_pair1], hidden_end, product))
+    grads0, hidden_pair0, attn_pair0, gains0 = layer_backward(
+        grads1, kept0, gain_pairs[0], weights[0], segs, on_first, first
+    )
+    items, product = hidden_items(kept0, 1, hidden_at)
+    base = weight_grads(
+        "joint_grads",
+        attn_items(kept1, 0, second_at) + items,
+        [attn_pair1, hidden_pair0],
+        total,
+        product,
+    )
+    gains = jnp.concatenate([gains0, gains1], axis=0)
+    gains = jnp.pad(gains, ((0, 128 - gains.shape[0]), (0, 0))).T.astype(jnp.bfloat16)
+    late = seq_sum(
+        weight_grads(
+            "attn_grads",
+            attn_items(kept0, 0, 0),
+            [attn_pair0],
+            total,
+            None,
+            (gains, attn_cols + out_cols),
+            base,
+        )
     )
 
     def placed(first, second):
@@ -672,28 +726,28 @@
     section_outputs = placed(middle, final)
     section_input_grads = placed(grads0, grads1)
 
-    totals = [summed_over_w(sums, w_place) for sums in (sums0, sums1)]
-    mine, got = (by_core(*totals), swapped(by_core(totals[1], totals[0])))
+    early_total, late_total = (summed_over_w(early, w_place), summed_over_w(late, w_place))
+    gain_at = attn_cols + out_cols
+    of_first = jnp.concatenate([late_total[:, :second_at], late_total[:, hidden_at:]], axis=1)
+    of_second = jnp.concatenate(
+        [late_total[:, second_at:hidden_at], late_total[:, gain_at:second_at], early_total], axis=1
+    )
+    mine, got = (by_core(of_first, of_second), swapped(by_core(of_second, of_first)))
     low, high = (by_core(mine, got), by_core(got, mine))
-    attn_end, hidden_at = (3 * width // 2, 2 * width)
-    down_at = hidden_at + GRAD_PAD
-    qkv_rows = jnp.concatenate([low[:, :attn_end], high[:, :attn_end]], axis=1)
-    attn_rows = jnp.concatenate([low[:, attn_end:hidden_at], high[:, attn_end:hidden_at]], axis=1)
+    qkv_rows = jnp.concatenate([low[:, :attn_cols], high[:, :attn_cols]], axis=1)
+    attn_rows = jnp.concatenate([low[:, attn_cols:gain_at], high[:, attn_cols:gain_at]], axis=1)
+    gain_part = (low + high)[:, gain_at:second_at]
+    gain_rows = by_core(gain_part[:, :2], gain_part[:, 2:4]).T
     hidden_rows = jnp.concatenate(
-        [low[:, hidden_at : hidden_at + FF], high[:, hidden_at : hidden_at + FF]], axis=1
-    )
-    gain_part = totals[0][:, down_at - 128 : down_at]
-    gain_part = gain_part + swapped(gain_part)
-    gain_rows = by_core(gain_part[:, :2], gain_part[:, 2:4]).T
+        [low[:, second_at : second_at + FF], high[:, second_at : second_at + FF]], axis=1
+    )
     down_total = jnp.concatenate(
         [
-            jnp.concatenate(
-                [h[:, at : at + width // 2] for h in (low, high)], axis=1
-            )
-            for at in range(down_at, low.shape[1], width // 2)
+            jnp.concatenate([h[:, at : at + half] for h in (low, high)], axis=1)
+            for at in range(second_at + FF_PAD, low.shape[1], half)
         ],
         axis=0,
-    )[: FF // (SEQ_DEV * W_DEV)]
+    )[:ROW_PIECE]
     return (
         section_outputs,
         section_input_grads,

time: 525 us -> 508 us (0.968)
  waiting for transfers between devices: 268 us -> 238 us
  starting transfers between devices: 61.6 us -> 68.7 us
    reduce_scatter x2, waiting for transfers between devices: 126 us -> 109 us  [seq_sum(): return lax.psum_scatter(total, 'seq', scatter_dimension=0, tiled=True)]
    ppermute x19 -> x20, starting transfers between devices: 23.9 us -> 33.6 us  [swapped(): return lax.ppermute(array, 'section', SWAP)]
    ppermute x4, waiting for transfers between devices: 19.3 us -> 11.2 us  [to_previous(): return lax.ppermute(array, 'seq', [(i + 1, i) for i in range(SEQ_DEV - 1)])]
    ppermute x19 -> x20, waiting for transfers between devices: 26.4 us -> 23 us  [swapped(): return lax.ppermute(array, 'section', SWAP)]
    unnamed x100 -> x116, local copies, waits for them, and re-layouts: 13.8 us -> 15.7 us
    pallas_call x10 -> x11, Pallas kernels: 70.1 us -> 71.3 us  [grid_call(): pl.pallas_call(kernel, grid_spec=pltpu.PrefetchScalarGridSpec(num_scalar_...]
  transfers between devices with their start and end apart: 40 -> 41, of which waited for: 23 -> 22; matrix products, arithmetic and copies ran while one was open for 9% -> 11% of each run, Pallas kernels for 9% -> 12%
where the time goes in v6:
time: 508 us; the launch traced here: 499 us
  waiting for transfers between devices  238 us (47%)
  Pallas kernels  88.7 us (17%)
  starting transfers between devices  68.7 us (14%)
  local copies, waits for them, and re-layouts  45.6 us (9%)
  other arithmetic  29.3 us (6%)
  between operations  15.6 us (3%)
  matrix products  13.5 us (3%)
    reduce_scatter x2, waiting for transfers between devices, seq_sum(): return lax.psum_scatter(total, 'seq', scatter_dimension=0, tiled=True)  109 us
    pallas_call x11, Pallas kernels, grid_call(): pl.pallas_call(kernel, grid_spec=pltpu.PrefetchScalarGridSpec(num_scalar_...  71.3 us
    ppermute x1, waiting for transfers between devices, per_device(): above = lax.ppermute(down_piece, 'wshard', w_down)  40.6 us
    ppermute x20, starting transfers between devices, swapped(): return lax.ppermute(array, 'section', SWAP)  33.6 us
    ppermute x20, waiting for transfers between devices, swapped(): return lax.ppermute(array, 'section', SWAP)  23 us
    ppermute x1, waiting for transfers between devices, per_device(): lax.ppermute(below[:, :half], 'wshard', w_up)  19.6 us
    ppermute x4, starting transfers between devices, to_next(): return lax.ppermute(array, 'seq', [(i, i + 1) for i in range(SEQ_DEV - 1)])  17.2 us
    unnamed x116, local copies, waits for them, and re-layouts  15.7 us
  transfers between devices with their start and end apart: 41, of which 22 were waited for; matrix products, arithmetic and copies ran while one was open for 11% of the time, Pallas kernels for 12%

profile of v6, /device:TPU:1, one launch (start us, length us, event | category | flops | bytes accessed | tf_op | source)
XLA Modules:
  0.0 499.2 jit_solution(12031966789514072352)
XLA Ops:
  21.8 3.8 collective-permute-start.2
  25.5 40.6 %collective-permute-done.2 = bf16[656,1024]{1,0:T(8,128)(2,1)} collective-permute-done((bf16[656,1024]{1,0:T(8,128)(2,1)}, bf16[656,1024]{1,0:T(8,128)(2,1)}, u32[]{:S(2)}, u32[]{:S(2)}) %collective-permute-start.2) | collective-permute-done | bytes 1343520 | tf_op jit(solution)/shard_map/ppermute | solution.py:601
  66.1 2.6 fusion.40
  68.7 3.4 collective-permute-start.5
  72.1 13.7 %collective-permute-done.5 = bf16[656,512]{1,0:T(8,128)(2,1)S(1)} collective-permute-done((bf16[656,512]{1,0:T(8,128)(2,1)}, bf16[656,512]{1,0:T(8,128)(2,1)S(1)}, u32[]{:S(2)}, u32[]{:S(2)}) %collective-permute-start.5) | collective-permute-done | bytes 671776 | tf_op jit(solution)/shard_map/ppermute | solution.py:604
  87.5 10.5 %collective-permute-start.7 = (bf16[2688,512]{1,0:T(8,128)(2,1)S(1)}, bf16[2688,512]{1,0:T(8,128)(2,1)}, u32[]{:S(2)}, u32[]{:S(2)}) collective-permute-start(bf16[2688,512]{1,0:T(8,128)(2,1)S(1)} %get-tuple-element.65.down_own), channel_id=1, source_target_pairs={{0,64},{64,0},{1,65},{65,1},{2,66},{66,2},{3,67},{67,3},{4,68},{68... | collective-permute-start | bytes 8257544 | tf_op jit(solution)/shard_map/ppermute | solution.py:30
  97.9 19.6 %collective-permute-done.4 = bf16[656,512]{1,0:T(8,128)(2,1)S(1)} collective-permute-done((bf16[656,512]{1,0:T(8,128)(2,1)S(1)}, bf16[656,512]{1,0:T(8,128)(2,1)S(1)}, u32[]{:S(2)}, u32[]{:S(2)}) %collective-permute-start.4) | collective-permute-done | bytes 671776 | tf_op jit(solution)/shard_map/ppermute | solution.py:603
  118.4 2.0 constant_dynamic-update-slice_fusion.21.down_own
  120.4 10.7 %collective-permute-start.6 = (bf16[2688,512]{1,0:T(8,128)(2,1)}, bf16[2688,512]{1,0:T(8,128)(2,1)}, u32[]{:S(2)}, u32[]{:S(2)}) collective-permute-start(bf16[2688,512]{1,0:T(8,128)(2,1)} %constant_dynamic-update-slice_fusion.21.down_own), channel_id=1, source_target_pairs={{0,64},{64,0},{1,65},{65,1},{2,66},{66,2},{3,67},{67,3},{4,68},{68... | collective-permute-start | bytes 8257544 | tf_op jit(solution)/shard_map/ppermute | solution.py:30
  132.0 3.7 collective-permute-done.8
  139.4 4.6 collective-permute-start.9
  145.8 1.9 pad_maximum_fusion.9
  147.6 4.8 all-gather.2.cloned.1.call-done.weight_own.gate_own.up_own
  152.4 2.1 slice.449
  155.3 5.3 %collective-permute-done.11.weight_other = bf16[512,3072]{1,0:T(8,128)(2,1)S(1)} collective-permute-done((bf16[512,3072]{1,0:T(8,128)(2,1)S(1)}, bf16[512,3072]{1,0:T(8,128)(2,1)S(1)}, u32[]{:S(2)}, u32[]{:S(2)}) %collective-permute-start.11) | collective-permute-done | bytes 3145760 | tf_op jit(solution)/shard_map/ppermute | solution.py:30
  160.6 6.5 %slice.450 = bf16[512,5376]{1,0:T(8,128)(2,1)} slice(bf16[512,18944]{1,0:T(8,128)(2,1)} %all-gather.2.cloned.1.call-done.weight_own.gate_own.up_own), slice={[0:512], [0:5376]} | slice | bytes 11010048 | tf_op jit(solution)/shard_map/slice | solution.py:641
  167.4 2.3 slice.451
  171.2 3.5 qkv.2
  174.8 3.2 collective-permute-done.13.refs_1_
  177.9 2.9 attend.2
  187.1 8.8 %hidden.2 = (f32[128,2688]{1,0:T(8,128)S(1)}, f32[128,2688]{1,0:T(8,128)S(1)}, bf16[128,2688]{1,0:T(8,128)(2,1)}, f32[128,1024]{1,0:T(8,128)S(1)}) custom-call(s32[1]{0:T(128)} %bitcast.first, bf16[128,512]{1,0:T(8,128)(2,1)S(1)} %get-tuple-element.246.own, bf16[128,512]{1,0:T(8,128)(2,1)S(1)} %get-tuple-element.245.other, ...), custom_call_target="tpu_custom_call" | custom-call | tf_op jit(solution)/shard_map/hidden/pallas_call | solution.py:182
  200.0 4.0 collective-permute-start.14
  206.7 4.7 collective-permute-done.16.weight_other.gate_other.up_other
  211.4 4.0 qkv.3
  215.3 2.9 attend.3
  220.6 1.8 fusion.60
  223.1 7.5 %hidden.3 = (f32[128,2688]{1,0:T(8,128)S(1)}, f32[128,2688]{1,0:T(8,128)S(1)}, bf16[128,2688]{1,0:T(8,128)(2,1)S(1)}, f32[128,1024]{1,0:T(8,128)S(1)}) custom-call(s32[1]{0:T(128)} %bitcast.first, bf16[128,512]{1,0:T(8,128)(2,1)S(1)} %get-tuple-element.226.own, bf16[128,512]{1,0:T(8,128)(2,1)S(1)} %get-tuple-element.225.other, ...), custom_call_target="tpu_custom_call" | custom-call | tf_op jit(solution)/shard_map/hidden/pallas_call | solution.py:182
  231.4 9.1 %hidden_back.2 = (bf16[128,2688]{1,0:T(8,128)(2,1)S(1)}, bf16[128,2688]{1,0:T(8,128)(2,1)S(1)}, f32[128,1024]{1,0:T(8,128)S(1)}) custom-call(s32[1]{0:T(128)} %bitcast.first, bf16[128,512]{1,0:T(8,128)(2,1)S(1)} %copy-done.22, bf16[128,512]{1,0:T(8,128)(2,1)S(1)} %copy-done.23, f32[128,2688]{1,0:T(8,128)S(1)} %get-tuple-element.68.gate_in, ...), custom_call_target="tpu_custom_call" | custom-call | tf_op jit(solution)/shard_map/hidden_back/pallas_call | solution.py:182
  242.1 3.2 collective-permute-done.33.refs_5_
  245.4 3.7 hidden_grads.1
  249.1 3.4 copy-done
  261.1 5.8 %attend_back.2 = (bf16[128,1024]{1,0:T(8,128)(2,1)S(1)}, f32[128,2048]{1,0:T(8,128)S(1)}, bf16[64,2048]{1,0:T(8,128)(2,1)S(1)}, bf16[64,2048]{1,0:T(8,128)(2,1)S(1)}) custom-call(s32[128,1]{1,0:T(8,128)S(1)} %copy.36.query_seg, s32[1,256]{1,0:T(1,128)S(1)} %bitcast.95, bf16[256,3072]{1,0:T(8,128)(2,1)S(1)} %qkv.3, f32[128,1024]{1,0:T(8,128)S(1)} %copy-done.27, ...), custom_call_target="tpu_custom_call" | custom-call | tf_op jit(solution)/shard_map/attend_back/pallas_call | solution.py:155
  268.2 4.0 collective-permute-start.18
  273.7 8.6 %collective-permute-done.19 = bf16[64,2048]{1,0:T(8,128)(2,1)S(1)} collective-permute-done((bf16[64,2048]{1,0:T(8,128)(2,1)S(1)}, bf16[64,2048]{1,0:T(8,128)(2,1)S(1)}, u32[]{:S(2)}, u32[]{:S(2)}) %collective-permute-start.19) | collective-permute-done | bytes 262176 | tf_op jit(solution)/shard_map/ppermute | solution.py:173
  283.4 4.7 qkv_back.2
  290.2 10.0 %hidden_back.3 = (bf16[128,2688]{1,0:T(8,128)(2,1)S(1)}, bf16[128,2688]{1,0:T(8,128)(2,1)S(1)}, f32[128,1024]{1,0:T(8,128)S(1)}) custom-call(s32[1]{0:T(128)} %bitcast.first, bf16[128,512]{1,0:T(8,128)(2,1)S(1)} %get-tuple-element.214.grad_own, bf16[128,512]{1,0:T(8,128)(2,1)S(1)} %get-tuple-element.215.grad_other, f32[128,2688]{1,0:T(8,128)S(1)} %copy-done.19, ...), custom_call_target="tpu_custom_call" | custom-call | tf_op jit(solution)/shard_map/hidden_back/pallas_call | solution.py:182
  301.6 1.8 fusion.31
  305.3 5.8 %attend_back.3 = (bf16[128,1024]{1,0:T(8,128)(2,1)S(1)}, f32[128,2048]{1,0:T(8,128)S(1)}, bf16[64,2048]{1,0:T(8,128)(2,1)S(1)}, bf16[64,2048]{1,0:T(8,128)(2,1)S(1)}) custom-call(s32[128,1]{1,0:T(8,128)S(1)} %copy.36.query_seg, s32[1,256]{1,0:T(1,128)S(1)} %bitcast.96, bf16[256,3072]{1,0:T(8,128)(2,1)S(1)} %copy-done.4, f32[128,1024]{1,0:T(8,128)S(1)} %copy-done.25, ...), custom_call_target="tpu_custom_call" | custom-call | tf_op jit(solution)/shard_map/attend_back/pallas_call | solution.py:155
  312.4 4.5 collective-permute-start.20
  318.2 1.9 collective-permute-start.26
  325.2 4.3 qkv_back.3
  333.9 10.4 %joint_grads.1.refs_7_ = bf16[1024,8448]{1,0:T(8,128)(2,1)} custom-call(bf16[3,128,1024]{2,1,0:T(8,128)(2,1)S(1)} %copy-done.6, bf16[3,128,1024]{2,1,0:T(8,128)(2,1)S(1)} %copy-done.10, bf16[3,128,1024]{2,1,0:T(8,128)(2,1)S(1)} %copy-done.6, bf16[3,128,1024]{2,1,0:T(8,128)(2,1)S(1)} %copy-done.10, ...), custom_call_target="tpu_custom_call" | custom-call | tf_op jit(solution)/shard_map/joint_grads/pallas_call | solution.py:182
  344.3 5.1 %attn_grads.1 = bf16[1024,8448]{1,0:T(8,128)(2,1)} custom-call(bf16[3,128,1024]{2,1,0:T(8,128)(2,1)S(1)} %pad_maximum_fusion.7.refs_4_.refs_0_.refs_2_, bf16[3,128,1024]{2,1,0:T(8,128)(2,1)} %collective-permute-done.23.refs_5_.refs_1_.refs_3_, bf16[3,128,1024]{2,1,0:T(8,128)(2,1)S(1)} %pad_maximum_fusion.7.refs_4_.refs_0_.refs_2_, ...), custom_call_target="tpu_custom_call", output_to_operand_aliasing={{}: (7, {})} | custom-call | tf_op jit(solution)/shard_map/attn_grads/pallas_call | solution.py:182
  356.5 109.1 %reduce-scatter.3.cloned.1.call-done = bf16[64,8448]{1,0:T(8,128)(2,1)} async-done(((bf16[1024,8448]{1,0:T(8,128)(2,1)}), bf16[64,8448]{1,0:T(8,128)(2,1)}) %reduce-scatter.3.cloned.1.call-update) | async-done | bytes 1081360 | tf_op jit(solution)/shard_map/reduce_scatter | solution.py:416
  466.7 2.7 collective-permute-start.31
  471.6 3.5 collective-permute-done.31
  475.0 2.6 collective-permute-done.30
  477.6 7.6 %collective-permute-done.29 = bf16[16,8448]{1,0:T(8,128)(2,1)S(1)} collective-permute-done((bf16[16,8448]{1,0:T(8,128)(2,1)S(1)}, bf16[16,8448]{1,0:T(8,128)(2,1)S(1)}, u32[]{:S(2)}, u32[]{:S(2)}) %collective-permute-start.29) | collective-permute-done | bytes 270368 | tf_op jit(solution)/shard_map/ppermute | solution.py:553
  (310 shorter events, 90.6 us)
Async XLA Ops:
  7.2 145.3 %all-gather.2.cloned.1.call-start = ((), (), s32[]{:S(2)}) async-start(), calls=%async_computation.2 | async-start | bytes 19701760 | tf_op jit(solution)/shard_map/all_gather | solution.py:594
  10.1 2.5 collective-permute-start
  13.4 340.5 %reduce-scatter.5.cloned.1.call-start = ((), (), s32[]{:S(2)}) async-start(), calls=%async_computation.4 | async-start | bytes 9191424 | tf_op jit(solution)/shard_map/reduce_scatter | solution.py:416
  13.5 2.2 collective-permute-start.1
  21.8 44.4 %collective-permute-start.2 = (bf16[656,1024]{1,0:T(8,128)(2,1)}, bf16[656,1024]{1,0:T(8,128)(2,1)}, u32[]{:S(2)}, u32[]{:S(2)}) collective-permute-start(bf16[656,1024]{1,0:T(8,128)(2,1)} %pad_maximum_fusion), channel_id=1, source_target_pairs={{1,0},{2,1},{3,2},{0,3},{5,4},{6,5},{7,6},{4,7},{9,8},{10,9},{11,1... | collective-permute-start | bytes 4030472 | tf_op jit(solution)/shard_map/ppermute | solution.py:601
  25.5 60.4 %collective-permute-start.3 = (bf16[656,1024]{1,0:T(8,128)(2,1)}, bf16[656,1024]{1,0:T(8,128)(2,1)}, u32[]{:S(2)}, u32[]{:S(2)}) collective-permute-start(bf16[656,1024]{1,0:T(8,128)(2,1)} %pad_maximum_fusion), channel_id=1, source_target_pairs={{0,1},{1,2},{2,3},{3,0},{4,5},{5,6},{6,7},{7,4},{8,9},{9,10},{10,1... | collective-permute-start | bytes 4030472 | tf_op jit(solution)/shard_map/ppermute | solution.py:600
  68.7 17.1 %collective-permute-start.5 = (bf16[656,512]{1,0:T(8,128)(2,1)}, bf16[656,512]{1,0:T(8,128)(2,1)S(1)}, u32[]{:S(2)}, u32[]{:S(2)}) collective-permute-start(bf16[656,512]{1,0:T(8,128)(2,1)} %get-tuple-element.159), channel_id=1, source_target_pairs={{1,0},{2,1},{3,2},{0,3},{5,4},{6,5},{7,6},{4,7},{9,8},{10,9},{11,1... | collective-permute-start | bytes 2015240 | tf_op jit(solution)/shard_map/ppermute | solution.py:604
  85.9 45.2 %copy-start.46 = (f32[1,2,1024]{2,1,0:T(2,128)S(1)}, f32[1,2,1024]{2,1,0:T(2,128)}, u32[]{:S(2)}) copy-start(f32[1,2,1024]{2,1,0:T(2,128)} %param.11) | copy-start | bytes 24580
  85.9 45.2 %copy-start.41 = (f32[2,1,128,1024]{3,2,1,0:T(8,128)S(1)}, f32[2,1,128,1024]{3,2,1,0:T(8,128)}, u32[]{:S(2)}) copy-start(f32[2,1,128,1024]{3,2,1,0:T(8,128)} %param.8) | copy-start | bytes 3145732
  87.4 49.3 %copy-start.1 = (bf16[2688,512]{1,0:T(8,128)(2,1)}, bf16[2688,512]{1,0:T(8,128)(2,1)S(1)}, u32[]{:S(2)}) copy-start(bf16[2688,512]{1,0:T(8,128)(2,1)S(1)} %get-tuple-element.65.down_own) | copy-start | bytes 8257540
  87.4 44.1 %copy-start.45 = (s32[2,1,2048]{2,1,0:T(1,128)S(1)}, s32[2,1,2048]{2,1,0:T(1,128)}, u32[]{:S(2)}) copy-start(s32[2,1,2048]{2,1,0:T(1,128)} %param.10) | copy-start | bytes 49156
  87.4 30.1 %collective-permute-start.4 = (bf16[656,512]{1,0:T(8,128)(2,1)S(1)}, bf16[656,512]{1,0:T(8,128)(2,1)S(1)}, u32[]{:S(2)}, u32[]{:S(2)}) collective-permute-start(bf16[656,512]{1,0:T(8,128)(2,1)S(1)} %get-tuple-element.158), channel_id=1, source_target_pairs={{0,1},{1,2},{2,3},{3,0},{4,5},{5,6},{6,7},{7,4},{8,9},{9,10},{10,1... | collective-permute-start | bytes 2015240 | tf_op jit(solution)/shard_map/ppermute | solution.py:603
  87.5 60.1 %collective-permute-start.7 = (bf16[2688,512]{1,0:T(8,128)(2,1)S(1)}, bf16[2688,512]{1,0:T(8,128)(2,1)}, u32[]{:S(2)}, u32[]{:S(2)}) collective-permute-start(bf16[2688,512]{1,0:T(8,128)(2,1)S(1)} %get-tuple-element.65.down_own), channel_id=1, source_target_pairs={{0,64},{64,0},{1,65},{65,1},{2,66},{66,2},{3,67},{67,3},{4,68},{68... | collective-permute-start | bytes 8257544 | tf_op jit(solution)/shard_map/ppermute | solution.py:30
  120.4 27.3 %collective-permute-start.6 = (bf16[2688,512]{1,0:T(8,128)(2,1)}, bf16[2688,512]{1,0:T(8,128)(2,1)}, u32[]{:S(2)}, u32[]{:S(2)}) collective-permute-start(bf16[2688,512]{1,0:T(8,128)(2,1)} %constant_dynamic-update-slice_fusion.21.down_own), channel_id=1, source_target_pairs={{0,64},{64,0},{1,65},{65,1},{2,66},{66,2},{3,67},{67,3},{4,68},{68... | collective-permute-start | bytes 8257544 | tf_op jit(solution)/shard_map/ppermute | solution.py:30
  131.1 4.6 collective-permute-start.8
  131.2 21.2 %copy-start.34 = (f32[1,1,128,1024]{3,2,1,0:T(8,128)}, f32[1,1,128,1024]{3,2,1,0:T(8,128)S(1)}, u32[]{:S(2)}) copy-start(f32[1,1,128,1024]{3,2,1,0:T(8,128)S(1)} %get-tuple-element.140) | copy-start | bytes 1572868
  138.1 7.2 %collective-permute-start.10 = (bf16[64,1024]{1,0:T(8,128)(2,1)}, bf16[64,1024]{1,0:T(8,128)(2,1)}, u32[]{:S(2)}, u32[]{:S(2)}) collective-permute-start(bf16[64,1024]{1,0:T(8,128)(2,1)} %get-tuple-element.264), channel_id=1, source_target_pairs={{4,0},{8,4},{12,8},{16,12},{20,16},{24,20},{28,24},{32,28},{36,32}... | collective-permute-start | bytes 393224 | tf_op jit(solution)/shard_map/ppermute | solution.py:173
  139.4 6.4 %collective-permute-start.9 = (bf16[64,1024]{1,0:T(8,128)(2,1)S(1)}, bf16[64,1024]{1,0:T(8,128)(2,1)}, u32[]{:S(2)}, u32[]{:S(2)}) collective-permute-start(bf16[64,1024]{1,0:T(8,128)(2,1)S(1)} %get-tuple-element.263), channel_id=1, source_target_pairs={{0,4},{4,8},{8,12},{12,16},{16,20},{20,24},{24,28},{28,32},{32,36}... | collective-permute-start | bytes 393224 | tf_op jit(solution)/shard_map/ppermute | solution.py:169
  154.5 6.0 %collective-permute-start.11 = (bf16[512,3072]{1,0:T(8,128)(2,1)S(1)}, bf16[512,3072]{1,0:T(8,128)(2,1)S(1)}, u32[]{:S(2)}, u32[]{:S(2)}) collective-permute-start(bf16[512,3072]{1,0:T(8,128)(2,1)S(1)} %slice.449), channel_id=1, source_target_pairs={{0,64},{64,0},{1,65},{65,1},{2,66},{66,2},{3,67},{67,3},{4,68},{68... | collective-permute-start | bytes 9437192 | tf_op jit(solution)/shard_map/ppermute | solution.py:30
  167.1 10.9 %collective-permute-start.12 = (bf16[512,5376]{1,0:T(8,128)(2,1)}, bf16[512,5376]{1,0:T(8,128)(2,1)}, u32[]{:S(2)}, u32[]{:S(2)}) collective-permute-start(bf16[512,5376]{1,0:T(8,128)(2,1)} %slice.450), channel_id=1, source_target_pairs={{0,64},{64,0},{1,65},{65,1},{2,66},{66,2},{3,67},{67,3},{4,68},{68... | collective-permute-start | bytes 16515080 | tf_op jit(solution)/shard_map/ppermute | solution.py:30
  169.7 8.2 %collective-permute-start.13 = (bf16[512,1024]{1,0:T(8,128)(2,1)}, bf16[512,1024]{1,0:T(8,128)(2,1)}, u32[]{:S(2)}, u32[]{:S(2)}) collective-permute-start(bf16[512,1024]{1,0:T(8,128)(2,1)} %slice.451), channel_id=1, source_target_pairs={{0,64},{64,0},{1,65},{65,1},{2,66},{66,2},{3,67},{67,3},{4,68},{68... | collective-permute-start | bytes 3145736 | tf_op jit(solution)/shard_map/ppermute | solution.py:30
  181.7 29.7 %collective-permute-start.16 = (bf16[512,18944]{1,0:T(8,128)(2,1)}, bf16[512,18944]{1,0:T(8,128)(2,1)}, u32[]{:S(2)}, u32[]{:S(2)}) collective-permute-start(bf16[512,18944]{1,0:T(8,128)(2,1)} %all-gather.2.cloned.1.call-done.weight_own.gate_own.up_own), channel_id=1, source_target_pairs={{0,64},{64,0},{1,65},{65,1},{2,66},{66,2},{3,67},{67,3},{4,68},{68... | collective-permute-start | bytes 58195976 | tf_op jit(solution)/shard_map/ppermute | solution.py:30
  198.7 6.8 %collective-permute-start.15 = (bf16[64,1024]{1,0:T(8,128)(2,1)S(1)}, bf16[64,1024]{1,0:T(8,128)(2,1)S(1)}, u32[]{:S(2)}, u32[]{:S(2)}) collective-permute-start(bf16[64,1024]{1,0:T(8,128)(2,1)S(1)} %get-tuple-element.244), channel_id=1, source_target_pairs={{4,0},{8,4},{12,8},{16,12},{20,16},{24,20},{28,24},{32,28},{36,32}... | collective-permute-start | bytes 393224 | tf_op jit(solution)/shard_map/ppermute | solution.py:173
  200.0 6.4 %collective-permute-start.14 = (bf16[64,1024]{1,0:T(8,128)(2,1)S(1)}, bf16[64,1024]{1,0:T(8,128)(2,1)S(1)}, u32[]{:S(2)}, u32[]{:S(2)}) collective-permute-start(bf16[64,1024]{1,0:T(8,128)(2,1)S(1)} %get-tuple-element.243), channel_id=1, source_target_pairs={{0,4},{4,8},{8,12},{12,16},{16,20},{20,24},{24,28},{28,32},{32,36}... | collective-permute-start | bytes 393224 | tf_op jit(solution)/shard_map/ppermute | solution.py:169
  240.8 4.5 collective-permute-start.32
  241.4 4.0 collective-permute-start.25
  241.6 3.8 collective-permute-start.33
  254.3 211.3 %reduce-scatter.3.cloned.1.call-start = ((), (), s32[]{:S(2)}) async-start(), calls=%async_computation.3 | async-start | bytes 18382848 | tf_op jit(solution)/shard_map/reduce_scatter | solution.py:416
  259.2 13.1 %copy-start.37 = (bf16[128,1024]{1,0:T(8,128)(2,1)S(1)}, bf16[128,1024]{1,0:T(8,128)(2,1)}, u32[]{:S(2)}) copy-start(bf16[128,1024]{1,0:T(8,128)(2,1)} %copy-done.36) | copy-start | bytes 786436
  266.9 15.4 %collective-permute-start.19 = (bf16[64,2048]{1,0:T(8,128)(2,1)S(1)}, bf16[64,2048]{1,0:T(8,128)(2,1)S(1)}, u32[]{:S(2)}, u32[]{:S(2)}) collective-permute-start(bf16[64,2048]{1,0:T(8,128)(2,1)S(1)} %get-tuple-element.75), channel_id=1, source_target_pairs={{4,0},{8,4},{12,8},{16,12},{20,16},{24,20},{28,24},{32,28},{36,32}... | collective-permute-start | bytes 786440 | tf_op jit(solution)/shard_map/ppermute | solution.py:173
  268.2 15.0 %collective-permute-start.18 = (bf16[64,2048]{1,0:T(8,128)(2,1)S(1)}, bf16[64,2048]{1,0:T(8,128)(2,1)S(1)}, u32[]{:S(2)}, u32[]{:S(2)}) collective-permute-start(bf16[64,2048]{1,0:T(8,128)(2,1)S(1)} %get-tuple-element.74), channel_id=1, source_target_pairs={{0,4},{4,8},{8,12},{12,16},{16,20},{20,24},{24,28},{28,32},{32,36}... | collective-permute-start | bytes 786440 | tf_op jit(solution)/shard_map/ppermute | solution.py:169
  272.3 59.3 %collective-permute-start.23 = (bf16[3,128,1024]{2,1,0:T(8,128)(2,1)S(1)}, bf16[3,128,1024]{2,1,0:T(8,128)(2,1)}, u32[]{:S(2)}, u32[]{:S(2)}) collective-permute-start(bf16[3,128,1024]{2,1,0:T(8,128)(2,1)S(1)} %pad_maximum_fusion.7.refs_4_.refs_0_.refs_2_), channel_id=1, source_target_pairs={{0,64},{64,0},{1,65},{65,1},{2,66},{66,2},{3,67},{67,3},{4,68},{68... | collective-permute-start | bytes 2359304 | tf_op jit(solution)/shard_map/ppermute | solution.py:30
  273.3 58.3 %collective-permute-start.28 = (bf16[128,2688]{1,0:T(8,128)(2,1)}, bf16[128,2688]{1,0:T(8,128)(2,1)}, u32[]{:S(2)}, u32[]{:S(2)}) collective-permute-start(bf16[128,2688]{1,0:T(8,128)(2,1)} %get-tuple-element.89.refs_10_), channel_id=1, source_target_pairs={{0,64},{64,0},{1,65},{65,1},{2,66},{66,2},{3,67},{67,3},{4,68},{68... | collective-permute-start | bytes 2064392 | tf_op jit(solution)/shard_map/ppermute | solution.py:30
  311.1 10.4 %collective-permute-start.21 = (bf16[64,2048]{1,0:T(8,128)(2,1)S(1)}, bf16[64,2048]{1,0:T(8,128)(2,1)S(1)}, u32[]{:S(2)}, u32[]{:S(2)}) collective-permute-start(bf16[64,2048]{1,0:T(8,128)(2,1)S(1)} %get-tuple-element.84), channel_id=1, source_target_pairs={{4,0},{8,4},{12,8},{16,12},{20,16},{24,20},{28,24},{32,28},{36,32}... | collective-permute-start | bytes 786440 | tf_op jit(solution)/shard_map/ppermute | solution.py:173
  312.4 10.2 %collective-permute-start.20 = (bf16[64,2048]{1,0:T(8,128)(2,1)S(1)}, bf16[64,2048]{1,0:T(8,128)(2,1)S(1)}, u32[]{:S(2)}, u32[]{:S(2)}) collective-permute-start(bf16[64,2048]{1,0:T(8,128)(2,1)S(1)} %get-tuple-element.83), channel_id=1, source_target_pairs={{0,4},{4,8},{8,12},{12,16},{16,20},{20,24},{24,28},{28,32},{32,36}... | collective-permute-start | bytes 786440 | tf_op jit(solution)/shard_map/ppermute | solution.py:169
  318.2 13.4 %collective-permute-start.26 = (bf16[128,2048]{1,0:T(8,128)(2,1)}, bf16[128,2048]{1,0:T(8,128)(2,1)}, u32[]{:S(2)}, u32[]{:S(2)}) collective-permute-start(bf16[128,2048]{1,0:T(8,128)(2,1)} %get-tuple-element.165), channel_id=1, source_target_pairs={{0,64},{64,0},{1,65},{65,1},{2,66},{66,2},{3,67},{67,3},{4,68},{68... | collective-permute-start | bytes 1572872 | tf_op jit(solution)/shard_map/ppermute | solution.py:30
  321.6 10.1 %collective-permute-start.27 = (bf16[128,3200]{1,0:T(8,128)(2,1)}, bf16[128,3200]{1,0:T(8,128)(2,1)}, u32[]{:S(2)}, u32[]{:S(2)}) collective-permute-start(bf16[128,3200]{1,0:T(8,128)(2,1)} %get-tuple-element.149), channel_id=1, source_target_pairs={{0,64},{64,0},{1,65},{65,1},{2,66},{66,2},{3,67},{67,3},{4,68},{68... | collective-permute-start | bytes 2457608 | tf_op jit(solution)/shard_map/ppermute | solution.py:30
  324.0 20.3 %collective-permute-start.24 = (bf16[128,2048]{1,0:T(8,128)(2,1)}, bf16[128,2048]{1,0:T(8,128)(2,1)}, u32[]{:S(2)}, u32[]{:S(2)}) collective-permute-start(bf16[128,2048]{1,0:T(8,128)(2,1)} %get-tuple-element.167), channel_id=1, source_target_pairs={{0,64},{64,0},{1,65},{65,1},{2,66},{66,2},{3,67},{67,3},{4,68},{68... | collective-permute-start | bytes 1572872 | tf_op jit(solution)/shard_map/ppermute | solution.py:30
  349.5 3.1 collective-permute-start.17
  352.0 135.0 %collective-permute-start.22 = (f32[128,1024]{1,0:T(8,128)}, f32[128,1024]{1,0:T(8,128)S(1)}, u32[]{:S(2)}, u32[]{:S(2)}) collective-permute-start(f32[128,1024]{1,0:T(8,128)} %get-tuple-element.129), channel_id=1, source_target_pairs={{0,64},{64,0},{1,65},{65,1},{2,66},{66,2},{3,67},{67,3},{4,68},{68... | collective-permute-start | bytes 1572872 | tf_op jit(solution)/shard_map/ppermute | solution.py:30
  354.9 114.5 %collective-permute-start.36 = (bf16[16,4224]{1,0:T(8,128)(2,1)S(1)}, bf16[16,4224]{1,0:T(8,128)(2,1)S(1)}, u32[]{:S(2)}, u32[]{:S(2)}) collective-permute-start(bf16[16,4224]{1,0:T(8,128)(2,1)S(1)} %get-tuple-element.170), channel_id=1, source_target_pairs={{0,3},{1,0},{2,1},{3,2},{4,7},{5,4},{6,5},{7,6},{8,11},{9,8},{10,9... | collective-permute-start | bytes 405512 | tf_op jit(solution)/shard_map/ppermute | solution.py:553
  355.2 114.7 %collective-permute-start.35 = (bf16[16,4224]{1,0:T(8,128)(2,1)S(1)}, bf16[16,4224]{1,0:T(8,128)(2,1)S(1)}, u32[]{:S(2)}, u32[]{:S(2)}) collective-permute-start(bf16[16,4224]{1,0:T(8,128)(2,1)S(1)} %get-tuple-element.171), channel_id=1, source_target_pairs={{0,2},{1,3},{2,0},{3,1},{4,6},{5,7},{6,4},{7,5},{8,10},{9,11},{10,... | collective-permute-start | bytes 405512 | tf_op jit(solution)/shard_map/ppermute | solution.py:553
  355.4 115.2 %collective-permute-start.34 = (bf16[16,4224]{1,0:T(8,128)(2,1)S(1)}, bf16[16,4224]{1,0:T(8,128)(2,1)S(1)}, u32[]{:S(2)}, u32[]{:S(2)}) collective-permute-start(bf16[16,4224]{1,0:T(8,128)(2,1)S(1)} %get-tuple-element.169), channel_id=1, source_target_pairs={{0,1},{1,2},{2,3},{3,0},{4,5},{5,6},{6,7},{7,4},{8,9},{9,10},{10,1... | collective-permute-start | bytes 405512 | tf_op jit(solution)/shard_map/ppermute | solution.py:553
  466.7 20.2 %copy-start.40 = (f32[128,1024]{1,0:T(8,128)S(1)}, f32[128,1024]{1,0:T(8,128)}, u32[]{:S(2)}) copy-start(f32[128,1024]{1,0:T(8,128)} %get-tuple-element.130) | copy-start | bytes 1572868
  466.7 8.3 %collective-permute-start.31 = (bf16[16,8448]{1,0:T(8,128)(2,1)S(1)}, bf16[16,8448]{1,0:T(8,128)(2,1)S(1)}, u32[]{:S(2)}, u32[]{:S(2)}) collective-permute-start(bf16[16,8448]{1,0:T(8,128)(2,1)S(1)} %get-tuple-element.163), channel_id=1, source_target_pairs={{0,3},{1,0},{2,1},{3,2},{4,7},{5,4},{6,5},{7,6},{8,11},{9,8},{10,9... | collective-permute-start | bytes 811016 | tf_op jit(solution)/shard_map/ppermute | solution.py:553
  469.5 8.1 %collective-permute-start.30 = (bf16[16,8448]{1,0:T(8,128)(2,1)S(1)}, bf16[16,8448]{1,0:T(8,128)(2,1)S(1)}, u32[]{:S(2)}, u32[]{:S(2)}) collective-permute-start(bf16[16,8448]{1,0:T(8,128)(2,1)S(1)} %get-tuple-element.164), channel_id=1, source_target_pairs={{0,2},{1,3},{2,0},{3,1},{4,6},{5,7},{6,4},{7,5},{8,10},{9,11},{10,... | collective-permute-start | bytes 811016 | tf_op jit(solution)/shard_map/ppermute | solution.py:553
  469.9 15.3 %collective-permute-start.29 = (bf16[16,8448]{1,0:T(8,128)(2,1)S(1)}, bf16[16,8448]{1,0:T(8,128)(2,1)S(1)}, u32[]{:S(2)}, u32[]{:S(2)}) collective-permute-start(bf16[16,8448]{1,0:T(8,128)(2,1)S(1)} %get-tuple-element.162), channel_id=1, source_target_pairs={{0,1},{1,2},{2,3},{3,0},{4,5},{5,6},{6,7},{7,4},{8,9},{9,10},{10,1... | collective-permute-start | bytes 811016 | tf_op jit(solution)/shard_map/ppermute | solution.py:553
  486.4 1.9 collective-permute-start.37
  (41 other events, 169.7 us)
Sparse Core Ops, SparseCore 0:
  13.5 138.9 all-gather.1
  254.4 86.8 reduce-scatter.4
  349.6 115.8 reduce-scatter.2

commit v7 on v6

--- a/solution.py
+++ b/solution.py
@@ -102,9 +102,8 @@
         )
 
 
-def attend_back_kernel(
-    query_seg, key_seg, qkv, log_total, grad_mixed, grad_query, own, before, after
-):
+def attend_back_kernel(query_seg, key_seg, qkv, log_total, grad_mixed, *refs):
+    grad_query, own, before, after = refs[-4:]
     allowed = window_allowed(query_seg[...], key_seg[...])
     width = HEADS * HEAD_DIM
     rows = grad_mixed.shape[0]
@@ -150,7 +149,7 @@
     )(query_seg, key_seg, qkv, *ready)
 
 
-def attend_back(query_seg, key_seg, qkv, log_total, grad_mixed):
+def attend_back(query_seg, key_seg, qkv, log_total, grad_mixed, ready):
     rows, width = (query_seg.shape[0], HEADS * HEAD_DIM)
     return pl.pallas_call(
         attend_back_kernel,
@@ -160,9 +159,11 @@
             jax.ShapeDtypeStruct((HALO, 2 * width), jnp.bfloat16),
             jax.ShapeDtypeStruct((HALO, 2 * width), jnp.bfloat16),
         ),
+        in_specs=[pl.BlockSpec(memory_space=pltpu.VMEM)] * 5
+        + [pl.BlockSpec(memory_space=pl.ANY)] * len(ready),
         compiler_params=params,
         name="attend_back",
-    )(query_seg, key_seg, qkv, log_total, grad_mixed)
+    )(query_seg, key_seg, qkv, log_total, grad_mixed, *ready)
 
 
 def to_next(array):
@@ -510,8 +511,8 @@
     return (jnp.where(on_first, low, high), swapped(jnp.where(on_first, high, low)))
 
 
-def layer_backward(grad_out, kept, gain_pair, weights, segs, on_first, first):
-    (normed1, factor1, qkv, log_total, normed2, factor2, gate, up, acts, got) = kept
+def layer_backward(grad_out, kept, gain_pair, weights, segs, on_first, first, ready_of):
+    (normed1, factor1, qkv, log_total, normed2, factor2, gate, up, _, _) = kept
     rows, width = normed1.shape
     half = width // 2
     grad_branch = grad_out.astype(jnp.bfloat16)
@@ -526,7 +527,9 @@
     grad_attn = grad_middle.astype(jnp.bfloat16)
     mine, theirs = [matmul_t(grad_attn, w) for w in weights["out"]]
     grad_mixed = from_halves(mine, theirs, on_first).astype(jnp.bfloat16)
-    grad_query, grad_own, grad_before, grad_after = attend_back(*segs, qkv, log_total, grad_mixed)
+    grad_query, grad_own, grad_before, grad_after = attend_back(
+        *segs, qkv, log_total, grad_mixed, ready_of(hidden_pair)
+    )
     from_previous = to_next(grad_after).astype(jnp.float32)
     from_next = to_previous(grad_before).astype(jnp.float32)
     grad_pairs = grad_own + jnp.concatenate([from_previous, from_next], axis=0)
@@ -553,6 +556,48 @@
         got = lax.ppermute(part, "wshard", [(j, (j + step) % W_DEV) for j in range(W_DEV)])
         total = total + got.astype(jnp.float32)
     return total
+
+
+def summed_by_steps(block, seq_place, w_place):
+    side = 4
+    columns = block.shape[1]
+
+    def phase(parts, axis, at, place, route):
+        size = parts.shape[at]
+
+        def part(step):
+            return lax.dynamic_index_in_dim(parts, lax.rem(place + step, size), at, keepdims=False)
+
+        total = part(0).astype(jnp.float32)
+        for step in range(1, size):
+            total = total + lax.ppermute(part(step), axis, route(step)).astype(jnp.float32)
+        return total
+
+    total = phase(
+        block.reshape(SEQ_DEV, W_DEV, 16, columns),
+        "wshard",
+        1,
+        w_place,
+        lambda step: [(j, (j + step) % W_DEV) for j in range(W_DEV)],
+    )
+    total = phase(
+        total.astype(jnp.bfloat16).reshape(side, side, 16, columns),
+        "seq",
+        1,
+        lax.rem(seq_place, side),
+        lambda step: [
+            (side * y + x, side * y + (x + step) % side) for y in range(side) for x in range(side)
+        ],
+    )
+    return phase(
+        total.astype(jnp.bfloat16),
+        "seq",
+        0,
+        seq_place // side,
+        lambda step: [
+            (side * y + x, side * ((y + step) % side) + x) for y in range(side) for x in range(side)
+        ],
+    )
 
 
 def per_device(
@@ -670,9 +715,10 @@
     upstream = by_core(cotangent[0, 0], cotangent[1, 0])
     attn_cols, out_cols, down_cols = (qkv_width // 2, half, ROW_GROUPS * half)
     hidden_end = FF_PAD + down_cols
-    second_at = attn_cols + out_cols + 128
-    hidden_at = second_at + attn_cols + out_cols
-    total = hidden_at + hidden_end
+    gain_at = attn_cols + out_cols
+    second_at = gain_at + 128
+    hidden_at = second_at + attn_cols
+    total = hidden_at + FF_PAD
 
     def attn_items(kept, which, at):
         acts, got = (kept[-2][0], kept[-1][0])
@@ -681,29 +727,34 @@
             (acts, got, 1, which, attn_cols, out_cols, at + attn_cols),
         ]
 
-    def hidden_items(kept, which, at):
+    def hidden_items(kept, which, at, down_at):
         acts, got = (kept[-2], kept[-1])
         return (
             [(acts[0], got[0], 2, which, 0, FF_PAD, at)],
-            (acts[1], got[1], which, FF_PAD, at + FF_PAD),
+            (acts[1], got[1], which, FF_PAD, down_at),
         )
 
-    grads1, hidden_pair1, attn_pair1, gains1 = layer_backward(
-        upstream, kept1, gain_pairs[1], weights[1], segs, on_first, first
-    )
-    items, product = hidden_items(kept1, 0, 0)
-    early = seq_sum(weight_grads("hidden_grads", items, [hidden_pair1], hidden_end, product))
+    early_grads = []
+
+    def make_early(hidden_pair):
+        items, product = hidden_items(kept1, 0, 0, FF_PAD)
+        early_grads.append(weight_grads("hidden_grads", items, [hidden_pair], hidden_end, product))
+        return early_grads
+
+    grads1, _, attn_pair1, gains1 = layer_backward(
+        upstream, kept1, gain_pairs[1], weights[1], segs, on_first, first, make_early
+    )
+    early = seq_sum(early_grads[0])
     grads0, hidden_pair0, attn_pair0, gains0 = layer_backward(
-        grads1, kept0, gain_pairs[0], weights[0], segs, on_first, first
-    )
-    items, product = hidden_items(kept0, 1, hidden_at)
-    base = weight_grads(
-        "joint_grads",
-        attn_items(kept1, 0, second_at) + items,
-        [attn_pair1, hidden_pair0],
-        total,
-        product,
-    )
+        grads1, kept0, gain_pairs[0], weights[0], segs, on_first, first,
+        lambda hidden_pair: (hidden_pair[1], *kept0[-1]),
+    )
+    items, product = hidden_items(kept0, 1, hidden_at, out_cols)
+    qkv_item, out_item = attn_items(kept1, 0, 0)
+    pairs = [attn_pair1, hidden_pair0]
+    side = weight_grads("side_grads", [out_item[:-1] + (0,)], pairs, out_cols + down_cols, product)
+    side_total = summed_by_steps(side, seq_place, w_place)
+    base = weight_grads("joint_grads", [qkv_item[:-1] + (second_at,)] + items, pairs, total)
     gains = jnp.concatenate([gains0, gains1], axis=0)
     gains = jnp.pad(gains, ((0, 128 - gains.shape[0]), (0, 0))).T.astype(jnp.bfloat16)
     late = seq_sum(
@@ -713,7 +764,7 @@
             [attn_pair0],
             total,
             None,
-            (gains, attn_cols + out_cols),
+            (gains, gain_at),
             base,
         )
     )
@@ -727,10 +778,17 @@
     section_input_grads = placed(grads0, grads1)
 
     early_total, late_total = (summed_over_w(early, w_place), summed_over_w(late, w_place))
-    gain_at = attn_cols + out_cols
-    of_first = jnp.concatenate([late_total[:, :second_at], late_total[:, hidden_at:]], axis=1)
+    of_first = jnp.concatenate(
+        [late_total[:, :second_at], late_total[:, hidden_at:], side_total[:, out_cols:]], axis=1
+    )
     of_second = jnp.concatenate(
-        [late_total[:, second_at:hidden_at], late_total[:, gain_at:second_at], early_total], axis=1
+        [
+            late_total[:, second_at:hidden_at],
+            side_total[:, :out_cols],
+            late_total[:, gain_at:second_at],
+            early_total,
+        ],
+        axis=1,
     )
     mine, got = (by_core(of_first, of_second), swapped(by_core(of_second, of_first)))
     low, high = (by_core(mine, got), by_core(got, mine))

time: 508 us -> 498 us (0.980)
  waiting for transfers between devices: 238 us -> 198 us
  starting transfers between devices: 68.7 us -> 84.9 us
  local copies, waits for them, and re-layouts: 45.6 us -> 57.9 us
    reduce_scatter x2, waiting for transfers between devices: 109 us -> 10 us  [seq_sum(): return lax.psum_scatter(total, 'seq', scatter_dimension=0, tiled=True)]
    ppermute x0 -> x9, waiting for transfers between devices: none -> 62.8 us  [phase(): lax.ppermute(part(step), axis, route(step)).astype(jnp.float32)]
    ppermute x0 -> x9, starting transfers between devices: none -> 18 us  [phase(): lax.ppermute(part(step), axis, route(step)).astype(jnp.float32)]
    unnamed x116 -> x180, local copies, waits for them, and re-layouts: 15.7 us -> 24.3 us
    pallas_call x11 -> x12, Pallas kernels: 71.3 us -> 68.2 us  [grid_call(): pl.pallas_call(kernel, grid_spec=pltpu.PrefetchScalarGridSpec(num_scalar_...]
  transfers between devices with their start and end apart: 41 -> 50, of which waited for: 22 -> 29; matrix products, arithmetic and copies ran while one was open for 11% -> 12% of each run, Pallas kernels for 12% -> 11%
where the time goes in v7:
time: 498 us; the launch traced here: 488 us
  waiting for transfers between devices  198 us (40%)
  Pallas kernels  85.7 us (17%)
  starting transfers between devices  84.9 us (17%)
  local copies, waits for them, and re-layouts  57.9 us (12%)
  other arithmetic  31.9 us (6%)
  between operations  16 us (3%)
  matrix products  13.5 us (3%)
    pallas_call x12, Pallas kernels, grid_call(): pl.pallas_call(kernel, grid_spec=pltpu.PrefetchScalarGridSpec(num_scalar_...  68.2 us
    ppermute x9, waiting for transfers between devices, phase(): lax.ppermute(part(step), axis, route(step)).astype(jnp.float32)  62.8 us
    ppermute x1, waiting for transfers between devices, per_device(): above = lax.ppermute(down_piece, 'wshard', w_down)  40.6 us
    ppermute x20, starting transfers between devices, swapped(): return lax.ppermute(array, 'section', SWAP)  33 us
    unnamed x180, local copies, waits for them, and re-layouts  24.3 us
    ppermute x20, waiting for transfers between devices, swapped(): return lax.ppermute(array, 'section', SWAP)  23.5 us
    ppermute x1, waiting for transfers between devices, per_device(): lax.ppermute(below[:, :half], 'wshard', w_up)  19.6 us
    ppermute x9, starting transfers between devices, phase(): lax.ppermute(part(step), axis, route(step)).astype(jnp.float32)  18 us
  transfers between devices with their start and end apart: 50, of which 29 were waited for; matrix products, arithmetic and copies ran while one was open for 12% of the time, Pallas kernels for 11%

profile of v7, /device:TPU:1, one launch (start us, length us, event | category | flops | bytes accessed | tf_op | source)
XLA Modules:
  0.0 488.2 jit_solution(14202292439660906564)
XLA Ops:
  21.8 3.8 collective-permute-start.2
  25.6 40.6 %collective-permute-done.2 = bf16[656,1024]{1,0:T(8,128)(2,1)} collective-permute-done((bf16[656,1024]{1,0:T(8,128)(2,1)}, bf16[656,1024]{1,0:T(8,128)(2,1)}, u32[]{:S(2)}, u32[]{:S(2)}) %collective-permute-start.2) | collective-permute-done | bytes 1343520 | tf_op jit(solution)/shard_map/ppermute | solution.py:646
  66.2 2.6 fusion.48
  68.8 3.4 collective-permute-start.5
  72.2 13.8 %collective-permute-done.5 = bf16[656,512]{1,0:T(8,128)(2,1)S(1)} collective-permute-done((bf16[656,512]{1,0:T(8,128)(2,1)}, bf16[656,512]{1,0:T(8,128)(2,1)S(1)}, u32[]{:S(2)}, u32[]{:S(2)}) %collective-permute-start.5) | collective-permute-done | bytes 671776 | tf_op jit(solution)/shard_map/ppermute | solution.py:649
  87.7 10.5 %collective-permute-start.7 = (bf16[2688,512]{1,0:T(8,128)(2,1)S(1)}, bf16[2688,512]{1,0:T(8,128)(2,1)}, u32[]{:S(2)}, u32[]{:S(2)}) collective-permute-start(bf16[2688,512]{1,0:T(8,128)(2,1)S(1)} %get-tuple-element.65.down_own), channel_id=1, source_target_pairs={{0,64},{64,0},{1,65},{65,1},{2,66},{66,2},{3,67},{67,3},{4,68},{68... | collective-permute-start | bytes 8257544 | tf_op jit(solution)/shard_map/ppermute | solution.py:30
  98.1 19.6 %collective-permute-done.4 = bf16[656,512]{1,0:T(8,128)(2,1)S(1)} collective-permute-done((bf16[656,512]{1,0:T(8,128)(2,1)S(1)}, bf16[656,512]{1,0:T(8,128)(2,1)S(1)}, u32[]{:S(2)}, u32[]{:S(2)}) %collective-permute-start.4) | collective-permute-done | bytes 671776 | tf_op jit(solution)/shard_map/ppermute | solution.py:648
  120.6 10.7 %collective-permute-start.6 = (bf16[2688,512]{1,0:T(8,128)(2,1)}, bf16[2688,512]{1,0:T(8,128)(2,1)}, u32[]{:S(2)}, u32[]{:S(2)}) collective-permute-start(bf16[2688,512]{1,0:T(8,128)(2,1)} %constant_dynamic-update-slice_fusion.21.down_own), channel_id=1, source_target_pairs={{0,64},{64,0},{1,65},{65,1},{2,66},{66,2},{3,67},{67,3},{4,68},{68... | collective-permute-start | bytes 8257544 | tf_op jit(solution)/shard_map/ppermute | solution.py:30
  132.7 3.2 collective-permute-done.8
  140.2 4.6 collective-permute-start.9
  148.7 3.8 all-gather.2.cloned.1.call-done.weight_own.gate_own.up_own
  155.4 5.3 %collective-permute-done.11.weight_other = bf16[512,3072]{1,0:T(8,128)(2,1)S(1)} collective-permute-done((bf16[512,3072]{1,0:T(8,128)(2,1)S(1)}, bf16[512,3072]{1,0:T(8,128)(2,1)S(1)}, u32[]{:S(2)}, u32[]{:S(2)}) %collective-permute-start.11) | collective-permute-done | bytes 3145760 | tf_op jit(solution)/shard_map/ppermute | solution.py:30
  160.7 6.5 %slice.456 = bf16[512,5376]{1,0:T(8,128)(2,1)} slice(bf16[512,18944]{1,0:T(8,128)(2,1)} %all-gather.2.cloned.1.call-done.weight_own.gate_own.up_own), slice={[0:512], [0:5376]} | slice | bytes 11010048 | tf_op jit(solution)/shard_map/slice | solution.py:686
  171.3 3.5 qkv.2
  174.9 3.2 collective-permute-done.13.refs_1_
  178.1 2.9 attend.2
  187.8 8.0 %hidden.2 = (f32[128,2688]{1,0:T(8,128)S(1)}, f32[128,2688]{1,0:T(8,128)S(1)}, bf16[128,2688]{1,0:T(8,128)(2,1)S(1)}, f32[128,1024]{1,0:T(8,128)S(1)}) custom-call(s32[1]{0:T(128)} %bitcast.first, bf16[128,512]{1,0:T(8,128)(2,1)S(1)} %get-tuple-element.255.own, bf16[128,512]{1,0:T(8,128)(2,1)S(1)} %get-tuple-element.254.other, ...), custom_call_target="tpu_custom_call" | custom-call | tf_op jit(solution)/shard_map/hidden/pallas_call | solution.py:183
  200.8 4.0 collective-permute-start.14
  207.6 3.9 collective-permute-done.16.weight_other.gate_other.up_other
  211.5 4.0 qkv.3
  215.4 2.9 attend.3
  223.5 7.6 %hidden.3 = (f32[128,2688]{1,0:T(8,128)S(1)}, f32[128,2688]{1,0:T(8,128)S(1)}, bf16[128,2688]{1,0:T(8,128)(2,1)S(1)}, f32[128,1024]{1,0:T(8,128)S(1)}) custom-call(s32[1]{0:T(128)} %bitcast.first, bf16[128,512]{1,0:T(8,128)(2,1)S(1)} %get-tuple-element.235.own, bf16[128,512]{1,0:T(8,128)(2,1)S(1)} %get-tuple-element.234.other, ...), custom_call_target="tpu_custom_call" | custom-call | tf_op jit(solution)/shard_map/hidden/pallas_call | solution.py:183
  231.9 9.1 %hidden_back.2 = (bf16[128,2688]{1,0:T(8,128)(2,1)S(1)}, bf16[128,2688]{1,0:T(8,128)(2,1)S(1)}, f32[128,1024]{1,0:T(8,128)S(1)}) custom-call(s32[1]{0:T(128)} %bitcast.first, bf16[128,512]{1,0:T(8,128)(2,1)S(1)} %copy-done.38, bf16[128,512]{1,0:T(8,128)(2,1)S(1)} %copy-done.39, f32[128,2688]{1,0:T(8,128)S(1)} %get-tuple-element.68.gate_in, ...), custom_call_target="tpu_custom_call" | custom-call | tf_op jit(solution)/shard_map/hidden_back/pallas_call | solution.py:183
  242.7 3.2 collective-permute-done.20.refs_5_
  245.9 3.7 hidden_grads.1.refs_0_
  249.6 3.3 copy-done
  263.6 5.8 %attend_back.2 = (bf16[128,1024]{1,0:T(8,128)(2,1)S(1)}, f32[128,2048]{1,0:T(8,128)S(1)}, bf16[64,2048]{1,0:T(8,128)(2,1)S(1)}, bf16[64,2048]{1,0:T(8,128)(2,1)S(1)}) custom-call(s32[128,1]{1,0:T(8,128)S(1)} %copy.38.query_seg, s32[1,256]{1,0:T(1,128)S(1)} %bitcast.130, bf16[256,3072]{1,0:T(8,128)(2,1)S(1)} %qkv.3, f32[128,1024]{1,0:T(8,128)S(1)} %copy-done.43, ...), custom_call_target="tpu_custom_call" | custom-call | tf_op jit(solution)/shard_map/attend_back/pallas_call | solution.py:154
  270.7 4.0 collective-permute-start.21
  276.0 8.4 %collective-permute-done.22 = bf16[64,2048]{1,0:T(8,128)(2,1)S(1)} collective-permute-done((bf16[64,2048]{1,0:T(8,128)(2,1)S(1)}, bf16[64,2048]{1,0:T(8,128)(2,1)S(1)}, u32[]{:S(2)}, u32[]{:S(2)}) %collective-permute-start.22) | collective-permute-done | bytes 262176 | tf_op jit(solution)/shard_map/ppermute | solution.py:174
  286.4 4.7 qkv_back.2
  293.2 10.0 %hidden_back.3 = (bf16[128,2688]{1,0:T(8,128)(2,1)S(1)}, bf16[128,2688]{1,0:T(8,128)(2,1)S(1)}, f32[128,1024]{1,0:T(8,128)S(1)}) custom-call(s32[1]{0:T(128)} %bitcast.first, bf16[128,512]{1,0:T(8,128)(2,1)S(1)} %get-tuple-element.223.grad_own, bf16[128,512]{1,0:T(8,128)(2,1)S(1)} %get-tuple-element.224.grad_other, f32[128,2688]{1,0:T(8,128)S(1)} %copy-done.30, ...), custom_call_target="tpu_custom_call" | custom-call | tf_op jit(solution)/shard_map/hidden_back/pallas_call | solution.py:183
  310.8 5.8 %attend_back.3 = (bf16[128,1024]{1,0:T(8,128)(2,1)S(1)}, f32[128,2048]{1,0:T(8,128)S(1)}, bf16[64,2048]{1,0:T(8,128)(2,1)S(1)}, bf16[64,2048]{1,0:T(8,128)(2,1)S(1)}) custom-call(s32[128,1]{1,0:T(8,128)S(1)} %copy.38.query_seg, s32[1,256]{1,0:T(1,128)S(1)} %bitcast.131, bf16[256,3072]{1,0:T(8,128)(2,1)S(1)} %copy-done.6, f32[128,1024]{1,0:T(8,128)S(1)} %copy-done.41, ...), custom_call_target="tpu_custom_call" | custom-call | tf_op jit(solution)/shard_map/attend_back/pallas_call | solution.py:154
  317.9 4.5 collective-permute-start.26
  322.6 6.5 %joint_grads.1.refs_7_ = bf16[1024,6400]{1,0:T(8,128)(2,1)} custom-call(bf16[3,128,1024]{2,1,0:T(8,128)(2,1)S(1)} %copy-done.8, bf16[3,128,1024]{2,1,0:T(8,128)(2,1)S(1)} %copy-done.16, bf16[3,128,1024]{2,1,0:T(8,128)(2,1)S(1)} %pad_maximum_fusion.8.refs_2_.refs_0_, bf16[3,128,1024]{2,1,0:T(8,128)(2,1)S(1)} %collective-permute-done.24.refs_1_.refs_3_, ...), custom_call_target="tpu_custom_call" | custom-call | tf_op jit(solution)/shard_map/joint_grads/pallas_call | solution.py:183
  331.4 4.2 qkv_back.3
  339.6 4.7 attn_grads.1
  350.1 2.3 side_grads.1
  362.1 17.5 %collective-permute-done.36 = bf16[16,16,2048]{2,1,0:T(8,128)(2,1)S(1)} collective-permute-done((bf16[16,16,2048]{2,1,0:T(8,128)(2,1)}, bf16[16,16,2048]{2,1,0:T(8,128)(2,1)S(1)}, u32[]{:S(2)}, u32[]{:S(2)}) %collective-permute-start.36) | collective-permute-done | bytes 1048608 | tf_op jit(solution)/shard_map/ppermute | solution.py:573
  381.0 23.7 %collective-permute-done.34 = bf16[16,16,2048]{2,1,0:T(8,128)(2,1)} collective-permute-done((bf16[16,16,2048]{2,1,0:T(8,128)(2,1)S(1)}, bf16[16,16,2048]{2,1,0:T(8,128)(2,1)}, u32[]{:S(2)}, u32[]{:S(2)}) %collective-permute-start.34) | collective-permute-done | bytes 1048608 | tf_op jit(solution)/shard_map/ppermute | solution.py:573
  404.8 2.8 fusion.2
  407.6 11.0 %collective-permute-start.39 = (bf16[4,16,2048]{2,1,0:T(8,128)(2,1)S(1)}, bf16[4,16,2048]{2,1,0:T(8,128)(2,1)S(1)}, u32[]{:S(2)}, u32[]{:S(2)}) collective-permute-start(bf16[4,16,2048]{2,1,0:T(8,128)(2,1)S(1)} %get-tuple-element.168), channel_id=1, source_target_pairs={{0,12},{4,0},{8,4},{12,8},{16,28},{20,16},{24,20},{28,24},{32,44},... | collective-permute-start | bytes 786440 | tf_op jit(solution)/shard_map/ppermute | solution.py:573
  419.3 12.1 %collective-permute-done.39 = bf16[4,16,2048]{2,1,0:T(8,128)(2,1)S(1)} collective-permute-done((bf16[4,16,2048]{2,1,0:T(8,128)(2,1)S(1)}, bf16[4,16,2048]{2,1,0:T(8,128)(2,1)S(1)}, u32[]{:S(2)}, u32[]{:S(2)}) %collective-permute-start.39) | collective-permute-done | bytes 262176 | tf_op jit(solution)/shard_map/ppermute | solution.py:573
  433.4 4.0 collective-permute-start.42
  439.5 2.6 collective-permute-done.41
  442.1 3.6 collective-permute-done.40
  448.4 10.0 %reduce-scatter.3.cloned.1.call-done = bf16[64,6400]{1,0:T(8,128)(2,1)} async-done(((bf16[1024,6400]{1,0:T(8,128)(2,1)}), bf16[64,6400]{1,0:T(8,128)(2,1)}) %reduce-scatter.3.cloned.1.call-update) | async-done | bytes 819216 | tf_op jit(solution)/shard_map/reduce_scatter | solution.py:417
  465.5 2.6 collective-permute-done.32
  468.1 6.0 %collective-permute-done.31 = bf16[16,6400]{1,0:T(8,128)(2,1)S(1)} collective-permute-done((bf16[16,6400]{1,0:T(8,128)(2,1)S(1)}, bf16[16,6400]{1,0:T(8,128)(2,1)S(1)}, u32[]{:S(2)}, u32[]{:S(2)}) %collective-permute-start.31) | collective-permute-done | bytes 204832 | tf_op jit(solution)/shard_map/ppermute | solution.py:556
  (401 shorter events, 127.9 us)
Async XLA Ops:
  7.2 145.3 %all-gather.2.cloned.1.call-start = ((), (), s32[]{:S(2)}) async-start(), calls=%async_computation.2 | async-start | bytes 19701760 | tf_op jit(solution)/shard_map/all_gather | solution.py:639
  10.1 2.5 collective-permute-start
  13.4 432.4 %reduce-scatter.5.cloned.1.call-start = ((), (), s32[]{:S(2)}) async-start(), calls=%async_computation.4 | async-start | bytes 9191424 | tf_op jit(solution)/shard_map/reduce_scatter | solution.py:417
  21.8 44.4 %collective-permute-start.2 = (bf16[656,1024]{1,0:T(8,128)(2,1)}, bf16[656,1024]{1,0:T(8,128)(2,1)}, u32[]{:S(2)}, u32[]{:S(2)}) collective-permute-start(bf16[656,1024]{1,0:T(8,128)(2,1)} %pad_maximum_fusion), channel_id=1, source_target_pairs={{1,0},{2,1},{3,2},{0,3},{5,4},{6,5},{7,6},{4,7},{9,8},{10,9},{11,1... | collective-permute-start | bytes 4030472 | tf_op jit(solution)/shard_map/ppermute | solution.py:646
  25.6 60.5 %collective-permute-start.3 = (bf16[656,1024]{1,0:T(8,128)(2,1)}, bf16[656,1024]{1,0:T(8,128)(2,1)}, u32[]{:S(2)}, u32[]{:S(2)}) collective-permute-start(bf16[656,1024]{1,0:T(8,128)(2,1)} %pad_maximum_fusion), channel_id=1, source_target_pairs={{0,1},{1,2},{2,3},{3,0},{4,5},{5,6},{6,7},{7,4},{8,9},{9,10},{10,1... | collective-permute-start | bytes 4030472 | tf_op jit(solution)/shard_map/ppermute | solution.py:645
  68.8 17.2 %collective-permute-start.5 = (bf16[656,512]{1,0:T(8,128)(2,1)}, bf16[656,512]{1,0:T(8,128)(2,1)S(1)}, u32[]{:S(2)}, u32[]{:S(2)}) collective-permute-start(bf16[656,512]{1,0:T(8,128)(2,1)} %get-tuple-element.162), channel_id=1, source_target_pairs={{1,0},{2,1},{3,2},{0,3},{5,4},{6,5},{7,6},{4,7},{9,8},{10,9},{11,1... | collective-permute-start | bytes 2015240 | tf_op jit(solution)/shard_map/ppermute | solution.py:649
  87.6 30.1 %collective-permute-start.4 = (bf16[656,512]{1,0:T(8,128)(2,1)S(1)}, bf16[656,512]{1,0:T(8,128)(2,1)S(1)}, u32[]{:S(2)}, u32[]{:S(2)}) collective-permute-start(bf16[656,512]{1,0:T(8,128)(2,1)S(1)} %get-tuple-element.161), channel_id=1, source_target_pairs={{0,1},{1,2},{2,3},{3,0},{4,5},{5,6},{6,7},{7,4},{8,9},{9,10},{10,1... | collective-permute-start | bytes 2015240 | tf_op jit(solution)/shard_map/ppermute | solution.py:648
  87.7 61.1 %collective-permute-start.7 = (bf16[2688,512]{1,0:T(8,128)(2,1)S(1)}, bf16[2688,512]{1,0:T(8,128)(2,1)}, u32[]{:S(2)}, u32[]{:S(2)}) collective-permute-start(bf16[2688,512]{1,0:T(8,128)(2,1)S(1)} %get-tuple-element.65.down_own), channel_id=1, source_target_pairs={{0,64},{64,0},{1,65},{65,1},{2,66},{66,2},{3,67},{67,3},{4,68},{68... | collective-permute-start | bytes 8257544 | tf_op jit(solution)/shard_map/ppermute | solution.py:30
  120.6 28.1 %collective-permute-start.6 = (bf16[2688,512]{1,0:T(8,128)(2,1)}, bf16[2688,512]{1,0:T(8,128)(2,1)}, u32[]{:S(2)}, u32[]{:S(2)}) collective-permute-start(bf16[2688,512]{1,0:T(8,128)(2,1)} %constant_dynamic-update-slice_fusion.21.down_own), channel_id=1, source_target_pairs={{0,64},{64,0},{1,65},{65,1},{2,66},{66,2},{3,67},{67,3},{4,68},{68... | collective-permute-start | bytes 8257544 | tf_op jit(solution)/shard_map/ppermute | solution.py:30
  131.3 4.6 collective-permute-start.8
  138.9 7.2 %collective-permute-start.10 = (bf16[64,1024]{1,0:T(8,128)(2,1)}, bf16[64,1024]{1,0:T(8,128)(2,1)}, u32[]{:S(2)}, u32[]{:S(2)}) collective-permute-start(bf16[64,1024]{1,0:T(8,128)(2,1)} %get-tuple-element.273), channel_id=1, source_target_pairs={{4,0},{8,4},{12,8},{16,12},{20,16},{24,20},{28,24},{32,28},{36,32}... | collective-permute-start | bytes 393224 | tf_op jit(solution)/shard_map/ppermute | solution.py:174
  140.2 6.7 %collective-permute-start.9 = (bf16[64,1024]{1,0:T(8,128)(2,1)}, bf16[64,1024]{1,0:T(8,128)(2,1)}, u32[]{:S(2)}, u32[]{:S(2)}) collective-permute-start(bf16[64,1024]{1,0:T(8,128)(2,1)} %get-tuple-element.272), channel_id=1, source_target_pairs={{0,4},{4,8},{8,12},{12,16},{16,20},{20,24},{24,28},{28,32},{32,36}... | collective-permute-start | bytes 393224 | tf_op jit(solution)/shard_map/ppermute | solution.py:170
  154.6 6.0 %collective-permute-start.11 = (bf16[512,3072]{1,0:T(8,128)(2,1)S(1)}, bf16[512,3072]{1,0:T(8,128)(2,1)S(1)}, u32[]{:S(2)}, u32[]{:S(2)}) collective-permute-start(bf16[512,3072]{1,0:T(8,128)(2,1)S(1)} %slice.455), channel_id=1, source_target_pairs={{0,64},{64,0},{1,65},{65,1},{2,66},{66,2},{3,67},{67,3},{4,68},{68... | collective-permute-start | bytes 9437192 | tf_op jit(solution)/shard_map/ppermute | solution.py:30
  167.2 10.9 %collective-permute-start.12 = (bf16[512,5376]{1,0:T(8,128)(2,1)}, bf16[512,5376]{1,0:T(8,128)(2,1)}, u32[]{:S(2)}, u32[]{:S(2)}) collective-permute-start(bf16[512,5376]{1,0:T(8,128)(2,1)} %slice.456), channel_id=1, source_target_pairs={{0,64},{64,0},{1,65},{65,1},{2,66},{66,2},{3,67},{67,3},{4,68},{68... | collective-permute-start | bytes 16515080 | tf_op jit(solution)/shard_map/ppermute | solution.py:30
  169.8 8.2 %collective-permute-start.13 = (bf16[512,1024]{1,0:T(8,128)(2,1)}, bf16[512,1024]{1,0:T(8,128)(2,1)}, u32[]{:S(2)}, u32[]{:S(2)}) collective-permute-start(bf16[512,1024]{1,0:T(8,128)(2,1)} %slice.457), channel_id=1, source_target_pairs={{0,64},{64,0},{1,65},{65,1},{2,66},{66,2},{3,67},{67,3},{4,68},{68... | collective-permute-start | bytes 3145736 | tf_op jit(solution)/shard_map/ppermute | solution.py:30
  181.8 29.7 %collective-permute-start.16 = (bf16[512,18944]{1,0:T(8,128)(2,1)}, bf16[512,18944]{1,0:T(8,128)(2,1)}, u32[]{:S(2)}, u32[]{:S(2)}) collective-permute-start(bf16[512,18944]{1,0:T(8,128)(2,1)} %all-gather.2.cloned.1.call-done.weight_own.gate_own.up_own), channel_id=1, source_target_pairs={{0,64},{64,0},{1,65},{65,1},{2,66},{66,2},{3,67},{67,3},{4,68},{68... | collective-permute-start | bytes 58195976 | tf_op jit(solution)/shard_map/ppermute | solution.py:30
  199.5 7.0 %collective-permute-start.15 = (bf16[64,1024]{1,0:T(8,128)(2,1)S(1)}, bf16[64,1024]{1,0:T(8,128)(2,1)S(1)}, u32[]{:S(2)}, u32[]{:S(2)}) collective-permute-start(bf16[64,1024]{1,0:T(8,128)(2,1)S(1)} %get-tuple-element.253), channel_id=1, source_target_pairs={{4,0},{8,4},{12,8},{16,12},{20,16},{24,20},{28,24},{32,28},{36,32}... | collective-permute-start | bytes 393224 | tf_op jit(solution)/shard_map/ppermute | solution.py:174
  200.8 6.5 %collective-permute-start.14 = (bf16[64,1024]{1,0:T(8,128)(2,1)S(1)}, bf16[64,1024]{1,0:T(8,128)(2,1)S(1)}, u32[]{:S(2)}, u32[]{:S(2)}) collective-permute-start(bf16[64,1024]{1,0:T(8,128)(2,1)S(1)} %get-tuple-element.252), channel_id=1, source_target_pairs={{0,4},{4,8},{8,12},{12,16},{16,20},{20,24},{24,28},{28,32},{32,36}... | collective-permute-start | bytes 393224 | tf_op jit(solution)/shard_map/ppermute | solution.py:170
  241.4 4.5 collective-permute-start.19
  241.9 4.0 collective-permute-start.18
  242.1 3.8 collective-permute-start.20
  254.7 203.7 %reduce-scatter.3.cloned.1.call-start = ((), (), s32[]{:S(2)}) async-start(), calls=%async_computation.3 | async-start | bytes 13926400 | tf_op jit(solution)/shard_map/reduce_scatter | solution.py:417
  269.4 14.9 %collective-permute-start.22 = (bf16[64,2048]{1,0:T(8,128)(2,1)S(1)}, bf16[64,2048]{1,0:T(8,128)(2,1)S(1)}, u32[]{:S(2)}, u32[]{:S(2)}) collective-permute-start(bf16[64,2048]{1,0:T(8,128)(2,1)S(1)} %get-tuple-element.78), channel_id=1, source_target_pairs={{4,0},{8,4},{12,8},{16,12},{20,16},{24,20},{28,24},{32,28},{36,32}... | collective-permute-start | bytes 786440 | tf_op jit(solution)/shard_map/ppermute | solution.py:174
  270.7 15.5 %collective-permute-start.21 = (bf16[64,2048]{1,0:T(8,128)(2,1)S(1)}, bf16[64,2048]{1,0:T(8,128)(2,1)S(1)}, u32[]{:S(2)}, u32[]{:S(2)}) collective-permute-start(bf16[64,2048]{1,0:T(8,128)(2,1)S(1)} %get-tuple-element.77), channel_id=1, source_target_pairs={{0,4},{4,8},{8,12},{12,16},{16,20},{20,24},{24,28},{28,32},{32,36}... | collective-permute-start | bytes 786440 | tf_op jit(solution)/shard_map/ppermute | solution.py:170
  274.8 35.9 %collective-permute-start.24 = (bf16[3,128,1024]{2,1,0:T(8,128)(2,1)S(1)}, bf16[3,128,1024]{2,1,0:T(8,128)(2,1)S(1)}, u32[]{:S(2)}, u32[]{:S(2)}) collective-permute-start(bf16[3,128,1024]{2,1,0:T(8,128)(2,1)S(1)} %pad_maximum_fusion.8.refs_2_.refs_0_), channel_id=1, source_target_pairs={{0,64},{64,0},{1,65},{65,1},{2,66},{66,2},{3,67},{67,3},{4,68},{68... | collective-permute-start | bytes 2359304 | tf_op jit(solution)/shard_map/ppermute | solution.py:30
  275.9 34.9 %collective-permute-start.25 = (bf16[128,2688]{1,0:T(8,128)(2,1)S(1)}, bf16[128,2688]{1,0:T(8,128)(2,1)S(1)}, u32[]{:S(2)}, u32[]{:S(2)}) collective-permute-start(bf16[128,2688]{1,0:T(8,128)(2,1)S(1)} %copy-done.36), channel_id=1, source_target_pairs={{0,64},{64,0},{1,65},{65,1},{2,66},{66,2},{3,67},{67,3},{4,68},{68... | collective-permute-start | bytes 2064392 | tf_op jit(solution)/shard_map/ppermute | solution.py:30
  303.4 7.3 %collective-permute-start.23 = (bf16[128,3200]{1,0:T(8,128)(2,1)S(1)}, bf16[128,3200]{1,0:T(8,128)(2,1)S(1)}, u32[]{:S(2)}, u32[]{:S(2)}) collective-permute-start(bf16[128,3200]{1,0:T(8,128)(2,1)S(1)} %get-tuple-element.151), channel_id=1, source_target_pairs={{0,64},{64,0},{1,65},{65,1},{2,66},{66,2},{3,67},{67,3},{4,68},{68... | collective-permute-start | bytes 2457608 | tf_op jit(solution)/shard_map/ppermute | solution.py:30
  310.4 12.1 %collective-permute-start.30 = (bf16[128,2048]{1,0:T(8,128)(2,1)S(1)}, bf16[128,2048]{1,0:T(8,128)(2,1)S(1)}, u32[]{:S(2)}, u32[]{:S(2)}) collective-permute-start(bf16[128,2048]{1,0:T(8,128)(2,1)S(1)} %get-tuple-element.170), channel_id=1, source_target_pairs={{0,64},{64,0},{1,65},{65,1},{2,66},{66,2},{3,67},{67,3},{4,68},{68... | collective-permute-start | bytes 1572872 | tf_op jit(solution)/shard_map/ppermute | solution.py:30
  316.6 12.4 %collective-permute-start.27 = (bf16[64,2048]{1,0:T(8,128)(2,1)S(1)}, bf16[64,2048]{1,0:T(8,128)(2,1)S(1)}, u32[]{:S(2)}, u32[]{:S(2)}) collective-permute-start(bf16[64,2048]{1,0:T(8,128)(2,1)S(1)} %get-tuple-element.91), channel_id=1, source_target_pairs={{4,0},{8,4},{12,8},{16,12},{20,16},{24,20},{28,24},{32,28},{36,32}... | collective-permute-start | bytes 786440 | tf_op jit(solution)/shard_map/ppermute | solution.py:174
  317.9 11.1 %collective-permute-start.26 = (bf16[64,2048]{1,0:T(8,128)(2,1)S(1)}, bf16[64,2048]{1,0:T(8,128)(2,1)S(1)}, u32[]{:S(2)}, u32[]{:S(2)}) collective-permute-start(bf16[64,2048]{1,0:T(8,128)(2,1)S(1)} %get-tuple-element.90), channel_id=1, source_target_pairs={{0,4},{4,8},{8,12},{12,16},{16,20},{20,24},{24,28},{28,32},{32,36}... | collective-permute-start | bytes 786440 | tf_op jit(solution)/shard_map/ppermute | solution.py:170
  330.4 8.2 %collective-permute-start.29 = (bf16[128,2048]{1,0:T(8,128)(2,1)}, bf16[128,2048]{1,0:T(8,128)(2,1)}, u32[]{:S(2)}, u32[]{:S(2)}) collective-permute-start(bf16[128,2048]{1,0:T(8,128)(2,1)} %get-tuple-element.165), channel_id=1, source_target_pairs={{0,64},{64,0},{1,65},{65,1},{2,66},{66,2},{3,67},{67,3},{4,68},{68... | collective-permute-start | bytes 1572872 | tf_op jit(solution)/shard_map/ppermute | solution.py:30
  355.1 24.5 %collective-permute-start.36 = (bf16[16,16,2048]{2,1,0:T(8,128)(2,1)}, bf16[16,16,2048]{2,1,0:T(8,128)(2,1)S(1)}, u32[]{:S(2)}, u32[]{:S(2)}) collective-permute-start(bf16[16,16,2048]{2,1,0:T(8,128)(2,1)} %get-tuple-element.146), channel_id=1, source_target_pairs={{0,3},{1,0},{2,1},{3,2},{4,7},{5,4},{6,5},{7,6},{8,11},{9,8},{10,9... | collective-permute-start | bytes 3145736 | tf_op jit(solution)/shard_map/ppermute | solution.py:573
  355.3 25.7 %collective-permute-start.35 = (bf16[16,16,2048]{2,1,0:T(8,128)(2,1)}, bf16[16,16,2048]{2,1,0:T(8,128)(2,1)}, u32[]{:S(2)}, u32[]{:S(2)}) collective-permute-start(bf16[16,16,2048]{2,1,0:T(8,128)(2,1)} %get-tuple-element.147), channel_id=1, source_target_pairs={{0,2},{1,3},{2,0},{3,1},{4,6},{5,7},{6,4},{7,5},{8,10},{9,11},{10,... | collective-permute-start | bytes 3145736 | tf_op jit(solution)/shard_map/ppermute | solution.py:573
  355.4 49.4 %collective-permute-start.34 = (bf16[16,16,2048]{2,1,0:T(8,128)(2,1)S(1)}, bf16[16,16,2048]{2,1,0:T(8,128)(2,1)}, u32[]{:S(2)}, u32[]{:S(2)}) collective-permute-start(bf16[16,16,2048]{2,1,0:T(8,128)(2,1)S(1)} %get-tuple-element.145), channel_id=1, source_target_pairs={{0,1},{1,2},{2,3},{3,0},{4,5},{5,6},{6,7},{7,4},{8,9},{9,10},{10,1... | collective-permute-start | bytes 3145736 | tf_op jit(solution)/shard_map/ppermute | solution.py:573
  356.8 3.1 collective-permute-start.17
  407.6 23.7 %collective-permute-start.39 = (bf16[4,16,2048]{2,1,0:T(8,128)(2,1)S(1)}, bf16[4,16,2048]{2,1,0:T(8,128)(2,1)S(1)}, u32[]{:S(2)}, u32[]{:S(2)}) collective-permute-start(bf16[4,16,2048]{2,1,0:T(8,128)(2,1)S(1)} %get-tuple-element.168), channel_id=1, source_target_pairs={{0,12},{4,0},{8,4},{12,8},{16,28},{20,16},{24,20},{28,24},{32,44},... | collective-permute-start | bytes 786440 | tf_op jit(solution)/shard_map/ppermute | solution.py:573
  418.6 12.7 %collective-permute-start.38 = (bf16[4,16,2048]{2,1,0:T(8,128)(2,1)S(1)}, bf16[4,16,2048]{2,1,0:T(8,128)(2,1)S(1)}, u32[]{:S(2)}, u32[]{:S(2)}) collective-permute-start(bf16[4,16,2048]{2,1,0:T(8,128)(2,1)S(1)} %get-tuple-element.169), channel_id=1, source_target_pairs={{0,8},{4,12},{8,0},{12,4},{16,24},{20,28},{24,16},{28,20},{32,40},... | collective-permute-start | bytes 786440 | tf_op jit(solution)/shard_map/ppermute | solution.py:573
  418.7 14.6 %collective-permute-start.37 = (bf16[4,16,2048]{2,1,0:T(8,128)(2,1)S(1)}, bf16[4,16,2048]{2,1,0:T(8,128)(2,1)S(1)}, u32[]{:S(2)}, u32[]{:S(2)}) collective-permute-start(bf16[4,16,2048]{2,1,0:T(8,128)(2,1)S(1)} %get-tuple-element.167), channel_id=1, source_target_pairs={{0,4},{4,8},{8,12},{12,0},{16,20},{20,24},{24,28},{28,16},{32,36},... | collective-permute-start | bytes 786440 | tf_op jit(solution)/shard_map/ppermute | solution.py:573
  433.4 6.0 %collective-permute-start.42 = (bf16[16,2048]{1,0:T(8,128)(2,1)S(1)}, bf16[16,2048]{1,0:T(8,128)(2,1)S(1)}, u32[]{:S(2)}, u32[]{:S(2)}) collective-permute-start(bf16[16,2048]{1,0:T(8,128)(2,1)S(1)} %get-tuple-element.218), channel_id=1, source_target_pairs={{0,48},{4,52},{8,56},{12,60},{16,0},{20,4},{24,8},{28,12},{32,16},... | collective-permute-start | bytes 196616 | tf_op jit(solution)/shard_map/ppermute | solution.py:573
  437.4 4.7 collective-permute-start.41
  437.8 7.9 %collective-permute-start.40 = (bf16[16,2048]{1,0:T(8,128)(2,1)S(1)}, bf16[16,2048]{1,0:T(8,128)(2,1)S(1)}, u32[]{:S(2)}, u32[]{:S(2)}) collective-permute-start(bf16[16,2048]{1,0:T(8,128)(2,1)S(1)} %get-tuple-element.217), channel_id=1, source_target_pairs={{0,16},{4,20},{8,24},{12,28},{16,32},{20,36},{24,40},{28,44},{32,4... | collective-permute-start | bytes 196616 | tf_op jit(solution)/shard_map/ppermute | solution.py:573
  438.3 37.5 %collective-permute-start.28 = (f32[128,1024]{1,0:T(8,128)S(1)}, f32[128,1024]{1,0:T(8,128)S(1)}, u32[]{:S(2)}, u32[]{:S(2)}) collective-permute-start(f32[128,1024]{1,0:T(8,128)S(1)} %get-tuple-element.129), channel_id=1, source_target_pairs={{0,64},{64,0},{1,65},{65,1},{2,66},{66,2},{3,67},{67,3},{4,68},{68... | collective-permute-start | bytes 1572872 | tf_op jit(solution)/shard_map/ppermute | solution.py:30
  446.9 14.3 %collective-permute-start.45 = (bf16[16,4224]{1,0:T(8,128)(2,1)S(1)}, bf16[16,4224]{1,0:T(8,128)(2,1)S(1)}, u32[]{:S(2)}, u32[]{:S(2)}) collective-permute-start(bf16[16,4224]{1,0:T(8,128)(2,1)S(1)} %get-tuple-element.176), channel_id=1, source_target_pairs={{0,3},{1,0},{2,1},{3,2},{4,7},{5,4},{6,5},{7,6},{8,11},{9,8},{10,9... | collective-permute-start | bytes 405512 | tf_op jit(solution)/shard_map/ppermute | solution.py:556
  447.0 14.7 %collective-permute-start.44 = (bf16[16,4224]{1,0:T(8,128)(2,1)S(1)}, bf16[16,4224]{1,0:T(8,128)(2,1)S(1)}, u32[]{:S(2)}, u32[]{:S(2)}) collective-permute-start(bf16[16,4224]{1,0:T(8,128)(2,1)S(1)} %get-tuple-element.177), channel_id=1, source_target_pairs={{0,2},{1,3},{2,0},{3,1},{4,6},{5,7},{6,4},{7,5},{8,10},{9,11},{10,... | collective-permute-start | bytes 405512 | tf_op jit(solution)/shard_map/ppermute | solution.py:556
  447.1 15.2 %collective-permute-start.43 = (bf16[16,4224]{1,0:T(8,128)(2,1)S(1)}, bf16[16,4224]{1,0:T(8,128)(2,1)S(1)}, u32[]{:S(2)}, u32[]{:S(2)}) collective-permute-start(bf16[16,4224]{1,0:T(8,128)(2,1)S(1)} %get-tuple-element.175), channel_id=1, source_target_pairs={{0,1},{1,2},{2,3},{3,0},{4,5},{5,6},{6,7},{7,4},{8,9},{9,10},{10,1... | collective-permute-start | bytes 405512 | tf_op jit(solution)/shard_map/ppermute | solution.py:556
  459.6 5.9 %collective-permute-start.33 = (bf16[16,6400]{1,0:T(8,128)(2,1)S(1)}, bf16[16,6400]{1,0:T(8,128)(2,1)S(1)}, u32[]{:S(2)}, u32[]{:S(2)}) collective-permute-start(bf16[16,6400]{1,0:T(8,128)(2,1)S(1)} %get-tuple-element.173), channel_id=1, source_target_pairs={{0,3},{1,0},{2,1},{3,2},{4,7},{5,4},{6,5},{7,6},{8,11},{9,8},{10,9... | collective-permute-start | bytes 614408 | tf_op jit(solution)/shard_map/ppermute | solution.py:556
  461.2 6.9 %collective-permute-start.32 = (bf16[16,6400]{1,0:T(8,128)(2,1)S(1)}, bf16[16,6400]{1,0:T(8,128)(2,1)S(1)}, u32[]{:S(2)}, u32[]{:S(2)}) collective-permute-start(bf16[16,6400]{1,0:T(8,128)(2,1)S(1)} %get-tuple-element.174), channel_id=1, source_target_pairs={{0,2},{1,3},{2,0},{3,1},{4,6},{5,7},{6,4},{7,5},{8,10},{9,11},{10,... | collective-permute-start | bytes 614408 | tf_op jit(solution)/shard_map/ppermute | solution.py:556
  461.7 12.4 %collective-permute-start.31 = (bf16[16,6400]{1,0:T(8,128)(2,1)S(1)}, bf16[16,6400]{1,0:T(8,128)(2,1)S(1)}, u32[]{:S(2)}, u32[]{:S(2)}) collective-permute-start(bf16[16,6400]{1,0:T(8,128)(2,1)S(1)} %get-tuple-element.172), channel_id=1, source_target_pairs={{0,1},{1,2},{2,3},{3,0},{4,5},{5,6},{6,7},{7,4},{8,9},{9,10},{10,1... | collective-permute-start | bytes 614408 | tf_op jit(solution)/shard_map/ppermute | solution.py:556
  (82 other events, 752.6 us)
Sparse Core Ops, SparseCore 0:
  13.5 138.9 all-gather.1
  254.8 91.4 reduce-scatter.4
  350.2 108.1 reduce-scatter.2

commit v8 on v7

--- a/solution.py
+++ b/solution.py
@@ -16,7 +16,7 @@
 W_DEV = 4
 PAD_ROWS = 48
 HIDDEN_BLOCK = 896
-QKV_BLOCK = 1536
+QKV_BLOCK = 768
 
 norm_eps = 1e-05
 root_half = 1.0 / math.sqrt(2.0)
@@ -81,8 +81,7 @@
     return (offset >= 0) & (offset <= 2 * HALO) & (query_seg == key_seg)
 
 
-def attend_kernel(query_seg, key_seg, qkv, *refs):
-    mixed, log_total = refs[-2:]
+def attend_kernel(query_seg, key_seg, qkv, mixed, log_total):
     allowed = window_allowed(query_seg[...], key_seg[...])
     width = HEADS * HEAD_DIM
     rows = mixed.shape[0]
@@ -134,7 +133,7 @@
 params = pltpu.CompilerParams(vmem_limit_bytes=40 * 1024 * 1024)
 
 
-def attend(query_seg, key_seg, qkv, ready):
+def attend(query_seg, key_seg, qkv):
     rows, width = (query_seg.shape[0], HEADS * HEAD_DIM)
     return pl.pallas_call(
         attend_kernel,
@@ -142,11 +141,9 @@
             jax.ShapeDtypeStruct((rows, width), jnp.bfloat16),
             jax.ShapeDtypeStruct((rows, width), jnp.float32),
         ),
-        in_specs=[pl.BlockSpec(memory_space=pltpu.VMEM)] * 3
-        + [pl.BlockSpec(memory_space=pl.ANY)] * len(ready),
         compiler_params=params,
         name="attend",
-    )(query_seg, key_seg, qkv, *ready)
+    )(query_seg, key_seg, qkv)
 
 
 def attend_back(query_seg, key_seg, qkv, log_total, grad_mixed, ready):
@@ -396,11 +393,10 @@
     return (normed, factor, act_in, jnp.concatenate([before, act_in, after], axis=0))
 
 
-def layer_forward(rows_in, entry, gain_pair, weights, segs, on_first, first, later=(), ready=()):
+def layer_forward(rows_in, entry, gain_pair, weights, segs, on_first, first):
     normed1, factor1, act_in, extended = entry
     qkv = qkv_of(*column_halves(extended, on_first), weights)
-    mixed, log_total = attend(*segs, qkv, ready)
-    mixed, *later = lax.optimization_barrier((mixed, *later))
+    mixed, log_total = attend(*segs, qkv)
     own, other = column_halves(mixed, on_first)
     middle = rows_in + matmul(own, weights["out"][0]) + matmul(other, weights["out"][1])
     normed2, factor2 = norm_parts(middle)
@@ -410,7 +406,7 @@
     acts = (jnp.stack([act_in, mixed, act_mid]), product)
     got = tuple(swapped(act) for act in acts)
     kept = (normed1, factor1, qkv, log_total, normed2, factor2, gate, up, acts, got)
-    return (output, kept, later)
+    return (output, kept)
 
 
 def seq_sum(total):
@@ -626,44 +622,38 @@
         ]
         return jnp.concatenate([hidden[:, :FF], pad, hidden[:, FF:], pad, qkv, out], axis=1)
 
-    def in_order(first, second):
-        ends = (0, 2 * FF_PAD, 2 * FF_PAD + 3 * width, 2 * FF_PAD + 4 * width)
-        return jnp.concatenate(
-            [piece[:, a:b] for a, b in zip(ends, ends[1:]) for piece in (first, second)], axis=1
-        )
-
     row_pieces = sections(row_slice(core), swapped(row_slice(1 - core)))
     hidden_width, qkv_width = (2 * FF_PAD, 3 * width)
-    qkv_at = 2 * hidden_width
-    out_at = qkv_at + 2 * qkv_width
-    all_own = lax.all_gather(in_order(*row_pieces), ("wshard", "seq"), axis=0, tiled=True)
+    out_at = hidden_width + qkv_width
+
+    def gathered(piece):
+        return lax.all_gather(piece, ("wshard", "seq"), axis=0, tiled=True)
+
+    first_own = gathered(row_pieces[0])
     half = hidden_out.shape[2] // 2
     low, high = (hidden_out[0, :, :half], hidden_out[0, :, half:])
-    down_piece = jnp.concatenate(sections(by_core(low, high), swapped(by_core(high, low))), axis=1)
+    down_pieces = sections(by_core(low, high), swapped(by_core(high, low)))
     w_up = [(j, (j + 1) % W_DEV) for j in range(W_DEV)]
     w_down = [(j, i) for i, j in w_up]
-    below = lax.ppermute(down_piece, "wshard", w_up)
-    above = lax.ppermute(down_piece, "wshard", w_down)
-    far = (
-        lax.ppermute(below[:, :half], "wshard", w_up),
-        lax.ppermute(above[:, half:], "wshard", w_down),
-    )
     gain_pairs = sections(norm_gains[0], swapped(norm_gains[0]))
-    piece_rows = down_piece.shape[0]
-
-    def down_of(section):
-        columns = slice(section * half, (section + 1) * half)
+
+    def neighbours(piece):
+        return (lax.ppermute(piece, "wshard", w_up), lax.ppermute(piece, "wshard", w_down))
+
+    def down_of(piece, below, above):
+        far = jnp.concatenate(
+            [
+                lax.ppermute(below[:, : half // 2], "wshard", w_up),
+                lax.ppermute(above[:, half // 2 :], "wshard", w_down),
+            ],
+            axis=1,
+        )
         own = jnp.zeros((FF_PAD, half), jnp.bfloat16)
-        for step, piece in (
-            (0, down_piece[:, columns]),
-            (1, above[:, columns]),
-            (2, far[section]),
-            (3, below[:, columns]),
-        ):
+        for step, part in enumerate((piece, above, far, below)):
             own = lax.dynamic_update_slice_in_dim(
-                own, piece, lax.rem(w_place + step, W_DEV) * piece_rows, 0
+                own, part, lax.rem(w_place + step, W_DEV) * piece.shape[0], 0
             )
-        return own
+        return (own, swapped(own))
 
     rows_in = by_core(inputs[0, 0], inputs[1, 0])
     row_count = rows_in.shape[0]
@@ -675,43 +665,45 @@
         lax.dynamic_slice_in_dim(padded, first_row, row_count + 2 * HALO)[None, :],
     )
     entry = attention_input(rows_in, gain_pairs[0][0])
-    down_own = (down_of(0), down_of(1))
-    all_own, down_own, down_other, entry, gain_pairs, segs = lax.optimization_barrier(
-        (all_own, down_own, tuple(swapped(d) for d in down_own), entry, gain_pairs, segs)
-    )
-    first_qkv, all_own = lax.optimization_barrier(
-        (swapped(all_own[:, qkv_at : qkv_at + qkv_width]), all_own)
-    )
-    first_out = swapped(all_own[:, out_at : out_at + width])
-    first_hidden = swapped(all_own[:, :hidden_width])
-    first_weights = {
-        "qkv": ((all_own, qkv_at), (first_qkv, 0)),
-        "gate": ((all_own, 0), (first_hidden, 0)),
-        "up": ((all_own, FF_PAD), (first_hidden, FF_PAD)),
-        "out": (all_own[:, out_at : out_at + width], first_out),
-        "down": (down_own[0], down_other[0]),
-    }
-
-    def second_weights(all_late):
-        all_other = swapped(all_late)
+    row_piece, entry = lax.optimization_barrier((row_pieces[1], entry))
+    second_own = gathered(row_piece)
+    first_own, down_piece, first_down, entry, gain_pairs, segs = lax.optimization_barrier(
+        (first_own, down_pieces[1], down_of(down_pieces[0], *neighbours(down_pieces[0])), entry, gain_pairs, segs)
+    )
+    near = neighbours(down_piece)
+
+    def weights_of(own, other, qkv_other, out_other, down):
         return {
-            "qkv": ((all_own, qkv_at + qkv_width), (all_other, qkv_at + qkv_width)),
-            "gate": ((all_own, hidden_width), (all_other, hidden_width)),
-            "up": ((all_own, hidden_width + FF_PAD), (all_other, hidden_width + FF_PAD)),
-            "out": (all_own[:, out_at + width :], all_other[:, out_at + width :]),
-            "down": (down_own[1], down_other[1]),
+            "qkv": ((own, hidden_width), qkv_other),
+            "gate": ((own, 0), (other, 0)),
+            "up": ((own, FF_PAD), (other, FF_PAD)),
+            "out": (own[:, out_at:], out_other),
+            "down": down,
         }
 
     first = on_first.astype(jnp.int32)[None]
-    middle, kept0, (all_late,) = layer_forward(
-        rows_in, entry, gain_pairs[0], first_weights, segs, on_first, first,
-        (all_own,), (first_hidden, first_out),
-    )
-    weights = (first_weights, second_weights(all_late))
-    entry = attention_input(middle, gain_pairs[1][0])
-    final, kept1, _ = layer_forward(
-        middle, entry, gain_pairs[1], weights[1], segs, on_first, first
-    )
+    other = swapped(first_own)
+    first_weights = weights_of(
+        first_own, other, (other, hidden_width), other[:, out_at:], first_down
+    )
+    middle, kept0 = layer_forward(
+        rows_in, entry, gain_pairs[0], first_weights, segs, on_first, first
+    )
+    middle, near = lax.optimization_barrier((middle, near))
+    second_own, second_down, entry = lax.optimization_barrier(
+        (
+            second_own, down_of(down_piece, *near), attention_input(middle, gain_pairs[1][0]),
+        )
+    )
+    out_other = swapped(second_own[:, out_at:])
+    qkv_other, second_own = lax.optimization_barrier(
+        (swapped(second_own[:, hidden_width:out_at]), second_own)
+    )
+    weights = (
+        first_weights,
+        weights_of(second_own, swapped(second_own), (qkv_other, 0), out_other, second_down),
+    )
+    final, kept1 = layer_forward(middle, entry, gain_pairs[1], weights[1], segs, on_first, first)
     upstream = by_core(cotangent[0, 0], cotangent[1, 0])
     attn_cols, out_cols, down_cols = (qkv_width // 2, half, ROW_GROUPS * half)
     hidden_end = FF_PAD + down_cols

time: 498 us -> 501 us (level)
  starting transfers between devices: 84.9 us -> 71.2 us
  waiting for transfers between devices: 198 us -> 209 us
  other arithmetic: 31.9 us -> 37.4 us
    ppermute x4 -> x8, waiting for transfers between devices: 74 us -> 26.9 us  [the longest x2 14.5 us: neighbours(): lax.ppermute(piece, 'wshard', w_up)]
    all_gather x1 -> x2, waiting for transfers between devices: 3.76 us -> 44.9 us  [gathered(): return lax.all_gather(piece, ('wshard', 'seq'), axis=0, tiled=True)]
    ppermute x20, starting transfers between devices: 33 us -> 16.7 us  [swapped(): return lax.ppermute(array, 'section', SWAP)]
    ppermute x9, waiting for transfers between devices: 62.8 us -> 50.5 us  [phase(): lax.ppermute(part(step), axis, route(step)).astype(jnp.float32)]
    ppermute x20, waiting for transfers between devices: 23.5 us -> 34.2 us  [swapped(): return lax.ppermute(array, 'section', SWAP)]
    ppermute x4, waiting for transfers between devices: 9.86 us -> 20.3 us  [to_previous(): return lax.ppermute(array, 'seq', [(i + 1, i) for i in range(SEQ_DEV - 1)])]
    ppermute x4, waiting for transfers between devices: 3.5 us -> 13.4 us  [to_next(): return lax.ppermute(array, 'seq', [(i, i + 1) for i in range(SEQ_DEV - 1)])]
    unnamed x180 -> x203, local copies, waits for them, and re-layouts: 24.3 us -> 31.9 us
  transfers between devices with their start and end apart: 50 -> 55, of which waited for: 29 -> 29; matrix products, arithmetic and copies ran while one was open for 12% -> 14% of each run, Pallas kernels for 11% -> 13%
where the time goes in v8:
time: 501 us; the launch traced here: 491 us
  waiting for transfers between devices  209 us (42%)
  Pallas kernels  87.3 us (17%)
  starting transfers between devices  71.2 us (14%)
  local copies, waits for them, and re-layouts  60.1 us (12%)
  other arithmetic  37.4 us (7%)
  between operations  16.1 us (3%)
  matrix products  9.73 us (2%)
    pallas_call x12, Pallas kernels, grid_call(): pl.pallas_call(kernel, grid_spec=pltpu.PrefetchScalarGridSpec(num_scalar_...  69.9 us
    ppermute x9, waiting for transfers between devices, phase(): lax.ppermute(part(step), axis, route(step)).astype(jnp.float32)  50.5 us
    all_gather x2, waiting for transfers between devices, gathered(): return lax.all_gather(piece, ('wshard', 'seq'), axis=0, tiled=True)  44.9 us
    ppermute x20, waiting for transfers between devices, swapped(): return lax.ppermute(array, 'section', SWAP)  34.2 us
    unnamed x203, local copies, waits for them, and re-layouts  31.9 us
    ppermute x4, waiting for transfers between devices, to_previous(): return lax.ppermute(array, 'seq', [(i + 1, i) for i in range(SEQ_DEV - 1)])  20.3 us
    ppermute x20, starting transfers between devices, swapped(): return lax.ppermute(array, 'section', SWAP)  16.7 us
    ppermute x9, starting transfers between devices, phase(): lax.ppermute(part(step), axis, route(step)).astype(jnp.float32)  15.5 us
  transfers between devices with their start and end apart: 55, of which 29 were waited for; matrix products, arithmetic and copies ran while one was open for 14% of the time, Pallas kernels for 13%

profile of v8, /device:TPU:1, one launch (start us, length us, event | category | flops | bytes accessed | tf_op | source)
XLA Modules:
  0.0 491.0 jit_solution(12949987082420812550)
XLA Ops:
  18.0 3.2 collective-permute-start.8
  23.7 3.8 collective-permute-done.9
  27.8 2.7 constant_dynamic-update-slice_fusion.21
  34.4 14.5 %collective-permute-done.3 = bf16[656,512]{1,0:T(8,128)(2,1)S(1)} collective-permute-done((bf16[656,512]{1,0:T(8,128)(2,1)S(1)}, bf16[656,512]{1,0:T(8,128)(2,1)S(1)}, u32[]{:S(2)}, u32[]{:S(2)}) %collective-permute-start.3) | collective-permute-done | bytes 671776 | tf_op jit(solution)/shard_map/ppermute | solution.py:641
  52.1 2.7 collective-permute-start.5
  56.0 9.0 %collective-permute-done.4 = bf16[656,256]{1,0:T(8,128)(2,1)} collective-permute-done((bf16[656,256]{1,0:T(8,128)(2,1)}, bf16[656,256]{1,0:T(8,128)(2,1)}, u32[]{:S(2)}, u32[]{:S(2)}) %collective-permute-start.4) | collective-permute-done | bytes 335904 | tf_op jit(solution)/shard_map/ppermute | solution.py:646
  68.1 4.7 collective-permute-done.6.down_other
  72.8 27.9 %all-gather.3.cloned.1.call-done.weight_own.gate_own.up_own = bf16[512,9472]{1,0:T(8,128)(2,1)} async-done(((bf16[8,9472]{1,0:T(8,128)(2,1)}), bf16[512,9472]{1,0:T(8,128)(2,1)}) %all-gather.3.cloned.1.call-update) | async-done | bytes 9699344 | tf_op jit(solution)/shard_map/all_gather | solution.py:630
  105.0 11.3 %collective-permute-done.10.weight_other.gate_other.up_other = bf16[512,9472]{1,0:T(8,128)(2,1)} collective-permute-done((bf16[512,9472]{1,0:T(8,128)(2,1)}, bf16[512,9472]{1,0:T(8,128)(2,1)}, u32[]{:S(2)}, u32[]{:S(2)}) %collective-permute-start.10) | collective-permute-done | bytes 9699360 | tf_op jit(solution)/shard_map/ppermute | solution.py:30
  116.4 3.8 copy-done
  120.1 4.4 qkv.2
  124.5 2.9 attend.2
  132.0 7.5 %hidden.2 = (f32[128,2688]{1,0:T(8,128)S(1)}, f32[128,2688]{1,0:T(8,128)S(1)}, bf16[128,2688]{1,0:T(8,128)(2,1)S(1)}, f32[128,1024]{1,0:T(8,128)S(1)}) custom-call(s32[1]{0:T(128)} %bitcast.first, bf16[128,512]{1,0:T(8,128)(2,1)S(1)} %get-tuple-element.274.own, bf16[128,512]{1,0:T(8,128)(2,1)S(1)} %get-tuple-element.273.other, ...), custom_call_target="tpu_custom_call" | custom-call | tf_op jit(solution)/shard_map/hidden/pallas_call | solution.py:180
  142.4 2.8 collective-permute-start.14
  150.9 3.4 collective-permute-done.13
  159.8 3.1 collective-permute-start.16
  164.2 4.6 collective-permute-done.16
  168.8 4.1 collective-permute-done.17
  173.0 17.0 %all-gather.5.cloned.1.call-done.weight_own.gate_own.up_own = bf16[512,9472]{1,0:T(8,128)(2,1)} async-done(((bf16[8,9472]{1,0:T(8,128)(2,1)}), bf16[512,9472]{1,0:T(8,128)(2,1)}) %all-gather.5.cloned.1.call-update) | async-done | bytes 9699344 | tf_op jit(solution)/shard_map/all_gather | solution.py:630
  192.9 5.3 %collective-permute-done.18.weight_other = bf16[512,3072]{1,0:T(8,128)(2,1)S(1)} collective-permute-done((bf16[512,3072]{1,0:T(8,128)(2,1)S(1)}, bf16[512,3072]{1,0:T(8,128)(2,1)S(1)}, u32[]{:S(2)}, u32[]{:S(2)}) %collective-permute-start.18) | collective-permute-done | bytes 3145760 | tf_op jit(solution)/shard_map/ppermute | solution.py:30
  201.2 4.2 qkv.3
  205.5 2.9 attend.3
  208.5 6.2 %collective-permute-done.19 = bf16[512,1024]{1,0:T(8,128)(2,1)S(1)} collective-permute-done((bf16[512,1024]{1,0:T(8,128)(2,1)S(1)}, bf16[512,1024]{1,0:T(8,128)(2,1)S(1)}, u32[]{:S(2)}, u32[]{:S(2)}) %collective-permute-start.19) | collective-permute-done | bytes 1048608 | tf_op jit(solution)/shard_map/ppermute | solution.py:30
  217.4 3.7 copy-done.50
  221.2 8.0 %hidden.3 = (f32[128,2688]{1,0:T(8,128)S(1)}, f32[128,2688]{1,0:T(8,128)S(1)}, bf16[128,2688]{1,0:T(8,128)(2,1)S(1)}, f32[128,1024]{1,0:T(8,128)S(1)}) custom-call(s32[1]{0:T(128)} %bitcast.first, bf16[128,512]{1,0:T(8,128)(2,1)S(1)} %get-tuple-element.254.own, bf16[128,512]{1,0:T(8,128)(2,1)S(1)} %get-tuple-element.253.other, ...), custom_call_target="tpu_custom_call" | custom-call | tf_op jit(solution)/shard_map/hidden/pallas_call | solution.py:180
  230.0 9.6 %hidden_back.2 = (bf16[128,2688]{1,0:T(8,128)(2,1)S(1)}, bf16[128,2688]{1,0:T(8,128)(2,1)S(1)}, f32[128,1024]{1,0:T(8,128)S(1)}) custom-call(s32[1]{0:T(128)} %bitcast.first, bf16[128,512]{1,0:T(8,128)(2,1)S(1)} %get-tuple-element.248.grad_own, bf16[128,512]{1,0:T(8,128)(2,1)S(1)} %get-tuple-element.249.grad_other, ...), custom_call_target="tpu_custom_call" | custom-call | tf_op jit(solution)/shard_map/hidden_back/pallas_call | solution.py:180
  244.4 3.7 hidden_grads.1.refs_0_
  248.1 3.4 copy-done.1
  262.1 3.5 copy-done.2
  265.7 5.8 %attend_back.2 = (bf16[128,1024]{1,0:T(8,128)(2,1)S(1)}, f32[128,2048]{1,0:T(8,128)S(1)}, bf16[64,2048]{1,0:T(8,128)(2,1)S(1)}, bf16[64,2048]{1,0:T(8,128)(2,1)S(1)}) custom-call(s32[128,1]{1,0:T(8,128)S(1)} %copy.38.query_seg, s32[1,256]{1,0:T(1,128)S(1)} %bitcast.135, bf16[256,3072]{1,0:T(8,128)(2,1)S(1)} %copy-done.10, f32[128,1024]{1,0:T(8,128)S(1)} %copy-done.49, ...), custom_call_target="tpu_custom_call" | custom-call | tf_op jit(solution)/shard_map/attend_back/pallas_call | solution.py:151
  277.0 7.6 %collective-permute-done.25 = bf16[64,2048]{1,0:T(8,128)(2,1)S(1)} collective-permute-done((bf16[64,2048]{1,0:T(8,128)(2,1)S(1)}, bf16[64,2048]{1,0:T(8,128)(2,1)S(1)}, u32[]{:S(2)}, u32[]{:S(2)}) %collective-permute-start.25) | collective-permute-done | bytes 262176 | tf_op jit(solution)/shard_map/ppermute | solution.py:167
  284.7 4.3 collective-permute-done.26
  293.2 4.0 qkv_back.2
  299.5 9.7 %hidden_back.3 = (bf16[128,2688]{1,0:T(8,128)(2,1)S(1)}, bf16[128,2688]{1,0:T(8,128)(2,1)S(1)}, f32[128,1024]{1,0:T(8,128)S(1)}) custom-call(s32[1]{0:T(128)} %bitcast.first, bf16[128,512]{1,0:T(8,128)(2,1)S(1)} %get-tuple-element.242.grad_own, bf16[128,512]{1,0:T(8,128)(2,1)S(1)} %get-tuple-element.243.grad_other, f32[128,2688]{1,0:T(8,128)S(1)} %copy-done.39, ...), custom_call_target="tpu_custom_call" | custom-call | tf_op jit(solution)/shard_map/hidden_back/pallas_call | solution.py:180
  314.3 5.8 %attend_back.3 = (bf16[128,1024]{1,0:T(8,128)(2,1)S(1)}, f32[128,2048]{1,0:T(8,128)S(1)}, bf16[64,2048]{1,0:T(8,128)(2,1)S(1)}, bf16[64,2048]{1,0:T(8,128)(2,1)S(1)}) custom-call(s32[128,1]{1,0:T(8,128)S(1)} %copy-done.37, s32[1,256]{1,0:T(1,128)S(1)} %bitcast.136, bf16[256,3072]{1,0:T(8,128)(2,1)S(1)} %copy-done.12, f32[128,1024]{1,0:T(8,128)S(1)} %copy-done.47, ...), custom_call_target="tpu_custom_call" | custom-call | tf_op jit(solution)/shard_map/attend_back/pallas_call | solution.py:151
  320.1 2.8 collective-permute-start.30
  324.3 6.4 %joint_grads.1.refs_7_ = bf16[1024,6400]{1,0:T(8,128)(2,1)} custom-call(bf16[3,128,1024]{2,1,0:T(8,128)(2,1)S(1)} %copy-done.14, bf16[3,128,1024]{2,1,0:T(8,128)(2,1)S(1)} %copy-done.22, bf16[3,128,1024]{2,1,0:T(8,128)(2,1)S(1)} %pad_maximum_fusion.7.refs_2_.refs_0_, bf16[3,128,1024]{2,1,0:T(8,128)(2,1)S(1)} %collective-permute-done.28.refs_1_.refs_3_, ...), custom_call_target="tpu_custom_call" | custom-call | tf_op jit(solution)/shard_map/joint_grads/pallas_call | solution.py:180
  330.7 8.0 %collective-permute-done.31 = bf16[64,2048]{1,0:T(8,128)(2,1)S(1)} collective-permute-done((bf16[64,2048]{1,0:T(8,128)(2,1)S(1)}, bf16[64,2048]{1,0:T(8,128)(2,1)S(1)}, u32[]{:S(2)}, u32[]{:S(2)}) %collective-permute-start.31) | collective-permute-done | bytes 262176 | tf_op jit(solution)/shard_map/ppermute | solution.py:171
  341.7 5.4 %qkv_back.3 = f32[128,1024]{1,0:T(8,128)S(1)} custom-call(s32[1]{0:T(128)} %bitcast.first, bf16[128,3072]{1,0:T(8,128)(2,1)S(1)} %pad_maximum_fusion.1.grad, bf16[512,9472]{1,0:T(8,128)(2,1)S(1)} %bitcast.128, bf16[512,9472]{1,0:T(8,128)(2,1)} %collective-permute-done.10.weight_other.gate_other.up_other), custom_call_target="tpu_custom_call" | custom-call | tf_op jit(solution)/shard_map/qkv_back/pallas_call | solution.py:180
  351.2 4.7 attn_grads.1
  377.3 15.4 %collective-permute-done.38 = bf16[16,16,2048]{2,1,0:T(8,128)(2,1)S(1)} collective-permute-done((bf16[16,16,2048]{2,1,0:T(8,128)(2,1)}, bf16[16,16,2048]{2,1,0:T(8,128)(2,1)S(1)}, u32[]{:S(2)}, u32[]{:S(2)}) %collective-permute-start.38) | collective-permute-done | bytes 1048608 | tf_op jit(solution)/shard_map/ppermute | solution.py:569
  392.7 23.7 %collective-permute-done.39 = bf16[16,16,2048]{2,1,0:T(8,128)(2,1)} collective-permute-done((bf16[16,16,2048]{2,1,0:T(8,128)(2,1)}, bf16[16,16,2048]{2,1,0:T(8,128)(2,1)}, u32[]{:S(2)}, u32[]{:S(2)}) %collective-permute-start.39) | collective-permute-done | bytes 1048608 | tf_op jit(solution)/shard_map/ppermute | solution.py:569
  419.1 3.1 collective-permute-start.41
  425.2 5.5 %collective-permute-done.41 = bf16[4,16,2048]{2,1,0:T(8,128)(2,1)S(1)} collective-permute-done((bf16[4,16,2048]{2,1,0:T(8,128)(2,1)S(1)}, bf16[4,16,2048]{2,1,0:T(8,128)(2,1)S(1)}, u32[]{:S(2)}, u32[]{:S(2)}) %collective-permute-start.41) | collective-permute-done | bytes 262176 | tf_op jit(solution)/shard_map/ppermute | solution.py:569
  430.7 6.0 %collective-permute-done.42 = bf16[4,16,2048]{2,1,0:T(8,128)(2,1)S(1)} collective-permute-done((bf16[4,16,2048]{2,1,0:T(8,128)(2,1)S(1)}, bf16[4,16,2048]{2,1,0:T(8,128)(2,1)S(1)}, u32[]{:S(2)}, u32[]{:S(2)}) %collective-permute-start.42) | collective-permute-done | bytes 262176 | tf_op jit(solution)/shard_map/ppermute | solution.py:569
  445.9 2.6 collective-permute-start.48
  449.5 12.5 %reduce-scatter.3.cloned.1.call-done = bf16[64,6400]{1,0:T(8,128)(2,1)} async-done(((bf16[1024,6400]{1,0:T(8,128)(2,1)}), bf16[64,6400]{1,0:T(8,128)(2,1)}) %reduce-scatter.3.cloned.1.call-update) | async-done | bytes 819216 | tf_op jit(solution)/shard_map/reduce_scatter | solution.py:413
  470.2 5.3 %collective-permute-done.36 = bf16[16,6400]{1,0:T(8,128)(2,1)S(1)} collective-permute-done((bf16[16,6400]{1,0:T(8,128)(2,1)S(1)}, bf16[16,6400]{1,0:T(8,128)(2,1)S(1)}, u32[]{:S(2)}, u32[]{:S(2)}) %collective-permute-start.36) | collective-permute-done | bytes 204832 | tf_op jit(solution)/shard_map/ppermute | solution.py:552
  (439 shorter events, 152.3 us)
Async XLA Ops:
  7.2 93.5 %all-gather.3.cloned.1.call-start = ((), (), s32[]{:S(2)}) async-start(), calls=%async_computation.2 | async-start | bytes 9850880 | tf_op jit(solution)/shard_map/all_gather | solution.py:630
  13.3 176.6 %all-gather.5.cloned.1.call-start = ((), (), s32[]{:S(2)}) async-start(), calls=%async_computation.3 | async-start | bytes 9850880 | tf_op jit(solution)/shard_map/all_gather | solution.py:630
  14.3 13.3 %collective-permute-start.1 = (bf16[656,512]{1,0:T(8,128)(2,1)}, bf16[656,512]{1,0:T(8,128)(2,1)}, u32[]{:S(2)}, u32[]{:S(2)}) collective-permute-start(bf16[656,512]{1,0:T(8,128)(2,1)} %select_bitcast_fusion), channel_id=1, source_target_pairs={{0,64},{64,0},{1,65},{65,1},{2,66},{66,2},{3,67},{67,3},{4,68},{68... | collective-permute-start | bytes 2015240 | tf_op jit(solution)/shard_map/ppermute | solution.py:30
  18.0 5.7 %collective-permute-start.8 = (bf16[64,1024]{1,0:T(8,128)(2,1)S(1)}, bf16[64,1024]{1,0:T(8,128)(2,1)S(1)}, u32[]{:S(2)}, u32[]{:S(2)}) collective-permute-start(bf16[64,1024]{1,0:T(8,128)(2,1)S(1)} %get-tuple-element.291), channel_id=1, source_target_pairs={{0,4},{4,8},{8,12},{12,16},{16,20},{20,24},{24,28},{28,32},{32,36}... | collective-permute-start | bytes 393224 | tf_op jit(solution)/shard_map/ppermute | solution.py:167
  21.2 6.3 %collective-permute-start.9 = (bf16[64,1024]{1,0:T(8,128)(2,1)S(1)}, bf16[64,1024]{1,0:T(8,128)(2,1)S(1)}, u32[]{:S(2)}, u32[]{:S(2)}) collective-permute-start(bf16[64,1024]{1,0:T(8,128)(2,1)S(1)} %get-tuple-element.292), channel_id=1, source_target_pairs={{4,0},{8,4},{12,8},{16,12},{20,16},{24,20},{28,24},{32,28},{36,32}... | collective-permute-start | bytes 393224 | tf_op jit(solution)/shard_map/ppermute | solution.py:171
  27.6 415.8 %reduce-scatter.5.cloned.1.call-start = ((), (), s32[]{:S(2)}) async-start(), calls=%async_computation.5 | async-start | bytes 9191424 | tf_op jit(solution)/shard_map/reduce_scatter | solution.py:413
  30.5 18.4 %collective-permute-start.3 = (bf16[656,512]{1,0:T(8,128)(2,1)S(1)}, bf16[656,512]{1,0:T(8,128)(2,1)S(1)}, u32[]{:S(2)}, u32[]{:S(2)}) collective-permute-start(bf16[656,512]{1,0:T(8,128)(2,1)S(1)} %get-tuple-element.164), channel_id=1, source_target_pairs={{0,1},{1,2},{2,3},{3,0},{4,5},{5,6},{6,7},{7,4},{8,9},{9,10},{10,1... | collective-permute-start | bytes 2015240 | tf_op jit(solution)/shard_map/ppermute | solution.py:641
  32.2 18.4 %collective-permute-start.2 = (bf16[656,512]{1,0:T(8,128)(2,1)S(1)}, bf16[656,512]{1,0:T(8,128)(2,1)S(1)}, u32[]{:S(2)}, u32[]{:S(2)}) collective-permute-start(bf16[656,512]{1,0:T(8,128)(2,1)S(1)} %get-tuple-element.164), channel_id=1, source_target_pairs={{1,0},{2,1},{3,2},{0,3},{5,4},{6,5},{7,6},{4,7},{9,8},{10,9},{11,1... | collective-permute-start | bytes 2015240 | tf_op jit(solution)/shard_map/ppermute | solution.py:641
  50.5 14.5 %collective-permute-start.4 = (bf16[656,256]{1,0:T(8,128)(2,1)}, bf16[656,256]{1,0:T(8,128)(2,1)}, u32[]{:S(2)}, u32[]{:S(2)}) collective-permute-start(bf16[656,256]{1,0:T(8,128)(2,1)} %slice.534), channel_id=1, source_target_pairs={{0,1},{1,2},{2,3},{3,0},{4,5},{5,6},{6,7},{7,4},{8,9},{9,10},{10,1... | collective-permute-start | bytes 1007624 | tf_op jit(solution)/shard_map/ppermute | solution.py:646
  52.1 12.9 %collective-permute-start.5 = (bf16[656,256]{1,0:T(8,128)(2,1)}, bf16[656,256]{1,0:T(8,128)(2,1)}, u32[]{:S(2)}, u32[]{:S(2)}) collective-permute-start(bf16[656,256]{1,0:T(8,128)(2,1)} %slice.535), channel_id=1, source_target_pairs={{1,0},{2,1},{3,2},{0,3},{5,4},{6,5},{7,6},{4,7},{9,8},{10,9},{11,1... | collective-permute-start | bytes 1007624 | tf_op jit(solution)/shard_map/ppermute | solution.py:647
  66.2 6.6 %collective-permute-start.6 = (bf16[2688,512]{1,0:T(8,128)(2,1)S(1)}, bf16[2688,512]{1,0:T(8,128)(2,1)}, u32[]{:S(2)}, u32[]{:S(2)}) collective-permute-start(bf16[2688,512]{1,0:T(8,128)(2,1)S(1)} %constant_dynamic-update-slice_fusion.19.down_own), channel_id=1, source_target_pairs={{0,64},{64,0},{1,65},{65,1},{2,66},{66,2},{3,67},{67,3},{4,68},{68... | collective-permute-start | bytes 8257544 | tf_op jit(solution)/shard_map/ppermute | solution.py:30
  100.7 15.7 %collective-permute-start.10 = (bf16[512,9472]{1,0:T(8,128)(2,1)}, bf16[512,9472]{1,0:T(8,128)(2,1)}, u32[]{:S(2)}, u32[]{:S(2)}) collective-permute-start(bf16[512,9472]{1,0:T(8,128)(2,1)} %all-gather.3.cloned.1.call-done.weight_own.gate_own.up_own), channel_id=1, source_target_pairs={{0,64},{64,0},{1,65},{65,1},{2,66},{66,2},{3,67},{67,3},{4,68},{68... | collective-permute-start | bytes 29097992 | tf_op jit(solution)/shard_map/ppermute | solution.py:30
  101.3 38.2 %collective-permute-start.11 = (bf16[656,512]{1,0:T(8,128)(2,1)}, bf16[656,512]{1,0:T(8,128)(2,1)}, u32[]{:S(2)}, u32[]{:S(2)}) collective-permute-start(bf16[656,512]{1,0:T(8,128)(2,1)} %get-tuple-element.75), channel_id=1, source_target_pairs={{0,1},{1,2},{2,3},{3,0},{4,5},{5,6},{6,7},{7,4},{8,9},{9,10},{10,1... | collective-permute-start | bytes 2015240 | tf_op jit(solution)/shard_map/ppermute | solution.py:641
  101.9 37.7 %collective-permute-start.12 = (bf16[656,512]{1,0:T(8,128)(2,1)}, bf16[656,512]{1,0:T(8,128)(2,1)}, u32[]{:S(2)}, u32[]{:S(2)}) collective-permute-start(bf16[656,512]{1,0:T(8,128)(2,1)} %get-tuple-element.75), channel_id=1, source_target_pairs={{1,0},{2,1},{3,2},{0,3},{5,4},{6,5},{7,6},{4,7},{9,8},{10,9},{11,1... | collective-permute-start | bytes 2015240 | tf_op jit(solution)/shard_map/ppermute | solution.py:641
  140.9 13.4 %collective-permute-start.13 = (bf16[656,256]{1,0:T(8,128)(2,1)S(1)}, bf16[656,256]{1,0:T(8,128)(2,1)S(1)}, u32[]{:S(2)}, u32[]{:S(2)}) collective-permute-start(bf16[656,256]{1,0:T(8,128)(2,1)S(1)} %slice.445), channel_id=1, source_target_pairs={{0,1},{1,2},{2,3},{3,0},{4,5},{5,6},{6,7},{7,4},{8,9},{9,10},{10,1... | collective-permute-start | bytes 1007624 | tf_op jit(solution)/shard_map/ppermute | solution.py:646
  142.4 11.9 %collective-permute-start.14 = (bf16[656,256]{1,0:T(8,128)(2,1)S(1)}, bf16[656,256]{1,0:T(8,128)(2,1)S(1)}, u32[]{:S(2)}, u32[]{:S(2)}) collective-permute-start(bf16[656,256]{1,0:T(8,128)(2,1)S(1)} %slice.446), channel_id=1, source_target_pairs={{1,0},{2,1},{3,2},{0,3},{5,4},{6,5},{7,6},{4,7},{9,8},{10,9},{11,1... | collective-permute-start | bytes 1007624 | tf_op jit(solution)/shard_map/ppermute | solution.py:647
  157.2 32.8 %collective-permute-start.15 = (bf16[2688,512]{1,0:T(8,128)(2,1)}, bf16[2688,512]{1,0:T(8,128)(2,1)}, u32[]{:S(2)}, u32[]{:S(2)}) collective-permute-start(bf16[2688,512]{1,0:T(8,128)(2,1)} %constant_dynamic-update-slice_fusion.16.down_own), channel_id=1, source_target_pairs={{0,64},{64,0},{1,65},{65,1},{2,66},{66,2},{3,67},{67,3},{4,68},{68... | collective-permute-start | bytes 8257544 | tf_op jit(solution)/shard_map/ppermute | solution.py:30
  159.8 9.0 %collective-permute-start.16 = (bf16[64,1024]{1,0:T(8,128)(2,1)S(1)}, bf16[64,1024]{1,0:T(8,128)(2,1)S(1)}, u32[]{:S(2)}, u32[]{:S(2)}) collective-permute-start(bf16[64,1024]{1,0:T(8,128)(2,1)S(1)} %get-tuple-element.271), channel_id=1, source_target_pairs={{0,4},{4,8},{8,12},{12,16},{16,20},{20,24},{24,28},{28,32},{32,36}... | collective-permute-start | bytes 393224 | tf_op jit(solution)/shard_map/ppermute | solution.py:167
  162.9 10.0 %collective-permute-start.17 = (bf16[64,1024]{1,0:T(8,128)(2,1)S(1)}, bf16[64,1024]{1,0:T(8,128)(2,1)S(1)}, u32[]{:S(2)}, u32[]{:S(2)}) collective-permute-start(bf16[64,1024]{1,0:T(8,128)(2,1)S(1)} %get-tuple-element.272), channel_id=1, source_target_pairs={{4,0},{8,4},{12,8},{16,12},{20,16},{24,20},{28,24},{32,28},{36,32}... | collective-permute-start | bytes 393224 | tf_op jit(solution)/shard_map/ppermute | solution.py:171
  192.1 6.0 %collective-permute-start.18 = (bf16[512,3072]{1,0:T(8,128)(2,1)S(1)}, bf16[512,3072]{1,0:T(8,128)(2,1)S(1)}, u32[]{:S(2)}, u32[]{:S(2)}) collective-permute-start(bf16[512,3072]{1,0:T(8,128)(2,1)S(1)} %slice.458), channel_id=1, source_target_pairs={{0,64},{64,0},{1,65},{65,1},{2,66},{66,2},{3,67},{67,3},{4,68},{68... | collective-permute-start | bytes 9437192 | tf_op jit(solution)/shard_map/ppermute | solution.py:30
  198.2 19.2 %collective-permute-start.20 = (bf16[512,9472]{1,0:T(8,128)(2,1)}, bf16[512,9472]{1,0:T(8,128)(2,1)S(1)}, u32[]{:S(2)}, u32[]{:S(2)}) collective-permute-start(bf16[512,9472]{1,0:T(8,128)(2,1)} %all-gather.5.cloned.1.call-done.weight_own.gate_own.up_own), channel_id=1, source_target_pairs={{0,64},{64,0},{1,65},{65,1},{2,66},{66,2},{3,67},{67,3},{4,68},{68... | collective-permute-start | bytes 29097992 | tf_op jit(solution)/shard_map/ppermute | solution.py:30
  200.6 14.1 %collective-permute-start.19 = (bf16[512,1024]{1,0:T(8,128)(2,1)S(1)}, bf16[512,1024]{1,0:T(8,128)(2,1)S(1)}, u32[]{:S(2)}, u32[]{:S(2)}) collective-permute-start(bf16[512,1024]{1,0:T(8,128)(2,1)S(1)} %slice.468), channel_id=1, source_target_pairs={{0,64},{64,0},{1,65},{65,1},{2,66},{66,2},{3,67},{67,3},{4,68},{68... | collective-permute-start | bytes 3145736 | tf_op jit(solution)/shard_map/ppermute | solution.py:30
  239.9 4.5 collective-permute-start.23
  253.3 208.8 %reduce-scatter.3.cloned.1.call-start = ((), (), s32[]{:S(2)}) async-start(), calls=%async_computation.4 | async-start | bytes 13926400 | tf_op jit(solution)/shard_map/reduce_scatter | solution.py:413
  271.5 13.2 %collective-permute-start.25 = (bf16[64,2048]{1,0:T(8,128)(2,1)S(1)}, bf16[64,2048]{1,0:T(8,128)(2,1)S(1)}, u32[]{:S(2)}, u32[]{:S(2)}) collective-permute-start(bf16[64,2048]{1,0:T(8,128)(2,1)S(1)} %get-tuple-element.100), channel_id=1, source_target_pairs={{0,4},{4,8},{8,12},{12,16},{16,20},{20,24},{24,28},{28,32},{32,36}... | collective-permute-start | bytes 786440 | tf_op jit(solution)/shard_map/ppermute | solution.py:167
  273.7 15.3 %collective-permute-start.26 = (bf16[64,2048]{1,0:T(8,128)(2,1)S(1)}, bf16[64,2048]{1,0:T(8,128)(2,1)S(1)}, u32[]{:S(2)}, u32[]{:S(2)}) collective-permute-start(bf16[64,2048]{1,0:T(8,128)(2,1)S(1)} %get-tuple-element.101), channel_id=1, source_target_pairs={{4,0},{8,4},{12,8},{16,12},{20,16},{24,20},{28,24},{32,28},{36,32}... | collective-permute-start | bytes 786440 | tf_op jit(solution)/shard_map/ppermute | solution.py:171
  276.2 38.0 %collective-permute-start.28 = (bf16[3,128,1024]{2,1,0:T(8,128)(2,1)S(1)}, bf16[3,128,1024]{2,1,0:T(8,128)(2,1)S(1)}, u32[]{:S(2)}, u32[]{:S(2)}) collective-permute-start(bf16[3,128,1024]{2,1,0:T(8,128)(2,1)S(1)} %pad_maximum_fusion.7.refs_2_.refs_0_), channel_id=1, source_target_pairs={{0,64},{64,0},{1,65},{65,1},{2,66},{66,2},{3,67},{67,3},{4,68},{68... | collective-permute-start | bytes 2359304 | tf_op jit(solution)/shard_map/ppermute | solution.py:30
  276.9 37.2 %collective-permute-start.29 = (bf16[128,2688]{1,0:T(8,128)(2,1)}, bf16[128,2688]{1,0:T(8,128)(2,1)S(1)}, u32[]{:S(2)}, u32[]{:S(2)}) collective-permute-start(bf16[128,2688]{1,0:T(8,128)(2,1)} %copy-done.44), channel_id=1, source_target_pairs={{0,64},{64,0},{1,65},{65,1},{2,66},{66,2},{3,67},{67,3},{4,68},{68... | collective-permute-start | bytes 2064392 | tf_op jit(solution)/shard_map/ppermute | solution.py:30
  291.6 32.6 %collective-permute-start.34 = (bf16[128,2048]{1,0:T(8,128)(2,1)}, bf16[128,2048]{1,0:T(8,128)(2,1)S(1)}, u32[]{:S(2)}, u32[]{:S(2)}) collective-permute-start(bf16[128,2048]{1,0:T(8,128)(2,1)} %get-tuple-element.190), channel_id=1, source_target_pairs={{0,64},{64,0},{1,65},{65,1},{2,66},{66,2},{3,67},{67,3},{4,68},{68... | collective-permute-start | bytes 1572872 | tf_op jit(solution)/shard_map/ppermute | solution.py:30
  309.5 4.7 collective-permute-start.27
  320.1 10.7 %collective-permute-start.30 = (bf16[64,2048]{1,0:T(8,128)(2,1)S(1)}, bf16[64,2048]{1,0:T(8,128)(2,1)S(1)}, u32[]{:S(2)}, u32[]{:S(2)}) collective-permute-start(bf16[64,2048]{1,0:T(8,128)(2,1)S(1)} %get-tuple-element.114), channel_id=1, source_target_pairs={{0,4},{4,8},{8,12},{12,16},{16,20},{20,24},{24,28},{28,32},{32,36}... | collective-permute-start | bytes 786440 | tf_op jit(solution)/shard_map/ppermute | solution.py:167
  322.9 15.9 %collective-permute-start.31 = (bf16[64,2048]{1,0:T(8,128)(2,1)S(1)}, bf16[64,2048]{1,0:T(8,128)(2,1)S(1)}, u32[]{:S(2)}, u32[]{:S(2)}) collective-permute-start(bf16[64,2048]{1,0:T(8,128)(2,1)S(1)} %get-tuple-element.115), channel_id=1, source_target_pairs={{4,0},{8,4},{12,8},{16,12},{20,16},{24,20},{28,24},{32,28},{36,32}... | collective-permute-start | bytes 786440 | tf_op jit(solution)/shard_map/ppermute | solution.py:171
  340.1 10.0 %collective-permute-start.33 = (bf16[128,2048]{1,0:T(8,128)(2,1)}, bf16[128,2048]{1,0:T(8,128)(2,1)}, u32[]{:S(2)}, u32[]{:S(2)}) collective-permute-start(bf16[128,2048]{1,0:T(8,128)(2,1)} %get-tuple-element.185), channel_id=1, source_target_pairs={{0,64},{64,0},{1,65},{65,1},{2,66},{66,2},{3,67},{67,3},{4,68},{68... | collective-permute-start | bytes 1572872 | tf_op jit(solution)/shard_map/ppermute | solution.py:30
  366.4 26.2 %collective-permute-start.38 = (bf16[16,16,2048]{2,1,0:T(8,128)(2,1)}, bf16[16,16,2048]{2,1,0:T(8,128)(2,1)S(1)}, u32[]{:S(2)}, u32[]{:S(2)}) collective-permute-start(bf16[16,16,2048]{2,1,0:T(8,128)(2,1)} %get-tuple-element.169), channel_id=1, source_target_pairs={{0,1},{1,2},{2,3},{3,0},{4,5},{5,6},{6,7},{7,4},{8,9},{9,10},{10,1... | collective-permute-start | bytes 3145736 | tf_op jit(solution)/shard_map/ppermute | solution.py:569
  367.7 48.7 %collective-permute-start.39 = (bf16[16,16,2048]{2,1,0:T(8,128)(2,1)}, bf16[16,16,2048]{2,1,0:T(8,128)(2,1)}, u32[]{:S(2)}, u32[]{:S(2)}) collective-permute-start(bf16[16,16,2048]{2,1,0:T(8,128)(2,1)} %get-tuple-element.171), channel_id=1, source_target_pairs={{0,2},{1,3},{2,0},{3,1},{4,6},{5,7},{6,4},{7,5},{8,10},{9,11},{10,... | collective-permute-start | bytes 3145736 | tf_op jit(solution)/shard_map/ppermute | solution.py:569
  370.3 46.1 %collective-permute-start.40 = (bf16[16,16,2048]{2,1,0:T(8,128)(2,1)S(1)}, bf16[16,16,2048]{2,1,0:T(8,128)(2,1)}, u32[]{:S(2)}, u32[]{:S(2)}) collective-permute-start(bf16[16,16,2048]{2,1,0:T(8,128)(2,1)S(1)} %get-tuple-element.170), channel_id=1, source_target_pairs={{0,3},{1,0},{2,1},{3,2},{4,7},{5,4},{6,5},{7,6},{8,11},{9,8},{10,9... | collective-permute-start | bytes 3145736 | tf_op jit(solution)/shard_map/ppermute | solution.py:569
  419.1 11.6 %collective-permute-start.41 = (bf16[4,16,2048]{2,1,0:T(8,128)(2,1)S(1)}, bf16[4,16,2048]{2,1,0:T(8,128)(2,1)S(1)}, u32[]{:S(2)}, u32[]{:S(2)}) collective-permute-start(bf16[4,16,2048]{2,1,0:T(8,128)(2,1)S(1)} %get-tuple-element.187), channel_id=1, source_target_pairs={{0,4},{4,8},{8,12},{12,0},{16,20},{20,24},{24,28},{28,16},{32,36},... | collective-permute-start | bytes 786440 | tf_op jit(solution)/shard_map/ppermute | solution.py:569
  422.2 14.5 %collective-permute-start.42 = (bf16[4,16,2048]{2,1,0:T(8,128)(2,1)S(1)}, bf16[4,16,2048]{2,1,0:T(8,128)(2,1)S(1)}, u32[]{:S(2)}, u32[]{:S(2)}) collective-permute-start(bf16[4,16,2048]{2,1,0:T(8,128)(2,1)S(1)} %get-tuple-element.189), channel_id=1, source_target_pairs={{0,8},{4,12},{8,0},{12,4},{16,24},{20,28},{24,16},{28,20},{32,40},... | collective-permute-start | bytes 786440 | tf_op jit(solution)/shard_map/ppermute | solution.py:569
  423.3 13.4 %collective-permute-start.43 = (bf16[4,16,2048]{2,1,0:T(8,128)(2,1)S(1)}, bf16[4,16,2048]{2,1,0:T(8,128)(2,1)S(1)}, u32[]{:S(2)}, u32[]{:S(2)}) collective-permute-start(bf16[4,16,2048]{2,1,0:T(8,128)(2,1)S(1)} %get-tuple-element.188), channel_id=1, source_target_pairs={{0,12},{4,0},{8,4},{12,8},{16,28},{20,16},{24,20},{28,24},{32,44},... | collective-permute-start | bytes 786440 | tf_op jit(solution)/shard_map/ppermute | solution.py:569
  436.8 6.4 %collective-permute-start.44 = (bf16[16,2048]{1,0:T(8,128)(2,1)S(1)}, bf16[16,2048]{1,0:T(8,128)(2,1)S(1)}, u32[]{:S(2)}, u32[]{:S(2)}) collective-permute-start(bf16[16,2048]{1,0:T(8,128)(2,1)S(1)} %get-tuple-element.236), channel_id=1, source_target_pairs={{0,16},{4,20},{8,24},{12,28},{16,32},{20,36},{24,40},{28,44},{32,4... | collective-permute-start | bytes 196616 | tf_op jit(solution)/shard_map/ppermute | solution.py:569
  437.4 5.9 %collective-permute-start.45 = (bf16[16,2048]{1,0:T(8,128)(2,1)S(1)}, bf16[16,2048]{1,0:T(8,128)(2,1)S(1)}, u32[]{:S(2)}, u32[]{:S(2)}) collective-permute-start(bf16[16,2048]{1,0:T(8,128)(2,1)S(1)} %get-tuple-element.238), channel_id=1, source_target_pairs={{0,32},{4,36},{8,40},{12,44},{16,48},{20,52},{24,56},{28,60},{32,0... | collective-permute-start | bytes 196616 | tf_op jit(solution)/shard_map/ppermute | solution.py:569
  441.4 37.3 %collective-permute-start.32 = (f32[128,1024]{1,0:T(8,128)S(1)}, f32[128,1024]{1,0:T(8,128)S(1)}, u32[]{:S(2)}, u32[]{:S(2)}) collective-permute-start(f32[128,1024]{1,0:T(8,128)S(1)} %get-tuple-element.153), channel_id=1, source_target_pairs={{0,64},{64,0},{1,65},{65,1},{2,66},{66,2},{3,67},{67,3},{4,68},{68... | collective-permute-start | bytes 1572872 | tf_op jit(solution)/shard_map/ppermute | solution.py:30
  444.6 19.9 %collective-permute-start.47 = (bf16[16,4224]{1,0:T(8,128)(2,1)S(1)}, bf16[16,4224]{1,0:T(8,128)(2,1)S(1)}, u32[]{:S(2)}, u32[]{:S(2)}) collective-permute-start(bf16[16,4224]{1,0:T(8,128)(2,1)S(1)} %get-tuple-element.195), channel_id=1, source_target_pairs={{0,1},{1,2},{2,3},{3,0},{4,5},{5,6},{6,7},{7,4},{8,9},{9,10},{10,1... | collective-permute-start | bytes 405512 | tf_op jit(solution)/shard_map/ppermute | solution.py:552
  445.9 21.1 %collective-permute-start.48 = (bf16[16,4224]{1,0:T(8,128)(2,1)S(1)}, bf16[16,4224]{1,0:T(8,128)(2,1)S(1)}, u32[]{:S(2)}, u32[]{:S(2)}) collective-permute-start(bf16[16,4224]{1,0:T(8,128)(2,1)S(1)} %get-tuple-element.197), channel_id=1, source_target_pairs={{0,2},{1,3},{2,0},{3,1},{4,6},{5,7},{6,4},{7,5},{8,10},{9,11},{10,... | collective-permute-start | bytes 405512 | tf_op jit(solution)/shard_map/ppermute | solution.py:552
  448.5 19.7 %collective-permute-start.49 = (bf16[16,4224]{1,0:T(8,128)(2,1)S(1)}, bf16[16,4224]{1,0:T(8,128)(2,1)S(1)}, u32[]{:S(2)}, u32[]{:S(2)}) collective-permute-start(bf16[16,4224]{1,0:T(8,128)(2,1)S(1)} %get-tuple-element.196), channel_id=1, source_target_pairs={{0,3},{1,0},{2,1},{3,2},{4,7},{5,4},{6,5},{7,6},{8,11},{9,8},{10,9... | collective-permute-start | bytes 405512 | tf_op jit(solution)/shard_map/ppermute | solution.py:552
  463.2 7.0 %collective-permute-start.35 = (bf16[16,6400]{1,0:T(8,128)(2,1)S(1)}, bf16[16,6400]{1,0:T(8,128)(2,1)S(1)}, u32[]{:S(2)}, u32[]{:S(2)}) collective-permute-start(bf16[16,6400]{1,0:T(8,128)(2,1)S(1)} %get-tuple-element.192), channel_id=1, source_target_pairs={{0,1},{1,2},{2,3},{3,0},{4,5},{5,6},{6,7},{7,4},{8,9},{9,10},{10,1... | collective-permute-start | bytes 614408 | tf_op jit(solution)/shard_map/ppermute | solution.py:552
  464.5 11.0 %collective-permute-start.36 = (bf16[16,6400]{1,0:T(8,128)(2,1)S(1)}, bf16[16,6400]{1,0:T(8,128)(2,1)S(1)}, u32[]{:S(2)}, u32[]{:S(2)}) collective-permute-start(bf16[16,6400]{1,0:T(8,128)(2,1)S(1)} %get-tuple-element.194), channel_id=1, source_target_pairs={{0,2},{1,3},{2,0},{3,1},{4,6},{5,7},{6,4},{7,5},{8,10},{9,11},{10,... | collective-permute-start | bytes 614408 | tf_op jit(solution)/shard_map/ppermute | solution.py:552
  467.0 8.5 %collective-permute-start.37 = (bf16[16,6400]{1,0:T(8,128)(2,1)S(1)}, bf16[16,6400]{1,0:T(8,128)(2,1)S(1)}, u32[]{:S(2)}, u32[]{:S(2)}) collective-permute-start(bf16[16,6400]{1,0:T(8,128)(2,1)S(1)} %get-tuple-element.193), channel_id=1, source_target_pairs={{0,3},{1,0},{2,1},{3,2},{4,7},{5,4},{6,5},{7,6},{8,11},{9,8},{10,9... | collective-permute-start | bytes 614408 | tf_op jit(solution)/shard_map/ppermute | solution.py:552
  (101 other events, 908.8 us)
Sparse Core Ops, SparseCore 0:
  13.5 87.1 all-gather.2
  104.0 85.8 all-gather.4
  253.4 91.0 reduce-scatter.4
  356.0 105.9 reduce-scatter.2
